TPU v7x, 128 devices: a whole 4x4x4 slice. The times are simulated.
128 devices in a mesh: context: 16 (over x_hi, z, core), expert: 8 (over y, x_lo).
Axes of the slice: x: 4 (x_hi: 2, x_lo: 2; x = x_hi * 2 + x_lo), y: 4, z: 4, core: 2. Of those that a mesh axis runs over, the one named last changes fastest.
Arguments:
- tokens: bfloat16 [8, 2048, 768], P('expert', 'context'), may hold values from -6 to 6
- gain_one: float32 [768], replicated, may hold values from 0.5 to 1.5
- w_query: bfloat16 [768, 768], replicated, may hold values from -0.21875 to 0.21875
- w_key: bfloat16 [768, 768], replicated, may hold values from -0.21875 to 0.21875
- w_value: bfloat16 [768, 768], replicated, may hold values from -0.21875 to 0.21875
- w_out: bfloat16 [768, 768], replicated, may hold values from -1.75 to 1.75
- rel_table: float32 [12, 32], replicated, may hold values from -4 to 4
- gain_two: float32 [768], replicated, may hold values from 0.5 to 1.5
- w_router: bfloat16 [768, 8], replicated, may hold values from -0.15625 to 0.15625
- expert_in: bfloat16 [8, 768, 3072], P('expert', None, 'context'), may hold values from -0.21875 to 0.21875
- expert_out: bfloat16 [8, 768, 3072], P('expert', None, 'context'), may hold values from -0.109375 to 0.109375
- routes: int32 [8, 2048, 2], P('expert', 'context'), may hold values from 0 to 7, all different within a row; in each aligned block of 128 rows (0 to 127, 128 to 255, ..., all dimensions but the last counted through in order) at most 48 rows name the same one
- cotangent: bfloat16 [8, 2048, 768], P('expert', 'context'), may hold values from -6 to 6
Outputs:
- block_out: bfloat16 [8, 2048, 768], P('expert', 'context')
- grad_tokens: float32 [8, 2048, 768], P('expert', 'context')
- grad_gain_one: float32 [768], replicated
- grad_query: float32 [768, 768], replicated
- grad_key: float32 [768, 768], replicated
- grad_value: float32 [768, 768], replicated
- grad_w_out: float32 [768, 768], replicated
- grad_rel_table: float32 [12, 32], replicated
- grad_gain_two: float32 [768], replicated
- grad_router: float32 [768, 8], replicated
- grad_expert_in: float32 [8, 768, 3072], P('expert', None, 'context')
- grad_expert_out: float32 [8, 768, 3072], P('expert', None, 'context')
Inputs may be any that keep to these rules, and one draw needn't show every extreme that they name: `routes`: A token's two experts differ. Within the rows of one device (aligned blocks of 128 rows of the flattened sequences and positions) no expert is named by more than 48 tokens, and in every draw some block has an expert named exactly 48 times.
All inputs are finite; a program needn't handle non-finite values.
Results may differ from a plain program's by a relative error of at most 0.022.
Values may be sent and summed in bfloat16 or wider, within the bound.
No kernel may reach another device: no remote copies, remote signals or barrier semaphores. Data moves between devices by JAX's collectives and lax.ppermute only.
A program may use at most 128 MiB of HBM per device.

v0:
```python
import math

import jax
import jax.numpy as jnp
from jax import lax
from jax.sharding import PartitionSpec as P

MAX_DIST = 128


EPSILON = 1e-06
NEG_LARGE = -1e30


def in_one_piece(arrays, axis, dim, along):
    widths = [a.shape[along] for a in arrays]
    both = jnp.concatenate(arrays, axis=along)
    filled = lax.all_gather(both, axis, axis=dim, tiled=True)
    return tuple(jnp.split(filled, [sum(widths[:k]) for k in range(1, len(widths))], axis=along))


def turned_gather(arrays, axis, dims):
    turned = [jnp.moveaxis(a, dim, 0) for a, dim in zip(arrays, dims)]
    widths = [t[0].size for t in turned]
    both = jnp.concatenate([t.reshape(-1, w) for t, w in zip(turned, widths)], axis=1)
    filled = lax.all_gather(both, axis, axis=0, tiled=True)
    pieces = jnp.split(filled, [sum(widths[:k]) for k in range(1, len(widths))], axis=1)
    return tuple(
        (
            jnp.moveaxis(b.reshape(-1, *t.shape[1:]), 0, dim)
            for b, t, dim in zip(pieces, turned, dims)
        )
    )


def gelu_tanh(values):
    return (
        0.5
        * values
        * (1.0 + jnp.tanh(0.7978845608 * (values + 0.044715 * values * values * values)))
    )


def relative_bucket(distance, buckets, far_reach):
    exact_span = buckets // 2
    near_dist = jnp.maximum(distance, 0)
    result = jnp.full(near_dist.shape, exact_span, jnp.int32)
    for level_step in range(1, buckets - exact_span):
        threshold = int(
            math.ceil(
                exact_span * (far_reach / exact_span) ** (level_step / (buckets - exact_span))
            )
        )
        result = result + (near_dist >= threshold).astype(jnp.int32)
    return jnp.where(near_dist < exact_span, near_dist, result)


def rms_scale(values):
    return lax.rsqrt(jnp.mean(values * values, axis=-1, keepdims=True) + EPSILON)


def norm_back(values, inv_root, gain_vec, grad_normed):
    weighted = grad_normed * gain_vec
    cubed = inv_root * inv_root * inv_root
    grad_values = inv_root * weighted - values * cubed * jnp.mean(
        weighted * values, axis=-1, keepdims=True
    )
    grad_gain = jnp.sum(grad_normed * values * inv_root, axis=0)
    return (grad_values, grad_gain)


def shards(
    tokens,
    gain_one,
    w_query,
    w_key,
    w_value,
    w_out,
    rel_table,
    gain_two,
    w_router,
    expert_in,
    expert_out,
    routes,
    cotangent,
):
    local_rows = tokens.shape[1]
    width = tokens.shape[2]
    head_count = rel_table.shape[0]
    bucket_count = rel_table.shape[1]
    head_size = width // head_count
    score_scale = head_size ** (-0.5)
    inputs = tokens[0].astype(jnp.float32)
    grad_out = cotangent[0].astype(jnp.float32)
    routes_here = routes[0]
    expert_count = lax.axis_size("expert")
    capacity = 3 * local_rows // expert_count
    query_pos = lax.axis_index("context") * local_rows + jnp.arange(local_rows, dtype=jnp.int32)
    first_query = query_pos[0]
    last_query = query_pos[local_rows - 1]
    bucket_ids = jnp.arange(bucket_count, dtype=jnp.int32)

    def block_scores(query_blk, key_blk, rows_pos, cols_pos):
        distance = rows_pos[:, None] - cols_pos[None, :]
        allowed = distance >= 0
        onehot = (
            relative_bucket(distance, bucket_count, MAX_DIST)[:, :, None] == bucket_ids
        ).astype(jnp.float32)
        raw_scores = (
            jnp.einsum("qhd,khd->hqk", query_blk, key_blk, preferred_element_type=jnp.float32)
            * score_scale
        )
        bias_terms = jnp.einsum("qkb,hb->hqk", onehot, rel_table)
        scores = jnp.where(allowed, raw_scores + bias_terms, NEG_LARGE)
        return (scores, allowed, onehot)

    def grad_block(query_blk, grad_blk, lse_blk, delta_blk, key_blk, value_blk, rows_pos, cols_pos):
        scores, allowed, onehot = block_scores(query_blk, key_blk, rows_pos, cols_pos)
        probabilities = jnp.where(allowed, jnp.exp(scores - lse_blk[:, :, None]), 0.0)
        grad_probs = jnp.einsum(
            "qhd,khd->hqk", grad_blk, value_blk, preferred_element_type=jnp.float32
        )
        grad_scores = (probabilities * (grad_probs - delta_blk[:, :, None])).astype(jnp.bfloat16)
        part_query = (
            jnp.einsum("hqk,khd->qhd", grad_scores, key_blk, preferred_element_type=jnp.float32)
            * score_scale
        )
        part_key = (
            jnp.einsum("hqk,qhd->khd", grad_scores, query_blk, preferred_element_type=jnp.float32)
            * score_scale
        )
        part_value = jnp.einsum(
            "hqk,qhd->khd",
            probabilities.astype(jnp.bfloat16),
            grad_blk,
            preferred_element_type=jnp.float32,
        )
        part_bias = jnp.einsum("hqk,qkb->hb", grad_scores.astype(jnp.float32), onehot)
        return (part_query, part_key, part_value, part_bias)

    scale_one = rms_scale(inputs)
    normed = (inputs * scale_one * gain_one).astype(jnp.bfloat16)
    queries = jnp.dot(normed, w_query, preferred_element_type=jnp.float32).astype(jnp.bfloat16)
    keys_here = jnp.dot(normed, w_key, preferred_element_type=jnp.float32).astype(jnp.bfloat16)
    values_here = jnp.dot(normed, w_value, preferred_element_type=jnp.float32).astype(jnp.bfloat16)
    query_heads = queries.reshape(local_rows, head_count, head_size)
    key_heads = keys_here.reshape(local_rows, head_count, head_size)
    value_heads = values_here.reshape(local_rows, head_count, head_size)
    start_state = (
        jnp.full((head_count, local_rows), NEG_LARGE, jnp.float32),
        jnp.zeros((head_count, local_rows), jnp.float32),
        jnp.zeros((local_rows, head_count, head_size), jnp.float32),
    )
    keys_piece, values_piece = in_one_piece((keys_here, values_here), "context", 0, 1)
    piece_rows = keys_piece.shape[0]
    sub_count = piece_rows // local_rows
    offsets = jnp.arange(sub_count, dtype=jnp.int32) * local_rows

    def one_block(carried, block_item):
        key_blk, value_blk, offset = block_item

        def one_live(state):
            run_max, run_sum, accum = state
            cols_pos = offset + jnp.arange(local_rows, dtype=jnp.int32)
            scores, allowed, onehot = block_scores(query_heads, key_blk, query_pos, cols_pos)
            new_max = jnp.maximum(run_max, jnp.max(scores, axis=2))
            weights = jnp.where(allowed, jnp.exp(scores - new_max[:, :, None]), 0.0)
            factor = jnp.exp(run_max - new_max)
            run_sum = run_sum * factor + jnp.sum(weights, axis=2)
            accum = accum * factor.T[:, :, None] + jnp.einsum(
                "hqk,khd->qhd",
                weights.astype(jnp.bfloat16),
                value_blk,
                preferred_element_type=jnp.float32,
            )
            return (new_max, run_sum, accum)

        def one_dead(state):
            return state

        return (lax.cond(offset <= last_query, one_live, one_dead, carried), None)

    carried, unused = lax.scan(
        one_block,
        start_state,
        (
            keys_piece.reshape(sub_count, local_rows, head_count, head_size),
            values_piece.reshape(sub_count, local_rows, head_count, head_size),
            offsets,
        ),
    )
    run_max, run_sum, accum = carried
    attended = accum / run_sum.T[:, :, None]
    log_total = run_max + jnp.log(run_sum)
    attended_low = attended.reshape(local_rows, width).astype(jnp.bfloat16)
    mixed_sum = inputs + jnp.dot(attended_low, w_out, preferred_element_type=jnp.float32)
    scale_two = rms_scale(mixed_sum)
    second = (mixed_sum * scale_two * gain_two).astype(jnp.bfloat16)
    logits = jnp.dot(second, w_router, preferred_element_type=jnp.float32)
    expert_ids = jnp.arange(expert_count, dtype=jnp.int32)
    route_onehot = (routes_here[:, :, None] == expert_ids).astype(jnp.float32)
    chosen = jnp.einsum("tke,te->tk", route_onehot, logits)
    chosen_exp = jnp.exp(chosen - jnp.max(chosen, axis=1, keepdims=True))
    gate_probs = chosen_exp / jnp.sum(chosen_exp, axis=1, keepdims=True)
    pair_expert = routes_here.reshape(-1)
    pair_onehot = (pair_expert[:, None] == expert_ids[None, :]).astype(jnp.int32)
    ranks = jnp.cumsum(pair_onehot, axis=0) - pair_onehot
    slots = jnp.sum(ranks * pair_onehot, axis=1)
    destination = pair_expert * capacity + slots
    pair_total = 2 * local_rows
    source_pair = (
        jnp.full((expert_count * capacity,), pair_total, jnp.int32)
        .at[destination]
        .set(jnp.arange(pair_total, dtype=jnp.int32))
    )
    source_token = source_pair // 2
    padded = jnp.concatenate([second, jnp.zeros((1, width), jnp.bfloat16)], axis=0)
    send_rows = padded[source_token].reshape(expert_count, capacity, width)
    full_in, full_out = turned_gather((expert_in, expert_out), "context", (2, 2))
    weight_in = full_in[0]
    weight_out = full_out[0]
    hidden_units = weight_in.shape[1]
    received = lax.all_to_all(send_rows, "expert", split_axis=0, concat_axis=0, tiled=True)
    source_count = received.shape[0]
    item_count = received.shape[1]
    rows_flat = received.reshape(-1, width)
    pre_act = jnp.dot(rows_flat, weight_in, preferred_element_type=jnp.float32)
    act_low = gelu_tanh(pre_act).astype(jnp.bfloat16)
    produced = jnp.einsum(
        "rf,df->rd", act_low, weight_out, preferred_element_type=jnp.float32
    ).astype(jnp.bfloat16)
    received_rows, pre_all, produced = (
        received,
        pre_act.reshape(source_count, item_count, hidden_units),
        produced.reshape(source_count, item_count, width),
    )
    returned = lax.all_to_all(produced, "expert", split_axis=0, concat_axis=0, tiled=True)
    picked = (
        returned.reshape(-1, width)[destination].reshape(local_rows, 2, width).astype(jnp.float32)
    )
    block_out = (mixed_sum + jnp.sum(gate_probs[:, :, None] * picked, axis=1)).astype(jnp.bfloat16)
    grad_gates = jnp.sum(picked * grad_out[:, None, :], axis=2)
    grad_chosen = gate_probs * (
        grad_gates - jnp.sum(gate_probs * grad_gates, axis=1, keepdims=True)
    )
    grad_logits = jnp.einsum("tk,tke->te", grad_chosen, route_onehot)
    slot_grads = (
        (gate_probs[:, :, None] * grad_out[:, None, :])
        .astype(jnp.bfloat16)
        .reshape(pair_total, width)
    )
    padded_grads = jnp.concatenate([slot_grads, jnp.zeros((1, width), jnp.bfloat16)], axis=0)
    grad_send = padded_grads[source_pair].reshape(expert_count, capacity, width)
    grad_received = lax.all_to_all(grad_send, "expert", split_axis=0, concat_axis=0, tiled=True)
    grad_rows = grad_received.reshape(-1, width)
    rows_flat = received_rows.reshape(-1, width)
    pre_flat = pre_all.reshape(-1, hidden_units)
    act_low = gelu_tanh(pre_flat).astype(jnp.bfloat16)
    grad_act = jnp.dot(grad_rows, weight_out, preferred_element_type=jnp.float32)
    unused_value, gelu_pull = jax.vjp(gelu_tanh, pre_flat)
    grad_pre = gelu_pull(grad_act)[0].astype(jnp.bfloat16)
    grad_weight_in = jnp.einsum(
        "rd,rf->df", rows_flat, grad_pre, preferred_element_type=jnp.float32
    )
    grad_weight_out = jnp.einsum(
        "rd,rf->df", grad_rows, act_low, preferred_element_type=jnp.float32
    )
    grad_rows_in = jnp.einsum(
        "rf,df->rd", grad_pre, weight_in, preferred_element_type=jnp.float32
    ).astype(jnp.bfloat16)
    returned_grads = lax.all_to_all(
        grad_rows_in.reshape(expert_count, capacity, width),
        "expert",
        split_axis=0,
        concat_axis=0,
        tiled=True,
    )
    shard_in, shard_out = (
        lax.psum_scatter(
            grad_weight_in.astype(jnp.bfloat16), "context", scatter_dimension=1, tiled=True
        ).astype(jnp.float32),
        lax.psum_scatter(
            grad_weight_out.astype(jnp.bfloat16), "context", scatter_dimension=1, tiled=True
        ).astype(jnp.float32),
    )
    grad_second = jnp.sum(
        returned_grads.reshape(-1, width)[destination]
        .reshape(local_rows, 2, width)
        .astype(jnp.float32),
        axis=1,
    )
    grad_second = grad_second + jnp.dot(grad_logits, w_router.astype(jnp.float32).T)
    grad_router = jnp.dot(second.astype(jnp.float32).T, grad_logits)
    grad_mixed, grad_gain_two = norm_back(mixed_sum, scale_two, gain_two, grad_second)
    grad_mixed = grad_mixed + grad_out
    grad_branch = grad_mixed.astype(jnp.bfloat16)
    grad_w_out = jnp.dot(attended_low.T, grad_branch, preferred_element_type=jnp.float32)
    grad_attended = jnp.dot(grad_branch, w_out.T, preferred_element_type=jnp.float32).astype(
        jnp.bfloat16
    )
    grad_heads = grad_attended.reshape(local_rows, head_count, head_size)
    row_delta = jnp.sum(grad_heads.astype(jnp.float32) * attended, axis=2).T
    zero_heads = jnp.zeros((local_rows, head_count, head_size), jnp.float32)
    zero_bias = jnp.zeros((head_count, bucket_count), jnp.float32)
    keys_piece, values_piece = in_one_piece((keys_here, values_here), "context", 0, 1)
    piece_rows = keys_piece.shape[0]
    sub_count = piece_rows // local_rows

    def query_step(running, block_item):
        key_blk, value_blk, offset = block_item

        def query_live(state):
            cols_pos = offset + jnp.arange(local_rows, dtype=jnp.int32)
            part_query, unused_key, unused_val, part_bias = grad_block(
                query_heads,
                grad_heads,
                log_total,
                row_delta,
                key_blk,
                value_blk,
                query_pos,
                cols_pos,
            )
            return (state[0] + part_query, state[1] + part_bias)

        def query_dead(state):
            return state

        return (lax.cond(offset <= last_query, query_live, query_dead, running), None)

    offsets = jnp.arange(sub_count, dtype=jnp.int32) * local_rows
    running, unused = lax.scan(
        query_step,
        (zero_heads, zero_bias),
        (
            keys_piece.reshape(sub_count, local_rows, head_count, head_size),
            values_piece.reshape(sub_count, local_rows, head_count, head_size),
            offsets,
        ),
    )
    grad_query_sum, grad_bias = running
    stats_lse, stats_delta = in_one_piece((log_total.T, row_delta.T), "context", 0, 1)
    query_piece, grad_piece = in_one_piece((queries, grad_attended), "context", 0, 1)
    piece_rows = query_piece.shape[0]
    sub_count = piece_rows // local_rows

    def key_step(running, block_item):
        query_blk, grad_blk, offset = block_item

        def key_live(state):
            rows_pos = offset + jnp.arange(local_rows, dtype=jnp.int32)
            lse_blk = lax.dynamic_slice_in_dim(stats_lse, offset, local_rows, 0).T
            delta_blk = lax.dynamic_slice_in_dim(stats_delta, offset, local_rows, 0).T
            unused_query, part_key, part_value, unused_bias = grad_block(
                query_blk, grad_blk, lse_blk, delta_blk, key_heads, value_heads, rows_pos, query_pos
            )
            return (state[0] + part_key, state[1] + part_value)

        def key_dead(state):
            return state

        return (lax.cond(offset + local_rows - 1 >= first_query, key_live, key_dead, running), None)

    offsets = jnp.arange(sub_count, dtype=jnp.int32) * local_rows
    running, unused = lax.scan(
        key_step,
        (zero_heads, zero_heads),
        (
            query_piece.reshape(sub_count, local_rows, head_count, head_size),
            grad_piece.reshape(sub_count, local_rows, head_count, head_size),
            offsets,
        ),
    )
    grad_key_sum, grad_value_sum = running
    grad_query_low = grad_query_sum.reshape(local_rows, width).astype(jnp.bfloat16)
    grad_key_low = grad_key_sum.reshape(local_rows, width).astype(jnp.bfloat16)
    grad_value_low = grad_value_sum.reshape(local_rows, width).astype(jnp.bfloat16)
    grad_w_query = jnp.dot(normed.T, grad_query_low, preferred_element_type=jnp.float32)
    grad_w_key = jnp.dot(normed.T, grad_key_low, preferred_element_type=jnp.float32)
    grad_w_value = jnp.dot(normed.T, grad_value_low, preferred_element_type=jnp.float32)
    grad_normed = jnp.dot(grad_query_low, w_query.T, preferred_element_type=jnp.float32)
    grad_normed = grad_normed + jnp.dot(grad_key_low, w_key.T, preferred_element_type=jnp.float32)
    grad_normed = grad_normed + jnp.dot(
        grad_value_low, w_value.T, preferred_element_type=jnp.float32
    )
    grad_inputs_part, grad_gain_one = norm_back(inputs, scale_one, gain_one, grad_normed)
    grad_inputs = grad_mixed + grad_inputs_part
    summed = lax.psum(
        (
            grad_w_query,
            grad_w_key,
            grad_w_value,
            grad_w_out,
            grad_bias,
            grad_router,
            grad_gain_one,
            grad_gain_two,
        ),
        ("context", "expert"),
    )
    return (
        block_out[None],
        grad_inputs[None],
        summed[6],
        summed[0],
        summed[1],
        summed[2],
        summed[3],
        summed[4],
        summed[7],
        summed[5],
        shard_in[None],
        shard_out[None],
    )


def solution(mesh):
    return jax.shard_map(
        shards,
        mesh=mesh,
        in_specs=(
            P("expert", "context", None),
            P(),
            P(),
            P(),
            P(),
            P(),
            P(),
            P(),
            P(),
            P("expert", None, "context"),
            P("expert", None, "context"),
            P("expert", "context", None),
            P("expert", "context", None),
        ),
        out_specs=(
            P("expert", "context", None),
            P("expert", "context", None),
            P(),
            P(),
            P(),
            P(),
            P(),
            P(),
            P(),
            P(),
            P("expert", None, "context"),
            P("expert", None, "context"),
        ),
        check_vma=False,
    )
```

profile of v0, /device:TPU:1, one launch (start us, length us, event | category | flops | bytes accessed | tf_op | source)
XLA Modules:
  0.0 868.9 jit_solution(13941749096710492495)
XLA Ops:
  22.9 58.9 %all-gather.4.cloned.1.call-done = bf16[2048,1536]{1,0:T(8,128)(2,1)} async-done(((bf16[128,1536]{1,0:T(8,128)(2,1)}), bf16[2048,1536]{1,0:T(8,128)(2,1)}) %all-gather.4.cloned.1.call-update) | async-done | bytes 6291472 | tf_op jit(solution)/shard_map/all_gather | solution.py:18
  81.8 5.9 fusion.210
  108.3 39.4 %while.45 = (s32[]{:T(128)}, f32[12,128]{1,0:T(8,128)S(1)}, f32[12,128]{1,0:T(8,128)S(1)}, f32[128,12,64]{0,2,1:T(8,128)S(1)}, s32[16]{0:T(128)S(1)}, /*index=5*...) while((s32[]{:T(128)}, f32[12,128]{1,0:T(8,128)S(1)}, ...), condition=%wide.region_6.7_spmd.clone, body=%wide.region_1.6_spmd.clone.sunk | while | flops 66441988 | bytes 7313719 | solution.py:183
  168.6 6.6 fusion.158
  176.6 7.8 fusion.154
  191.0 7.4 fusion.161
  208.3 5.4 all-to-all-done.1
  231.1 6.8 convolution_convert_fusion.1
  237.9 7.7 convolution_convert_fusion
  249.0 41.8 %while.46 = (s32[]{:T(128)}, f32[128,12,64]{0,2,1:T(8,128)S(1)}, f32[12,32]{1,0:T(8,128)S(1)}, s32[16]{0:T(128)S(1)}, s32[]{:T(128)}, /*index=5*/bf16[16,128,12,...) while((s32[]{:T(128)}, f32[128,12,64]{0,2,1:T(8,128)S(1)}, ...), condition=%wide.region_23.24_spmd.clone, body=%wide.region_20.23_spmd.clone.sunk | while | flops 104317568 | bytes 6346695 | solution.py:332
  250.9 6.0 conditional.10
  258.7 6.0 conditional.10
  290.9 169.2 %all_gather.16 = f32[2048,24]{0,1:T(8,128)S(1)} all-gather(f32[128,24]{0,1:T(8,128)S(1)} %pad_maximum_fusion.3), channel_id=1, replica_groups=mesh['context'=16,'expert'=8] {'context'}, dimensions={0}, use_global_device_ids=true | all-gather | bytes 208896 | tf_op jit(solution)/shard_map/all_gather | solution.py:18
  464.7 6.4 fusion.209
  493.1 183.7 %while.47 = (s32[]{:T(128)}, f32[128,12,64]{0,2,1:T(8,128)}, f32[128,12,64]{0,2,1:T(8,128)}, s32[16]{0:T(128)S(1)}, s32[]{:T(128)}, /*index=5*/bf16[16,128,12,64...) while((s32[]{:T(128)}, f32[128,12,64]{0,2,1:T(8,128)}, ...), condition=%wide.region_27.28_spmd.clone, body=%wide.region_24.27_spmd.clone.sunk | while | flops 116670720 | bytes 7220609 | solution.py:365
  496.8 10.4 %conditional.11 = ((f32[128,12,64]{0,2,1:T(8,128)}, f32[128,12,64]{0,2,1:T(8,128)})) conditional(s32[]{:T(128)} %convert_element_type.766, (f32[128,12,64]{0,2,1:T(8,128)}, f32[128,12,64]{0,2,1:T(8,128)}) %tuple.156, (s32[]{:T(128)}, s32[]{:T(128)}, bf16[16,128,12,64]{1,3,2,0:T(8,128)(2,1)}, s32[]{:T(128)}, bf16[128,12,64]{0,2,1:T(8,128)(2,1)}, ...), branch_computations={%region_25.25_spmd, %region_26.26_spmd} | conditional | flops 116670720 | bytes 7219654 | solution.py:362
  509.0 10.3 %conditional.11 = ((f32[128,12,64]{0,2,1:T(8,128)}, f32[128,12,64]{0,2,1:T(8,128)})) conditional(s32[]{:T(128)} %convert_element_type.766, (f32[128,12,64]{0,2,1:T(8,128)}, f32[128,12,64]{0,2,1:T(8,128)}) %tuple.156, (s32[]{:T(128)}, s32[]{:T(128)}, bf16[16,128,12,64]{1,3,2,0:T(8,128)(2,1)}, s32[]{:T(128)}, bf16[128,12,64]{0,2,1:T(8,128)(2,1)}, ...), branch_computations={%region_25.25_spmd, %region_26.26_spmd} | conditional | flops 116670720 | bytes 7219654 | solution.py:362
  521.1 10.3 %conditional.11 = ((f32[128,12,64]{0,2,1:T(8,128)}, f32[128,12,64]{0,2,1:T(8,128)})) conditional(s32[]{:T(128)} %convert_element_type.766, (f32[128,12,64]{0,2,1:T(8,128)}, f32[128,12,64]{0,2,1:T(8,128)}) %tuple.156, (s32[]{:T(128)}, s32[]{:T(128)}, bf16[16,128,12,64]{1,3,2,0:T(8,128)(2,1)}, s32[]{:T(128)}, bf16[128,12,64]{0,2,1:T(8,128)(2,1)}, ...), branch_computations={%region_25.25_spmd, %region_26.26_spmd} | conditional | flops 116670720 | bytes 7219654 | solution.py:362
  533.2 10.3 %conditional.11 = ((f32[128,12,64]{0,2,1:T(8,128)}, f32[128,12,64]{0,2,1:T(8,128)})) conditional(s32[]{:T(128)} %convert_element_type.766, (f32[128,12,64]{0,2,1:T(8,128)}, f32[128,12,64]{0,2,1:T(8,128)}) %tuple.156, (s32[]{:T(128)}, s32[]{:T(128)}, bf16[16,128,12,64]{1,3,2,0:T(8,128)(2,1)}, s32[]{:T(128)}, bf16[128,12,64]{0,2,1:T(8,128)(2,1)}, ...), branch_computations={%region_25.25_spmd, %region_26.26_spmd} | conditional | flops 116670720 | bytes 7219654 | solution.py:362
  545.4 10.3 %conditional.11 = ((f32[128,12,64]{0,2,1:T(8,128)}, f32[128,12,64]{0,2,1:T(8,128)})) conditional(s32[]{:T(128)} %convert_element_type.766, (f32[128,12,64]{0,2,1:T(8,128)}, f32[128,12,64]{0,2,1:T(8,128)}) %tuple.156, (s32[]{:T(128)}, s32[]{:T(128)}, bf16[16,128,12,64]{1,3,2,0:T(8,128)(2,1)}, s32[]{:T(128)}, bf16[128,12,64]{0,2,1:T(8,128)(2,1)}, ...), branch_computations={%region_25.25_spmd, %region_26.26_spmd} | conditional | flops 116670720 | bytes 7219654 | solution.py:362
  557.5 10.3 %conditional.11 = ((f32[128,12,64]{0,2,1:T(8,128)}, f32[128,12,64]{0,2,1:T(8,128)})) conditional(s32[]{:T(128)} %convert_element_type.766, (f32[128,12,64]{0,2,1:T(8,128)}, f32[128,12,64]{0,2,1:T(8,128)}) %tuple.156, (s32[]{:T(128)}, s32[]{:T(128)}, bf16[16,128,12,64]{1,3,2,0:T(8,128)(2,1)}, s32[]{:T(128)}, bf16[128,12,64]{0,2,1:T(8,128)(2,1)}, ...), branch_computations={%region_25.25_spmd, %region_26.26_spmd} | conditional | flops 116670720 | bytes 7219654 | solution.py:362
  569.6 10.3 %conditional.11 = ((f32[128,12,64]{0,2,1:T(8,128)}, f32[128,12,64]{0,2,1:T(8,128)})) conditional(s32[]{:T(128)} %convert_element_type.766, (f32[128,12,64]{0,2,1:T(8,128)}, f32[128,12,64]{0,2,1:T(8,128)}) %tuple.156, (s32[]{:T(128)}, s32[]{:T(128)}, bf16[16,128,12,64]{1,3,2,0:T(8,128)(2,1)}, s32[]{:T(128)}, bf16[128,12,64]{0,2,1:T(8,128)(2,1)}, ...), branch_computations={%region_25.25_spmd, %region_26.26_spmd} | conditional | flops 116670720 | bytes 7219654 | solution.py:362
  581.7 10.3 %conditional.11 = ((f32[128,12,64]{0,2,1:T(8,128)}, f32[128,12,64]{0,2,1:T(8,128)})) conditional(s32[]{:T(128)} %convert_element_type.766, (f32[128,12,64]{0,2,1:T(8,128)}, f32[128,12,64]{0,2,1:T(8,128)}) %tuple.156, (s32[]{:T(128)}, s32[]{:T(128)}, bf16[16,128,12,64]{1,3,2,0:T(8,128)(2,1)}, s32[]{:T(128)}, bf16[128,12,64]{0,2,1:T(8,128)(2,1)}, ...), branch_computations={%region_25.25_spmd, %region_26.26_spmd} | conditional | flops 116670720 | bytes 7219654 | solution.py:362
  593.9 10.3 %conditional.11 = ((f32[128,12,64]{0,2,1:T(8,128)}, f32[128,12,64]{0,2,1:T(8,128)})) conditional(s32[]{:T(128)} %convert_element_type.766, (f32[128,12,64]{0,2,1:T(8,128)}, f32[128,12,64]{0,2,1:T(8,128)}) %tuple.156, (s32[]{:T(128)}, s32[]{:T(128)}, bf16[16,128,12,64]{1,3,2,0:T(8,128)(2,1)}, s32[]{:T(128)}, bf16[128,12,64]{0,2,1:T(8,128)(2,1)}, ...), branch_computations={%region_25.25_spmd, %region_26.26_spmd} | conditional | flops 116670720 | bytes 7219654 | solution.py:362
  606.0 10.3 %conditional.11 = ((f32[128,12,64]{0,2,1:T(8,128)}, f32[128,12,64]{0,2,1:T(8,128)})) conditional(s32[]{:T(128)} %convert_element_type.766, (f32[128,12,64]{0,2,1:T(8,128)}, f32[128,12,64]{0,2,1:T(8,128)}) %tuple.156, (s32[]{:T(128)}, s32[]{:T(128)}, bf16[16,128,12,64]{1,3,2,0:T(8,128)(2,1)}, s32[]{:T(128)}, bf16[128,12,64]{0,2,1:T(8,128)(2,1)}, ...), branch_computations={%region_25.25_spmd, %region_26.26_spmd} | conditional | flops 116670720 | bytes 7219654 | solution.py:362
  618.1 10.3 %conditional.11 = ((f32[128,12,64]{0,2,1:T(8,128)}, f32[128,12,64]{0,2,1:T(8,128)})) conditional(s32[]{:T(128)} %convert_element_type.766, (f32[128,12,64]{0,2,1:T(8,128)}, f32[128,12,64]{0,2,1:T(8,128)}) %tuple.156, (s32[]{:T(128)}, s32[]{:T(128)}, bf16[16,128,12,64]{1,3,2,0:T(8,128)(2,1)}, s32[]{:T(128)}, bf16[128,12,64]{0,2,1:T(8,128)(2,1)}, ...), branch_computations={%region_25.25_spmd, %region_26.26_spmd} | conditional | flops 116670720 | bytes 7219654 | solution.py:362
  630.2 10.3 %conditional.11 = ((f32[128,12,64]{0,2,1:T(8,128)}, f32[128,12,64]{0,2,1:T(8,128)})) conditional(s32[]{:T(128)} %convert_element_type.766, (f32[128,12,64]{0,2,1:T(8,128)}, f32[128,12,64]{0,2,1:T(8,128)}) %tuple.156, (s32[]{:T(128)}, s32[]{:T(128)}, bf16[16,128,12,64]{1,3,2,0:T(8,128)(2,1)}, s32[]{:T(128)}, bf16[128,12,64]{0,2,1:T(8,128)(2,1)}, ...), branch_computations={%region_25.25_spmd, %region_26.26_spmd} | conditional | flops 116670720 | bytes 7219654 | solution.py:362
  642.3 10.3 %conditional.11 = ((f32[128,12,64]{0,2,1:T(8,128)}, f32[128,12,64]{0,2,1:T(8,128)})) conditional(s32[]{:T(128)} %convert_element_type.766, (f32[128,12,64]{0,2,1:T(8,128)}, f32[128,12,64]{0,2,1:T(8,128)}) %tuple.156, (s32[]{:T(128)}, s32[]{:T(128)}, bf16[16,128,12,64]{1,3,2,0:T(8,128)(2,1)}, s32[]{:T(128)}, bf16[128,12,64]{0,2,1:T(8,128)(2,1)}, ...), branch_computations={%region_25.25_spmd, %region_26.26_spmd} | conditional | flops 116670720 | bytes 7219654 | solution.py:362
  654.5 10.3 %conditional.11 = ((f32[128,12,64]{0,2,1:T(8,128)}, f32[128,12,64]{0,2,1:T(8,128)})) conditional(s32[]{:T(128)} %convert_element_type.766, (f32[128,12,64]{0,2,1:T(8,128)}, f32[128,12,64]{0,2,1:T(8,128)}) %tuple.156, (s32[]{:T(128)}, s32[]{:T(128)}, bf16[16,128,12,64]{1,3,2,0:T(8,128)(2,1)}, s32[]{:T(128)}, bf16[128,12,64]{0,2,1:T(8,128)(2,1)}, ...), branch_computations={%region_25.25_spmd, %region_26.26_spmd} | conditional | flops 116670720 | bytes 7219654 | solution.py:362
  666.6 10.3 %conditional.11 = ((f32[128,12,64]{0,2,1:T(8,128)}, f32[128,12,64]{0,2,1:T(8,128)})) conditional(s32[]{:T(128)} %convert_element_type.766, (f32[128,12,64]{0,2,1:T(8,128)}, f32[128,12,64]{0,2,1:T(8,128)}) %tuple.156, (s32[]{:T(128)}, s32[]{:T(128)}, bf16[16,128,12,64]{1,3,2,0:T(8,128)(2,1)}, s32[]{:T(128)}, bf16[128,12,64]{0,2,1:T(8,128)(2,1)}, ...), branch_computations={%region_25.25_spmd, %region_26.26_spmd} | conditional | flops 116670720 | bytes 7219654 | solution.py:362
  690.9 73.6 %all-reduce.2 = (f32[768]{0:T(1024)}, f32[12,32]{1,0:T(8,128)}, f32[768]{0:T(1024)}, f32[768,8]{0,1:T(8,128)}) all-reduce(f32[768]{0:T(1024)S(1)} %get-tuple-element.934, f32[12,32]{1,0:T(8,128)S(1)} %get-tuple-element.753, f32[768]{0:T(1024)S(1)} %copy-done.34, ...), channel_id=1, replica_groups=mesh['context'=16,'expert'=8] {'context','expert'}, use_global_device_ids=true, to_apply=%region_30.31 | all-reduce | flops 8064 | bytes 64512 | tf_op jit(solution)/shard_map/psum | solution.py:388
  765.5 86.6 %all-reduce.6.cloned.1.call-done = (f32[768,768]{1,0:T(8,128)}, f32[768,768]{1,0:T(8,128)}, f32[768,768]{1,0:T(8,128)}, f32[768,768]{1,0:T(8,128)}) async-done(((f32[768,768]{1,0:T(8,128)}, f32[768,768]{1,0:T(8,128)}, f32[768,768]{1,0:T(8,128)}, f32[768,768]{1,0:T(8,128)}), (f32[768,768]{1,0:T(8,128)}, f32[768,768]{1,0:T(8,128)}, f32[768,768]{1,0:T(8,128)}, ...) | async-done | bytes 9437200 | tf_op jit(solution)/shard_map/psum | solution.py:388
  (550 shorter events, 334.4 us)
Async XLA Ops:
  7.2 6.6 copy-start.27
  7.2 6.6 copy-start.28
  7.2 7.5 copy-start.35
  7.2 74.6 %all-gather.4.cloned.1.call-start = ((), (), s32[]{:S(2)}) async-start(), calls=%async_computation.6 | async-start | bytes 6684672 | tf_op jit(solution)/shard_map/all_gather | solution.py:18
  10.4 7.7 copy-start.25
  13.7 154.9 %all-gather.6.cloned.1.call-start = ((), (), s32[]{:S(2)}) async-start(), calls=%async_computation.7 | async-start | bytes 10027008 | tf_op jit(solution)/shard_map/all_gather | solution.py:26
  15.5 72.2 %copy-start.23 = (bf16[128,768]{1,0:T(8,128)(2,1)}, bf16[128,768]{1,0:T(8,128)(2,1)S(1)}, u32[]{:S(2)}) copy-start(bf16[128,768]{1,0:T(8,128)(2,1)S(1)} %convolution_convert_fusion.3) | copy-start | bytes 589828
  20.8 136.6 %copy-start.31 = (s32[128,2]{1,0:T(8,128)}, s32[128,2]{1,0:T(8,128)S(1)}, u32[]{:S(2)}) copy-start(s32[128,2]{1,0:T(8,128)S(1)} %copy.58) | copy-start | bytes 3076
  108.3 41.6 %copy-start.33 = (f32[768]{0:T(1024)S(1)}, f32[768]{0:T(1024)}, u32[]{:S(2)}) copy-start(f32[768]{0:T(1024)} %param.32) | copy-start | bytes 9220
  150.0 7.1 copy-start.32
  150.1 8.2 copy-start.11
  152.7 12.3 %all-to-all-start = ((bf16[8,48,768]{2,1,0:T(8,128)(2,1)}), bf16[8,48,768]{2,1,0:T(8,128)(2,1)}, u32[]{:S(2)}, u32[]{:S(2)}) async-start(bf16[8,48,768]{2,1,0:T(8,128)(2,1)} %bitcast.296), calls=%async_computation | async-start | bytes 1179648 | tf_op jit(solution)/shard_map/all_to_all | solution.py:223
  165.0 11.5 %all-to-all-start.2 = ((bf16[8,48,768]{2,1,0:T(8,128)(2,1)}), bf16[8,48,768]{2,1,0:T(8,128)(2,1)S(1)}, u32[]{:S(2)}, u32[]{:S(2)}) async-start(bf16[8,48,768]{2,1,0:T(8,128)(2,1)} %bitcast.53), calls=%async_computation.2 | async-start | bytes 1179648 | tf_op jit(solution)/shard_map/all_to_all | solution.py:254
  176.6 7.8 copy-start.26
  176.6 7.8 copy-start.37
  187.3 12.6 %all-to-all-start.3 = ((bf16[8,48,768]{2,1,0:T(8,128)(2,1)}), bf16[8,48,768]{2,1,0:T(8,128)(2,1)S(1)}, u32[]{:S(2)}, u32[]{:S(2)}) async-start(bf16[8,48,768]{2,1,0:T(8,128)(2,1)} %bitcast.59), calls=%async_computation.3 | async-start | bytes 1179648 | tf_op jit(solution)/shard_map/all_to_all | solution.py:271
  199.8 13.9 %all-to-all-start.1 = ((bf16[8,48,768]{2,1,0:T(8,128)(2,1)}), bf16[8,48,768]{2,1,0:T(8,128)(2,1)S(1)}, u32[]{:S(2)}, u32[]{:S(2)}) async-start(bf16[8,48,768]{2,1,0:T(8,128)(2,1)} %bitcast.315), calls=%async_computation.1 | async-start | bytes 1179648 | tf_op jit(solution)/shard_map/all_to_all | solution.py:237
  203.5 261.2 %all-gather.8.cloned.1.call-start = ((), (), s32[]{:S(2)}) async-start(), calls=%async_computation.8 | async-start | bytes 6684672 | tf_op jit(solution)/shard_map/all_gather | solution.py:18
  205.9 12.0 %copy-start.9 = (f32[128,768]{1,0:T(8,128)S(1)}, f32[128,768]{1,0:T(8,128)}, u32[]{:S(2)}) copy-start(f32[128,768]{1,0:T(8,128)} %copy-done.8) | copy-start | bytes 1179652
  215.6 7.1 copy-start.10
  222.8 7.5 copy-start.24
  228.3 233.9 %copy-start.4 = (f32[128,768]{1,0:T(8,128)}, f32[128,768]{1,0:T(8,128)S(1)}, u32[]{:S(2)}) copy-start(f32[128,768]{1,0:T(8,128)S(1)} %get-tuple-element.1034) | copy-start | bytes 1179652
  231.0 453.7 %reduce-scatter.3.cloned.1.call-start = ((), (), s32[]{:S(2)}) async-start(), calls=%async_computation.9 | async-start | bytes 5013504 | tf_op jit(solution)/shard_map/reduce_scatter | solution.py:279
  237.9 448.8 %reduce-scatter.5.cloned.1.call-start = ((), (), s32[]{:S(2)}) async-start(), calls=%async_computation.10 | async-start | bytes 5013504 | tf_op jit(solution)/shard_map/reduce_scatter | solution.py:282
  245.6 606.5 %all-reduce.6.cloned.1.call-start = ((), (), s32[]{:S(2)}) async-start(), calls=%async_computation.11 | async-start | bytes 18874368 | tf_op jit(solution)/shard_map/psum | solution.py:388
  249.0 211.1 %copy-start.3 = (bf16[1,128,768]{2,1,0:T(8,128)(2,1)S(1)}, bf16[1,128,768]{2,1,0:T(8,128)(2,1)}, u32[]{:S(2)}) copy-start(bf16[1,128,768]{2,1,0:T(8,128)(2,1)} %param.25) | copy-start | bytes 589828
  290.9 171.3 %copy-start.16 = (bf16[128,12,64]{0,2,1:T(8,128)(2,1)S(1)}, bf16[128,12,64]{0,2,1:T(8,128)(2,1)}, u32[]{:S(2)}) copy-start(bf16[128,12,64]{0,2,1:T(8,128)(2,1)} %copy-done.15) | copy-start | bytes 589828
  290.9 173.8 %copy-start.17 = (bf16[128,12,64]{0,2,1:T(8,128)(2,1)}, bf16[128,12,64]{0,2,1:T(8,128)(2,1)S(1)}, u32[]{:S(2)}) copy-start(bf16[128,12,64]{0,2,1:T(8,128)(2,1)S(1)} %convert_element_type.603) | copy-start | bytes 589828
  684.7 6.2 copy-start.30
  684.7 6.2 copy-start.34
  684.7 79.8 %copy-start.5 = (f32[128,768]{1,0:T(8,128)S(1)}, f32[128,768]{1,0:T(8,128)}, u32[]{:S(2)}) copy-start(f32[128,768]{1,0:T(8,128)} %copy-done.4) | copy-start | bytes 1179652
  684.7 79.8 %copy-start.36 = (f32[128]{0:T(128)S(1)}, f32[128]{0:T(128)}, u32[]{:S(2)}) copy-start(f32[128]{0:T(128)} %get-tuple-element.1043) | copy-start | bytes 1540
  (19 other events, 51.2 us)
Sparse Core Ops, SparseCore 0:
  13.9 67.8 all-gather.3
  84.8 75.2 all-gather.5
  231.1 127.8 all-gather.7
  363.0 79.2 reduce-scatter.2
  446.7 81.5 reduce-scatter.4
  683.0 169.0 all-reduce.5
where the time goes:
time: 882 us; the launch traced here: 869 us
  blocking collectives  243 us (28%)
  matrix products  182 us (21%)
  waiting for transfers between devices  158 us (18%)
  local copies, waits for them, and re-layouts  131 us (15%)
  loops' own time  87.2 us (10%)
  other arithmetic  36.7 us (4%)
  starting transfers between devices  16.2 us (2%)
  between operations  15.1 us (2%)
    all_gather x1, blocking collectives, in_one_piece(): filled = lax.all_gather(both, axis, axis=dim, tiled=True)  169 us
    psum x1, waiting for transfers between devices, shards(): lax.psum((grad_w_query, grad_w_key, grad_w_value, grad_w_out, grad_bias,...  86.6 us
    psum x1, blocking collectives, shards(): lax.psum((grad_w_query, grad_w_key, grad_w_value, grad_w_out, grad_bias,...  73.6 us
    all_gather x2, waiting for transfers between devices, in_one_piece(): filled = lax.all_gather(both, axis, axis=dim, tiled=True)  58.9 us
    dot_general x15, matrix products, grad_block(): jnp.einsum('hqk,qhd->khd', grad_scores, query_blk, preferred_element_type...  40.8 us
    unnamed x96, local copies, waits for them, and re-layouts  35.8 us
    split x7, local copies, waits for them, and re-layouts, in_one_piece(): jnp.split(filled, [sum(widths[:k]) for k in range(1, len(widths))], axis=...  32 us
    dot_general x15, matrix products, grad_block(): jnp.einsum('hqk,qhd->khd', probabilities.astype(jnp.bfloat16), grad_blk,...  31.3 us
  transfers between devices with their start and end apart: 10, of which 6 were waited for; matrix products, arithmetic and copies ran while one was open for 35% of the time, Pallas kernels for 0%

commit v1 on v0

v1 whole, which is shorter than its diff:
```python
import math

import jax
import jax.numpy as jnp
from jax import lax
from jax.experimental import pallas as pl
from jax.experimental.pallas import tpu as pltpu
from jax.sharding import PartitionSpec as P

MAX_DIST = 128
EPSILON = 1e-06
NEG_LARGE = -1e30
BLK = 256
HEAD_SLOTS = 16

F32 = jnp.float32
BF16 = jnp.bfloat16
HIGHEST = lax.Precision.HIGHEST

NN = (((1,), (0,)), ((), ()))
NT = (((1,), (1,)), ((), ()))
TN = (((0,), (0,)), ((), ()))


def dot(a, b, dims=NN, precision=None):
    return lax.dot_general(a, b, dims, precision=precision, preferred_element_type=F32)


def bucket_starts(buckets, far_reach):
    span = buckets // 2
    rest = [
        int(math.ceil(span * (far_reach / span) ** (step / (buckets - span))))
        for step in range(1, buckets - span)
    ]
    return list(range(span + 1)) + rest


def rms_scale(values):
    return lax.rsqrt(jnp.mean(values * values, axis=-1, keepdims=True) + EPSILON)


def norm_back(values, inv_root, gain_vec, grad_normed):
    weighted = grad_normed * gain_vec
    cubed = inv_root * inv_root * inv_root
    return inv_root * weighted - values * cubed * jnp.mean(
        weighted * values, axis=-1, keepdims=True
    )


def whole(vmem_mib=56):
    return pltpu.CompilerParams(vmem_limit_bytes=vmem_mib * 2**20)


def vspec():
    return pl.BlockSpec(memory_space=pltpu.VMEM)


def sspec():
    return pl.BlockSpec(memory_space=pltpu.SMEM)


def project_kernel(tok_ref, gain_ref, wq_ref, wk_ref, wv_ref, normed_ref, out_ref):
    inputs = tok_ref[...].astype(F32)
    normed = (inputs * rms_scale(inputs) * gain_ref[...]).astype(BF16)
    normed_ref[...] = normed
    half = normed.shape[0] // 2
    queries = (dot(normed, wq_ref[...]).astype(BF16).astype(F32) * 0.125).astype(BF16)
    keys = dot(normed, wk_ref[...]).astype(BF16)
    values = dot(normed, wv_ref[...]).astype(BF16)
    heads = queries.shape[1] // 64
    for h in range(heads):
        cols = slice(64 * h, 64 * h + 64)
        out_ref[h, : 2 * half, :] = jnp.concatenate([queries[:, cols], keys[:, cols]], axis=1)
        out_ref[h, 2 * half :, :] = jnp.concatenate(
            [values[:half, cols], values[half:, cols]], axis=1
        )
    for h in range(heads, HEAD_SLOTS):
        out_ref[h] = jnp.zeros_like(out_ref[h])


def project(tokens, gain_one, w_query, w_key, w_value):
    rows, width = tokens.shape
    return pl.pallas_call(
        project_kernel,
        name="project",
        out_shape=(
            jax.ShapeDtypeStruct((rows, width), BF16),
            jax.ShapeDtypeStruct((HEAD_SLOTS, rows + rows // 2, 128), BF16),
        ),
        in_specs=[vspec()] * 5,
        out_specs=(vspec(), vspec()),
        compiler_params=whole(),
    )(tokens, gain_one.reshape(1, width), w_query, w_key, w_value)


def bias_tile(table_ref, head, buckets, rows_first, shape, key_dim):
    sign = [1, -1] if key_dim == 1 else [-1, 1]
    dist = (
        rows_first
        + sign[0] * lax.broadcasted_iota(jnp.int32, shape, 0)
        + sign[1] * lax.broadcasted_iota(jnp.int32, shape, 1)
    )
    far = table_ref[head, buckets - 1]
    tile = jnp.full(shape, NEG_LARGE, F32)
    for b, start in enumerate(bucket_starts(buckets, MAX_DIST)):
        tile = jnp.where(dist >= start, table_ref[head, b] - far, tile)
    return tile


def unpack_qkv(qkv_ref, q_s, k_s, v_s, ones_lane):
    count = qkv_ref.shape[0]
    lane = lax.broadcasted_iota(jnp.int32, (64, 64), 1)
    one = jnp.where(lane == 0, 1.0, 0.0).astype(BF16)
    for c in range(count):
        pair = qkv_ref[c, :128, :]
        q_s[128 * c : 128 * c + 128, :] = pair[:, :64]
        k_s[128 * c : 128 * c + 128, :] = pair[:, 64:]
        two = qkv_ref[c, 128:192, :]
        top, bottom = two[:, :64], two[:, 64:]
        if ones_lane:
            top = jnp.concatenate([top, one], axis=1)
            bottom = jnp.concatenate([bottom, one], axis=1)
        v_s[128 * c : 128 * c + 64, :] = top
        v_s[128 * c + 64 : 128 * c + 128, :] = bottom


def attend_kernel(buckets, head_ref, table_ref, qkv_ref, out_ref, keep_ref, lse_ref, q_s, k_s, v_s, bias_s, s_s):
    head = head_ref[0]
    unpack_qkv(qkv_ref, q_s, k_s, v_s, True)
    bias_s[0] = bias_tile(table_ref, head, buckets, BLK, (BLK, BLK), 1)
    bias_s[1] = bias_tile(table_ref, head, buckets, 0, (BLK, BLK), 1)
    blocks = q_s.shape[0] // BLK

    def fold(scores):
        return jnp.maximum(scores[:, :128], scores[:, 128:])

    def one_query(qb, unused):
        rows = pl.ds(pl.multiple_of(qb * BLK, BLK), BLK)
        query = q_s[rows, :]

        def score(kb):
            return dot(query, k_s[pl.ds(pl.multiple_of(kb * BLK, BLK), BLK), :], NT)

        def far(kb, top):
            scores = score(kb)
            s_s[kb] = scores
            return jnp.maximum(top, fold(scores))

        top = lax.fori_loop(0, qb - 1, far, jnp.full((BLK, 128), NEG_LARGE, F32))
        before = jnp.maximum(qb - 1, 0)
        scores = jnp.where(qb > 0, score(before) + bias_s[0], NEG_LARGE)
        s_s[before] = scores
        top = jnp.maximum(top, fold(scores))
        scores = score(qb) + bias_s[1]
        s_s[qb] = scores
        top = jnp.max(jnp.maximum(top, fold(scores)), axis=1, keepdims=True)

        def weigh(kb, total):
            weights = jnp.exp(s_s[kb] - top).astype(BF16)
            return total + dot(weights, v_s[pl.ds(pl.multiple_of(kb * BLK, BLK), BLK), :])

        total = lax.fori_loop(0, qb + 1, weigh, jnp.zeros((BLK, 128), F32))
        norm = total[:, 64:65]
        out = total[:, :64] / norm
        log_total = top + jnp.log(norm)
        spread = jnp.broadcast_to(log_total, (BLK, 128)).T
        lse_ref[qb] = spread[:8, :]
        for part in range(BLK // 128):
            two = jnp.concatenate(
                [out[128 * part : 128 * part + 64], out[128 * part + 64 : 128 * part + 128]], axis=1
            )
            place = qb * (BLK // 128) + part
            out_ref[place] = two.astype(BF16)
            keep_ref[place] = two
        return unused

    lax.fori_loop(0, blocks, one_query, 0)


def attend(head, rel_table, qkv):
    count = qkv.shape[0]
    length = 128 * count
    blocks = length // BLK
    return pl.pallas_call(
        lambda *refs: attend_kernel(rel_table.shape[1], *refs),
        name="attend",
        out_shape=(
            jax.ShapeDtypeStruct((count, 64, 128), BF16),
            jax.ShapeDtypeStruct((count, 64, 128), F32),
            jax.ShapeDtypeStruct((blocks, 8, BLK), F32),
        ),
        in_specs=[sspec(), sspec(), vspec()],
        out_specs=(vspec(), vspec(), vspec()),
        scratch_shapes=[
            pltpu.VMEM((length, 64), BF16),
            pltpu.VMEM((length, 64), BF16),
            pltpu.VMEM((length, 128), BF16),
            pltpu.VMEM((2, BLK, BLK), F32),
            pltpu.VMEM((blocks, BLK, BLK), F32),
        ],
        compiler_params=whole(),
    )(head, rel_table, qkv)


def attend_back_kernel(
    buckets,
    head_ref,
    table_ref,
    qkv_ref,
    go_ref,
    keep_ref,
    lse_ref,
    normed_ref,
    dqkv_ref,
    dw_ref,
    q_s,
    k_s,
    v_s,
    kt_s,
    go_s,
    delta_s,
    dq_s,
    dk_s,
    dv_s,
    bias_s,
    acc_s,
    low_s,
):
    head = head_ref[0]
    length = q_s.shape[0]
    count = qkv_ref.shape[0]
    blocks = length // BLK
    unpack_qkv(qkv_ref, q_s, k_s, v_s, False)
    ones = jnp.ones((8, 64), F32)
    for c in range(count):
        kt_s[:, 128 * c : 128 * c + 128] = k_s[128 * c : 128 * c + 128, :].T
        two, kept = go_ref[c], keep_ref[c]
        go_s[128 * c : 128 * c + 64, :] = two[:, :64]
        go_s[128 * c + 64 : 128 * c + 128, :] = two[:, 64:]
        both = two.astype(F32) * kept
        prod = jnp.concatenate([both[:, :64], both[:, 64:]], axis=0)
        delta_s[:, 128 * c : 128 * c + 128] = dot(ones, prod, NT, HIGHEST)
    bias_s[0] = bias_tile(table_ref, head, buckets, BLK, (BLK, BLK), 0)
    bias_s[1] = bias_tile(table_ref, head, buckets, 0, (BLK, BLK), 0)
    acc_s[...] = jnp.zeros_like(acc_s)
    dk_s[...] = jnp.zeros_like(dk_s)
    dv_s[...] = jnp.zeros_like(dv_s)

    def one_query(qb, far_sum):
        rows = pl.ds(pl.multiple_of(qb * BLK, BLK), BLK)
        query, grad = q_s[rows, :], go_s[rows, :]
        lse = lse_ref[qb][:1, :]
        delta = delta_s[:1, rows]

        def block(kb, near, grad_query, far_sum):
            cols = pl.ds(pl.multiple_of(kb * BLK, BLK), BLK)
            scores = dot(k_s[cols, :], query, NT)
            if near is not None:
                scores = scores + bias_s[near]
            probs = jnp.exp(scores - lse)
            grad_probs = dot(v_s[cols, :], grad, NT)
            grad_scores = (probs * (grad_probs - delta)).astype(BF16)
            dv_s[cols, :] += dot(probs.astype(BF16), grad)
            dk_s[cols, :] += dot(grad_scores, query)
            grad_query = grad_query + dot(kt_s[:, cols], grad_scores)
            wide = grad_scores.astype(F32)
            if near is None:
                far_sum = far_sum + jnp.sum(wide.reshape(BLK // 8, 8, BLK), axis=0)
            else:
                acc_s[near] += wide
            return grad_query, far_sum

        start = (jnp.zeros((64, BLK), F32), far_sum)
        grad_query, far_sum = lax.fori_loop(
            0, qb - 1, lambda kb, state: block(kb, None, *state), start
        )
        dq_s[:, rows] = grad_query

        @pl.when(qb > 0)
        def _():
            more, unused = block(qb - 1, 0, jnp.zeros((64, BLK), F32), None)
            dq_s[:, rows] += more

        more, unused = block(qb, 1, jnp.zeros((64, BLK), F32), None)
        dq_s[:, rows] += more
        return far_sum

    far_sum = lax.fori_loop(0, blocks, one_query, jnp.zeros((8, BLK), F32))

    for c in range(count):
        here = slice(128 * c, 128 * c + 128)
        dq_t = (dq_s[:, here] * 0.125).astype(BF16)
        dk = dk_s[here, :].astype(BF16)
        dv = dv_s[here, :].astype(BF16)
        pair = jnp.concatenate([dq_t.T, dk], axis=1)
        dqkv_ref[c, :128, :] = pair
        dqkv_ref[c, 128:192, :] = jnp.concatenate([dv[:64], dv[64:]], axis=1)
        low_s[:128, here] = pair.T
        low_s[128:192, here] = dv.T

    width = normed_ref.shape[1]
    grads = dot(low_s[...], normed_ref[...])
    pair, third = grads[:128].T, grads[128:192].T
    shares = dw_ref.shape[0]
    each = width // shares
    lane = lax.broadcasted_iota(jnp.int32, (16, 128), 1)
    dist0 = (
        BLK
        - lax.broadcasted_iota(jnp.int32, (BLK, BLK), 0)
        + lax.broadcasted_iota(jnp.int32, (BLK, BLK), 1)
    )
    dist1 = dist0 - BLK

    def total(values):
        return jnp.sum(jnp.sum(values, axis=1, keepdims=True), axis=0, keepdims=True)

    starts = bucket_starts(buckets, MAX_DIST)
    row = jnp.zeros((16, 128), F32)
    above = None
    for b in reversed(range(buckets)):
        reach = total(
            jnp.where(dist0 >= starts[b], acc_s[0], 0.0)
            + jnp.where(dist1 >= starts[b], acc_s[1], 0.0)
        )
        mine = reach + total(far_sum) if b == buckets - 1 else reach - above
        above = reach
        row = jnp.where(lane == b, mine, row)
    row = row.astype(BF16)
    for s in range(shares):
        mine = slice(each * s, each * s + each)
        dw_ref[s, :each, :] = pair[mine].astype(BF16)
        last = third[mine].astype(BF16)
        dw_ref[s, each : each + each // 2, :] = jnp.concatenate(
            [last[: each // 2], last[each // 2 :]], axis=1
        )
        dw_ref[s, each + each // 2 :, :] = row


def attend_back(head, rel_table, qkv, grad_heads, keep, lse, normed_all, shares):
    count = qkv.shape[0]
    length = 128 * count
    width = normed_all.shape[1]
    each = width // shares
    return pl.pallas_call(
        lambda *refs: attend_back_kernel(rel_table.shape[1], *refs),
        name="attend_back",
        out_shape=(
            jax.ShapeDtypeStruct(qkv.shape, BF16),
            jax.ShapeDtypeStruct((shares, each + each // 2 + 16, 128), BF16),
        ),
        in_specs=[sspec(), sspec()] + [vspec()] * 5,
        out_specs=(vspec(), vspec()),
        scratch_shapes=[
            pltpu.VMEM((length, 64), BF16),
            pltpu.VMEM((length, 64), BF16),
            pltpu.VMEM((length, 64), BF16),
            pltpu.VMEM((64, length), BF16),
            pltpu.VMEM((length, 64), BF16),
            pltpu.VMEM((8, length), F32),
            pltpu.VMEM((64, length), F32),
            pltpu.VMEM((length, 64), F32),
            pltpu.VMEM((length, 64), F32),
            pltpu.VMEM((2, BLK, BLK), F32),
            pltpu.VMEM((2, BLK, BLK), F32),
            pltpu.VMEM((192, length), BF16),
        ],
        compiler_params=whole(),
    )(head, rel_table, qkv, grad_heads, keep, lse, normed_all)


def heads_to_rows(ref, scratch):
    for j in range(scratch.shape[1] // 128):
        one, two = ref[2 * j], ref[2 * j + 1]
        scratch[:64, 128 * j : 128 * j + 128] = jnp.concatenate([one[:, :64], two[:, :64]], axis=1)
        scratch[64:, 128 * j : 128 * j + 128] = jnp.concatenate([one[:, 64:], two[:, 64:]], axis=1)


def dispatch_kernel(
    experts,
    capacity,
    tok_ref,
    cot_ref,
    heads_ref,
    wo_ref,
    gain_ref,
    wr_ref,
    routes_ref,
    send_ref,
    att_ref,
    mixed_ref,
    second_ref,
    pick_ref,
    gates_ref,
):
    rows = tok_ref.shape[0]
    heads_to_rows(heads_ref, att_ref)
    mixed = tok_ref[...].astype(F32) + dot(att_ref[...], wo_ref[...])
    mixed_ref[...] = mixed
    second = (mixed * rms_scale(mixed) * gain_ref[...]).astype(BF16)
    second_ref[...] = second
    logits = dot(second, wr_ref[...])
    ids = lax.broadcasted_iota(jnp.int32, (rows, experts), 1)
    routes = routes_ref[...]
    marks = [(routes[:, k : k + 1] == ids).astype(F32) for k in range(2)]
    earlier = (
        lax.broadcasted_iota(jnp.int32, (rows, rows), 0)
        > lax.broadcasted_iota(jnp.int32, (rows, rows), 1)
    ).astype(F32)
    ranks = dot(earlier.astype(BF16), (marks[0] + marks[1]).astype(BF16))
    chosen = [jnp.sum(m * logits, axis=1, keepdims=True) for m in marks]
    top = jnp.maximum(chosen[0], chosen[1])
    exps = [jnp.exp(c - top) for c in chosen]
    gates = [e / (exps[0] + exps[1]) for e in exps]
    slot_ids = lax.broadcasted_iota(jnp.int32, (rows, experts * capacity), 1)
    grad_out = cot_ref[...].astype(F32)
    picks = []
    for k in range(2):
        slot = jnp.sum(marks[k] * ranks, axis=1, keepdims=True).astype(jnp.int32)
        place = routes[:, k : k + 1] * capacity + slot
        picks.append((place == slot_ids).astype(F32).astype(BF16))
        pick_ref[k] = picks[k]
    send_rows = dot(picks[0] + picks[1], second, TN).astype(BF16)
    send_grads = dot(picks[0], (gates[0] * grad_out).astype(BF16), TN) + dot(
        picks[1], (gates[1] * grad_out).astype(BF16), TN
    )
    send_grads = send_grads.astype(BF16)
    for e in range(experts):
        here = slice(capacity * e, capacity * e + capacity)
        send_ref[e, :capacity, :] = send_rows[here]
        send_ref[e, capacity:, :] = send_grads[here]
    lane = lax.broadcasted_iota(jnp.int32, (rows, 128), 1)
    gates_ref[...] = jnp.where(lane == 0, gates[0], gates[1])


def dispatch(tokens, cotangent, heads, w_out, gain_two, w_router, routes, experts):
    rows, width = tokens.shape
    capacity = 3 * rows // experts
    return pl.pallas_call(
        lambda *refs: dispatch_kernel(experts, capacity, *refs),
        name="dispatch",
        out_shape=(
            jax.ShapeDtypeStruct((experts, 2 * capacity, width), BF16),
            jax.ShapeDtypeStruct((rows, width), BF16),
            jax.ShapeDtypeStruct((rows, width), F32),
            jax.ShapeDtypeStruct((rows, width), BF16),
            jax.ShapeDtypeStruct((2, rows, experts * capacity), BF16),
            jax.ShapeDtypeStruct((rows, 128), F32),
        ),
        in_specs=[vspec()] * 7,
        out_specs=(vspec(),) * 6,
        compiler_params=whole(),
    )(tokens, cotangent, heads, w_out, gain_two.reshape(1, width), w_router, routes)


def expert_kernel(rows_ref, w_ref, back_ref, dw_ref, x_s, g_s, y_s, dx_s):
    step = pl.program_id(0)
    sources, both, width = rows_ref.shape
    capacity = both // 2

    @pl.when(step == 0)
    def _():
        for s in range(sources):
            x_s[capacity * s : capacity * s + capacity, :] = rows_ref[s, :capacity, :]
            g_s[capacity * s : capacity * s + capacity, :] = rows_ref[s, capacity:, :]
        y_s[...] = jnp.zeros_like(y_s)
        dx_s[...] = jnp.zeros_like(dx_s)

    w_in, w_back = w_ref[:, :width], w_ref[:, width:]
    pre = dot(x_s[...], w_in, NT)
    square = pre * pre
    curve = jnp.tanh(0.7978845608 * (pre + 0.044715 * square * pre))
    act = (0.5 * pre * (1.0 + curve)).astype(BF16)
    slope = 0.5 * (1.0 + curve) + 0.5 * pre * (1.0 - curve * curve) * (
        0.7978845608 * (1.0 + 3.0 * 0.044715 * square)
    )
    grad_pre = (dot(g_s[...], w_back, NT) * slope).astype(BF16)
    y_s[...] += dot(act, w_back)
    dx_s[...] += dot(grad_pre, w_in)
    dw_ref[:, :width] = dot(grad_pre, x_s[...], TN).astype(BF16)
    dw_ref[:, width:] = dot(act, g_s[...], TN).astype(BF16)

    @pl.when(step == pl.num_programs(0) - 1)
    def _():
        for s in range(sources):
            here = slice(capacity * s, capacity * s + capacity)
            back_ref[s, :capacity, :] = y_s[here, :].astype(BF16)
            back_ref[s, capacity:, :] = dx_s[here, :].astype(BF16)


def expert_both(rows, weights):
    sources, both, width = rows.shape
    hidden = weights.shape[0]
    chunk = 512
    held = sources * both // 2
    return pl.pallas_call(
        expert_kernel,
        name="expert_both",
        grid=(hidden // chunk,),
        out_shape=(
            jax.ShapeDtypeStruct(rows.shape, BF16),
            jax.ShapeDtypeStruct(weights.shape, BF16),
        ),
        in_specs=[
            pl.BlockSpec(rows.shape, lambda i: (0, 0, 0)),
            pl.BlockSpec((chunk, 2 * width), lambda i: (i, 0)),
        ],
        out_specs=(
            pl.BlockSpec(rows.shape, lambda i: (0, 0, 0)),
            pl.BlockSpec((chunk, 2 * width), lambda i: (i, 0)),
        ),
        scratch_shapes=[
            pltpu.VMEM((held, width), BF16),
            pltpu.VMEM((held, width), BF16),
            pltpu.VMEM((held, width), F32),
            pltpu.VMEM((held, width), F32),
        ],
        compiler_params=whole(),
    )(rows, weights)


def combine_kernel(
    cot_ref,
    back_ref,
    pick_ref,
    gates_ref,
    mixed_ref,
    second_ref,
    att_ref,
    routes_ref,
    gain_ref,
    wr_ref,
    wo_ref,
    out_ref,
    grad_mixed_ref,
    heads_ref,
    sums_ref,
    y_s,
    dx_s,
):
    experts, both, width = back_ref.shape
    capacity = both // 2
    rows = cot_ref.shape[0]
    for s in range(experts):
        here = slice(capacity * s, capacity * s + capacity)
        y_s[here, :] = back_ref[s, :capacity, :]
        dx_s[here, :] = back_ref[s, capacity:, :]
    grad_out = cot_ref[...].astype(F32)
    mixed = mixed_ref[...]
    gates = [gates_ref[:, k : k + 1] for k in range(2)]
    picked = [dot(pick_ref[k], y_s[...]) for k in range(2)]
    out_ref[...] = (mixed + (gates[0] * picked[0] + gates[1] * picked[1])).astype(BF16)
    grad_gates = [jnp.sum(p * grad_out, axis=1, keepdims=True) for p in picked]
    mean = gates[0] * grad_gates[0] + gates[1] * grad_gates[1]
    grad_chosen = [gates[k] * (grad_gates[k] - mean) for k in range(2)]
    ids = lax.broadcasted_iota(jnp.int32, (rows, experts), 1)
    routes = routes_ref[...]
    grad_logits = jnp.where(routes[:, :1] == ids, grad_chosen[0], 0.0) + jnp.where(
        routes[:, 1:2] == ids, grad_chosen[1], 0.0
    )
    grad_second = dot(pick_ref[0], dx_s[...]) + dot(pick_ref[1], dx_s[...])
    grad_second = grad_second + dot(grad_logits, wr_ref[...].astype(F32), NT, HIGHEST)
    second = second_ref[...]
    grad_router = dot(grad_logits, second.astype(F32), TN, HIGHEST)
    scale = rms_scale(mixed)
    grad_gain = jnp.sum(grad_second * mixed * scale, axis=0, keepdims=True)
    grad_mixed = grad_out + norm_back(mixed, scale, gain_ref[...], grad_second)
    grad_mixed_ref[...] = grad_mixed
    grad_branch = grad_mixed.astype(BF16)
    grad_att = dot(grad_branch, wo_ref[...], NT).astype(BF16)
    heads = width // 64
    for h in range(heads):
        cols = slice(64 * h, 64 * h + 64)
        heads_ref[h] = jnp.concatenate([grad_att[:64, cols], grad_att[64:, cols]], axis=1)
    for h in range(heads, HEAD_SLOTS):
        heads_ref[h] = jnp.zeros_like(heads_ref[h])
    grad_wo = dot(att_ref[...], grad_branch, TN).astype(BF16)
    slots, each, unused = sums_ref.shape
    used = width // each
    for c in range(used):
        sums_ref[c] = grad_wo[each * c : each * c + each]
    small = jnp.concatenate([grad_router, jnp.broadcast_to(grad_gain, (8, width))], axis=0)
    for c in range(used, slots):
        sums_ref[c] = jnp.zeros_like(sums_ref[c])
    sums_ref[used, :16, :] = small.astype(BF16)


def combine(cotangent, back, picks, gates, mixed, second, attended, routes, gain_two, w_router, w_out):
    rows, width = cotangent.shape
    experts, both, unused = back.shape
    held = experts * both // 2
    return pl.pallas_call(
        combine_kernel,
        name="combine",
        out_shape=(
            jax.ShapeDtypeStruct((rows, width), BF16),
            jax.ShapeDtypeStruct((rows, width), F32),
            jax.ShapeDtypeStruct((HEAD_SLOTS, rows // 2, 128), BF16),
            jax.ShapeDtypeStruct((HEAD_SLOTS, 64, width), BF16),
        ),
        in_specs=[vspec()] * 11,
        out_specs=(vspec(),) * 4,
        scratch_shapes=[pltpu.VMEM((held, width), BF16), pltpu.VMEM((held, width), BF16)],
        compiler_params=whole(),
    )(
        cotangent,
        back,
        picks,
        gates,
        mixed,
        second,
        attended,
        routes,
        gain_two.reshape(1, width),
        w_router,
        w_out,
    )


def input_grad_kernel(tok_ref, gain_ref, grads_ref, wq_ref, wk_ref, wv_ref, mixed_ref, out_ref, dq_s, dk_s, dv_s):
    for j in range(dq_s.shape[1] // 128):
        cols = slice(128 * j, 128 * j + 128)
        one, two = grads_ref[2 * j], grads_ref[2 * j + 1]
        dq_s[:, cols] = jnp.concatenate([one[:128, :64], two[:128, :64]], axis=1)
        dk_s[:, cols] = jnp.concatenate([one[:128, 64:], two[:128, 64:]], axis=1)
        dv_s[:64, cols] = jnp.concatenate([one[128:, :64], two[128:, :64]], axis=1)
        dv_s[64:, cols] = jnp.concatenate([one[128:, 64:], two[128:, 64:]], axis=1)
    grad_normed = dot(dq_s[...], wq_ref[...], NT)
    grad_normed = grad_normed + dot(dk_s[...], wk_ref[...], NT)
    grad_normed = grad_normed + dot(dv_s[...], wv_ref[...], NT)
    inputs = tok_ref[...].astype(F32)
    out_ref[...] = mixed_ref[...] + norm_back(inputs, rms_scale(inputs), gain_ref[...], grad_normed)


def input_grad(tokens, gain_one, grads, w_query, w_key, w_value, grad_mixed):
    rows, width = tokens.shape
    return pl.pallas_call(
        input_grad_kernel,
        name="input_grad",
        out_shape=jax.ShapeDtypeStruct((rows, width), F32),
        in_specs=[vspec()] * 7,
        out_specs=vspec(),
        scratch_shapes=[pltpu.VMEM((rows, width), BF16)] * 3,
        compiler_params=whole(),
    )(tokens, gain_one.reshape(1, width), grads, w_query, w_key, w_value, grad_mixed)


def coordinates(index):
    context, expert = index // 8, index % 8
    return (context // 8 * 2 + expert % 2, expert // 2, context // 2 % 4, context % 2)


def device_at(x, y, z, core):
    return ((x // 2 * 4 + z) * 2 + core) * 8 + y * 2 + x % 2


def shifted(dim, by):
    pairs = []
    for index in range(128):
        place = list(coordinates(index))
        place[dim] = (place[dim] + by) % (2 if dim == 3 else 4)
        pairs.append((index, device_at(*place)))
    return pairs


def ring_gather(block, dim):
    axes = ("context", "expert")
    ahead = lax.ppermute(block, axes, shifted(dim, -1))
    behind = lax.ppermute(block, axes, shifted(dim, 1))
    half = block.shape[0] // 2
    across = jnp.concatenate(
        [
            lax.ppermute(ahead[:half], axes, shifted(dim, -1)),
            lax.ppermute(behind[half:], axes, shifted(dim, 1)),
        ],
        axis=0,
    )
    return jnp.stack([block, ahead, across, behind])


def gather_all(piece):
    filled = ring_gather(piece, 2)
    filled = ring_gather(filled, 1)
    filled = ring_gather(filled, 0)
    other = lax.ppermute(filled, ("context", "expert"), shifted(3, 1))
    return jnp.stack([filled, other])


def unpack_kernel(
    buckets,
    place_ref,
    piece_ref,
    late_ref,
    gain_ref,
    wq_ref,
    wk_ref,
    wv_ref,
    dwq_ref,
    dwk_ref,
    dwv_ref,
    dwo_ref,
    bias_ref,
    small_ref,
    gain_grad_ref,
):
    expert = pl.program_id(0)
    my_x, my_y, my_z, my_core = (place_ref[i] for i in range(4))
    each = dwq_ref.shape[0]
    half = each // 2
    width = dwq_ref.shape[1]
    y = expert // 2
    rel_y = lax.rem(y - my_y + 4, 4)

    def rel(context):
        x = context // 8 * 2 + lax.rem(expert, 2)
        return (
            jnp.where(my_core == context % 2, 0, 1),
            lax.rem(x - my_x + 4, 4),
            rel_y,
            lax.rem(context // 2 % 4 - my_z + 4, 4),
        )

    bias = []
    for j in range(width // 128):
        cols = slice(128 * j, 128 * j + 128)
        one, two = piece_ref[rel(2 * j)].astype(F32), piece_ref[rel(2 * j + 1)].astype(F32)
        dwq_ref[:, cols] = jnp.concatenate([one[:each, :64], two[:each, :64]], axis=1)
        dwk_ref[:, cols] = jnp.concatenate([one[:each, 64:], two[:each, 64:]], axis=1)
        dwv_ref[:half, cols] = jnp.concatenate(
            [one[each : each + half, :64], two[each : each + half, :64]], axis=1
        )
        dwv_ref[half:, cols] = jnp.concatenate(
            [one[each : each + half, 64:], two[each : each + half, 64:]], axis=1
        )
        bias += [one[each + half : each + half + 1], two[each + half : each + half + 1]]
    bias_ref[...] = jnp.concatenate(bias, axis=0)[:, :buckets]
    for c in range(width // 64):
        dwo_ref[c] = late_ref[rel(c)].astype(F32)
    small_ref[0] = late_ref[rel(width // 64)].astype(F32)
    summed = jnp.sum(
        dwq_ref[...] * wq_ref[...].astype(F32)
        + dwk_ref[...] * wk_ref[...].astype(F32)
        + dwv_ref[...] * wv_ref[...].astype(F32),
        axis=1,
        keepdims=True,
    )
    gain_grad_ref[...] = summed / gain_ref[...]


def unpack(place, pieces, late, gain_one, w_query, w_key, w_value, heads, buckets, experts):
    width = w_query.shape[0]
    each = width // experts
    rows = pl.BlockSpec((each, width), lambda i: (i, 0))
    return pl.pallas_call(
        lambda *refs: unpack_kernel(buckets, *refs),
        name="unpack",
        grid=(experts,),
        out_shape=(
            jax.ShapeDtypeStruct((width, width), F32),
            jax.ShapeDtypeStruct((width, width), F32),
            jax.ShapeDtypeStruct((width, width), F32),
            jax.ShapeDtypeStruct((heads, experts, 8, width), F32),
            jax.ShapeDtypeStruct((heads, buckets), F32),
            jax.ShapeDtypeStruct((experts, 8, width), F32),
            jax.ShapeDtypeStruct((width, 1), F32),
        ),
        in_specs=[
            sspec(),
            vspec(),
            vspec(),
            pl.BlockSpec((each, 1), lambda i: (i, 0)),
            rows,
            rows,
            rows,
        ],
        out_specs=(
            rows,
            rows,
            rows,
            pl.BlockSpec((heads, None, 8, width), lambda i: (0, i, 0, 0)),
            pl.BlockSpec((heads, buckets), lambda i: (0, 0)),
            pl.BlockSpec((1, 8, width), lambda i: (i, 0, 0)),
            pl.BlockSpec((each, 1), lambda i: (i, 0)),
        ),
        compiler_params=whole(),
    )(place, pieces, late, gain_one.reshape(width, 1), w_query, w_key, w_value)


def add_up(received):
    return jnp.sum(received.astype(F32), axis=0)


def shards(
    tokens,
    gain_one,
    w_query,
    w_key,
    w_value,
    w_out,
    rel_table,
    gain_two,
    w_router,
    expert_in,
    expert_out,
    routes,
    cotangent,
):
    width = tokens.shape[2]
    heads, buckets = rel_table.shape
    experts = lax.axis_size("expert")
    inputs, grad_out, routes_here = tokens[0], cotangent[0], routes[0]
    context = lax.axis_index("context")
    head = jnp.minimum(context, heads - 1).astype(jnp.int32).reshape(1)

    normed, packed = project(inputs, gain_one, w_query, w_key, w_value)
    qkv = lax.all_to_all(packed, "context", split_axis=0, concat_axis=0, tiled=True)
    own_weights = jnp.concatenate([expert_in[0].T, expert_out[0].T], axis=1)
    weights = lax.all_gather(own_weights, "context", axis=0, tiled=True)
    normed_all = lax.all_gather(normed, "context", axis=0, tiled=True)

    out_heads, keep, lse = attend(head, rel_table, qkv)
    out_rows = lax.all_to_all(out_heads, "context", split_axis=0, concat_axis=0, tiled=True)
    send, attended, mixed, second, picks, gates = dispatch(
        inputs, grad_out, out_rows, w_out, gain_two, w_router, routes_here, experts
    )
    received = lax.all_to_all(send, "expert", split_axis=0, concat_axis=0, tiled=True)
    back, weight_grads = expert_both(received, weights)
    returned = lax.all_to_all(back, "expert", split_axis=0, concat_axis=0, tiled=True)
    own_grads = lax.psum_scatter(weight_grads, "context", scatter_dimension=0, tiled=True)
    block_out, grad_mixed, grad_heads, sums = combine(
        grad_out, returned, picks, gates, mixed, second, attended, routes_here, gain_two, w_router, w_out
    )
    grad_here = lax.all_to_all(grad_heads, "context", split_axis=0, concat_axis=0, tiled=True)
    sums = lax.all_to_all(sums, "context", split_axis=0, concat_axis=0, tiled=True)
    sums = add_up(sums).astype(BF16).reshape(experts, 8, width)
    sums = lax.all_to_all(sums, "expert", split_axis=0, concat_axis=0, tiled=True)
    late = gather_all(add_up(sums).astype(BF16))

    dqkv, dw = attend_back(head, rel_table, qkv, grad_here, keep, lse, normed_all, experts)
    dw = lax.all_to_all(dw, "expert", split_axis=0, concat_axis=0, tiled=True)
    pieces = gather_all(add_up(dw).astype(BF16))
    grads = lax.all_to_all(dqkv, "context", split_axis=0, concat_axis=0, tiled=True)
    grad_tokens = input_grad(inputs, gain_one, grads, w_query, w_key, w_value, grad_mixed)

    expert = lax.axis_index("expert")
    place = jnp.stack(coordinates(context * experts + expert)).astype(jnp.int32)
    dwq, dwk, dwv, dwo, bias, small, gain_grad = unpack(
        place, pieces, late, gain_one, w_query, w_key, w_value, heads, buckets, experts
    )
    own_grads = own_grads.astype(F32)
    return (
        block_out[None],
        grad_tokens[None],
        gain_grad.reshape(width),
        dwq,
        dwk,
        dwv,
        dwo.reshape(width, width),
        bias,
        small[1, 0],
        small[0].T,
        own_grads[:, :width].T[None],
        own_grads[:, width:].T[None],
    )


def solution(mesh):
    return jax.shard_map(
        shards,
        mesh=mesh,
        in_specs=(
            P("expert", "context", None),
            P(),
            P(),
            P(),
            P(),
            P(),
            P(),
            P(),
            P(),
            P("expert", None, "context"),
            P("expert", None, "context"),
            P("expert", "context", None),
            P("expert", "context", None),
        ),
        out_specs=(
            P("expert", "context", None),
            P("expert", "context", None),
            P(),
            P(),
            P(),
            P(),
            P(),
            P(),
            P(),
            P(),
            P("expert", None, "context"),
            P("expert", None, "context"),
        ),
        check_vma=False,
    )
```

time: 882 us -> 397 us (0.45); the launches traced: 869 us -> 395 us
  matrix products: 182 us -> 0 us
  blocking collectives: 243 us -> 65.6 us
  local copies, waits for them, and re-layouts: 131 us -> 11.8 us
  Pallas kernels: 0 us -> 89.2 us
  loops' own time: 87.2 us -> 0 us
  starting transfers between devices: 16.2 us -> 88.6 us
  waiting for transfers between devices: 158 us -> 108 us
  other arithmetic: 36.7 us -> 18.3 us
    dot_general x99 -> x0, matrix products: 182 us -> none  [the longest x15 40.8 us: grad_block(): jnp.einsum('hqk,qhd->khd', grad_scores, query_blk, preferred_element_type...]
    all_gather x1 -> x0, blocking collectives: 169 us -> none  [in_one_piece(): filled = lax.all_gather(both, axis, axis=dim, tiled=True)]
    pallas_call x0 -> x8, Pallas kernels: none -> 89.2 us  [the longest x1 23.5 us: attend_back(): pl.pallas_call(lambda *refs: attend_back_kernel(rel_table.shape[1], *refs...]
    another operation x51 -> x0, loops' own time: 87.2 us -> none  [the longest x16 26.4 us: key_step(): lax.cond(offset + local_rows - 1 >= first_query, key_live, key_dead, runn...]
    psum x1 -> x0, waiting for transfers between devices: 86.6 us -> none  [shards(): lax.psum((grad_w_query, grad_w_key, grad_w_value, grad_w_out, grad_bias,...]
    psum x1 -> x0, blocking collectives: 73.6 us -> none  [shards(): lax.psum((grad_w_query, grad_w_key, grad_w_value, grad_w_out, grad_bias,...]
    all_to_all x0 -> x4, blocking collectives: none -> 65.6 us  [the longest x1 21.8 us: shards(): lax.all_to_all(back, 'expert', split_axis=0, concat_axis=0, tiled=True)]
    all_gather x3 -> x2, waiting for transfers between devices: 58.9 us -> 0.02 us  [the longest x1 0.02 us: shards(): normed_all = lax.all_gather(normed, 'context', axis=0, tiled=True)]
  transfers between devices with their start and end apart: 10 -> 34, of which waited for: 6 -> 17; matrix products, arithmetic and copies ran while one was open for 35% -> 6% of each run, Pallas kernels for 0% -> 23%
where the time goes in v1:
time: 397 us; the launch traced here: 395 us
  waiting for transfers between devices  108 us (27%)
  Pallas kernels  89.2 us (22%)
  starting transfers between devices  88.6 us (22%)
  blocking collectives  65.6 us (17%)
  other arithmetic  18.3 us (5%)
  between operations  14 us (4%)
  local copies, waits for them, and re-layouts  11.8 us (3%)
    ppermute x6, waiting for transfers between devices, ring_gather(): lax.ppermute(behind[half:], axes, shifted(dim, 1))  34.9 us
    pallas_call x1, Pallas kernels, attend_back(): pl.pallas_call(lambda *refs: attend_back_kernel(rel_table.shape[1], *refs...  23.5 us
    all_to_all x1, blocking collectives, shards(): lax.all_to_all(back, 'expert', split_axis=0, concat_axis=0, tiled=True)  21.8 us
    all_to_all x1, waiting for transfers between devices, shards(): lax.all_to_all(packed, 'context', split_axis=0, concat_axis=0, tiled=True)  20.7 us
    ppermute x6, waiting for transfers between devices, ring_gather(): behind = lax.ppermute(block, axes, shifted(dim, 1))  20.6 us
    all_to_all x1, blocking collectives, shards(): lax.all_to_all(send, 'expert', split_axis=0, concat_axis=0, tiled=True)  20 us
    pallas_call x1, Pallas kernels, attend(): pl.pallas_call(lambda *refs: attend_kernel(rel_table.shape[1], *refs), na...  18.6 us
    pallas_call x1, Pallas kernels, expert_both(): pl.pallas_call(expert_kernel, name='expert_both', grid=(hidden // chunk,)...  18.3 us
  transfers between devices with their start and end apart: 34, of which 17 were waited for; matrix products, arithmetic and copies ran while one was open for 6% of the time, Pallas kernels for 23%

profile of v1, /device:TPU:1, one launch (start us, length us, event | category | flops | bytes accessed | tf_op | source)
XLA Modules:
  0.0 395.4 jit_solution(4186211439811190146)
XLA Ops:
  10.5 3.7 project.1
  14.2 9.4 %all-to-all-start = ((bf16[16,192,128]{2,1,0:T(8,128)(2,1)}), bf16[16,192,128]{2,1,0:T(8,128)(2,1)S(1)}, u32[]{:S(2)}, u32[]{:S(2)}) async-start(bf16[16,192,128]{2,1,0:T(8,128)(2,1)} %get-tuple-element.38), calls=%async_computation | async-start | bytes 1572864 | tf_op jit(solution)/shard_map/all_to_all | solution.py:815
  23.6 20.7 %all-to-all-done.refs_2_ = bf16[16,192,128]{2,1,0:T(8,128)(2,1)S(1)} async-done(((bf16[16,192,128]{2,1,0:T(8,128)(2,1)}), bf16[16,192,128]{2,1,0:T(8,128)(2,1)S(1)}, u32[]{:S(2)}, u32[]{:S(2)}) %all-to-all-start) | async-done | bytes 786464 | tf_op jit(solution)/shard_map/all_to_all | solution.py:815
  45.2 18.6 %attend.1 = (bf16[16,64,128]{2,1,0:T(8,128)(2,1)}, f32[16,64,128]{2,1,0:T(8,128)}, f32[8,8,256]{2,1,0:T(8,128)}) custom-call(s32[1]{0:T(128)} %bitcast.2.refs_0_, f32[12,32]{1,0:T(8,128)} %refs_1_.3, bf16[16,192,128]{2,1,0:T(8,128)(2,1)} %copy-done), custom_call_target="tpu_custom_call" | custom-call | tf_op jit(solution)/shard_map/attend/pallas_call | solution.py:184
  63.8 4.2 %all-to-all-start.1 = ((bf16[16,64,128]{2,1,0:T(8,128)(2,1)}), bf16[16,64,128]{2,1,0:T(8,128)(2,1)S(1)}, u32[]{:S(2)}, u32[]{:S(2)}) async-start(bf16[16,64,128]{2,1,0:T(8,128)(2,1)} %get-tuple-element.39), calls=%async_computation.1 | async-start | bytes 524288 | tf_op jit(solution)/shard_map/all_to_all | solution.py:821
  70.2 9.4 %all-to-all-done.1.refs_2_ = bf16[16,64,128]{2,1,0:T(8,128)(2,1)S(1)} async-done(((bf16[16,64,128]{2,1,0:T(8,128)(2,1)}), bf16[16,64,128]{2,1,0:T(8,128)(2,1)S(1)}, u32[]{:S(2)}, u32[]{:S(2)}) %all-to-all-start.1) | async-done | bytes 262176 | tf_op jit(solution)/shard_map/all_to_all | solution.py:821
  80.4 3.9 dispatch.1
  84.3 20.0 %all_to_all.45.rows_ref = bf16[8,96,768]{2,1,0:T(8,128)(2,1)} all-to-all(bf16[8,96,768]{2,1,0:T(8,128)(2,1)} %get-tuple-element.40), channel_id=1, replica_groups=mesh['context'=16,'expert'=8] {'expert'}, dimensions={0} | all-to-all | bytes 2359296 | tf_op jit(solution)/shard_map/all_to_all | solution.py:825
  104.3 18.3 %expert_both.1 = (bf16[8,96,768]{2,1,0:T(8,128)(2,1)}, bf16[3072,1536]{1,0:T(8,128)(2,1)}) custom-call(bf16[8,96,768]{2,1,0:T(8,128)(2,1)} %all_to_all.45.rows_ref, bf16[3072,1536]{1,0:T(8,128)(2,1)} %all-gather.3.cloned.1.call-done.w_ref), custom_call_target="tpu_custom_call" | custom-call | tf_op jit(solution)/shard_map/expert_both/pallas_call | solution.py:495
  123.9 21.8 %all_to_all.46.back_ref = bf16[8,96,768]{2,1,0:T(8,128)(2,1)} all-to-all(bf16[8,96,768]{2,1,0:T(8,128)(2,1)S(1)} %copy-done.3), channel_id=1, replica_groups=mesh['context'=16,'expert'=8] {'expert'}, dimensions={0} | all-to-all | bytes 2359296 | tf_op jit(solution)/shard_map/all_to_all | solution.py:827
  145.7 5.3 %combine.1 = (bf16[128,768]{1,0:T(8,128)(2,1)}, f32[128,768]{1,0:T(8,128)}, bf16[16,64,128]{2,1,0:T(8,128)(2,1)}, bf16[16,64,768]{2,1,0:T(8,128)(2,1)}) custom-call(bf16[128,768]{1,0:T(8,128)(2,1)} %bitcast.76, bf16[8,96,768]{2,1,0:T(8,128)(2,1)} %all_to_all.46.back_ref, bf16[2,128,384]{2,1,0:T(8,128)(2,1)} %get-tuple-element.42.pick_ref, ...), custom_call_target="tpu_custom_call" | custom-call | tf_op jit(solution)/shard_map/combine/pallas_call | solution.py:591
  151.0 12.4 %all-to-all-start.4 = ((bf16[16,64,128]{2,1,0:T(8,128)(2,1)}), bf16[16,64,128]{2,1,0:T(8,128)(2,1)S(1)}, u32[]{:S(2)}, u32[]{:S(2)}) async-start(bf16[16,64,128]{2,1,0:T(8,128)(2,1)} %get-tuple-element.48), calls=%async_computation.4 | async-start | bytes 524288 | tf_op jit(solution)/shard_map/all_to_all | solution.py:832
  163.5 8.7 %all-to-all-done.4.refs_3_ = bf16[16,64,128]{2,1,0:T(8,128)(2,1)S(1)} async-done(((bf16[16,64,128]{2,1,0:T(8,128)(2,1)}), bf16[16,64,128]{2,1,0:T(8,128)(2,1)S(1)}, u32[]{:S(2)}, u32[]{:S(2)}) %all-to-all-start.4) | async-done | bytes 262176 | tf_op jit(solution)/shard_map/all_to_all | solution.py:832
  172.8 23.5 %attend_back.1 = (bf16[16,192,128]{2,1,0:T(8,128)(2,1)}, bf16[8,160,128]{2,1,0:T(8,128)(2,1)}) custom-call(s32[1]{0:T(128)} %bitcast.2.refs_0_, f32[12,32]{1,0:T(8,128)} %refs_1_.3, bf16[16,192,128]{2,1,0:T(8,128)(2,1)} %copy-done, bf16[16,64,128]{2,1,0:T(8,128)(2,1)} %copy-done.4, f32[16,64,128]{2,1,0:T(8,128)} %get-tuple-element.49.refs_4_, ...), custom_call_target="tpu_custom_call" | custom-call | tf_op jit(solution)/shard_map/attend_back/pallas_call | solution.py:344
  196.3 14.7 %all_to_all.47 = bf16[8,160,128]{2,1,0:T(8,128)(2,1)S(1)} all-to-all(bf16[8,160,128]{2,1,0:T(8,128)(2,1)} %get-tuple-element.54), channel_id=1, replica_groups=mesh['context'=16,'expert'=8] {'expert'}, dimensions={0} | all-to-all | bytes 655360 | tf_op jit(solution)/shard_map/all_to_all | solution.py:839
  222.8 3.1 collective-permute-done.6
  225.9 2.7 collective-permute-start.5
  234.1 10.5 %all-to-all-start.7 = ((bf16[16,64,768]{2,1,0:T(8,128)(2,1)}), bf16[16,64,768]{2,1,0:T(8,128)(2,1)}, u32[]{:S(2)}, u32[]{:S(2)}) async-start(bf16[16,64,768]{2,1,0:T(8,128)(2,1)} %get-tuple-element.55), calls=%async_computation.7 | async-start | bytes 3145728 | tf_op jit(solution)/shard_map/all_to_all | solution.py:833
  244.6 9.6 %collective-permute-done.10 = bf16[4,4,160,128]{3,2,1,0:T(8,128)(2,1)S(1)} collective-permute-done((bf16[4,4,160,128]{3,2,1,0:T(8,128)(2,1)S(1)}, bf16[4,4,160,128]{3,2,1,0:T(8,128)(2,1)S(1)}, u32[]{:S(2)}, u32[]{:S(2)}) %collective-permute-start.10) | collective-permute-done | bytes 655392 | tf_op jit(solution)/shard_map/ppermute | solution.py:668
  257.1 25.2 %collective-permute-done.11 = bf16[2,4,160,128]{3,2,1,0:T(8,128)(2,1)S(1)} collective-permute-done((bf16[2,4,160,128]{3,2,1,0:T(8,128)(2,1)S(1)}, bf16[2,4,160,128]{3,2,1,0:T(8,128)(2,1)S(1)}, u32[]{:S(2)}, u32[]{:S(2)}) %collective-permute-start.11) | collective-permute-done | bytes 327712 | tf_op jit(solution)/shard_map/ppermute | solution.py:673
  282.4 2.8 fusion.5
  285.2 6.1 %collective-permute-start.12 = (bf16[4,4,4,160,128]{4,3,2,1,0:T(8,128)(2,1)}, bf16[4,4,4,160,128]{4,3,2,1,0:T(8,128)(2,1)}, u32[]{:S(2)}, u32[]{:S(2)}) collective-permute-start(bf16[4,4,4,160,128]{4,3,2,1,0:T(8,128)(2,1)} %get-tuple-element.65), channel_id=1, source_target_pairs={{0,8},{1,9},{2,10},{3,11},{4,12},{5,13},{6,14},{7,15},{8,0},{9,1},... | collective-permute-start | bytes 7864328 | tf_op jit(solution)/shard_map/ppermute | solution.py:684
  293.0 9.2 %all_to_all.48 = bf16[8,8,768]{2,1,0:T(8,128)(2,1)S(1)} all-to-all(bf16[8,8,768]{2,1,0:T(8,128)(2,1)S(1)} %bitcast.81), channel_id=1, replica_groups=mesh['context'=16,'expert'=8] {'expert'}, dimensions={0} | all-to-all | bytes 196608 | tf_op jit(solution)/shard_map/all_to_all | solution.py:835
  319.1 2.9 collective-permute-start.21
  321.9 3.0 collective-permute-done.23
  327.7 3.2 collective-permute-done.24
  332.0 7.5 %collective-permute-start.25 = (bf16[4,4,4,8,768]{4,3,2,1,0:T(8,128)(2,1)}, bf16[4,4,4,8,768]{4,3,2,1,0:T(8,128)(2,1)}, u32[]{:S(2)}, u32[]{:S(2)}) collective-permute-start(bf16[4,4,4,8,768]{4,3,2,1,0:T(8,128)(2,1)} %get-tuple-element.69), channel_id=1, source_target_pairs={{0,8},{1,9},{2,10},{3,11},{4,12},{5,13},{6,14},{7,15},{8,0},{9,1},... | collective-permute-start | bytes 2359304 | tf_op jit(solution)/shard_map/ppermute | solution.py:684
  339.4 5.3 %all-to-all-start.5 = ((bf16[16,192,128]{2,1,0:T(8,128)(2,1)}), bf16[16,192,128]{2,1,0:T(8,128)(2,1)}, u32[]{:S(2)}, u32[]{:S(2)}) async-start(bf16[16,192,128]{2,1,0:T(8,128)(2,1)} %get-tuple-element.52), calls=%async_computation.5 | async-start | bytes 1572864 | tf_op jit(solution)/shard_map/all_to_all | solution.py:841
  346.2 13.0 %all-to-all-done.5.grads_ref = bf16[16,192,128]{2,1,0:T(8,128)(2,1)} async-done(((bf16[16,192,128]{2,1,0:T(8,128)(2,1)}), bf16[16,192,128]{2,1,0:T(8,128)(2,1)}, u32[]{:S(2)}, u32[]{:S(2)}) %all-to-all-start.5) | async-done | bytes 786464 | tf_op jit(solution)/shard_map/all_to_all | solution.py:841
  359.2 4.6 %input_grad.1 = f32[128,768]{1,0:T(8,128)} custom-call(bf16[128,768]{1,0:T(8,128)(2,1)} %bitcast.72, f32[1,768]{1,0:T(1,128)} %reshape.48.gain_ref, bf16[16,192,128]{2,1,0:T(8,128)(2,1)} %all-to-all-done.5.grads_ref, bf16[768,768]{1,0:T(8,128)(2,1)} %refs_4_.1, bf16[768,768]{1,0:T(8,128)(2,1)} %refs_5_.2, bf16[768,768]{1,0:T(8,128)(2,1)} %refs_6_.1, ...), custom_call_target="tpu_custom_call" | custom-call | tf_op jit(solution)/shard_map/input_grad/pallas_call | solution.py:636
  366.2 4.6 %pad_maximum_fusion.refs_1_ = bf16[2,4,4,4,160,128]{5,4,3,2,1,0:T(8,128)(2,1)} fusion(bf16[1,4,4,4,160,128]{5,4,3,2,1,0:T(8,128)(2,1)} %bitcast.27, bf16[1,4,4,4,160,128]{5,4,3,2,1,0:T(8,128)(2,1)S(1)} %get-tuple-element.64), kind=kLoop, calls=%fused_computation | loop fusion | flops 2621440 | bytes 10485760 | tf_op jit(solution)/shard_map/stack | solution.py:685
  370.8 11.3 %unpack.1 = (f32[768,768]{1,0:T(8,128)}, f32[768,768]{1,0:T(8,128)}, f32[768,768]{1,0:T(8,128)}, f32[12,8,8,768]{3,2,1,0:T(8,128)}, f32[12,32]{1,0:T(8,128)}, /*index=5*/f32[8,8,768]{2,1,0:T(8,128)}, f32[768,1]{1,0:T(8,128)}) custom-call(s32[4]{0:T(128)} %pad_add_fusion.refs_0_, bf16[2,4,4,4,160,128]{5,4,3,2,1,0:T(8,128)(2,1)} %pad_maximum_fusion.refs_1_, ...), custom_call_target="tpu_custom_call" | custom-call | tf_op jit(solution)/shard_map/unpack/pallas_call | solution.py:753
  (112 shorter events, 62.1 us)
Async XLA Ops:
  7.2 97.1 %all-gather.3.cloned.1.call-start = ((), (), s32[]{:S(2)}) async-start(), calls=%async_computation.10 | async-start | bytes 10027008 | tf_op jit(solution)/shard_map/all_gather | solution.py:817
  9.2 154.3 %all-gather.5.cloned.1.call-start = ((), (), s32[]{:S(2)}) async-start(), calls=%async_computation.11 | async-start | bytes 3342336 | tf_op jit(solution)/shard_map/all_gather | solution.py:818
  14.2 30.1 %all-to-all-start = ((bf16[16,192,128]{2,1,0:T(8,128)(2,1)}), bf16[16,192,128]{2,1,0:T(8,128)(2,1)S(1)}, u32[]{:S(2)}, u32[]{:S(2)}) async-start(bf16[16,192,128]{2,1,0:T(8,128)(2,1)} %get-tuple-element.38), calls=%async_computation | async-start | bytes 1572864 | tf_op jit(solution)/shard_map/all_to_all | solution.py:815
  63.8 15.8 %all-to-all-start.1 = ((bf16[16,64,128]{2,1,0:T(8,128)(2,1)}), bf16[16,64,128]{2,1,0:T(8,128)(2,1)S(1)}, u32[]{:S(2)}, u32[]{:S(2)}) async-start(bf16[16,64,128]{2,1,0:T(8,128)(2,1)} %get-tuple-element.39), calls=%async_computation.1 | async-start | bytes 524288 | tf_op jit(solution)/shard_map/all_to_all | solution.py:821
  68.0 318.5 %reduce-scatter.2.cloned.1.call-start = ((), (), s32[]{:S(2)}) async-start(), calls=%async_computation.12 | async-start | bytes 10027008 | tf_op jit(solution)/shard_map/reduce_scatter | solution.py:828
  151.0 21.1 %all-to-all-start.4 = ((bf16[16,64,128]{2,1,0:T(8,128)(2,1)}), bf16[16,64,128]{2,1,0:T(8,128)(2,1)S(1)}, u32[]{:S(2)}, u32[]{:S(2)}) async-start(bf16[16,64,128]{2,1,0:T(8,128)(2,1)} %get-tuple-element.48), calls=%async_computation.4 | async-start | bytes 524288 | tf_op jit(solution)/shard_map/all_to_all | solution.py:832
  211.0 5.2 %collective-permute-start.2 = (bf16[160,128]{1,0:T(8,128)(2,1)S(1)}, bf16[160,128]{1,0:T(8,128)(2,1)S(1)}, u32[]{:S(2)}, u32[]{:S(2)}) collective-permute-start(bf16[160,128]{1,0:T(8,128)(2,1)S(1)} %reduce_sum.36), channel_id=1, source_target_pairs={{0,16},{1,17},{2,18},{3,19},{4,20},{5,21},{6,22},{7,23},{8,24},{9,... | collective-permute-start | bytes 122888 | tf_op jit(solution)/shard_map/ppermute | solution.py:668
  212.1 4.1 %collective-permute-start = (bf16[160,128]{1,0:T(8,128)(2,1)S(1)}, bf16[160,128]{1,0:T(8,128)(2,1)S(1)}, u32[]{:S(2)}, u32[]{:S(2)}) collective-permute-start(bf16[160,128]{1,0:T(8,128)(2,1)S(1)} %reduce_sum.36), channel_id=1, source_target_pairs={{0,48},{1,49},{2,50},{3,51},{4,52},{5,53},{6,54},{7,55},{8,56},{9,... | collective-permute-start | bytes 122888 | tf_op jit(solution)/shard_map/ppermute | solution.py:667
  216.2 3.8 collective-permute-start.3
  216.2 3.8 collective-permute-start.1
  220.0 5.8 %collective-permute-start.6 = (bf16[4,160,128]{2,1,0:T(8,128)(2,1)S(1)}, bf16[4,160,128]{2,1,0:T(8,128)(2,1)S(1)}, u32[]{:S(2)}, u32[]{:S(2)}) collective-permute-start(bf16[4,160,128]{2,1,0:T(8,128)(2,1)S(1)} %get-tuple-element.75), channel_id=1, source_target_pairs={{0,2},{1,3},{2,4},{3,5},{4,6},{5,7},{6,0},{7,1},{8,10},{9,11},{10,... | collective-permute-start | bytes 491528 | tf_op jit(solution)/shard_map/ppermute | solution.py:668
  220.1 5.8 %collective-permute-start.4 = (bf16[4,160,128]{2,1,0:T(8,128)(2,1)S(1)}, bf16[4,160,128]{2,1,0:T(8,128)(2,1)S(1)}, u32[]{:S(2)}, u32[]{:S(2)}) collective-permute-start(bf16[4,160,128]{2,1,0:T(8,128)(2,1)S(1)} %get-tuple-element.75), channel_id=1, source_target_pairs={{0,6},{1,7},{2,0},{3,1},{4,2},{5,3},{6,4},{7,5},{8,14},{9,15},{10,... | collective-permute-start | bytes 491528 | tf_op jit(solution)/shard_map/ppermute | solution.py:667
  225.9 5.4 %collective-permute-start.7 = (bf16[2,160,128]{2,1,0:T(8,128)(2,1)S(1)}, bf16[2,160,128]{2,1,0:T(8,128)(2,1)S(1)}, u32[]{:S(2)}, u32[]{:S(2)}) collective-permute-start(bf16[2,160,128]{2,1,0:T(8,128)(2,1)S(1)} %slice.67), channel_id=1, source_target_pairs={{0,2},{1,3},{2,4},{3,5},{4,6},{5,7},{6,0},{7,1},{8,10},{9,11},{10,... | collective-permute-start | bytes 245768 | tf_op jit(solution)/shard_map/ppermute | solution.py:673
  225.9 5.3 %collective-permute-start.5 = (bf16[2,160,128]{2,1,0:T(8,128)(2,1)S(1)}, bf16[2,160,128]{2,1,0:T(8,128)(2,1)S(1)}, u32[]{:S(2)}, u32[]{:S(2)}) collective-permute-start(bf16[2,160,128]{2,1,0:T(8,128)(2,1)S(1)} %slice.66), channel_id=1, source_target_pairs={{0,6},{1,7},{2,0},{3,1},{4,2},{5,3},{6,4},{7,5},{8,14},{9,15},{10,... | collective-permute-start | bytes 245768 | tf_op jit(solution)/shard_map/ppermute | solution.py:672
  231.4 22.8 %collective-permute-start.10 = (bf16[4,4,160,128]{3,2,1,0:T(8,128)(2,1)S(1)}, bf16[4,4,160,128]{3,2,1,0:T(8,128)(2,1)S(1)}, u32[]{:S(2)}, u32[]{:S(2)}) collective-permute-start(bf16[4,4,160,128]{3,2,1,0:T(8,128)(2,1)S(1)} %get-tuple-element.71), channel_id=1, source_target_pairs={{0,1},{1,64},{2,3},{3,66},{4,5},{5,68},{6,7},{7,70},{8,9},{9,72},{... | collective-permute-start | bytes 1966088 | tf_op jit(solution)/shard_map/ppermute | solution.py:668
  231.5 22.8 %collective-permute-start.8 = (bf16[4,4,160,128]{3,2,1,0:T(8,128)(2,1)S(1)}, bf16[4,4,160,128]{3,2,1,0:T(8,128)(2,1)S(1)}, u32[]{:S(2)}, u32[]{:S(2)}) collective-permute-start(bf16[4,4,160,128]{3,2,1,0:T(8,128)(2,1)S(1)} %get-tuple-element.71), channel_id=1, source_target_pairs={{0,65},{1,0},{2,67},{3,2},{4,69},{5,4},{6,71},{7,6},{8,73},{9,8},{... | collective-permute-start | bytes 1966088 | tf_op jit(solution)/shard_map/ppermute | solution.py:667
  234.1 57.2 %all-to-all-start.7 = ((bf16[16,64,768]{2,1,0:T(8,128)(2,1)}), bf16[16,64,768]{2,1,0:T(8,128)(2,1)}, u32[]{:S(2)}, u32[]{:S(2)}) async-start(bf16[16,64,768]{2,1,0:T(8,128)(2,1)} %get-tuple-element.55), calls=%async_computation.7 | async-start | bytes 3145728 | tf_op jit(solution)/shard_map/all_to_all | solution.py:833
  254.2 28.1 %collective-permute-start.11 = (bf16[2,4,160,128]{3,2,1,0:T(8,128)(2,1)S(1)}, bf16[2,4,160,128]{3,2,1,0:T(8,128)(2,1)S(1)}, u32[]{:S(2)}, u32[]{:S(2)}) collective-permute-start(bf16[2,4,160,128]{3,2,1,0:T(8,128)(2,1)S(1)} %slice.69), channel_id=1, source_target_pairs={{0,1},{1,64},{2,3},{3,66},{4,5},{5,68},{6,7},{7,70},{8,9},{9,72},{... | collective-permute-start | bytes 983048 | tf_op jit(solution)/shard_map/ppermute | solution.py:673
  254.4 28.0 %collective-permute-start.9 = (bf16[2,4,160,128]{3,2,1,0:T(8,128)(2,1)S(1)}, bf16[2,4,160,128]{3,2,1,0:T(8,128)(2,1)S(1)}, u32[]{:S(2)}, u32[]{:S(2)}) collective-permute-start(bf16[2,4,160,128]{3,2,1,0:T(8,128)(2,1)S(1)} %slice.68), channel_id=1, source_target_pairs={{0,65},{1,0},{2,67},{3,2},{4,69},{5,4},{6,71},{7,6},{8,73},{9,8},{... | collective-permute-start | bytes 983048 | tf_op jit(solution)/shard_map/ppermute | solution.py:672
  285.2 81.0 %collective-permute-start.12 = (bf16[4,4,4,160,128]{4,3,2,1,0:T(8,128)(2,1)}, bf16[4,4,4,160,128]{4,3,2,1,0:T(8,128)(2,1)}, u32[]{:S(2)}, u32[]{:S(2)}) collective-permute-start(bf16[4,4,4,160,128]{4,3,2,1,0:T(8,128)(2,1)} %get-tuple-element.65), channel_id=1, source_target_pairs={{0,8},{1,9},{2,10},{3,11},{4,12},{5,13},{6,14},{7,15},{8,0},{9,1},... | collective-permute-start | bytes 7864328 | tf_op jit(solution)/shard_map/ppermute | solution.py:684
  302.3 3.8 collective-permute-start.15
  302.3 3.8 collective-permute-start.13
  309.9 4.2 %collective-permute-start.19 = (bf16[4,8,768]{2,1,0:T(8,128)(2,1)S(1)}, bf16[4,8,768]{2,1,0:T(8,128)(2,1)S(1)}, u32[]{:S(2)}, u32[]{:S(2)}) collective-permute-start(bf16[4,8,768]{2,1,0:T(8,128)(2,1)S(1)} %get-tuple-element.77), channel_id=1, source_target_pairs={{0,2},{1,3},{2,4},{3,5},{4,6},{5,7},{6,0},{7,1},{8,10},{9,11},{10,... | collective-permute-start | bytes 147464 | tf_op jit(solution)/shard_map/ppermute | solution.py:668
  310.1 4.0 %collective-permute-start.17 = (bf16[4,8,768]{2,1,0:T(8,128)(2,1)S(1)}, bf16[4,8,768]{2,1,0:T(8,128)(2,1)S(1)}, u32[]{:S(2)}, u32[]{:S(2)}) collective-permute-start(bf16[4,8,768]{2,1,0:T(8,128)(2,1)S(1)} %get-tuple-element.77), channel_id=1, source_target_pairs={{0,6},{1,7},{2,0},{3,1},{4,2},{5,3},{6,4},{7,5},{8,14},{9,15},{10,... | collective-permute-start | bytes 147464 | tf_op jit(solution)/shard_map/ppermute | solution.py:667
  314.1 4.4 %collective-permute-start.20 = (bf16[2,8,768]{2,1,0:T(8,128)(2,1)S(1)}, bf16[2,8,768]{2,1,0:T(8,128)(2,1)S(1)}, u32[]{:S(2)}, u32[]{:S(2)}) collective-permute-start(bf16[2,8,768]{2,1,0:T(8,128)(2,1)S(1)} %slice.73), channel_id=1, source_target_pairs={{0,2},{1,3},{2,4},{3,5},{4,6},{5,7},{6,0},{7,1},{8,10},{9,11},{10,... | collective-permute-start | bytes 73736 | tf_op jit(solution)/shard_map/ppermute | solution.py:673
  314.1 4.4 %collective-permute-start.18 = (bf16[2,8,768]{2,1,0:T(8,128)(2,1)S(1)}, bf16[2,8,768]{2,1,0:T(8,128)(2,1)S(1)}, u32[]{:S(2)}, u32[]{:S(2)}) collective-permute-start(bf16[2,8,768]{2,1,0:T(8,128)(2,1)S(1)} %slice.72), channel_id=1, source_target_pairs={{0,6},{1,7},{2,0},{3,1},{4,2},{5,3},{6,4},{7,5},{8,14},{9,15},{10,... | collective-permute-start | bytes 73736 | tf_op jit(solution)/shard_map/ppermute | solution.py:672
  318.6 6.3 %collective-permute-start.23 = (bf16[4,4,8,768]{3,2,1,0:T(8,128)(2,1)S(1)}, bf16[4,4,8,768]{3,2,1,0:T(8,128)(2,1)S(1)}, u32[]{:S(2)}, u32[]{:S(2)}) collective-permute-start(bf16[4,4,8,768]{3,2,1,0:T(8,128)(2,1)S(1)} %get-tuple-element.73), channel_id=1, source_target_pairs={{0,1},{1,64},{2,3},{3,66},{4,5},{5,68},{6,7},{7,70},{8,9},{9,72},{... | collective-permute-start | bytes 589832 | tf_op jit(solution)/shard_map/ppermute | solution.py:668
  319.1 6.3 %collective-permute-start.21 = (bf16[4,4,8,768]{3,2,1,0:T(8,128)(2,1)S(1)}, bf16[4,4,8,768]{3,2,1,0:T(8,128)(2,1)S(1)}, u32[]{:S(2)}, u32[]{:S(2)}) collective-permute-start(bf16[4,4,8,768]{3,2,1,0:T(8,128)(2,1)S(1)} %get-tuple-element.73), channel_id=1, source_target_pairs={{0,65},{1,0},{2,67},{3,2},{4,69},{5,4},{6,71},{7,6},{8,73},{9,8},{... | collective-permute-start | bytes 589832 | tf_op jit(solution)/shard_map/ppermute | solution.py:667
  324.9 6.0 %collective-permute-start.24 = (bf16[2,4,8,768]{3,2,1,0:T(8,128)(2,1)S(1)}, bf16[2,4,8,768]{3,2,1,0:T(8,128)(2,1)S(1)}, u32[]{:S(2)}, u32[]{:S(2)}) collective-permute-start(bf16[2,4,8,768]{3,2,1,0:T(8,128)(2,1)S(1)} %slice.75), channel_id=1, source_target_pairs={{0,1},{1,64},{2,3},{3,66},{4,5},{5,68},{6,7},{7,70},{8,9},{9,72},{... | collective-permute-start | bytes 294920 | tf_op jit(solution)/shard_map/ppermute | solution.py:673
  325.4 5.5 %collective-permute-start.22 = (bf16[2,4,8,768]{3,2,1,0:T(8,128)(2,1)S(1)}, bf16[2,4,8,768]{3,2,1,0:T(8,128)(2,1)S(1)}, u32[]{:S(2)}, u32[]{:S(2)}) collective-permute-start(bf16[2,4,8,768]{3,2,1,0:T(8,128)(2,1)S(1)} %slice.74), channel_id=1, source_target_pairs={{0,65},{1,0},{2,67},{3,2},{4,69},{5,4},{6,71},{7,6},{8,73},{9,8},{... | collective-permute-start | bytes 294920 | tf_op jit(solution)/shard_map/ppermute | solution.py:672
  332.0 31.9 %collective-permute-start.25 = (bf16[4,4,4,8,768]{4,3,2,1,0:T(8,128)(2,1)}, bf16[4,4,4,8,768]{4,3,2,1,0:T(8,128)(2,1)}, u32[]{:S(2)}, u32[]{:S(2)}) collective-permute-start(bf16[4,4,4,8,768]{4,3,2,1,0:T(8,128)(2,1)} %get-tuple-element.69), channel_id=1, source_target_pairs={{0,8},{1,9},{2,10},{3,11},{4,12},{5,13},{6,14},{7,15},{8,0},{9,1},... | collective-permute-start | bytes 2359304 | tf_op jit(solution)/shard_map/ppermute | solution.py:684
  339.4 19.8 %all-to-all-start.5 = ((bf16[16,192,128]{2,1,0:T(8,128)(2,1)}), bf16[16,192,128]{2,1,0:T(8,128)(2,1)}, u32[]{:S(2)}, u32[]{:S(2)}) async-start(bf16[16,192,128]{2,1,0:T(8,128)(2,1)} %get-tuple-element.52), calls=%async_computation.5 | async-start | bytes 1572864 | tf_op jit(solution)/shard_map/all_to_all | solution.py:841
  (12 other events, 250.8 us)
Sparse Core Ops, SparseCore 0:
  11.1 90.3 all-gather.2
  104.5 54.1 all-gather.4
  163.1 123.9 reduce-scatter.1

commit v2 on v1

--- a/solution.py
+++ b/solution.py
@@ -59,38 +59,42 @@
     return pl.BlockSpec(memory_space=pltpu.SMEM)
 
 
-def project_kernel(tok_ref, gain_ref, wq_ref, wk_ref, wv_ref, normed_ref, out_ref):
+def project_kernel(tok_ref, gain_ref, wq_ref, wk_ref, wv_ref, win_ref, wback_ref, share_ref, out_ref):
     inputs = tok_ref[...].astype(F32)
-    normed = (inputs * rms_scale(inputs) * gain_ref[...]).astype(BF16)
-    normed_ref[...] = normed
-    half = normed.shape[0] // 2
+    normed = (inputs * rms_scale(inputs) * gain_ref[...][None, :]).astype(BF16)
+    rows, width = normed.shape
+    half = rows // 2
+    hidden = win_ref.shape[2]
+    share_ref[:hidden, :width] = win_ref[0].T
+    share_ref[:hidden, width:] = wback_ref[0].T
+    share_ref[hidden:, :width] = normed[:half]
+    share_ref[hidden:, width:] = normed[half:]
     queries = (dot(normed, wq_ref[...]).astype(BF16).astype(F32) * 0.125).astype(BF16)
     keys = dot(normed, wk_ref[...]).astype(BF16)
     values = dot(normed, wv_ref[...]).astype(BF16)
-    heads = queries.shape[1] // 64
+    heads = width // 64
     for h in range(heads):
         cols = slice(64 * h, 64 * h + 64)
-        out_ref[h, : 2 * half, :] = jnp.concatenate([queries[:, cols], keys[:, cols]], axis=1)
-        out_ref[h, 2 * half :, :] = jnp.concatenate(
-            [values[:half, cols], values[half:, cols]], axis=1
-        )
+        out_ref[h, :rows, :] = jnp.concatenate([queries[:, cols], keys[:, cols]], axis=1)
+        out_ref[h, rows:, :] = jnp.concatenate([values[:half, cols], values[half:, cols]], axis=1)
     for h in range(heads, HEAD_SLOTS):
         out_ref[h] = jnp.zeros_like(out_ref[h])
 
 
-def project(tokens, gain_one, w_query, w_key, w_value):
+def project(tokens, gain_one, w_query, w_key, w_value, expert_in, expert_out):
     rows, width = tokens.shape
+    hidden = expert_in.shape[2]
     return pl.pallas_call(
         project_kernel,
         name="project",
         out_shape=(
-            jax.ShapeDtypeStruct((rows, width), BF16),
+            jax.ShapeDtypeStruct((hidden + rows // 2, 2 * width), BF16),
             jax.ShapeDtypeStruct((HEAD_SLOTS, rows + rows // 2, 128), BF16),
         ),
-        in_specs=[vspec()] * 5,
+        in_specs=[vspec()] * 7,
         out_specs=(vspec(), vspec()),
         compiler_params=whole(),
-    )(tokens, gain_one.reshape(1, width), w_query, w_key, w_value)
+    )(tokens, gain_one, w_query, w_key, w_value, expert_in, expert_out)
 
 
 def bias_tile(table_ref, head, buckets, rows_first, shape, key_dim):
@@ -124,42 +128,32 @@
         v_s[128 * c + 64 : 128 * c + 128, :] = bottom
 
 
-def attend_kernel(buckets, head_ref, table_ref, qkv_ref, out_ref, keep_ref, lse_ref, q_s, k_s, v_s, bias_s, s_s):
+def attend_kernel(buckets, head_ref, table_ref, qkv_ref, out_ref, keep_ref, lse_ref, q_s, k_s, v_s, bias_s):
     head = head_ref[0]
     unpack_qkv(qkv_ref, q_s, k_s, v_s, True)
     bias_s[0] = bias_tile(table_ref, head, buckets, BLK, (BLK, BLK), 1)
     bias_s[1] = bias_tile(table_ref, head, buckets, 0, (BLK, BLK), 1)
     blocks = q_s.shape[0] // BLK
 
-    def fold(scores):
-        return jnp.maximum(scores[:, :128], scores[:, 128:])
-
-    def one_query(qb, unused):
-        rows = pl.ds(pl.multiple_of(qb * BLK, BLK), BLK)
-        query = q_s[rows, :]
-
-        def score(kb):
-            return dot(query, k_s[pl.ds(pl.multiple_of(kb * BLK, BLK), BLK), :], NT)
-
-        def far(kb, top):
-            scores = score(kb)
-            s_s[kb] = scores
-            return jnp.maximum(top, fold(scores))
-
-        top = lax.fori_loop(0, qb - 1, far, jnp.full((BLK, 128), NEG_LARGE, F32))
-        before = jnp.maximum(qb - 1, 0)
-        scores = jnp.where(qb > 0, score(before) + bias_s[0], NEG_LARGE)
-        s_s[before] = scores
-        top = jnp.maximum(top, fold(scores))
-        scores = score(qb) + bias_s[1]
-        s_s[qb] = scores
-        top = jnp.max(jnp.maximum(top, fold(scores)), axis=1, keepdims=True)
-
-        def weigh(kb, total):
-            weights = jnp.exp(s_s[kb] - top).astype(BF16)
-            return total + dot(weights, v_s[pl.ds(pl.multiple_of(kb * BLK, BLK), BLK), :])
-
-        total = lax.fori_loop(0, qb + 1, weigh, jnp.zeros((BLK, 128), F32))
+    for qb in range(blocks):
+        query = q_s[BLK * qb : BLK * qb + BLK, :]
+        near = max(qb - 1, 0) * BLK
+        parts = []
+        if near:
+            parts.append((0, dot(query, k_s[:near, :], NT)))
+        if qb:
+            parts.append((near, dot(query, k_s[near : near + BLK, :], NT) + bias_s[0]))
+        parts.append((BLK * qb, dot(query, k_s[BLK * qb : BLK * qb + BLK, :], NT) + bias_s[1]))
+        top = parts[-1][1]
+        top = jnp.maximum(top[:, :128], top[:, 128:])
+        for unused, scores in parts[:-1]:
+            for j in range(scores.shape[1] // 128):
+                top = jnp.maximum(top, scores[:, 128 * j : 128 * j + 128])
+        top = jnp.max(top, axis=1, keepdims=True)
+        total = jnp.zeros((BLK, 128), F32)
+        for first, scores in parts:
+            weights = jnp.exp(scores - top).astype(BF16)
+            total = total + dot(weights, v_s[first : first + scores.shape[1], :])
         norm = total[:, 64:65]
         out = total[:, :64] / norm
         log_total = top + jnp.log(norm)
@@ -172,9 +166,6 @@
             place = qb * (BLK // 128) + part
             out_ref[place] = two.astype(BF16)
             keep_ref[place] = two
-        return unused
-
-    lax.fori_loop(0, blocks, one_query, 0)
 
 
 def attend(head, rel_table, qkv):
@@ -196,7 +187,6 @@
             pltpu.VMEM((length, 64), BF16),
             pltpu.VMEM((length, 128), BF16),
             pltpu.VMEM((2, BLK, BLK), F32),
-            pltpu.VMEM((blocks, BLK, BLK), F32),
         ],
         compiler_params=whole(),
     )(head, rel_table, qkv)
@@ -210,9 +200,8 @@
     go_ref,
     keep_ref,
     lse_ref,
-    normed_ref,
     dqkv_ref,
-    dw_ref,
+    bias_ref,
     q_s,
     k_s,
     v_s,
@@ -224,7 +213,6 @@
     dv_s,
     bias_s,
     acc_s,
-    low_s,
 ):
     head = head_ref[0]
     length = q_s.shape[0]
@@ -246,16 +234,18 @@
     dk_s[...] = jnp.zeros_like(dk_s)
     dv_s[...] = jnp.zeros_like(dv_s)
 
-    def one_query(qb, far_sum):
-        rows = pl.ds(pl.multiple_of(qb * BLK, BLK), BLK)
+    far_sum = jnp.zeros((8, BLK), F32)
+    for qb in range(blocks):
+        rows = slice(BLK * qb, BLK * qb + BLK)
         query, grad = q_s[rows, :], go_s[rows, :]
         lse = lse_ref[qb][:1, :]
         delta = delta_s[:1, rows]
-
-        def block(kb, near, grad_query, far_sum):
-            cols = pl.ds(pl.multiple_of(kb * BLK, BLK), BLK)
+        grad_query = jnp.zeros((64, BLK), F32)
+        for kb in range(qb + 1):
+            cols = slice(BLK * kb, BLK * kb + BLK)
+            near = kb - qb + 1
             scores = dot(k_s[cols, :], query, NT)
-            if near is not None:
+            if near >= 0:
                 scores = scores + bias_s[near]
             probs = jnp.exp(scores - lse)
             grad_probs = dot(v_s[cols, :], grad, NT)
@@ -264,45 +254,20 @@
             dk_s[cols, :] += dot(grad_scores, query)
             grad_query = grad_query + dot(kt_s[:, cols], grad_scores)
             wide = grad_scores.astype(F32)
-            if near is None:
+            if near < 0:
                 far_sum = far_sum + jnp.sum(wide.reshape(BLK // 8, 8, BLK), axis=0)
             else:
                 acc_s[near] += wide
-            return grad_query, far_sum
-
-        start = (jnp.zeros((64, BLK), F32), far_sum)
-        grad_query, far_sum = lax.fori_loop(
-            0, qb - 1, lambda kb, state: block(kb, None, *state), start
-        )
         dq_s[:, rows] = grad_query
-
-        @pl.when(qb > 0)
-        def _():
-            more, unused = block(qb - 1, 0, jnp.zeros((64, BLK), F32), None)
-            dq_s[:, rows] += more
-
-        more, unused = block(qb, 1, jnp.zeros((64, BLK), F32), None)
-        dq_s[:, rows] += more
-        return far_sum
-
-    far_sum = lax.fori_loop(0, blocks, one_query, jnp.zeros((8, BLK), F32))
 
     for c in range(count):
         here = slice(128 * c, 128 * c + 128)
         dq_t = (dq_s[:, here] * 0.125).astype(BF16)
         dk = dk_s[here, :].astype(BF16)
         dv = dv_s[here, :].astype(BF16)
-        pair = jnp.concatenate([dq_t.T, dk], axis=1)
-        dqkv_ref[c, :128, :] = pair
+        dqkv_ref[c, :128, :] = jnp.concatenate([dq_t.T, dk], axis=1)
         dqkv_ref[c, 128:192, :] = jnp.concatenate([dv[:64], dv[64:]], axis=1)
-        low_s[:128, here] = pair.T
-        low_s[128:192, here] = dv.T
-
-    width = normed_ref.shape[1]
-    grads = dot(low_s[...], normed_ref[...])
-    pair, third = grads[:128].T, grads[128:192].T
-    shares = dw_ref.shape[0]
-    each = width // shares
+
     lane = lax.broadcasted_iota(jnp.int32, (16, 128), 1)
     dist0 = (
         BLK
@@ -325,30 +290,20 @@
         mine = reach + total(far_sum) if b == buckets - 1 else reach - above
         above = reach
         row = jnp.where(lane == b, mine, row)
-    row = row.astype(BF16)
-    for s in range(shares):
-        mine = slice(each * s, each * s + each)
-        dw_ref[s, :each, :] = pair[mine].astype(BF16)
-        last = third[mine].astype(BF16)
-        dw_ref[s, each : each + each // 2, :] = jnp.concatenate(
-            [last[: each // 2], last[each // 2 :]], axis=1
-        )
-        dw_ref[s, each + each // 2 :, :] = row
-
-
-def attend_back(head, rel_table, qkv, grad_heads, keep, lse, normed_all, shares):
+    bias_ref[...] = row
+
+
+def attend_back(head, rel_table, qkv, grad_heads, keep, lse):
     count = qkv.shape[0]
     length = 128 * count
-    width = normed_all.shape[1]
-    each = width // shares
     return pl.pallas_call(
         lambda *refs: attend_back_kernel(rel_table.shape[1], *refs),
         name="attend_back",
         out_shape=(
             jax.ShapeDtypeStruct(qkv.shape, BF16),
-            jax.ShapeDtypeStruct((shares, each + each // 2 + 16, 128), BF16),
-        ),
-        in_specs=[sspec(), sspec()] + [vspec()] * 5,
+            jax.ShapeDtypeStruct((16, 128), F32),
+        ),
+        in_specs=[sspec(), sspec()] + [vspec()] * 4,
         out_specs=(vspec(), vspec()),
         scratch_shapes=[
             pltpu.VMEM((length, 64), BF16),
@@ -362,10 +317,63 @@
             pltpu.VMEM((length, 64), F32),
             pltpu.VMEM((2, BLK, BLK), F32),
             pltpu.VMEM((2, BLK, BLK), F32),
-            pltpu.VMEM((192, length), BF16),
         ],
         compiler_params=whole(),
-    )(head, rel_table, qkv, grad_heads, keep, lse, normed_all)
+    )(head, rel_table, qkv, grad_heads, keep, lse)
+
+
+def head_grads_kernel(dqkv_ref, normed_ref, bias_ref, sums_ref, out_ref):
+    count = dqkv_ref.shape[0]
+    width = normed_ref.shape[2] // 2
+    tokens = count * 64
+    first = normed_ref[:, :, :width].reshape(tokens, width)
+    second = normed_ref[:, :, width:].reshape(tokens, width)
+    pairs = dot(dqkv_ref[:, :64, :].reshape(tokens, 128), first, TN) + dot(
+        dqkv_ref[:, 64:128, :].reshape(tokens, 128), second, TN
+    )
+    two = dqkv_ref[:, 128:192, :].reshape(tokens, 128)
+    third = dot(two, first, TN)[:64] + dot(two, second, TN)[64:]
+    pairs, third = pairs.T, third.T
+    total = sums_ref[0].astype(F32)
+    for c in range(1, count):
+        total = total + sums_ref[c].astype(F32)
+    shares = out_ref.shape[0]
+    each = width // shares
+    row = bias_ref[...].astype(BF16)
+    for s in range(shares):
+        mine = slice(each * s, each * s + each)
+        out_ref[s, :each, :] = pairs[mine].astype(BF16)
+        last = third[mine].astype(BF16)
+        out_ref[s, each : each + each // 2, :] = jnp.concatenate(
+            [last[: each // 2], last[each // 2 :]], axis=1
+        )
+        at = each + each // 2
+        out_ref[s, at : at + 16, :] = row
+        part = total[8 * s : 8 * s + 8]
+        out_ref[s, at + 16 :, :] = jnp.concatenate(
+            [part[:, 128 * j : 128 * j + 128] for j in range(width // 128)], axis=0
+        ).astype(BF16)
+
+
+def head_grads(dqkv, shared, bias, sums, shares):
+    count, rows, wide = shared.shape
+    width = wide // 2
+    each = width // shares
+    held = each + each // 2 + 16 + width // 16
+    return pl.pallas_call(
+        head_grads_kernel,
+        name="head_grads",
+        grid=(1,),
+        out_shape=jax.ShapeDtypeStruct((shares, held, 128), BF16),
+        in_specs=[
+            vspec(),
+            pl.BlockSpec((count, 64, wide), lambda i: (0, rows // 64 - 1, 0)),
+            vspec(),
+            vspec(),
+        ],
+        out_specs=vspec(),
+        compiler_params=whole(),
+    )(dqkv, shared, bias, sums)
 
 
 def heads_to_rows(ref, scratch):
@@ -396,7 +404,7 @@
     heads_to_rows(heads_ref, att_ref)
     mixed = tok_ref[...].astype(F32) + dot(att_ref[...], wo_ref[...])
     mixed_ref[...] = mixed
-    second = (mixed * rms_scale(mixed) * gain_ref[...]).astype(BF16)
+    second = (mixed * rms_scale(mixed) * gain_ref[...][None, :]).astype(BF16)
     second_ref[...] = second
     logits = dot(second, wr_ref[...])
     ids = lax.broadcasted_iota(jnp.int32, (rows, experts), 1)
@@ -449,7 +457,7 @@
         in_specs=[vspec()] * 7,
         out_specs=(vspec(),) * 6,
         compiler_params=whole(),
-    )(tokens, cotangent, heads, w_out, gain_two.reshape(1, width), w_router, routes)
+    )(tokens, cotangent, heads, w_out, gain_two, w_router, routes)
 
 
 def expert_kernel(rows_ref, w_ref, back_ref, dw_ref, x_s, g_s, y_s, dx_s):
@@ -465,7 +473,8 @@
         y_s[...] = jnp.zeros_like(y_s)
         dx_s[...] = jnp.zeros_like(dx_s)
 
-    w_in, w_back = w_ref[:, :width], w_ref[:, width:]
+    weights = w_ref[...].reshape(-1, 2 * width)
+    w_in, w_back = weights[:, :width], weights[:, width:]
     pre = dot(x_s[...], w_in, NT)
     square = pre * pre
     curve = jnp.tanh(0.7978845608 * (pre + 0.044715 * square * pre))
@@ -487,26 +496,28 @@
             back_ref[s, capacity:, :] = dx_s[here, :].astype(BF16)
 
 
-def expert_both(rows, weights):
+def expert_both(rows, shared):
     sources, both, width = rows.shape
-    hidden = weights.shape[0]
-    chunk = 512
+    count, given, wide = shared.shape
+    each = given - 64
+    at_once = 2
+    chunk = at_once * each
     held = sources * both // 2
     return pl.pallas_call(
         expert_kernel,
         name="expert_both",
-        grid=(hidden // chunk,),
+        grid=(count // at_once,),
         out_shape=(
             jax.ShapeDtypeStruct(rows.shape, BF16),
-            jax.ShapeDtypeStruct(weights.shape, BF16),
+            jax.ShapeDtypeStruct((count * each, wide), BF16),
         ),
         in_specs=[
             pl.BlockSpec(rows.shape, lambda i: (0, 0, 0)),
-            pl.BlockSpec((chunk, 2 * width), lambda i: (i, 0)),
+            pl.BlockSpec((at_once, each, wide), lambda i: (i, 0, 0)),
         ],
         out_specs=(
             pl.BlockSpec(rows.shape, lambda i: (0, 0, 0)),
-            pl.BlockSpec((chunk, 2 * width), lambda i: (i, 0)),
+            pl.BlockSpec((chunk, wide), lambda i: (i, 0)),
         ),
         scratch_shapes=[
             pltpu.VMEM((held, width), BF16),
@@ -515,7 +526,7 @@
             pltpu.VMEM((held, width), F32),
         ],
         compiler_params=whole(),
-    )(rows, weights)
+    )(rows, shared)
 
 
 def combine_kernel(
@@ -563,7 +574,7 @@
     grad_router = dot(grad_logits, second.astype(F32), TN, HIGHEST)
     scale = rms_scale(mixed)
     grad_gain = jnp.sum(grad_second * mixed * scale, axis=0, keepdims=True)
-    grad_mixed = grad_out + norm_back(mixed, scale, gain_ref[...], grad_second)
+    grad_mixed = grad_out + norm_back(mixed, scale, gain_ref[...][None, :], grad_second)
     grad_mixed_ref[...] = grad_mixed
     grad_branch = grad_mixed.astype(BF16)
     grad_att = dot(grad_branch, wo_ref[...], NT).astype(BF16)
@@ -610,7 +621,7 @@
         second,
         attended,
         routes,
-        gain_two.reshape(1, width),
+        gain_two,
         w_router,
         w_out,
     )
@@ -628,7 +639,7 @@
     grad_normed = grad_normed + dot(dk_s[...], wk_ref[...], NT)
     grad_normed = grad_normed + dot(dv_s[...], wv_ref[...], NT)
     inputs = tok_ref[...].astype(F32)
-    out_ref[...] = mixed_ref[...] + norm_back(inputs, rms_scale(inputs), gain_ref[...], grad_normed)
+    out_ref[...] = mixed_ref[...] + norm_back(inputs, rms_scale(inputs), gain_ref[...][None, :], grad_normed)
 
 
 def input_grad(tokens, gain_one, grads, w_query, w_key, w_value, grad_mixed):
@@ -641,7 +652,7 @@
         out_specs=vspec(),
         scratch_shapes=[pltpu.VMEM((rows, width), BF16)] * 3,
         compiler_params=whole(),
-    )(tokens, gain_one.reshape(1, width), grads, w_query, w_key, w_value, grad_mixed)
+    )(tokens, gain_one, grads, w_query, w_key, w_value, grad_mixed)
 
 
 def coordinates(index):
@@ -662,93 +673,111 @@
     return pairs
 
 
-def ring_gather(block, dim):
-    axes = ("context", "expert")
-    ahead = lax.ppermute(block, axes, shifted(dim, -1))
-    behind = lax.ppermute(block, axes, shifted(dim, 1))
-    half = block.shape[0] // 2
-    across = jnp.concatenate(
-        [
-            lax.ppermute(ahead[:half], axes, shifted(dim, -1)),
-            lax.ppermute(behind[half:], axes, shifted(dim, 1)),
-        ],
-        axis=0,
-    )
-    return jnp.stack([block, ahead, across, behind])
+AXES = ("context", "expert")
+
+
+def direct_gather(block, dim):
+    return jnp.stack([block] + [lax.ppermute(block, AXES, shifted(dim, -by)) for by in (1, 2, 3)])
 
 
 def gather_all(piece):
-    filled = ring_gather(piece, 2)
-    filled = ring_gather(filled, 1)
-    filled = ring_gather(filled, 0)
-    other = lax.ppermute(filled, ("context", "expert"), shifted(3, 1))
-    return jnp.stack([filled, other])
+    filled = direct_gather(direct_gather(piece, 2), 0)
+    half = filled.shape[0] // 2
+    ahead = lax.ppermute(filled, AXES, shifted(1, -1))
+    behind = lax.ppermute(filled, AXES, shifted(1, 1))
+    across = (
+        lax.ppermute(ahead[:half], AXES, shifted(1, -1)),
+        lax.ppermute(behind[half:], AXES, shifted(1, 1)),
+    )
+    mine = (filled, ahead, behind) + across
+    other = tuple(lax.ppermute(part, AXES, shifted(3, 1)) for part in mine)
+    return mine + other
 
 
 def unpack_kernel(
     buckets,
     place_ref,
-    piece_ref,
-    late_ref,
-    gain_ref,
     wq_ref,
     wk_ref,
     wv_ref,
-    dwq_ref,
-    dwk_ref,
-    dwv_ref,
-    dwo_ref,
-    bias_ref,
-    small_ref,
-    gain_grad_ref,
+    *rest,
 ):
+    parts, (dwq_ref, dwk_ref, dwv_ref, dwo_ref, bias_ref, small_ref, router_ref, gain_grad_ref) = rest[:10], rest[10:18]
+    all_s, sems = rest[18:]
     expert = pl.program_id(0)
+
+    @pl.when(expert == 0)
+    def _():
+        copies = []
+        for core in range(2):
+            for i in range(5):
+                part = parts[5 * core + i]
+                half = all_s.shape[2] // 2
+                place = (
+                    all_s.at[core, (0, 1, 3)[i]]
+                    if i < 3
+                    else all_s.at[core, 2, pl.ds(half * (i - 3), half)]
+                )
+                copies.append(pltpu.make_async_copy(part, place, sems.at[5 * core + i]))
+        for copy in copies:
+            copy.start()
+        for copy in copies:
+            copy.wait()
+
     my_x, my_y, my_z, my_core = (place_ref[i] for i in range(4))
     each = dwq_ref.shape[0]
     half = each // 2
     width = dwq_ref.shape[1]
-    y = expert // 2
-    rel_y = lax.rem(y - my_y + 4, 4)
+    rel_y = lax.rem(expert // 2 - my_y + 4, 4)
 
     def rel(context):
         x = context // 8 * 2 + lax.rem(expert, 2)
         return (
             jnp.where(my_core == context % 2, 0, 1),
+            rel_y,
             lax.rem(x - my_x + 4, 4),
-            rel_y,
             lax.rem(context // 2 % 4 - my_z + 4, 4),
         )
 
+    at = each + half
     bias = []
     for j in range(width // 128):
         cols = slice(128 * j, 128 * j + 128)
-        one, two = piece_ref[rel(2 * j)].astype(F32), piece_ref[rel(2 * j + 1)].astype(F32)
+        one, two = all_s[rel(2 * j)].astype(F32), all_s[rel(2 * j + 1)].astype(F32)
         dwq_ref[:, cols] = jnp.concatenate([one[:each, :64], two[:each, :64]], axis=1)
         dwk_ref[:, cols] = jnp.concatenate([one[:each, 64:], two[:each, 64:]], axis=1)
-        dwv_ref[:half, cols] = jnp.concatenate(
-            [one[each : each + half, :64], two[each : each + half, :64]], axis=1
-        )
-        dwv_ref[half:, cols] = jnp.concatenate(
-            [one[each : each + half, 64:], two[each : each + half, 64:]], axis=1
-        )
-        bias += [one[each + half : each + half + 1], two[each + half : each + half + 1]]
+        dwv_ref[:half, cols] = jnp.concatenate([one[each:at, :64], two[each:at, :64]], axis=1)
+        dwv_ref[half:, cols] = jnp.concatenate([one[each:at, 64:], two[each:at, 64:]], axis=1)
+        bias += [one[at : at + 1], two[at : at + 1]]
+        for i, block in enumerate((one, two)):
+            for k in range(width // 128):
+                dwo_ref[2 * j + i, :, 128 * k : 128 * k + 128] = block[at + 16 + 8 * k : at + 24 + 8 * k]
     bias_ref[...] = jnp.concatenate(bias, axis=0)[:, :buckets]
-    for c in range(width // 64):
-        dwo_ref[c] = late_ref[rel(c)].astype(F32)
-    small_ref[0] = late_ref[rel(width // 64)].astype(F32)
-    summed = jnp.sum(
+    block = all_s[rel(width // 64)].astype(F32)
+    small = jnp.concatenate(
+        [block[at + 16 + 8 * k : at + 24 + 8 * k] for k in range(width // 128)], axis=1
+    )
+
+    @pl.when(expert == 0)
+    def _():
+        router_ref[...] = small.T
+
+    @pl.when(expert == 1)
+    def _():
+        small_ref[...] = small
+
+    prod = (
         dwq_ref[...] * wq_ref[...].astype(F32)
         + dwk_ref[...] * wk_ref[...].astype(F32)
-        + dwv_ref[...] * wv_ref[...].astype(F32),
-        axis=1,
-        keepdims=True,
-    )
-    gain_grad_ref[...] = summed / gain_ref[...]
-
-
-def unpack(place, pieces, late, gain_one, w_query, w_key, w_value, heads, buckets, experts):
+        + dwv_ref[...] * wv_ref[...].astype(F32)
+    )
+    gain_grad_ref[...] = dot(jnp.ones((8, width), F32), prod, NT, HIGHEST)
+
+
+def unpack(place, parts, w_query, w_key, w_value, heads, buckets, experts):
     width = w_query.shape[0]
     each = width // experts
+    held = parts[0].shape[2]
     rows = pl.BlockSpec((each, width), lambda i: (i, 0))
     return pl.pallas_call(
         lambda *refs: unpack_kernel(buckets, *refs),
@@ -760,33 +789,64 @@
             jax.ShapeDtypeStruct((width, width), F32),
             jax.ShapeDtypeStruct((heads, experts, 8, width), F32),
             jax.ShapeDtypeStruct((heads, buckets), F32),
-            jax.ShapeDtypeStruct((experts, 8, width), F32),
-            jax.ShapeDtypeStruct((width, 1), F32),
-        ),
-        in_specs=[
-            sspec(),
-            vspec(),
-            vspec(),
-            pl.BlockSpec((each, 1), lambda i: (i, 0)),
-            rows,
-            rows,
-            rows,
-        ],
+            jax.ShapeDtypeStruct((8, width), F32),
+            jax.ShapeDtypeStruct((width, 8), F32),
+            jax.ShapeDtypeStruct((experts, 8, each), F32),
+        ),
+        in_specs=[sspec(), rows, rows, rows] + [pl.BlockSpec(memory_space=pl.ANY)] * 10,
         out_specs=(
             rows,
             rows,
             rows,
             pl.BlockSpec((heads, None, 8, width), lambda i: (0, i, 0, 0)),
             pl.BlockSpec((heads, buckets), lambda i: (0, 0)),
-            pl.BlockSpec((1, 8, width), lambda i: (i, 0, 0)),
-            pl.BlockSpec((each, 1), lambda i: (i, 0)),
-        ),
-        compiler_params=whole(),
-    )(place, pieces, late, gain_one.reshape(width, 1), w_query, w_key, w_value)
+            pl.BlockSpec((8, width), lambda i: (0, 0)),
+            pl.BlockSpec((width, 8), lambda i: (0, 0)),
+            pl.BlockSpec((None, 8, each), lambda i: (i, 0, 0)),
+        ),
+        scratch_shapes=[
+            pltpu.VMEM((2, 4, 4, 4, held, 128), BF16),
+            pltpu.SemaphoreType.DMA((10,)),
+        ],
+        compiler_params=whole(),
+    )(place, w_query, w_key, w_value, *parts)
+
+
+def add_kernel(in_ref, out_ref):
+    total = in_ref[0].astype(F32)
+    for i in range(1, in_ref.shape[0]):
+        total = total + in_ref[i].astype(F32)
+    out_ref[...] = total.astype(BF16)
 
 
 def add_up(received):
-    return jnp.sum(received.astype(F32), axis=0)
+    return pl.pallas_call(
+        add_kernel,
+        name="add_up",
+        out_shape=jax.ShapeDtypeStruct(received.shape[1:], BF16),
+        in_specs=[vspec()],
+        out_specs=vspec(),
+        compiler_params=whole(),
+    )(received)
+
+
+def split_kernel(in_ref, first_ref, second_ref):
+    width = first_ref.shape[1]
+    first_ref[0] = in_ref[:, :width].astype(F32).T
+    second_ref[0] = in_ref[:, width:].astype(F32).T
+
+
+def split_back(grads):
+    rows, wide = grads.shape
+    width = wide // 2
+    return pl.pallas_call(
+        split_kernel,
+        name="split_back",
+        out_shape=(jax.ShapeDtypeStruct((1, width, rows), F32),) * 2,
+        in_specs=[vspec()],
+        out_specs=(vspec(),) * 2,
+        compiler_params=whole(),
+    )(grads)
 
 
 def shards(
@@ -811,11 +871,9 @@
     context = lax.axis_index("context")
     head = jnp.minimum(context, heads - 1).astype(jnp.int32).reshape(1)
 
-    normed, packed = project(inputs, gain_one, w_query, w_key, w_value)
+    share, packed = project(inputs, gain_one, w_query, w_key, w_value, expert_in, expert_out)
     qkv = lax.all_to_all(packed, "context", split_axis=0, concat_axis=0, tiled=True)
-    own_weights = jnp.concatenate([expert_in[0].T, expert_out[0].T], axis=1)
-    weights = lax.all_gather(own_weights, "context", axis=0, tiled=True)
-    normed_all = lax.all_gather(normed, "context", axis=0, tiled=True)
+    shared = lax.all_gather(share, "context", axis=0, tiled=False)
 
     out_heads, keep, lse = attend(head, rel_table, qkv)
     out_rows = lax.all_to_all(out_heads, "context", split_axis=0, concat_axis=0, tiled=True)
@@ -823,7 +881,7 @@
         inputs, grad_out, out_rows, w_out, gain_two, w_router, routes_here, experts
     )
     received = lax.all_to_all(send, "expert", split_axis=0, concat_axis=0, tiled=True)
-    back, weight_grads = expert_both(received, weights)
+    back, weight_grads = expert_both(received, shared)
     returned = lax.all_to_all(back, "expert", split_axis=0, concat_axis=0, tiled=True)
     own_grads = lax.psum_scatter(weight_grads, "context", scatter_dimension=0, tiled=True)
     block_out, grad_mixed, grad_heads, sums = combine(
@@ -831,35 +889,33 @@
     )
     grad_here = lax.all_to_all(grad_heads, "context", split_axis=0, concat_axis=0, tiled=True)
     sums = lax.all_to_all(sums, "context", split_axis=0, concat_axis=0, tiled=True)
-    sums = add_up(sums).astype(BF16).reshape(experts, 8, width)
-    sums = lax.all_to_all(sums, "expert", split_axis=0, concat_axis=0, tiled=True)
-    late = gather_all(add_up(sums).astype(BF16))
-
-    dqkv, dw = attend_back(head, rel_table, qkv, grad_here, keep, lse, normed_all, experts)
-    dw = lax.all_to_all(dw, "expert", split_axis=0, concat_axis=0, tiled=True)
-    pieces = gather_all(add_up(dw).astype(BF16))
+
+    dqkv, bias = attend_back(head, rel_table, qkv, grad_here, keep, lse)
     grads = lax.all_to_all(dqkv, "context", split_axis=0, concat_axis=0, tiled=True)
+    terms = head_grads(dqkv, shared, bias, sums, experts)
+    terms = lax.all_to_all(terms, "expert", split_axis=0, concat_axis=0, tiled=True)
+    parts = gather_all(add_up(terms))
     grad_tokens = input_grad(inputs, gain_one, grads, w_query, w_key, w_value, grad_mixed)
 
     expert = lax.axis_index("expert")
     place = jnp.stack(coordinates(context * experts + expert)).astype(jnp.int32)
-    dwq, dwk, dwv, dwo, bias, small, gain_grad = unpack(
-        place, pieces, late, gain_one, w_query, w_key, w_value, heads, buckets, experts
-    )
-    own_grads = own_grads.astype(F32)
+    dwq, dwk, dwv, dwo, bias, small, router, gain_grad = unpack(
+        place, parts, w_query, w_key, w_value, heads, buckets, experts
+    )
+    grad_in, grad_back = split_back(own_grads)
     return (
         block_out[None],
         grad_tokens[None],
-        gain_grad.reshape(width),
+        gain_grad[:, 0, :].reshape(width) / gain_one,
         dwq,
         dwk,
         dwv,
         dwo.reshape(width, width),
         bias,
-        small[1, 0],
-        small[0].T,
-        own_grads[:, :width].T[None],
-        own_grads[:, width:].T[None],
+        small[0],
+        router,
+        grad_in,
+        grad_back,
     )
 
 

time: 397 us -> 350 us (0.88)
  starting transfers between devices: 88.6 us -> 43.5 us
  blocking collectives: 65.6 us -> 83.6 us
  other arithmetic: 18.3 us -> 2.15 us
  Pallas kernels: 89.2 us -> 80.3 us
  local copies, waits for them, and re-layouts: 11.8 us -> 19.1 us
    ppermute x26 -> x15, starting transfers between devices: 46.7 us -> 18 us  [the longest x5 6.66 us: gather_all(): other = tuple((lax.ppermute(part, AXES, shifted(3, 1)) for part in mine))]
    ppermute x26 -> x15, waiting for transfers between devices: 55.9 us -> 31.1 us  [the longest x1 15.8 us: gather_all(): behind = lax.ppermute(filled, AXES, shifted(1, 1))]
    all_gather x2 -> x1, waiting for transfers between devices: 0.02 us -> 23.1 us  [shards(): shared = lax.all_gather(share, 'context', axis=0, tiled=False)]
    all_to_all x1, waiting for transfers between devices: 0.01 us -> 15.2 us  [shards(): lax.all_to_all(sums, 'context', split_axis=0, concat_axis=0, tiled=True)]
    all_to_all x1, blocking collectives: 20 us -> 34.3 us  [shards(): lax.all_to_all(send, 'expert', split_axis=0, concat_axis=0, tiled=True)]
    all_to_all x1 -> x0, starting transfers between devices: 12.4 us -> none  [shards(): lax.all_to_all(grad_heads, 'context', split_axis=0, concat_axis=0, tiled=...]
    pallas_call x1, Pallas kernels: 18.6 us -> 7.03 us  [attend(): pl.pallas_call(lambda *refs: attend_kernel(rel_table.shape[1], *refs), na...]
    pallas_call x1 -> x4, Pallas kernels: 18.3 us -> 29.4 us  [the longest x1 20.1 us: expert_both(): pl.pallas_call(expert_kernel, name='expert_both', grid=(count // at_once,...]
  transfers between devices with their start and end apart: 34 -> 21, of which waited for: 17 -> 11; matrix products, arithmetic and copies ran while one was open for 6% -> 3% of each run, Pallas kernels for 23% -> 15%
where the time goes in v2:
time: 350 us; the launch traced here: 349 us
  waiting for transfers between devices  106 us (30%)
  blocking collectives  83.6 us (24%)
  Pallas kernels  80.3 us (23%)
  starting transfers between devices  43.5 us (12%)
  local copies, waits for them, and re-layouts  19.1 us (5%)
  between operations  14.2 us (4%)
    all_to_all x1, blocking collectives, shards(): lax.all_to_all(send, 'expert', split_axis=0, concat_axis=0, tiled=True)  34.3 us
    all_gather x1, waiting for transfers between devices, shards(): shared = lax.all_gather(share, 'context', axis=0, tiled=False)  23.1 us
    all_to_all x1, blocking collectives, shards(): lax.all_to_all(back, 'expert', split_axis=0, concat_axis=0, tiled=True)  20.6 us
    pallas_call x1, Pallas kernels, expert_both(): pl.pallas_call(expert_kernel, name='expert_both', grid=(count // at_once,...  20.1 us
    all_to_all x1, waiting for transfers between devices, shards(): lax.all_to_all(packed, 'context', split_axis=0, concat_axis=0, tiled=True)  17.6 us
    all_to_all x1, blocking collectives, shards(): lax.all_to_all(grad_heads, 'context', split_axis=0, concat_axis=0, tiled=...  16.1 us
    ppermute x1, waiting for transfers between devices, gather_all(): behind = lax.ppermute(filled, AXES, shifted(1, 1))  15.8 us
    unnamed x31, local copies, waits for them, and re-layouts  15.2 us
  transfers between devices with their start and end apart: 21, of which 11 were waited for; matrix products, arithmetic and copies ran while one was open for 3% of the time, Pallas kernels for 15%

profile of v2, /device:TPU:1, one launch (start us, length us, event | category | flops | bytes accessed | tf_op | source)
XLA Modules:
  0.0 348.8 jit_solution(3003420688670073272)
XLA Ops:
  11.0 3.9 %project.1 = (bf16[256,1536]{1,0:T(8,128)(2,1)}, bf16[16,192,128]{2,1,0:T(8,128)(2,1)}) custom-call(bf16[128,768]{1,0:T(8,128)(2,1)} %bitcast.23, f32[768]{0:T(1024)} %gain_ref.5, bf16[768,768]{1,0:T(8,128)(2,1)} %refs_1_.5, bf16[768,768]{1,0:T(8,128)(2,1)} %refs_2_.1, bf16[768,768]{1,0:T(8,128)(2,1)} %refs_3_.3, bf16[1,768,192]{2,1,0:T(8,128)(2,1)} %copy.25.win_ref, ...), custom_call_target="tpu_custom_call" | custom-call | tf_op jit(solution)/shard_map/project/pallas_call | solution.py:87
  14.9 9.3 %all-to-all-start = ((bf16[16,192,128]{2,1,0:T(8,128)(2,1)}), bf16[16,192,128]{2,1,0:T(8,128)(2,1)S(1)}, u32[]{:S(2)}, u32[]{:S(2)}) async-start(bf16[16,192,128]{2,1,0:T(8,128)(2,1)} %get-tuple-element.41), calls=%async_computation | async-start | bytes 1572864 | tf_op jit(solution)/shard_map/all_to_all | solution.py:875
  24.3 17.6 %all-to-all-done.refs_2_ = bf16[16,192,128]{2,1,0:T(8,128)(2,1)S(1)} async-done(((bf16[16,192,128]{2,1,0:T(8,128)(2,1)}), bf16[16,192,128]{2,1,0:T(8,128)(2,1)S(1)}, u32[]{:S(2)}, u32[]{:S(2)}) %all-to-all-start) | async-done | bytes 786464 | tf_op jit(solution)/shard_map/all_to_all | solution.py:875
  42.8 7.0 %attend.1 = (bf16[16,64,128]{2,1,0:T(8,128)(2,1)}, f32[16,64,128]{2,1,0:T(8,128)}, f32[8,8,256]{2,1,0:T(8,128)}) custom-call(s32[1]{0:T(128)} %bitcast.2.refs_0_, f32[12,32]{1,0:T(8,128)} %refs_1_.4, bf16[16,192,128]{2,1,0:T(8,128)(2,1)} %copy-done), custom_call_target="tpu_custom_call" | custom-call | tf_op jit(solution)/shard_map/attend/pallas_call | solution.py:175
  49.8 5.1 %all-to-all-start.1 = ((bf16[16,64,128]{2,1,0:T(8,128)(2,1)}), bf16[16,64,128]{2,1,0:T(8,128)(2,1)S(1)}, u32[]{:S(2)}, u32[]{:S(2)}) async-start(bf16[16,64,128]{2,1,0:T(8,128)(2,1)} %get-tuple-element.42), calls=%async_computation.1 | async-start | bytes 524288 | tf_op jit(solution)/shard_map/all_to_all | solution.py:879
  56.5 7.2 %all-to-all-done.1.refs_2_ = bf16[16,64,128]{2,1,0:T(8,128)(2,1)S(1)} async-done(((bf16[16,64,128]{2,1,0:T(8,128)(2,1)}), bf16[16,64,128]{2,1,0:T(8,128)(2,1)S(1)}, u32[]{:S(2)}, u32[]{:S(2)}) %all-to-all-start.1) | async-done | bytes 262176 | tf_op jit(solution)/shard_map/all_to_all | solution.py:879
  64.4 3.9 %dispatch.1 = (bf16[8,96,768]{2,1,0:T(8,128)(2,1)}, bf16[128,768]{1,0:T(8,128)(2,1)}, f32[128,768]{1,0:T(8,128)}, bf16[128,768]{1,0:T(8,128)(2,1)}, bf16[2,128,384]{2,1,0:T(8,128)(2,1)}, /*index=5*/f32[128,128]{1,0:T(8,128)}) custom-call(bf16[128,768]{1,0:T(8,128)(2,1)} %bitcast.24, bf16[128,768]{1,0:T(8,128)(2,1)} %bitcast.26, ...), custom_call_target="tpu_custom_call" | custom-call | tf_op jit(solution)/shard_map/dispatch/pallas_call | solution.py:446
  68.3 34.3 %all_to_all.40.rows_ref = bf16[8,96,768]{2,1,0:T(8,128)(2,1)} all-to-all(bf16[8,96,768]{2,1,0:T(8,128)(2,1)} %get-tuple-element.43), channel_id=1, replica_groups=mesh['context'=16,'expert'=8] {'expert'}, dimensions={0} | all-to-all | bytes 2359296 | tf_op jit(solution)/shard_map/all_to_all | solution.py:883
  102.6 23.1 %all-gather.3.cloned.1.call-done = bf16[4096,1536]{1,0:T(8,128)(2,1)} async-done(((bf16[256,1536]{1,0:T(8,128)(2,1)}), bf16[4096,1536]{1,0:T(8,128)(2,1)}) %all-gather.3.cloned.1.call-update) | async-done | bytes 12582928 | tf_op jit(solution)/shard_map/all_gather | solution.py:876
  125.7 20.1 %expert_both.1 = (bf16[8,96,768]{2,1,0:T(8,128)(2,1)}, bf16[3072,1536]{1,0:T(8,128)(2,1)}) custom-call(bf16[8,96,768]{2,1,0:T(8,128)(2,1)} %all_to_all.40.rows_ref, bf16[16,256,1536]{2,1,0:T(8,128)(2,1)} %bitcast.21), custom_call_target="tpu_custom_call" | custom-call | tf_op jit(solution)/shard_map/expert_both/pallas_call | solution.py:506
  147.1 20.6 %all_to_all.41.back_ref = bf16[8,96,768]{2,1,0:T(8,128)(2,1)} all-to-all(bf16[8,96,768]{2,1,0:T(8,128)(2,1)S(1)} %copy-done.6), channel_id=1, replica_groups=mesh['context'=16,'expert'=8] {'expert'}, dimensions={0} | all-to-all | bytes 2359296 | tf_op jit(solution)/shard_map/all_to_all | solution.py:885
  167.7 5.6 %combine.1 = (bf16[128,768]{1,0:T(8,128)(2,1)}, f32[128,768]{1,0:T(8,128)}, bf16[16,64,128]{2,1,0:T(8,128)(2,1)}, bf16[16,64,768]{2,1,0:T(8,128)(2,1)}) custom-call(bf16[128,768]{1,0:T(8,128)(2,1)} %bitcast.27, bf16[8,96,768]{2,1,0:T(8,128)(2,1)} %all_to_all.41.back_ref, bf16[2,128,384]{2,1,0:T(8,128)(2,1)} %get-tuple-element.46.pick_ref, ...), custom_call_target="tpu_custom_call" | custom-call | tf_op jit(solution)/shard_map/combine/pallas_call | solution.py:602
  173.2 16.1 %all_to_all.42.refs_3_ = bf16[16,64,128]{2,1,0:T(8,128)(2,1)} all-to-all(bf16[16,64,128]{2,1,0:T(8,128)(2,1)} %get-tuple-element.52), channel_id=1, replica_groups=mesh['context'=16,'expert'=8] {'context'}, dimensions={0} | all-to-all | bytes 524288 | tf_op jit(solution)/shard_map/all_to_all | solution.py:890
  189.3 5.4 %all-to-all-start.6 = ((bf16[16,64,768]{2,1,0:T(8,128)(2,1)}), bf16[16,64,768]{2,1,0:T(8,128)(2,1)S(1)}, u32[]{:S(2)}, u32[]{:S(2)}) async-start(bf16[16,64,768]{2,1,0:T(8,128)(2,1)} %get-tuple-element.58), calls=%async_computation.6 | async-start | bytes 3145728 | tf_op jit(solution)/shard_map/all_to_all | solution.py:891
  194.7 13.9 %attend_back.1 = (bf16[16,192,128]{2,1,0:T(8,128)(2,1)}, f32[16,128]{1,0:T(8,128)}) custom-call(s32[1]{0:T(128)} %bitcast.2.refs_0_, f32[12,32]{1,0:T(8,128)} %refs_1_.4, bf16[16,192,128]{2,1,0:T(8,128)(2,1)} %copy-done, bf16[16,64,128]{2,1,0:T(8,128)(2,1)} %all_to_all.42.refs_3_, f32[16,64,128]{2,1,0:T(8,128)} %get-tuple-element.53.refs_4_, ...), custom_call_target="tpu_custom_call" | custom-call | tf_op jit(solution)/shard_map/attend_back/pallas_call | solution.py:299
  208.7 15.2 %all-to-all-done.6.sums_ref = bf16[16,64,768]{2,1,0:T(8,128)(2,1)S(1)} async-done(((bf16[16,64,768]{2,1,0:T(8,128)(2,1)}), bf16[16,64,768]{2,1,0:T(8,128)(2,1)S(1)}, u32[]{:S(2)}, u32[]{:S(2)}) %all-to-all-start.6) | async-done | bytes 1572896 | tf_op jit(solution)/shard_map/all_to_all | solution.py:891
  225.0 5.2 %head_grads.1 = bf16[8,208,128]{2,1,0:T(8,128)(2,1)} custom-call(bf16[16,192,128]{2,1,0:T(8,128)(2,1)} %get-tuple-element.55.dqkv_ref, bf16[16,256,1536]{2,1,0:T(8,128)(2,1)} %bitcast.22, f32[16,128]{1,0:T(8,128)} %get-tuple-element.57.bias_ref, bf16[16,64,768]{2,1,0:T(8,128)(2,1)} %copy-done.1), custom_call_target="tpu_custom_call" | custom-call | tf_op jit(solution)/shard_map/head_grads/pallas_call | solution.py:363
  230.1 12.7 %all_to_all.43.in_ref = bf16[8,208,128]{2,1,0:T(8,128)(2,1)} all-to-all(bf16[8,208,128]{2,1,0:T(8,128)(2,1)} %head_grads.1), channel_id=1, replica_groups=mesh['context'=16,'expert'=8] {'expert'}, dimensions={0} | all-to-all | bytes 851968 | tf_op jit(solution)/shard_map/all_to_all | solution.py:896
  245.3 2.1 collective-permute-start
  247.4 4.0 %collective-permute-done.2 = bf16[208,128]{1,0:T(8,128)(2,1)S(1)} collective-permute-done((bf16[208,128]{1,0:T(8,128)(2,1)}, bf16[208,128]{1,0:T(8,128)(2,1)S(1)}, u32[]{:S(2)}, u32[]{:S(2)}) %collective-permute-start.2) | collective-permute-done | bytes 53280 | tf_op jit(solution)/shard_map/ppermute | solution.py:680
  257.1 4.3 %collective-permute-done.4 = bf16[4,208,128]{2,1,0:T(8,128)(2,1)S(1)} collective-permute-done((bf16[4,208,128]{2,1,0:T(8,128)(2,1)S(1)}, bf16[4,208,128]{2,1,0:T(8,128)(2,1)S(1)}, u32[]{:S(2)}, u32[]{:S(2)}) %collective-permute-start.4) | collective-permute-done | bytes 213024 | tf_op jit(solution)/shard_map/ppermute | solution.py:680
  261.4 3.1 collective-permute-done.3
  264.5 2.0 collective-permute-done.5
  271.2 15.8 %collective-permute-done.7.refs_6_ = bf16[4,4,208,128]{3,2,1,0:T(8,128)(2,1)S(1)} collective-permute-done((bf16[4,4,208,128]{3,2,1,0:T(8,128)(2,1)S(1)}, bf16[4,4,208,128]{3,2,1,0:T(8,128)(2,1)S(1)}, u32[]{:S(2)}, u32[]{:S(2)}) %collective-permute-start.7) | collective-permute-done | bytes 852000 | tf_op jit(solution)/shard_map/ppermute | solution.py:687
  289.3 2.2 collective-permute-start.8
  291.4 2.8 collective-permute-start.12
  294.2 5.6 %all-to-all-start.5 = ((bf16[16,192,128]{2,1,0:T(8,128)(2,1)}), bf16[16,192,128]{2,1,0:T(8,128)(2,1)S(1)}, u32[]{:S(2)}, u32[]{:S(2)}) async-start(bf16[16,192,128]{2,1,0:T(8,128)(2,1)} %get-tuple-element.55.dqkv_ref), calls=%async_computation.5 | async-start | bytes 1572864 | tf_op jit(solution)/shard_map/all_to_all | solution.py:894
  302.4 11.8 %all-to-all-done.5.grads_ref = bf16[16,192,128]{2,1,0:T(8,128)(2,1)S(1)} async-done(((bf16[16,192,128]{2,1,0:T(8,128)(2,1)}), bf16[16,192,128]{2,1,0:T(8,128)(2,1)S(1)}, u32[]{:S(2)}, u32[]{:S(2)}) %all-to-all-start.5) | async-done | bytes 786464 | tf_op jit(solution)/shard_map/all_to_all | solution.py:894
  315.0 4.6 %input_grad.1 = f32[128,768]{1,0:T(8,128)} custom-call(bf16[128,768]{1,0:T(8,128)(2,1)} %bitcast.25, f32[768]{0:T(1024)} %gain_ref.5, bf16[16,192,128]{2,1,0:T(8,128)(2,1)} %copy-done.3, bf16[768,768]{1,0:T(8,128)(2,1)} %refs_1_.5, bf16[768,768]{1,0:T(8,128)(2,1)} %refs_2_.1, bf16[768,768]{1,0:T(8,128)(2,1)} %refs_3_.3, f32[128,768]{1,0:T(8,128)} %get-tuple-element.56.mixed_ref), custom_call_target="tpu_custom_call" | custom-call | tf_op jit(solution)/shard_map/input_grad/pallas_call | solution.py:647
  319.7 11.9 %unpack.1 = (f32[768,768]{1,0:T(8,128)}, f32[768,768]{1,0:T(8,128)}, f32[768,768]{1,0:T(8,128)}, f32[12,8,8,768]{3,2,1,0:T(8,128)}, f32[12,32]{1,0:T(8,128)}, /*...) custom-call(s32[4]{0:T(128)} %pad_add_fusion.refs_0_, bf16[768,768]{1,0:T(8,128)(2,1)} %refs_1_.5, ...), custom_call_target="tpu_custom_call" | custom-call | tf_op jit(solution)/shard_map/unpack/pallas_call | solution.py:782
  336.1 2.4 split_back.1
  338.6 2.3 copy.31
  (67 shorter events, 33.6 us)
Async XLA Ops:
  7.2 118.5 %all-gather.3.cloned.1.call-start = ((), (), s32[]{:S(2)}) async-start(), calls=%async_computation.10 | async-start | bytes 13369344 | tf_op jit(solution)/shard_map/all_gather | solution.py:876
  14.9 40.1 %copy-start.11 = (s32[1,128,2]{1,2,0:T(2,128)S(1)}, s32[1,128,2]{1,2,0:T(2,128)}, u32[]{:S(2)}) copy-start(s32[1,128,2]{1,2,0:T(2,128)} %param.24) | copy-start | bytes 3076
  14.9 40.8 %copy-start.10 = (bf16[768,8]{0,1:T(8,128)(2,1)S(1)}, bf16[768,8]{0,1:T(8,128)(2,1)}, u32[]{:S(2)}) copy-start(bf16[768,8]{0,1:T(8,128)(2,1)} %param.21) | copy-start | bytes 36868
  14.9 26.9 %all-to-all-start = ((bf16[16,192,128]{2,1,0:T(8,128)(2,1)}), bf16[16,192,128]{2,1,0:T(8,128)(2,1)S(1)}, u32[]{:S(2)}, u32[]{:S(2)}) async-start(bf16[16,192,128]{2,1,0:T(8,128)(2,1)} %get-tuple-element.41), calls=%async_computation | async-start | bytes 1572864 | tf_op jit(solution)/shard_map/all_to_all | solution.py:875
  41.9 0.9 copy-start
  49.8 13.9 %all-to-all-start.1 = ((bf16[16,64,128]{2,1,0:T(8,128)(2,1)}), bf16[16,64,128]{2,1,0:T(8,128)(2,1)S(1)}, u32[]{:S(2)}, u32[]{:S(2)}) async-start(bf16[16,64,128]{2,1,0:T(8,128)(2,1)} %get-tuple-element.42), calls=%async_computation.1 | async-start | bytes 524288 | tf_op jit(solution)/shard_map/all_to_all | solution.py:879
  55.0 281.2 %reduce-scatter.2.cloned.1.call-start = ((), (), s32[]{:S(2)}) async-start(), calls=%async_computation.9 | async-start | bytes 10027008 | tf_op jit(solution)/shard_map/reduce_scatter | solution.py:886
  145.8 1.3 copy-start.6
  189.3 34.5 %all-to-all-start.6 = ((bf16[16,64,768]{2,1,0:T(8,128)(2,1)}), bf16[16,64,768]{2,1,0:T(8,128)(2,1)S(1)}, u32[]{:S(2)}, u32[]{:S(2)}) async-start(bf16[16,64,768]{2,1,0:T(8,128)(2,1)} %get-tuple-element.58), calls=%async_computation.6 | async-start | bytes 3145728 | tf_op jit(solution)/shard_map/all_to_all | solution.py:891
  223.8 1.1 copy-start.1
  244.5 6.8 %collective-permute-start.2 = (bf16[208,128]{1,0:T(8,128)(2,1)}, bf16[208,128]{1,0:T(8,128)(2,1)S(1)}, u32[]{:S(2)}, u32[]{:S(2)}) collective-permute-start(bf16[208,128]{1,0:T(8,128)(2,1)} %add_up.1), channel_id=1, source_target_pairs={{0,16},{1,17},{2,18},{3,19},{4,20},{5,21},{6,22},{7,23},{8,24},{9,... | collective-permute-start | bytes 159752 | tf_op jit(solution)/shard_map/ppermute | solution.py:680
  244.5 6.8 %collective-permute-start.1 = (bf16[208,128]{1,0:T(8,128)(2,1)}, bf16[208,128]{1,0:T(8,128)(2,1)S(1)}, u32[]{:S(2)}, u32[]{:S(2)}) collective-permute-start(bf16[208,128]{1,0:T(8,128)(2,1)} %add_up.1), channel_id=1, source_target_pairs={{0,32},{1,33},{2,34},{3,35},{4,36},{5,37},{6,38},{7,39},{8,40},{9,... | collective-permute-start | bytes 159752 | tf_op jit(solution)/shard_map/ppermute | solution.py:680
  245.3 7.9 %collective-permute-start = (bf16[208,128]{1,0:T(8,128)(2,1)}, bf16[208,128]{1,0:T(8,128)(2,1)S(1)}, u32[]{:S(2)}, u32[]{:S(2)}) collective-permute-start(bf16[208,128]{1,0:T(8,128)(2,1)} %add_up.1), channel_id=1, source_target_pairs={{0,48},{1,49},{2,50},{3,51},{4,52},{5,53},{6,54},{7,55},{8,56},{9,... | collective-permute-start | bytes 159752 | tf_op jit(solution)/shard_map/ppermute | solution.py:680
  254.0 7.4 %collective-permute-start.4 = (bf16[4,208,128]{2,1,0:T(8,128)(2,1)S(1)}, bf16[4,208,128]{2,1,0:T(8,128)(2,1)S(1)}, u32[]{:S(2)}, u32[]{:S(2)}) collective-permute-start(bf16[4,208,128]{2,1,0:T(8,128)(2,1)S(1)} %get-tuple-element.83), channel_id=1, source_target_pairs={{0,64},{1,65},{2,66},{3,67},{4,68},{5,69},{6,70},{7,71},{8,72},{9,... | collective-permute-start | bytes 638984 | tf_op jit(solution)/shard_map/ppermute | solution.py:680
  255.6 8.9 %collective-permute-start.3 = (bf16[4,208,128]{2,1,0:T(8,128)(2,1)S(1)}, bf16[4,208,128]{2,1,0:T(8,128)(2,1)S(1)}, u32[]{:S(2)}, u32[]{:S(2)}) collective-permute-start(bf16[4,208,128]{2,1,0:T(8,128)(2,1)S(1)} %get-tuple-element.83), channel_id=1, source_target_pairs={{0,65},{1,0},{2,67},{3,2},{4,69},{5,4},{6,71},{7,6},{8,73},{9,8},{... | collective-permute-start | bytes 638984 | tf_op jit(solution)/shard_map/ppermute | solution.py:680
  257.1 9.5 %collective-permute-start.5 = (bf16[4,208,128]{2,1,0:T(8,128)(2,1)S(1)}, bf16[4,208,128]{2,1,0:T(8,128)(2,1)S(1)}, u32[]{:S(2)}, u32[]{:S(2)}) collective-permute-start(bf16[4,208,128]{2,1,0:T(8,128)(2,1)S(1)} %get-tuple-element.83), channel_id=1, source_target_pairs={{0,1},{1,64},{2,3},{3,66},{4,5},{5,68},{6,7},{7,70},{8,9},{9,72},{... | collective-permute-start | bytes 638984 | tf_op jit(solution)/shard_map/ppermute | solution.py:680
  266.6 27.6 %copy-start.2 = (bf16[4,4,208,128]{3,2,1,0:T(8,128)(2,1)}, bf16[4,4,208,128]{3,2,1,0:T(8,128)(2,1)S(1)}, u32[]{:S(2)}) copy-start(bf16[4,4,208,128]{3,2,1,0:T(8,128)(2,1)S(1)} %pad_maximum_fusion.refs_4_) | copy-start | bytes 2555908
  266.6 20.4 %collective-permute-start.7 = (bf16[4,4,208,128]{3,2,1,0:T(8,128)(2,1)S(1)}, bf16[4,4,208,128]{3,2,1,0:T(8,128)(2,1)S(1)}, u32[]{:S(2)}, u32[]{:S(2)}) collective-permute-start(bf16[4,4,208,128]{3,2,1,0:T(8,128)(2,1)S(1)} %pad_maximum_fusion.refs_4_), channel_id=1, source_target_pairs={{0,2},{1,3},{2,4},{3,5},{4,6},{5,7},{6,0},{7,1},{8,10},{9,11},{10,... | collective-permute-start | bytes 2555912 | tf_op jit(solution)/shard_map/ppermute | solution.py:687
  267.8 20.6 %collective-permute-start.6 = (bf16[4,4,208,128]{3,2,1,0:T(8,128)(2,1)S(1)}, bf16[4,4,208,128]{3,2,1,0:T(8,128)(2,1)S(1)}, u32[]{:S(2)}, u32[]{:S(2)}) collective-permute-start(bf16[4,4,208,128]{3,2,1,0:T(8,128)(2,1)S(1)} %pad_maximum_fusion.refs_4_), channel_id=1, source_target_pairs={{0,6},{1,7},{2,0},{3,1},{4,2},{5,3},{6,4},{7,5},{8,14},{9,15},{10,... | collective-permute-start | bytes 2555912 | tf_op jit(solution)/shard_map/ppermute | solution.py:686
  269.4 50.2 %collective-permute-start.10 = (bf16[4,4,208,128]{3,2,1,0:T(8,128)(2,1)S(1)}, bf16[4,4,208,128]{3,2,1,0:T(8,128)(2,1)}, u32[]{:S(2)}, u32[]{:S(2)}) collective-permute-start(bf16[4,4,208,128]{3,2,1,0:T(8,128)(2,1)S(1)} %pad_maximum_fusion.refs_4_), channel_id=1, source_target_pairs={{0,8},{1,9},{2,10},{3,11},{4,12},{5,13},{6,14},{7,15},{8,0},{9,1},... | collective-permute-start | bytes 2555912 | tf_op jit(solution)/shard_map/ppermute | solution.py:693
  287.1 7.1 %copy-start.4 = (bf16[4,4,208,128]{3,2,1,0:T(8,128)(2,1)}, bf16[4,4,208,128]{3,2,1,0:T(8,128)(2,1)S(1)}, u32[]{:S(2)}) copy-start(bf16[4,4,208,128]{3,2,1,0:T(8,128)(2,1)S(1)} %collective-permute-done.7.refs_6_) | copy-start | bytes 2555908
  287.9 11.8 %collective-permute-start.9 = (bf16[2,4,208,128]{3,2,1,0:T(8,128)(2,1)}, bf16[2,4,208,128]{3,2,1,0:T(8,128)(2,1)}, u32[]{:S(2)}, u32[]{:S(2)}) collective-permute-start(bf16[2,4,208,128]{3,2,1,0:T(8,128)(2,1)} %slice.17), channel_id=1, source_target_pairs={{0,2},{1,3},{2,4},{3,5},{4,6},{5,7},{6,0},{7,1},{8,10},{9,11},{10,... | collective-permute-start | bytes 1277960 | tf_op jit(solution)/shard_map/ppermute | solution.py:690
  288.4 31.2 %copy-start.5 = (bf16[4,4,208,128]{3,2,1,0:T(8,128)(2,1)}, bf16[4,4,208,128]{3,2,1,0:T(8,128)(2,1)S(1)}, u32[]{:S(2)}) copy-start(bf16[4,4,208,128]{3,2,1,0:T(8,128)(2,1)S(1)} %collective-permute-done.6.refs_5_) | copy-start | bytes 2555908
  289.3 12.4 %collective-permute-start.8 = (bf16[2,4,208,128]{3,2,1,0:T(8,128)(2,1)}, bf16[2,4,208,128]{3,2,1,0:T(8,128)(2,1)}, u32[]{:S(2)}, u32[]{:S(2)}) collective-permute-start(bf16[2,4,208,128]{3,2,1,0:T(8,128)(2,1)} %slice.16), channel_id=1, source_target_pairs={{0,6},{1,7},{2,0},{3,1},{4,2},{5,3},{6,4},{7,5},{8,14},{9,15},{10,... | collective-permute-start | bytes 1277960 | tf_op jit(solution)/shard_map/ppermute | solution.py:689
  291.4 28.2 %collective-permute-start.12 = (bf16[4,4,208,128]{3,2,1,0:T(8,128)(2,1)S(1)}, bf16[4,4,208,128]{3,2,1,0:T(8,128)(2,1)}, u32[]{:S(2)}, u32[]{:S(2)}) collective-permute-start(bf16[4,4,208,128]{3,2,1,0:T(8,128)(2,1)S(1)} %collective-permute-done.7.refs_6_), channel_id=1, source_target_pairs={{0,8},{1,9},{2,10},{3,11},{4,12},{5,13},{6,14},{7,15},{8,0},{9,1},... | collective-permute-start | bytes 2555912 | tf_op jit(solution)/shard_map/ppermute | solution.py:693
  294.2 25.5 %collective-permute-start.11 = (bf16[4,4,208,128]{3,2,1,0:T(8,128)(2,1)S(1)}, bf16[4,4,208,128]{3,2,1,0:T(8,128)(2,1)}, u32[]{:S(2)}, u32[]{:S(2)}) collective-permute-start(bf16[4,4,208,128]{3,2,1,0:T(8,128)(2,1)S(1)} %collective-permute-done.6.refs_5_), channel_id=1, source_target_pairs={{0,8},{1,9},{2,10},{3,11},{4,12},{5,13},{6,14},{7,15},{8,0},{9,1},... | collective-permute-start | bytes 2555912 | tf_op jit(solution)/shard_map/ppermute | solution.py:693
  294.2 20.0 %all-to-all-start.5 = ((bf16[16,192,128]{2,1,0:T(8,128)(2,1)}), bf16[16,192,128]{2,1,0:T(8,128)(2,1)S(1)}, u32[]{:S(2)}, u32[]{:S(2)}) async-start(bf16[16,192,128]{2,1,0:T(8,128)(2,1)} %get-tuple-element.55.dqkv_ref), calls=%async_computation.5 | async-start | bytes 1572864 | tf_op jit(solution)/shard_map/all_to_all | solution.py:894
  299.8 19.9 %collective-permute-start.14 = (bf16[2,4,208,128]{3,2,1,0:T(8,128)(2,1)}, bf16[2,4,208,128]{3,2,1,0:T(8,128)(2,1)}, u32[]{:S(2)}, u32[]{:S(2)}) collective-permute-start(bf16[2,4,208,128]{3,2,1,0:T(8,128)(2,1)} %collective-permute-done.9.refs_8_), channel_id=1, source_target_pairs={{0,8},{1,9},{2,10},{3,11},{4,12},{5,13},{6,14},{7,15},{8,0},{9,1},... | collective-permute-start | bytes 1277960 | tf_op jit(solution)/shard_map/ppermute | solution.py:693
  301.7 18.0 %collective-permute-start.13 = (bf16[2,4,208,128]{3,2,1,0:T(8,128)(2,1)}, bf16[2,4,208,128]{3,2,1,0:T(8,128)(2,1)}, u32[]{:S(2)}, u32[]{:S(2)}) collective-permute-start(bf16[2,4,208,128]{3,2,1,0:T(8,128)(2,1)} %collective-permute-done.8.refs_7_), channel_id=1, source_target_pairs={{0,8},{1,9},{2,10},{3,11},{4,12},{5,13},{6,14},{7,15},{8,0},{9,1},... | collective-permute-start | bytes 1277960 | tf_op jit(solution)/shard_map/ppermute | solution.py:693
  314.2 0.9 copy-start.3
  319.6 12.8 %copy-start.9 = (f32[768]{0:T(1024)S(1)}, f32[768]{0:T(1024)}, u32[]{:S(2)}) copy-start(f32[768]{0:T(1024)} %gain_ref.5) | copy-start | bytes 9220
  338.6 2.3 copy-start.8
  (1 other events, 0.7 us)
Sparse Core Ops, SparseCore 0:
  15.0 110.6 all-gather.2
  146.0 118.2 reduce-scatter.1

commit v3 on v2

--- a/solution.py
+++ b/solution.py
@@ -59,16 +59,12 @@
     return pl.BlockSpec(memory_space=pltpu.SMEM)
 
 
-def project_kernel(tok_ref, gain_ref, wq_ref, wk_ref, wv_ref, win_ref, wback_ref, share_ref, out_ref):
+def project_kernel(tok_ref, gain_ref, wq_ref, wk_ref, wv_ref, normed_ref, out_ref):
     inputs = tok_ref[...].astype(F32)
     normed = (inputs * rms_scale(inputs) * gain_ref[...][None, :]).astype(BF16)
     rows, width = normed.shape
     half = rows // 2
-    hidden = win_ref.shape[2]
-    share_ref[:hidden, :width] = win_ref[0].T
-    share_ref[:hidden, width:] = wback_ref[0].T
-    share_ref[hidden:, :width] = normed[:half]
-    share_ref[hidden:, width:] = normed[half:]
+    normed_ref[...] = normed
     queries = (dot(normed, wq_ref[...]).astype(BF16).astype(F32) * 0.125).astype(BF16)
     keys = dot(normed, wk_ref[...]).astype(BF16)
     values = dot(normed, wv_ref[...]).astype(BF16)
@@ -81,20 +77,19 @@
         out_ref[h] = jnp.zeros_like(out_ref[h])
 
 
-def project(tokens, gain_one, w_query, w_key, w_value, expert_in, expert_out):
+def project(tokens, gain_one, w_query, w_key, w_value):
     rows, width = tokens.shape
-    hidden = expert_in.shape[2]
     return pl.pallas_call(
         project_kernel,
         name="project",
         out_shape=(
-            jax.ShapeDtypeStruct((hidden + rows // 2, 2 * width), BF16),
+            jax.ShapeDtypeStruct((rows, width), BF16),
             jax.ShapeDtypeStruct((HEAD_SLOTS, rows + rows // 2, 128), BF16),
         ),
-        in_specs=[vspec()] * 7,
+        in_specs=[vspec()] * 5,
         out_specs=(vspec(), vspec()),
         compiler_params=whole(),
-    )(tokens, gain_one, w_query, w_key, w_value, expert_in, expert_out)
+    )(tokens, gain_one, w_query, w_key, w_value)
 
 
 def bias_tile(table_ref, head, buckets, rows_first, shape, key_dim):
@@ -324,10 +319,10 @@
 
 def head_grads_kernel(dqkv_ref, normed_ref, bias_ref, sums_ref, out_ref):
     count = dqkv_ref.shape[0]
-    width = normed_ref.shape[2] // 2
+    width = normed_ref.shape[2]
     tokens = count * 64
-    first = normed_ref[:, :, :width].reshape(tokens, width)
-    second = normed_ref[:, :, width:].reshape(tokens, width)
+    first = normed_ref[:, :64, :].reshape(tokens, width)
+    second = normed_ref[:, 64:, :].reshape(tokens, width)
     pairs = dot(dqkv_ref[:, :64, :].reshape(tokens, 128), first, TN) + dot(
         dqkv_ref[:, 64:128, :].reshape(tokens, 128), second, TN
     )
@@ -355,25 +350,18 @@
         ).astype(BF16)
 
 
-def head_grads(dqkv, shared, bias, sums, shares):
-    count, rows, wide = shared.shape
-    width = wide // 2
+def head_grads(dqkv, normed_all, bias, sums, shares):
+    width = normed_all.shape[2]
     each = width // shares
     held = each + each // 2 + 16 + width // 16
     return pl.pallas_call(
         head_grads_kernel,
         name="head_grads",
-        grid=(1,),
         out_shape=jax.ShapeDtypeStruct((shares, held, 128), BF16),
-        in_specs=[
-            vspec(),
-            pl.BlockSpec((count, 64, wide), lambda i: (0, rows // 64 - 1, 0)),
-            vspec(),
-            vspec(),
-        ],
+        in_specs=[vspec()] * 4,
         out_specs=vspec(),
         compiler_params=whole(),
-    )(dqkv, shared, bias, sums)
+    )(dqkv, normed_all, bias, sums)
 
 
 def heads_to_rows(ref, scratch):
@@ -473,8 +461,9 @@
         y_s[...] = jnp.zeros_like(y_s)
         dx_s[...] = jnp.zeros_like(dx_s)
 
-    weights = w_ref[...].reshape(-1, 2 * width)
-    w_in, w_back = weights[:, :width], weights[:, width:]
+    each = w_ref.shape[1] // 2
+    w_in = w_ref[:, :each, :].reshape(-1, width)
+    w_back = w_ref[:, each:, :].reshape(-1, width)
     pre = dot(x_s[...], w_in, NT)
     square = pre * pre
     curve = jnp.tanh(0.7978845608 * (pre + 0.044715 * square * pre))
@@ -485,8 +474,8 @@
     grad_pre = (dot(g_s[...], w_back, NT) * slope).astype(BF16)
     y_s[...] += dot(act, w_back)
     dx_s[...] += dot(grad_pre, w_in)
-    dw_ref[:, :width] = dot(grad_pre, x_s[...], TN).astype(BF16)
-    dw_ref[:, width:] = dot(act, g_s[...], TN).astype(BF16)
+    dw_ref[:, :each, :] = dot(grad_pre, x_s[...], TN).astype(BF16).reshape(-1, each, width)
+    dw_ref[:, each:, :] = dot(act, g_s[...], TN).astype(BF16).reshape(-1, each, width)
 
     @pl.when(step == pl.num_programs(0) - 1)
     def _():
@@ -496,28 +485,28 @@
             back_ref[s, capacity:, :] = dx_s[here, :].astype(BF16)
 
 
+AT_ONCE = 2
+
+
 def expert_both(rows, shared):
     sources, both, width = rows.shape
-    count, given, wide = shared.shape
-    each = given - 64
-    at_once = 2
-    chunk = at_once * each
+    count, given, unused = shared.shape
     held = sources * both // 2
     return pl.pallas_call(
         expert_kernel,
         name="expert_both",
-        grid=(count // at_once,),
+        grid=(count // AT_ONCE,),
         out_shape=(
             jax.ShapeDtypeStruct(rows.shape, BF16),
-            jax.ShapeDtypeStruct((count * each, wide), BF16),
+            jax.ShapeDtypeStruct(shared.shape, BF16),
         ),
         in_specs=[
             pl.BlockSpec(rows.shape, lambda i: (0, 0, 0)),
-            pl.BlockSpec((at_once, each, wide), lambda i: (i, 0, 0)),
+            pl.BlockSpec((AT_ONCE, given, width), lambda i: (i, 0, 0)),
         ],
         out_specs=(
             pl.BlockSpec(rows.shape, lambda i: (0, 0, 0)),
-            pl.BlockSpec((chunk, wide), lambda i: (i, 0)),
+            pl.BlockSpec((AT_ONCE, given, width), lambda i: (i, 0, 0)),
         ),
         scratch_shapes=[
             pltpu.VMEM((held, width), BF16),
@@ -536,7 +525,6 @@
     gates_ref,
     mixed_ref,
     second_ref,
-    att_ref,
     routes_ref,
     gain_ref,
     wr_ref,
@@ -544,7 +532,7 @@
     out_ref,
     grad_mixed_ref,
     heads_ref,
-    sums_ref,
+    small_ref,
     y_s,
     dx_s,
 ):
@@ -584,18 +572,33 @@
         heads_ref[h] = jnp.concatenate([grad_att[:64, cols], grad_att[64:, cols]], axis=1)
     for h in range(heads, HEAD_SLOTS):
         heads_ref[h] = jnp.zeros_like(heads_ref[h])
-    grad_wo = dot(att_ref[...], grad_branch, TN).astype(BF16)
-    slots, each, unused = sums_ref.shape
+    small_ref[...] = jnp.concatenate([grad_router, jnp.broadcast_to(grad_gain, (8, width))], axis=0)
+
+
+def out_grad_kernel(att_ref, grad_mixed_ref, small_ref, sums_ref):
+    grad_wo = dot(att_ref[...], grad_mixed_ref[...].astype(BF16), TN).astype(BF16)
+    slots, each, width = sums_ref.shape
     used = width // each
     for c in range(used):
         sums_ref[c] = grad_wo[each * c : each * c + each]
-    small = jnp.concatenate([grad_router, jnp.broadcast_to(grad_gain, (8, width))], axis=0)
     for c in range(used, slots):
         sums_ref[c] = jnp.zeros_like(sums_ref[c])
-    sums_ref[used, :16, :] = small.astype(BF16)
-
-
-def combine(cotangent, back, picks, gates, mixed, second, attended, routes, gain_two, w_router, w_out):
+    sums_ref[used, :16, :] = small_ref[...].astype(BF16)
+
+
+def out_grad(attended, grad_mixed, small):
+    width = attended.shape[1]
+    return pl.pallas_call(
+        out_grad_kernel,
+        name="out_grad",
+        out_shape=jax.ShapeDtypeStruct((HEAD_SLOTS, 64, width), BF16),
+        in_specs=[vspec()] * 3,
+        out_specs=vspec(),
+        compiler_params=whole(),
+    )(attended, grad_mixed, small)
+
+
+def combine(cotangent, back, picks, gates, mixed, second, routes, gain_two, w_router, w_out):
     rows, width = cotangent.shape
     experts, both, unused = back.shape
     held = experts * both // 2
@@ -606,9 +609,9 @@
             jax.ShapeDtypeStruct((rows, width), BF16),
             jax.ShapeDtypeStruct((rows, width), F32),
             jax.ShapeDtypeStruct((HEAD_SLOTS, rows // 2, 128), BF16),
-            jax.ShapeDtypeStruct((HEAD_SLOTS, 64, width), BF16),
-        ),
-        in_specs=[vspec()] * 11,
+            jax.ShapeDtypeStruct((16, width), F32),
+        ),
+        in_specs=[vspec()] * 10,
         out_specs=(vspec(),) * 4,
         scratch_shapes=[pltpu.VMEM((held, width), BF16), pltpu.VMEM((held, width), BF16)],
         compiler_params=whole(),
@@ -619,7 +622,6 @@
         gates,
         mixed,
         second,
-        attended,
         routes,
         gain_two,
         w_router,
@@ -680,8 +682,9 @@
     return jnp.stack([block] + [lax.ppermute(block, AXES, shifted(dim, -by)) for by in (1, 2, 3)])
 
 
-def gather_all(piece):
-    filled = direct_gather(direct_gather(piece, 2), 0)
+def gather_all(piece, beside):
+    filled, beside = lax.optimization_barrier((direct_gather(piece, 2), beside))
+    filled = direct_gather(filled, 0)
     half = filled.shape[0] // 2
     ahead = lax.ppermute(filled, AXES, shifted(1, -1))
     behind = lax.ppermute(filled, AXES, shifted(1, 1))
@@ -691,7 +694,7 @@
     )
     mine = (filled, ahead, behind) + across
     other = tuple(lax.ppermute(part, AXES, shifted(3, 1)) for part in mine)
-    return mine + other
+    return mine + other, beside
 
 
 def unpack_kernel(
@@ -760,7 +763,7 @@
 
     @pl.when(expert == 0)
     def _():
-        router_ref[...] = small.T
+        router_ref[...] = small
 
     @pl.when(expert == 1)
     def _():
@@ -790,7 +793,7 @@
             jax.ShapeDtypeStruct((heads, experts, 8, width), F32),
             jax.ShapeDtypeStruct((heads, buckets), F32),
             jax.ShapeDtypeStruct((8, width), F32),
-            jax.ShapeDtypeStruct((width, 8), F32),
+            jax.ShapeDtypeStruct((8, width), F32),
             jax.ShapeDtypeStruct((experts, 8, each), F32),
         ),
         in_specs=[sspec(), rows, rows, rows] + [pl.BlockSpec(memory_space=pl.ANY)] * 10,
@@ -801,7 +804,7 @@
             pl.BlockSpec((heads, None, 8, width), lambda i: (0, i, 0, 0)),
             pl.BlockSpec((heads, buckets), lambda i: (0, 0)),
             pl.BlockSpec((8, width), lambda i: (0, 0)),
-            pl.BlockSpec((width, 8), lambda i: (0, 0)),
+            pl.BlockSpec((8, width), lambda i: (0, 0)),
             pl.BlockSpec((None, 8, each), lambda i: (i, 0, 0)),
         ),
         scratch_shapes=[
@@ -828,25 +831,6 @@
         out_specs=vspec(),
         compiler_params=whole(),
     )(received)
-
-
-def split_kernel(in_ref, first_ref, second_ref):
-    width = first_ref.shape[1]
-    first_ref[0] = in_ref[:, :width].astype(F32).T
-    second_ref[0] = in_ref[:, width:].astype(F32).T
-
-
-def split_back(grads):
-    rows, wide = grads.shape
-    width = wide // 2
-    return pl.pallas_call(
-        split_kernel,
-        name="split_back",
-        out_shape=(jax.ShapeDtypeStruct((1, width, rows), F32),) * 2,
-        in_specs=[vspec()],
-        out_specs=(vspec(),) * 2,
-        compiler_params=whole(),
-    )(grads)
 
 
 def shards(
@@ -871,9 +855,11 @@
     context = lax.axis_index("context")
     head = jnp.minimum(context, heads - 1).astype(jnp.int32).reshape(1)
 
-    share, packed = project(inputs, gain_one, w_query, w_key, w_value, expert_in, expert_out)
+    own_weights = jnp.concatenate([expert_in[0].T, expert_out[0].T], axis=0)
+    shared = lax.all_gather(own_weights, "context", axis=0, tiled=False)
+    normed, packed = project(inputs, gain_one, w_query, w_key, w_value)
     qkv = lax.all_to_all(packed, "context", split_axis=0, concat_axis=0, tiled=True)
-    shared = lax.all_gather(share, "context", axis=0, tiled=False)
+    normed_all = lax.all_gather(normed, "context", axis=0, tiled=False)
 
     out_heads, keep, lse = attend(head, rel_table, qkv)
     out_rows = lax.all_to_all(out_heads, "context", split_axis=0, concat_axis=0, tiled=True)
@@ -883,18 +869,19 @@
     received = lax.all_to_all(send, "expert", split_axis=0, concat_axis=0, tiled=True)
     back, weight_grads = expert_both(received, shared)
     returned = lax.all_to_all(back, "expert", split_axis=0, concat_axis=0, tiled=True)
-    own_grads = lax.psum_scatter(weight_grads, "context", scatter_dimension=0, tiled=True)
-    block_out, grad_mixed, grad_heads, sums = combine(
-        grad_out, returned, picks, gates, mixed, second, attended, routes_here, gain_two, w_router, w_out
-    )
+    own_grads = lax.psum_scatter(weight_grads, "context", scatter_dimension=0, tiled=False)
+    block_out, grad_mixed, grad_heads, small = combine(
+        grad_out, returned, picks, gates, mixed, second, routes_here, gain_two, w_router, w_out
+    )
+    sums = out_grad(attended, grad_mixed, small)
     grad_here = lax.all_to_all(grad_heads, "context", split_axis=0, concat_axis=0, tiled=True)
     sums = lax.all_to_all(sums, "context", split_axis=0, concat_axis=0, tiled=True)
 
     dqkv, bias = attend_back(head, rel_table, qkv, grad_here, keep, lse)
     grads = lax.all_to_all(dqkv, "context", split_axis=0, concat_axis=0, tiled=True)
-    terms = head_grads(dqkv, shared, bias, sums, experts)
+    terms = head_grads(dqkv, normed_all, bias, sums, experts)
     terms = lax.all_to_all(terms, "expert", split_axis=0, concat_axis=0, tiled=True)
-    parts = gather_all(add_up(terms))
+    parts, grads = gather_all(add_up(terms), grads)
     grad_tokens = input_grad(inputs, gain_one, grads, w_query, w_key, w_value, grad_mixed)
 
     expert = lax.axis_index("expert")
@@ -902,7 +889,8 @@
     dwq, dwk, dwv, dwo, bias, small, router, gain_grad = unpack(
         place, parts, w_query, w_key, w_value, heads, buckets, experts
     )
-    grad_in, grad_back = split_back(own_grads)
+    own_grads = own_grads.astype(F32)
+    hidden = own_grads.shape[0] // 2
     return (
         block_out[None],
         grad_tokens[None],
@@ -913,9 +901,9 @@
         dwo.reshape(width, width),
         bias,
         small[0],
-        router,
-        grad_in,
-        grad_back,
+        router.T,
+        own_grads[:hidden].T[None],
+        own_grads[hidden:].T[None],
     )
 
 

time: 350 us -> 338 us (0.966)
  blocking collectives: 83.6 us -> 72.1 us
  starting transfers between devices: 43.5 us -> 54.9 us
  local copies, waits for them, and re-layouts: 19.1 us -> 10.5 us
  waiting for transfers between devices: 106 us -> 101 us
    all_to_all x1 -> x0, blocking collectives: 16.1 us -> none  [shards(): lax.all_to_all(grad_heads, 'context', split_axis=0, concat_axis=0, tiled=...]
    ppermute x1, waiting for transfers between devices: 0.01 us -> 15.9 us  [gather_all(): ahead = lax.ppermute(filled, AXES, shifted(1, -1))]
    ppermute x1, waiting for transfers between devices: 15.8 us -> 0.01 us  [gather_all(): behind = lax.ppermute(filled, AXES, shifted(1, 1))]
    all_gather x1 -> x2, waiting for transfers between devices: 23.1 us -> 11.3 us  [the longest x1 11.3 us: shards(): shared = lax.all_gather(own_weights, 'context', axis=0, tiled=False)]
    unnamed x31 -> x28, local copies, waits for them, and re-layouts: 15.2 us -> 7.15 us
    all_to_all x1, blocking collectives: 20.6 us -> 27.7 us  [shards(): lax.all_to_all(back, 'expert', split_axis=0, concat_axis=0, tiled=True)]
    all_to_all x1, waiting for transfers between devices: 15.2 us -> 8.84 us  [shards(): lax.all_to_all(sums, 'context', split_axis=0, concat_axis=0, tiled=True)]
    all_to_all x0 -> x1, starting transfers between devices: none -> 6.29 us  [shards(): lax.all_to_all(grad_heads, 'context', split_axis=0, concat_axis=0, tiled=...]
  transfers between devices with their start and end apart: 21 -> 23, of which waited for: 11 -> 13; matrix products, arithmetic and copies ran while one was open for 3% -> 2% of each run, Pallas kernels for 15% -> 24%
where the time goes in v3:
time: 338 us; the launch traced here: 336 us
  waiting for transfers between devices  101 us (30%)
  Pallas kernels  79.1 us (23%)
  blocking collectives  72.1 us (21%)
  starting transfers between devices  54.9 us (16%)
  between operations  13.9 us (4%)
  local copies, waits for them, and re-layouts  10.5 us (3%)
  other arithmetic  5.2 us (2%)
    all_to_all x1, blocking collectives, shards(): lax.all_to_all(send, 'expert', split_axis=0, concat_axis=0, tiled=True)  29.5 us
    all_to_all x1, blocking collectives, shards(): lax.all_to_all(back, 'expert', split_axis=0, concat_axis=0, tiled=True)  27.7 us
    pallas_call x1, Pallas kernels, expert_both(): pl.pallas_call(expert_kernel, name='expert_both', grid=(count // AT_ONCE,...  20 us
    all_to_all x1, waiting for transfers between devices, shards(): lax.all_to_all(packed, 'context', split_axis=0, concat_axis=0, tiled=True)  19.7 us
    ppermute x1, waiting for transfers between devices, gather_all(): ahead = lax.ppermute(filled, AXES, shifted(1, -1))  15.9 us
    all_to_all x1, blocking collectives, shards(): lax.all_to_all(terms, 'expert', split_axis=0, concat_axis=0, tiled=True)  14.9 us
    pallas_call x1, Pallas kernels, attend_back(): pl.pallas_call(lambda *refs: attend_back_kernel(rel_table.shape[1], *refs...  14.1 us
    ppermute x6, waiting for transfers between devices, direct_gather(): lax.ppermute(block, AXES, shifted(dim, -by))  13.6 us
  transfers between devices with their start and end apart: 23, of which 13 were waited for; matrix products, arithmetic and copies ran while one was open for 2% of the time, Pallas kernels for 24%

profile of v3, /device:TPU:1, one launch (start us, length us, event | category | flops | bytes accessed | tf_op | source)
XLA Modules:
  0.0 336.4 jit_solution(8997198077063593730)
XLA Ops:
  9.2 3.7 %project.1 = (bf16[128,768]{1,0:T(8,128)(2,1)}, bf16[16,192,128]{2,1,0:T(8,128)(2,1)}) custom-call(bf16[128,768]{1,0:T(8,128)(2,1)} %bitcast.42, f32[768]{0:T(1024)} %gain_ref.5, bf16[768,768]{1,0:T(8,128)(2,1)} %refs_1_.5, bf16[768,768]{1,0:T(8,128)(2,1)} %refs_2_.1, bf16[768,768]{1,0:T(8,128)(2,1)} %refs_3_.3), custom_call_target="tpu_custom_call" | custom-call | tf_op jit(solution)/shard_map/project/pallas_call | solution.py:82
  13.0 9.3 %all-to-all-start = ((bf16[16,192,128]{2,1,0:T(8,128)(2,1)}), bf16[16,192,128]{2,1,0:T(8,128)(2,1)S(1)}, u32[]{:S(2)}, u32[]{:S(2)}) async-start(bf16[16,192,128]{2,1,0:T(8,128)(2,1)} %get-tuple-element.41), calls=%async_computation | async-start | bytes 1572864 | tf_op jit(solution)/shard_map/all_to_all | solution.py:861
  22.3 19.7 %all-to-all-done.refs_2_ = bf16[16,192,128]{2,1,0:T(8,128)(2,1)S(1)} async-done(((bf16[16,192,128]{2,1,0:T(8,128)(2,1)}), bf16[16,192,128]{2,1,0:T(8,128)(2,1)S(1)}, u32[]{:S(2)}, u32[]{:S(2)}) %all-to-all-start) | async-done | bytes 786464 | tf_op jit(solution)/shard_map/all_to_all | solution.py:861
  42.9 7.0 %attend.1 = (bf16[16,64,128]{2,1,0:T(8,128)(2,1)}, f32[16,64,128]{2,1,0:T(8,128)}, f32[8,8,256]{2,1,0:T(8,128)}) custom-call(s32[1]{0:T(128)} %bitcast.2.refs_0_, f32[12,32]{1,0:T(8,128)} %refs_1_.4, bf16[16,192,128]{2,1,0:T(8,128)(2,1)} %copy-done), custom_call_target="tpu_custom_call" | custom-call | tf_op jit(solution)/shard_map/attend/pallas_call | solution.py:170
  49.9 5.1 %all-to-all-start.1 = ((bf16[16,64,128]{2,1,0:T(8,128)(2,1)}), bf16[16,64,128]{2,1,0:T(8,128)(2,1)S(1)}, u32[]{:S(2)}, u32[]{:S(2)}) async-start(bf16[16,64,128]{2,1,0:T(8,128)(2,1)} %get-tuple-element.42), calls=%async_computation.1 | async-start | bytes 524288 | tf_op jit(solution)/shard_map/all_to_all | solution.py:865
  56.6 8.9 %all-to-all-done.1.refs_2_ = bf16[16,64,128]{2,1,0:T(8,128)(2,1)S(1)} async-done(((bf16[16,64,128]{2,1,0:T(8,128)(2,1)}), bf16[16,64,128]{2,1,0:T(8,128)(2,1)S(1)}, u32[]{:S(2)}, u32[]{:S(2)}) %all-to-all-start.1) | async-done | bytes 262176 | tf_op jit(solution)/shard_map/all_to_all | solution.py:865
  66.2 4.0 %dispatch.1 = (bf16[8,96,768]{2,1,0:T(8,128)(2,1)}, bf16[128,768]{1,0:T(8,128)(2,1)}, f32[128,768]{1,0:T(8,128)}, bf16[128,768]{1,0:T(8,128)(2,1)}, bf16[2,128,384]{2,1,0:T(8,128)(2,1)}, /*index=5*/f32[128,128]{1,0:T(8,128)}) custom-call(bf16[128,768]{1,0:T(8,128)(2,1)} %bitcast.43, bf16[128,768]{1,0:T(8,128)(2,1)} %bitcast.46, ...), custom_call_target="tpu_custom_call" | custom-call | tf_op jit(solution)/shard_map/dispatch/pallas_call | solution.py:434
  70.2 29.5 %all_to_all.40.rows_ref = bf16[8,96,768]{2,1,0:T(8,128)(2,1)} all-to-all(bf16[8,96,768]{2,1,0:T(8,128)(2,1)} %get-tuple-element.43), channel_id=1, replica_groups=mesh['context'=16,'expert'=8] {'expert'}, dimensions={0} | all-to-all | bytes 2359296 | tf_op jit(solution)/shard_map/all_to_all | solution.py:869
  99.7 11.3 %all-gather.5.cloned.1.call-done = bf16[6144,768]{1,0:T(8,128)(2,1)} async-done(((bf16[384,768]{1,0:T(8,128)(2,1)}), bf16[6144,768]{1,0:T(8,128)(2,1)}) %all-gather.5.cloned.1.call-update) | async-done | bytes 9437200 | tf_op jit(solution)/shard_map/all_gather | solution.py:859
  111.0 20.0 %expert_both.1 = (bf16[8,96,768]{2,1,0:T(8,128)(2,1)}, bf16[16,384,768]{2,1,0:T(8,128)(2,1)}) custom-call(bf16[8,96,768]{2,1,0:T(8,128)(2,1)} %all_to_all.40.rows_ref, bf16[16,384,768]{2,1,0:T(8,128)(2,1)} %bitcast.40), custom_call_target="tpu_custom_call" | custom-call | tf_op jit(solution)/shard_map/expert_both/pallas_call | solution.py:495
  132.3 27.7 %all_to_all.41.back_ref = bf16[8,96,768]{2,1,0:T(8,128)(2,1)} all-to-all(bf16[8,96,768]{2,1,0:T(8,128)(2,1)S(1)} %copy-done.6), channel_id=1, replica_groups=mesh['context'=16,'expert'=8] {'expert'}, dimensions={0} | all-to-all | bytes 2359296 | tf_op jit(solution)/shard_map/all_to_all | solution.py:871
  160.0 4.8 %combine.1 = (bf16[128,768]{1,0:T(8,128)(2,1)}, f32[128,768]{1,0:T(8,128)}, bf16[16,64,128]{2,1,0:T(8,128)(2,1)}, f32[16,768]{1,0:T(8,128)}) custom-call(bf16[128,768]{1,0:T(8,128)(2,1)} %bitcast.47, bf16[8,96,768]{2,1,0:T(8,128)(2,1)} %all_to_all.41.back_ref, bf16[2,128,384]{2,1,0:T(8,128)(2,1)} %get-tuple-element.45.pick_ref, ...), custom_call_target="tpu_custom_call" | custom-call | tf_op jit(solution)/shard_map/combine/pallas_call | solution.py:605
  164.8 6.3 %all-to-all-start.4 = ((bf16[16,64,128]{2,1,0:T(8,128)(2,1)}), bf16[16,64,128]{2,1,0:T(8,128)(2,1)S(1)}, u32[]{:S(2)}, u32[]{:S(2)}) async-start(bf16[16,64,128]{2,1,0:T(8,128)(2,1)} %get-tuple-element.50), calls=%async_computation.4 | async-start | bytes 524288 | tf_op jit(solution)/shard_map/all_to_all | solution.py:877
  171.1 2.7 out_grad.1
  173.8 6.1 %all-to-all-done.4.refs_3_ = bf16[16,64,128]{2,1,0:T(8,128)(2,1)S(1)} async-done(((bf16[16,64,128]{2,1,0:T(8,128)(2,1)}), bf16[16,64,128]{2,1,0:T(8,128)(2,1)S(1)}, u32[]{:S(2)}, u32[]{:S(2)}) %all-to-all-start.4) | async-done | bytes 262176 | tf_op jit(solution)/shard_map/all_to_all | solution.py:877
  180.5 4.5 %all-to-all-start.5 = ((bf16[16,64,768]{2,1,0:T(8,128)(2,1)}), bf16[16,64,768]{2,1,0:T(8,128)(2,1)S(1)}, u32[]{:S(2)}, u32[]{:S(2)}) async-start(bf16[16,64,768]{2,1,0:T(8,128)(2,1)} %out_grad.1), calls=%async_computation.5 | async-start | bytes 3145728 | tf_op jit(solution)/shard_map/all_to_all | solution.py:878
  185.0 14.1 %attend_back.1 = (bf16[16,192,128]{2,1,0:T(8,128)(2,1)}, f32[16,128]{1,0:T(8,128)}) custom-call(s32[1]{0:T(128)} %bitcast.2.refs_0_, f32[12,32]{1,0:T(8,128)} %refs_1_.4, bf16[16,192,128]{2,1,0:T(8,128)(2,1)} %copy-done, bf16[16,64,128]{2,1,0:T(8,128)(2,1)} %copy-done.7, f32[16,64,128]{2,1,0:T(8,128)} %get-tuple-element.51.refs_4_, ...), custom_call_target="tpu_custom_call" | custom-call | tf_op jit(solution)/shard_map/attend_back/pallas_call | solution.py:294
  199.1 8.8 %all-to-all-done.5.sums_ref = bf16[16,64,768]{2,1,0:T(8,128)(2,1)S(1)} async-done(((bf16[16,64,768]{2,1,0:T(8,128)(2,1)}), bf16[16,64,768]{2,1,0:T(8,128)(2,1)S(1)}, u32[]{:S(2)}, u32[]{:S(2)}) %all-to-all-start.5) | async-done | bytes 1572896 | tf_op jit(solution)/shard_map/all_to_all | solution.py:878
  209.1 5.0 %head_grads.1 = bf16[8,208,128]{2,1,0:T(8,128)(2,1)} custom-call(bf16[16,192,128]{2,1,0:T(8,128)(2,1)} %get-tuple-element.53.dqkv_ref, bf16[16,128,768]{2,1,0:T(8,128)(2,1)} %bitcast.41, f32[16,128]{1,0:T(8,128)} %get-tuple-element.55.bias_ref, bf16[16,64,768]{2,1,0:T(8,128)(2,1)} %copy-done.1), custom_call_target="tpu_custom_call" | custom-call | tf_op jit(solution)/shard_map/head_grads/pallas_call | solution.py:357
  214.1 14.9 %all_to_all.42.in_ref = bf16[8,208,128]{2,1,0:T(8,128)(2,1)} all-to-all(bf16[8,208,128]{2,1,0:T(8,128)(2,1)} %head_grads.1), channel_id=1, replica_groups=mesh['context'=16,'expert'=8] {'expert'}, dimensions={0} | all-to-all | bytes 851968 | tf_op jit(solution)/shard_map/all_to_all | solution.py:883
  228.9 7.3 %all-to-all-start.7 = ((bf16[16,192,128]{2,1,0:T(8,128)(2,1)}), bf16[16,192,128]{2,1,0:T(8,128)(2,1)S(1)}, u32[]{:S(2)}, u32[]{:S(2)}) async-start(bf16[16,192,128]{2,1,0:T(8,128)(2,1)} %get-tuple-element.53.dqkv_ref), calls=%async_computation.7 | async-start | bytes 1572864 | tf_op jit(solution)/shard_map/all_to_all | solution.py:881
  242.9 3.5 %collective-permute-done.2 = bf16[208,128]{1,0:T(8,128)(2,1)S(1)} collective-permute-done((bf16[208,128]{1,0:T(8,128)(2,1)}, bf16[208,128]{1,0:T(8,128)(2,1)S(1)}, u32[]{:S(2)}, u32[]{:S(2)}) %collective-permute-start.2) | collective-permute-done | bytes 53280 | tf_op jit(solution)/shard_map/ppermute | solution.py:682
  249.3 7.0 %all-to-all-done.7.grads_ref = bf16[16,192,128]{2,1,0:T(8,128)(2,1)S(1)} async-done(((bf16[16,192,128]{2,1,0:T(8,128)(2,1)}), bf16[16,192,128]{2,1,0:T(8,128)(2,1)S(1)}, u32[]{:S(2)}, u32[]{:S(2)}) %all-to-all-start.7) | async-done | bytes 786464 | tf_op jit(solution)/shard_map/all_to_all | solution.py:881
  256.7 3.3 collective-permute-start.4
  263.7 5.8 %collective-permute-done.4 = bf16[4,208,128]{2,1,0:T(8,128)(2,1)S(1)} collective-permute-done((bf16[4,208,128]{2,1,0:T(8,128)(2,1)S(1)}, bf16[4,208,128]{2,1,0:T(8,128)(2,1)S(1)}, u32[]{:S(2)}, u32[]{:S(2)}) %collective-permute-start.4) | collective-permute-done | bytes 213024 | tf_op jit(solution)/shard_map/ppermute | solution.py:682
  273.0 15.9 %collective-permute-done.6.refs_5_ = bf16[4,4,208,128]{3,2,1,0:T(8,128)(2,1)S(1)} collective-permute-done((bf16[4,4,208,128]{3,2,1,0:T(8,128)(2,1)S(1)}, bf16[4,4,208,128]{3,2,1,0:T(8,128)(2,1)S(1)}, u32[]{:S(2)}, u32[]{:S(2)}) %collective-permute-start.6) | collective-permute-done | bytes 852000 | tf_op jit(solution)/shard_map/ppermute | solution.py:689
  290.5 2.8 collective-permute-start.11
  293.5 4.8 %collective-permute-done.8.refs_7_ = bf16[2,4,208,128]{3,2,1,0:T(8,128)(2,1)} collective-permute-done((bf16[2,4,208,128]{3,2,1,0:T(8,128)(2,1)S(1)}, bf16[2,4,208,128]{3,2,1,0:T(8,128)(2,1)}, u32[]{:S(2)}, u32[]{:S(2)}) %collective-permute-start.8) | collective-permute-done | bytes 426016 | tf_op jit(solution)/shard_map/ppermute | solution.py:692
  298.3 3.0 collective-permute-start.13
  301.3 4.5 %collective-permute-done.9.refs_8_ = bf16[2,4,208,128]{3,2,1,0:T(8,128)(2,1)} collective-permute-done((bf16[2,4,208,128]{3,2,1,0:T(8,128)(2,1)S(1)}, bf16[2,4,208,128]{3,2,1,0:T(8,128)(2,1)}, u32[]{:S(2)}, u32[]{:S(2)}) %collective-permute-start.9) | collective-permute-done | bytes 426016 | tf_op jit(solution)/shard_map/ppermute | solution.py:693
  307.7 4.6 %input_grad.1 = f32[128,768]{1,0:T(8,128)} custom-call(bf16[128,768]{1,0:T(8,128)(2,1)} %bitcast.44, f32[768]{0:T(1024)} %gain_ref.5, bf16[16,192,128]{2,1,0:T(8,128)(2,1)} %copy-done.3, bf16[768,768]{1,0:T(8,128)(2,1)} %refs_1_.5, bf16[768,768]{1,0:T(8,128)(2,1)} %refs_2_.1, bf16[768,768]{1,0:T(8,128)(2,1)} %refs_3_.3, ...), custom_call_target="tpu_custom_call" | custom-call | tf_op jit(solution)/shard_map/input_grad/pallas_call | solution.py:649
  313.2 11.6 %unpack.1 = (f32[768,768]{1,0:T(8,128)}, f32[768,768]{1,0:T(8,128)}, f32[768,768]{1,0:T(8,128)}, f32[12,8,8,768]{3,2,1,0:T(8,128)}, f32[12,32]{1,0:T(8,128)}, /*...) custom-call(s32[4]{0:T(128)} %pad_add_fusion.refs_0_, bf16[768,768]{1,0:T(8,128)(2,1)} %refs_1_.5, ...), custom_call_target="tpu_custom_call" | custom-call | tf_op jit(solution)/shard_map/unpack/pallas_call | solution.py:785
  (71 shorter events, 35.1 us)
Async XLA Ops:
  7.2 103.9 %all-gather.5.cloned.1.call-start = ((), (), s32[]{:S(2)}) async-start(), calls=%async_computation.10 | async-start | bytes 10027008 | tf_op jit(solution)/shard_map/all_gather | solution.py:859
  9.2 190.0 %all-gather.7.cloned.1.call-start = ((), (), s32[]{:S(2)}) async-start(), calls=%async_computation.11 | async-start | bytes 3342336 | tf_op jit(solution)/shard_map/all_gather | solution.py:862
  12.9 42.1 %copy-start.11 = (bf16[768,8]{0,1:T(8,128)(2,1)S(1)}, bf16[768,8]{0,1:T(8,128)(2,1)}, u32[]{:S(2)}) copy-start(bf16[768,8]{0,1:T(8,128)(2,1)} %param.21) | copy-start | bytes 36868
  13.0 42.9 %copy-start.12 = (s32[1,128,2]{1,2,0:T(2,128)S(1)}, s32[1,128,2]{1,2,0:T(2,128)}, u32[]{:S(2)}) copy-start(s32[1,128,2]{1,2,0:T(2,128)} %param.24) | copy-start | bytes 3076
  13.0 29.0 %all-to-all-start = ((bf16[16,192,128]{2,1,0:T(8,128)(2,1)}), bf16[16,192,128]{2,1,0:T(8,128)(2,1)S(1)}, u32[]{:S(2)}, u32[]{:S(2)}) async-start(bf16[16,192,128]{2,1,0:T(8,128)(2,1)} %get-tuple-element.41), calls=%async_computation | async-start | bytes 1572864 | tf_op jit(solution)/shard_map/all_to_all | solution.py:861
  49.9 15.6 %all-to-all-start.1 = ((bf16[16,64,128]{2,1,0:T(8,128)(2,1)}), bf16[16,64,128]{2,1,0:T(8,128)(2,1)S(1)}, u32[]{:S(2)}, u32[]{:S(2)}) async-start(bf16[16,64,128]{2,1,0:T(8,128)(2,1)} %get-tuple-element.42), calls=%async_computation.1 | async-start | bytes 524288 | tf_op jit(solution)/shard_map/all_to_all | solution.py:865
  55.0 272.6 %reduce-scatter.2.cloned.1.call-start = ((), (), s32[]{:S(2)}) async-start(), calls=%async_computation.9 | async-start | bytes 10027008 | tf_op jit(solution)/shard_map/reduce_scatter | solution.py:872
  131.0 1.3 copy-start.6
  164.8 15.0 %all-to-all-start.4 = ((bf16[16,64,128]{2,1,0:T(8,128)(2,1)}), bf16[16,64,128]{2,1,0:T(8,128)(2,1)S(1)}, u32[]{:S(2)}, u32[]{:S(2)}) async-start(bf16[16,64,128]{2,1,0:T(8,128)(2,1)} %get-tuple-element.50), calls=%async_computation.4 | async-start | bytes 524288 | tf_op jit(solution)/shard_map/all_to_all | solution.py:877
  180.5 27.4 %all-to-all-start.5 = ((bf16[16,64,768]{2,1,0:T(8,128)(2,1)}), bf16[16,64,768]{2,1,0:T(8,128)(2,1)S(1)}, u32[]{:S(2)}, u32[]{:S(2)}) async-start(bf16[16,64,768]{2,1,0:T(8,128)(2,1)} %out_grad.1), calls=%async_computation.5 | async-start | bytes 3145728 | tf_op jit(solution)/shard_map/all_to_all | solution.py:878
  208.0 1.1 copy-start.1
  228.9 27.4 %all-to-all-start.7 = ((bf16[16,192,128]{2,1,0:T(8,128)(2,1)}), bf16[16,192,128]{2,1,0:T(8,128)(2,1)S(1)}, u32[]{:S(2)}, u32[]{:S(2)}) async-start(bf16[16,192,128]{2,1,0:T(8,128)(2,1)} %get-tuple-element.53.dqkv_ref), calls=%async_computation.7 | async-start | bytes 1572864 | tf_op jit(solution)/shard_map/all_to_all | solution.py:881
  238.0 8.4 %collective-permute-start.2 = (bf16[208,128]{1,0:T(8,128)(2,1)}, bf16[208,128]{1,0:T(8,128)(2,1)S(1)}, u32[]{:S(2)}, u32[]{:S(2)}) collective-permute-start(bf16[208,128]{1,0:T(8,128)(2,1)} %add_up.1), channel_id=1, source_target_pairs={{0,16},{1,17},{2,18},{3,19},{4,20},{5,21},{6,22},{7,23},{8,24},{9,... | collective-permute-start | bytes 159752 | tf_op jit(solution)/shard_map/ppermute | solution.py:682
  239.4 9.1 %collective-permute-start.1 = (bf16[208,128]{1,0:T(8,128)(2,1)}, bf16[208,128]{1,0:T(8,128)(2,1)S(1)}, u32[]{:S(2)}, u32[]{:S(2)}) collective-permute-start(bf16[208,128]{1,0:T(8,128)(2,1)} %add_up.1), channel_id=1, source_target_pairs={{0,32},{1,33},{2,34},{3,35},{4,36},{5,37},{6,38},{7,39},{8,40},{9,... | collective-permute-start | bytes 159752 | tf_op jit(solution)/shard_map/ppermute | solution.py:682
  241.7 6.7 %collective-permute-start = (bf16[208,128]{1,0:T(8,128)(2,1)}, bf16[208,128]{1,0:T(8,128)(2,1)S(1)}, u32[]{:S(2)}, u32[]{:S(2)}) collective-permute-start(bf16[208,128]{1,0:T(8,128)(2,1)} %add_up.1), channel_id=1, source_target_pairs={{0,48},{1,49},{2,50},{3,51},{4,52},{5,53},{6,54},{7,55},{8,56},{9,... | collective-permute-start | bytes 159752 | tf_op jit(solution)/shard_map/ppermute | solution.py:682
  256.3 32.6 %copy-start.3 = (bf16[16,192,128]{2,1,0:T(8,128)(2,1)}, bf16[16,192,128]{2,1,0:T(8,128)(2,1)S(1)}, u32[]{:S(2)}) copy-start(bf16[16,192,128]{2,1,0:T(8,128)(2,1)S(1)} %all-to-all-done.7.grads_ref) | copy-start | bytes 2359300
  256.3 7.4 %collective-permute-start.5 = (bf16[4,208,128]{2,1,0:T(8,128)(2,1)S(1)}, bf16[4,208,128]{2,1,0:T(8,128)(2,1)S(1)}, u32[]{:S(2)}, u32[]{:S(2)}) collective-permute-start(bf16[4,208,128]{2,1,0:T(8,128)(2,1)S(1)} %pad_maximum_fusion.2), channel_id=1, source_target_pairs={{0,1},{1,64},{2,3},{3,66},{4,5},{5,68},{6,7},{7,70},{8,9},{9,72},{... | collective-permute-start | bytes 638984 | tf_op jit(solution)/shard_map/ppermute | solution.py:682
  256.7 12.8 %collective-permute-start.4 = (bf16[4,208,128]{2,1,0:T(8,128)(2,1)S(1)}, bf16[4,208,128]{2,1,0:T(8,128)(2,1)S(1)}, u32[]{:S(2)}, u32[]{:S(2)}) collective-permute-start(bf16[4,208,128]{2,1,0:T(8,128)(2,1)S(1)} %pad_maximum_fusion.2), channel_id=1, source_target_pairs={{0,64},{1,65},{2,66},{3,67},{4,68},{5,69},{6,70},{7,71},{8,72},{9,... | collective-permute-start | bytes 638984 | tf_op jit(solution)/shard_map/ppermute | solution.py:682
  260.0 9.5 %collective-permute-start.3 = (bf16[4,208,128]{2,1,0:T(8,128)(2,1)S(1)}, bf16[4,208,128]{2,1,0:T(8,128)(2,1)S(1)}, u32[]{:S(2)}, u32[]{:S(2)}) collective-permute-start(bf16[4,208,128]{2,1,0:T(8,128)(2,1)S(1)} %pad_maximum_fusion.2), channel_id=1, source_target_pairs={{0,65},{1,0},{2,67},{3,2},{4,69},{5,4},{6,71},{7,6},{8,73},{9,8},{... | collective-permute-start | bytes 638984 | tf_op jit(solution)/shard_map/ppermute | solution.py:682
  269.6 42.7 %copy-start.2 = (bf16[4,4,208,128]{3,2,1,0:T(8,128)(2,1)}, bf16[4,4,208,128]{3,2,1,0:T(8,128)(2,1)S(1)}, u32[]{:S(2)}) copy-start(bf16[4,4,208,128]{3,2,1,0:T(8,128)(2,1)S(1)} %pad_maximum_fusion.refs_4_) | copy-start | bytes 2555908
  269.6 19.3 %collective-permute-start.6 = (bf16[4,4,208,128]{3,2,1,0:T(8,128)(2,1)S(1)}, bf16[4,4,208,128]{3,2,1,0:T(8,128)(2,1)S(1)}, u32[]{:S(2)}, u32[]{:S(2)}) collective-permute-start(bf16[4,4,208,128]{3,2,1,0:T(8,128)(2,1)S(1)} %pad_maximum_fusion.refs_4_), channel_id=1, source_target_pairs={{0,6},{1,7},{2,0},{3,1},{4,2},{5,3},{6,4},{7,5},{8,14},{9,15},{10,... | collective-permute-start | bytes 2555912 | tf_op jit(solution)/shard_map/ppermute | solution.py:689
  270.3 23.0 %collective-permute-start.7 = (bf16[4,4,208,128]{3,2,1,0:T(8,128)(2,1)S(1)}, bf16[4,4,208,128]{3,2,1,0:T(8,128)(2,1)S(1)}, u32[]{:S(2)}, u32[]{:S(2)}) collective-permute-start(bf16[4,4,208,128]{3,2,1,0:T(8,128)(2,1)S(1)} %pad_maximum_fusion.refs_4_), channel_id=1, source_target_pairs={{0,2},{1,3},{2,4},{3,5},{4,6},{5,7},{6,0},{7,1},{8,10},{9,11},{10,... | collective-permute-start | bytes 2555912 | tf_op jit(solution)/shard_map/ppermute | solution.py:690
  271.1 41.2 %collective-permute-start.10 = (bf16[4,4,208,128]{3,2,1,0:T(8,128)(2,1)S(1)}, bf16[4,4,208,128]{3,2,1,0:T(8,128)(2,1)}, u32[]{:S(2)}, u32[]{:S(2)}) collective-permute-start(bf16[4,4,208,128]{3,2,1,0:T(8,128)(2,1)S(1)} %pad_maximum_fusion.refs_4_), channel_id=1, source_target_pairs={{0,8},{1,9},{2,10},{3,11},{4,12},{5,13},{6,14},{7,15},{8,0},{9,1},... | collective-permute-start | bytes 2555912 | tf_op jit(solution)/shard_map/ppermute | solution.py:696
  288.9 23.4 %copy-start.4 = (bf16[4,4,208,128]{3,2,1,0:T(8,128)(2,1)}, bf16[4,4,208,128]{3,2,1,0:T(8,128)(2,1)S(1)}, u32[]{:S(2)}) copy-start(bf16[4,4,208,128]{3,2,1,0:T(8,128)(2,1)S(1)} %collective-permute-done.6.refs_5_) | copy-start | bytes 2555908
  288.9 9.4 %collective-permute-start.8 = (bf16[2,4,208,128]{3,2,1,0:T(8,128)(2,1)S(1)}, bf16[2,4,208,128]{3,2,1,0:T(8,128)(2,1)}, u32[]{:S(2)}, u32[]{:S(2)}) collective-permute-start(bf16[2,4,208,128]{3,2,1,0:T(8,128)(2,1)S(1)} %slice.32), channel_id=1, source_target_pairs={{0,6},{1,7},{2,0},{3,1},{4,2},{5,3},{6,4},{7,5},{8,14},{9,15},{10,... | collective-permute-start | bytes 1277960 | tf_op jit(solution)/shard_map/ppermute | solution.py:692
  290.5 21.7 %collective-permute-start.11 = (bf16[4,4,208,128]{3,2,1,0:T(8,128)(2,1)S(1)}, bf16[4,4,208,128]{3,2,1,0:T(8,128)(2,1)S(1)}, u32[]{:S(2)}, u32[]{:S(2)}) collective-permute-start(bf16[4,4,208,128]{3,2,1,0:T(8,128)(2,1)S(1)} %collective-permute-done.6.refs_5_), channel_id=1, source_target_pairs={{0,8},{1,9},{2,10},{3,11},{4,12},{5,13},{6,14},{7,15},{8,0},{9,1},... | collective-permute-start | bytes 2555912 | tf_op jit(solution)/shard_map/ppermute | solution.py:696
  293.3 18.9 %copy-start.5 = (bf16[4,4,208,128]{3,2,1,0:T(8,128)(2,1)}, bf16[4,4,208,128]{3,2,1,0:T(8,128)(2,1)S(1)}, u32[]{:S(2)}) copy-start(bf16[4,4,208,128]{3,2,1,0:T(8,128)(2,1)S(1)} %collective-permute-done.7.refs_6_) | copy-start | bytes 2555908
  293.3 19.0 %collective-permute-start.12 = (bf16[4,4,208,128]{3,2,1,0:T(8,128)(2,1)S(1)}, bf16[4,4,208,128]{3,2,1,0:T(8,128)(2,1)}, u32[]{:S(2)}, u32[]{:S(2)}) collective-permute-start(bf16[4,4,208,128]{3,2,1,0:T(8,128)(2,1)S(1)} %collective-permute-done.7.refs_6_), channel_id=1, source_target_pairs={{0,8},{1,9},{2,10},{3,11},{4,12},{5,13},{6,14},{7,15},{8,0},{9,1},... | collective-permute-start | bytes 2555912 | tf_op jit(solution)/shard_map/ppermute | solution.py:696
  293.4 12.3 %collective-permute-start.9 = (bf16[2,4,208,128]{3,2,1,0:T(8,128)(2,1)S(1)}, bf16[2,4,208,128]{3,2,1,0:T(8,128)(2,1)}, u32[]{:S(2)}, u32[]{:S(2)}) collective-permute-start(bf16[2,4,208,128]{3,2,1,0:T(8,128)(2,1)S(1)} %slice.33), channel_id=1, source_target_pairs={{0,2},{1,3},{2,4},{3,5},{4,6},{5,7},{6,0},{7,1},{8,10},{9,11},{10,... | collective-permute-start | bytes 1277960 | tf_op jit(solution)/shard_map/ppermute | solution.py:693
  298.3 14.0 %collective-permute-start.13 = (bf16[2,4,208,128]{3,2,1,0:T(8,128)(2,1)}, bf16[2,4,208,128]{3,2,1,0:T(8,128)(2,1)}, u32[]{:S(2)}, u32[]{:S(2)}) collective-permute-start(bf16[2,4,208,128]{3,2,1,0:T(8,128)(2,1)} %collective-permute-done.8.refs_7_), channel_id=1, source_target_pairs={{0,8},{1,9},{2,10},{3,11},{4,12},{5,13},{6,14},{7,15},{8,0},{9,1},... | collective-permute-start | bytes 1277960 | tf_op jit(solution)/shard_map/ppermute | solution.py:696
  305.8 6.5 %collective-permute-start.14 = (bf16[2,4,208,128]{3,2,1,0:T(8,128)(2,1)}, bf16[2,4,208,128]{3,2,1,0:T(8,128)(2,1)}, u32[]{:S(2)}, u32[]{:S(2)}) collective-permute-start(bf16[2,4,208,128]{3,2,1,0:T(8,128)(2,1)} %collective-permute-done.9.refs_8_), channel_id=1, source_target_pairs={{0,8},{1,9},{2,10},{3,11},{4,12},{5,13},{6,14},{7,15},{8,0},{9,1},... | collective-permute-start | bytes 1277960 | tf_op jit(solution)/shard_map/ppermute | solution.py:696
  312.3 13.5 %copy-start.10 = (f32[768]{0:T(1024)S(1)}, f32[768]{0:T(1024)}, u32[]{:S(2)}) copy-start(f32[768]{0:T(1024)} %gain_ref.5) | copy-start | bytes 9220
  (4 other events, 3.2 us)
Sparse Core Ops, SparseCore 0:
  11.1 99.9 all-gather.4
  113.5 50.4 all-gather.6
  168.4 124.7 reduce-scatter.1

commit v4 on v3

--- a/solution.py
+++ b/solution.py
@@ -82,6 +82,7 @@
     return pl.pallas_call(
         project_kernel,
         name="project",
+        cost_estimate=pl.CostEstimate(flops=500000000, bytes_accessed=6000000, transcendentals=0),
         out_shape=(
             jax.ShapeDtypeStruct((rows, width), BF16),
             jax.ShapeDtypeStruct((HEAD_SLOTS, rows + rows // 2, 128), BF16),
@@ -170,6 +171,7 @@
     return pl.pallas_call(
         lambda *refs: attend_kernel(rel_table.shape[1], *refs),
         name="attend",
+        cost_estimate=pl.CostEstimate(flops=7000000000, bytes_accessed=3000000, transcendentals=3000000),
         out_shape=(
             jax.ShapeDtypeStruct((count, 64, 128), BF16),
             jax.ShapeDtypeStruct((count, 64, 128), F32),
@@ -294,6 +296,7 @@
     return pl.pallas_call(
         lambda *refs: attend_back_kernel(rel_table.shape[1], *refs),
         name="attend_back",
+        cost_estimate=pl.CostEstimate(flops=14000000000, bytes_accessed=4000000, transcendentals=3000000),
         out_shape=(
             jax.ShapeDtypeStruct(qkv.shape, BF16),
             jax.ShapeDtypeStruct((16, 128), F32),
@@ -317,17 +320,25 @@
     )(head, rel_table, qkv, grad_heads, keep, lse)
 
 
-def head_grads_kernel(dqkv_ref, normed_ref, bias_ref, sums_ref, out_ref):
+def head_grads_kernel(place_ref, dqkv_ref, mine_ref, other_ref, bias_ref, sums_ref, out_ref, turned_s):
     count = dqkv_ref.shape[0]
-    width = normed_ref.shape[2]
-    tokens = count * 64
-    first = normed_ref[:, :64, :].reshape(tokens, width)
-    second = normed_ref[:, 64:, :].reshape(tokens, width)
-    pairs = dot(dqkv_ref[:, :64, :].reshape(tokens, 128), first, TN) + dot(
-        dqkv_ref[:, 64:128, :].reshape(tokens, 128), second, TN
-    )
-    two = dqkv_ref[:, 128:192, :].reshape(tokens, 128)
-    third = dot(two, first, TN)[:64] + dot(two, second, TN)[64:]
+    width = mine_ref.shape[-1]
+    held = mine_ref.shape[0] * mine_ref.shape[1]
+    my_x, my_z, my_core = place_ref[0] // 2, place_ref[2], place_ref[3]
+    for i in range(count):
+        core, z, x = i // 8, i % 8 // 2, i % 2
+        there = (lax.rem(my_x + x, 2) * 4 + lax.rem(my_z + z, 4)) * 2 + lax.rem(my_core + core, 2)
+        turned_s[i] = dqkv_ref[there]
+    pairs, third = 0.0, 0.0
+    for core, normed_ref in enumerate((mine_ref, other_ref)):
+        normed = normed_ref[...].reshape(held, 128, width)
+        here = slice(held * core, held * core + held)
+        two = turned_s[here, 128:192, :].reshape(held * 64, 128)
+        for half in range(2):
+            rows = slice(64 * half, 64 * half + 64)
+            part = normed[:, rows, :].reshape(held * 64, width)
+            pairs = pairs + dot(turned_s[here, rows, :].reshape(held * 64, 128), part, TN)
+            third = third + dot(two, part, TN)[rows]
     pairs, third = pairs.T, third.T
     total = sums_ref[0].astype(F32)
     for c in range(1, count):
@@ -350,18 +361,20 @@
         ).astype(BF16)
 
 
-def head_grads(dqkv, normed_all, bias, sums, shares):
-    width = normed_all.shape[2]
+def head_grads(place, dqkv, mine, other, bias, sums, shares):
+    width = mine.shape[-1]
     each = width // shares
     held = each + each // 2 + 16 + width // 16
     return pl.pallas_call(
         head_grads_kernel,
         name="head_grads",
+        cost_estimate=pl.CostEstimate(flops=3000000000, bytes_accessed=8000000, transcendentals=0),
         out_shape=jax.ShapeDtypeStruct((shares, held, 128), BF16),
-        in_specs=[vspec()] * 4,
+        in_specs=[sspec()] + [vspec()] * 5,
         out_specs=vspec(),
-        compiler_params=whole(),
-    )(dqkv, normed_all, bias, sums)
+        scratch_shapes=[pltpu.VMEM(dqkv.shape, BF16)],
+        compiler_params=whole(),
+    )(place, dqkv, mine, other, bias, sums)
 
 
 def heads_to_rows(ref, scratch):
@@ -434,6 +447,7 @@
     return pl.pallas_call(
         lambda *refs: dispatch_kernel(experts, capacity, *refs),
         name="dispatch",
+        cost_estimate=pl.CostEstimate(flops=500000000, bytes_accessed=4000000, transcendentals=0),
         out_shape=(
             jax.ShapeDtypeStruct((experts, 2 * capacity, width), BF16),
             jax.ShapeDtypeStruct((rows, width), BF16),
@@ -485,7 +499,7 @@
             back_ref[s, capacity:, :] = dx_s[here, :].astype(BF16)
 
 
-AT_ONCE = 2
+AT_ONCE = 4
 
 
 def expert_both(rows, shared):
@@ -495,6 +509,7 @@
     return pl.pallas_call(
         expert_kernel,
         name="expert_both",
+        cost_estimate=pl.CostEstimate(flops=18000000000, bytes_accessed=22000000, transcendentals=5000000),
         grid=(count // AT_ONCE,),
         out_shape=(
             jax.ShapeDtypeStruct(rows.shape, BF16),
@@ -591,6 +606,7 @@
     return pl.pallas_call(
         out_grad_kernel,
         name="out_grad",
+        cost_estimate=pl.CostEstimate(flops=500000000, bytes_accessed=4000000, transcendentals=0),
         out_shape=jax.ShapeDtypeStruct((HEAD_SLOTS, 64, width), BF16),
         in_specs=[vspec()] * 3,
         out_specs=vspec(),
@@ -605,6 +621,7 @@
     return pl.pallas_call(
         combine_kernel,
         name="combine",
+        cost_estimate=pl.CostEstimate(flops=1000000000, bytes_accessed=5000000, transcendentals=0),
         out_shape=(
             jax.ShapeDtypeStruct((rows, width), BF16),
             jax.ShapeDtypeStruct((rows, width), F32),
@@ -649,6 +666,7 @@
     return pl.pallas_call(
         input_grad_kernel,
         name="input_grad",
+        cost_estimate=pl.CostEstimate(flops=500000000, bytes_accessed=5000000, transcendentals=0),
         out_shape=jax.ShapeDtypeStruct((rows, width), F32),
         in_specs=[vspec()] * 7,
         out_specs=vspec(),
@@ -683,11 +701,11 @@
 
 
 def gather_all(piece, beside):
-    filled, beside = lax.optimization_barrier((direct_gather(piece, 2), beside))
-    filled = direct_gather(filled, 0)
+    filled = direct_gather(direct_gather(piece, 2), 0)
     half = filled.shape[0] // 2
     ahead = lax.ppermute(filled, AXES, shifted(1, -1))
     behind = lax.ppermute(filled, AXES, shifted(1, 1))
+    ahead, behind, beside = lax.optimization_barrier((ahead, behind, beside))
     across = (
         lax.ppermute(ahead[:half], AXES, shifted(1, -1)),
         lax.ppermute(behind[half:], AXES, shifted(1, 1)),
@@ -785,6 +803,7 @@
     return pl.pallas_call(
         lambda *refs: unpack_kernel(buckets, *refs),
         name="unpack",
+        cost_estimate=pl.CostEstimate(flops=1000000000, bytes_accessed=24000000, transcendentals=0),
         grid=(experts,),
         out_shape=(
             jax.ShapeDtypeStruct((width, width), F32),
@@ -859,7 +878,10 @@
     shared = lax.all_gather(own_weights, "context", axis=0, tiled=False)
     normed, packed = project(inputs, gain_one, w_query, w_key, w_value)
     qkv = lax.all_to_all(packed, "context", split_axis=0, concat_axis=0, tiled=True)
-    normed_all = lax.all_gather(normed, "context", axis=0, tiled=False)
+    expert = lax.axis_index("expert")
+    place = jnp.stack(coordinates(context * experts + expert)).astype(jnp.int32)
+    normed, qkv = lax.optimization_barrier((normed, qkv))
+    normed_two = jnp.stack([normed, lax.ppermute(normed, AXES, shifted(0, 2))])
 
     out_heads, keep, lse = attend(head, rel_table, qkv)
     out_rows = lax.all_to_all(out_heads, "context", split_axis=0, concat_axis=0, tiled=True)
@@ -867,8 +889,12 @@
         inputs, grad_out, out_rows, w_out, gain_two, w_router, routes_here, experts
     )
     received = lax.all_to_all(send, "expert", split_axis=0, concat_axis=0, tiled=True)
+    normed_two, received, shared = lax.optimization_barrier((normed_two, received, shared))
+    normed_mine = direct_gather(normed_two, 2)
     back, weight_grads = expert_both(received, shared)
     returned = lax.all_to_all(back, "expert", split_axis=0, concat_axis=0, tiled=True)
+    normed_mine, returned = lax.optimization_barrier((normed_mine, returned))
+    normed_other = lax.ppermute(normed_mine, AXES, shifted(3, 1))
     own_grads = lax.psum_scatter(weight_grads, "context", scatter_dimension=0, tiled=False)
     block_out, grad_mixed, grad_heads, small = combine(
         grad_out, returned, picks, gates, mixed, second, routes_here, gain_two, w_router, w_out
@@ -879,18 +905,19 @@
 
     dqkv, bias = attend_back(head, rel_table, qkv, grad_here, keep, lse)
     grads = lax.all_to_all(dqkv, "context", split_axis=0, concat_axis=0, tiled=True)
-    terms = head_grads(dqkv, normed_all, bias, sums, experts)
+    terms = head_grads(place, dqkv, normed_mine, normed_other, bias, sums, experts)
+    terms, grads = lax.optimization_barrier((terms, grads))
     terms = lax.all_to_all(terms, "expert", split_axis=0, concat_axis=0, tiled=True)
-    parts, grads = gather_all(add_up(terms), grads)
     grad_tokens = input_grad(inputs, gain_one, grads, w_query, w_key, w_value, grad_mixed)
-
-    expert = lax.axis_index("expert")
-    place = jnp.stack(coordinates(context * experts + expert)).astype(jnp.int32)
+    own_grads = own_grads.astype(F32)
+    hidden = own_grads.shape[0] // 2
+    parts, (grad_tokens, grad_in, grad_back) = gather_all(
+        add_up(terms), (grad_tokens, own_grads[:hidden], own_grads[hidden:])
+    )
+
     dwq, dwk, dwv, dwo, bias, small, router, gain_grad = unpack(
         place, parts, w_query, w_key, w_value, heads, buckets, experts
     )
-    own_grads = own_grads.astype(F32)
-    hidden = own_grads.shape[0] // 2
     return (
         block_out[None],
         grad_tokens[None],
@@ -902,8 +929,8 @@
         bias,
         small[0],
         router.T,
-        own_grads[:hidden].T[None],
-        own_grads[hidden:].T[None],
+        grad_in.T[None],
+        grad_back.T[None],
     )
 
 

time: 338 us -> 328 us (0.970)
  blocking collectives: 72.1 us -> 13.9 us
  waiting for transfers between devices: 101 us -> 135 us
  starting transfers between devices: 54.9 us -> 69.5 us
    all_to_all x2 -> x0, blocking collectives: 57.2 us -> none  [the longest x1 29.5 us: shards(): lax.all_to_all(send, 'expert', split_axis=0, concat_axis=0, tiled=True)]
    ppermute x0 -> x2, waiting for transfers between devices: none -> 27.6 us  [the longest x1 27.6 us: shards(): normed_two = jnp.stack([normed, lax.ppermute(normed, AXES, shifted(0, 2))])]
    ppermute x1, waiting for transfers between devices: 15.9 us -> 0.01 us  [gather_all(): ahead = lax.ppermute(filled, AXES, shifted(1, -1))]
    ppermute x6 -> x9, waiting for transfers between devices: 13.6 us -> 27.2 us  [direct_gather(): lax.ppermute(block, AXES, shifted(dim, -by))]
    all_to_all x0 -> x2, starting transfers between devices: none -> 10.3 us  [the longest x1 5.75 us: shards(): lax.all_to_all(send, 'expert', split_axis=0, concat_axis=0, tiled=True)]
    ppermute x1, waiting for transfers between devices: 0.01 us -> 7.38 us  [gather_all(): behind = lax.ppermute(filled, AXES, shifted(1, 1))]
    all_to_all x1, waiting for transfers between devices: 8.84 us -> 14.6 us  [shards(): lax.all_to_all(sums, 'context', split_axis=0, concat_axis=0, tiled=True)]
    ppermute x1, waiting for transfers between devices: 4.77 us -> 0.01 us  [gather_all(): lax.ppermute(ahead[:half], AXES, shifted(1, -1))]
  transfers between devices with their start and end apart: 23 -> 29, of which waited for: 13 -> 19; matrix products, arithmetic and copies ran while one was open for 2% -> 2% of each run, Pallas kernels for 24% -> 14%
where the time goes in v4:
time: 328 us; the launch traced here: 326 us
  waiting for transfers between devices  135 us (41%)
  Pallas kernels  76.8 us (23%)
  starting transfers between devices  69.5 us (21%)
  between operations  14.3 us (4%)
  blocking collectives  13.9 us (4%)
  local copies, waits for them, and re-layouts  11.4 us (3%)
  other arithmetic  5.43 us (2%)
    ppermute x1, waiting for transfers between devices, shards(): normed_two = jnp.stack([normed, lax.ppermute(normed, AXES, shifted(0, 2))])  27.6 us
    ppermute x9, waiting for transfers between devices, direct_gather(): lax.ppermute(block, AXES, shifted(dim, -by))  27.2 us
    all_to_all x1, waiting for transfers between devices, shards(): lax.all_to_all(packed, 'context', split_axis=0, concat_axis=0, tiled=True)  19.6 us
    pallas_call x1, Pallas kernels, expert_both(): pl.pallas_call(expert_kernel, name='expert_both', cost_estimate=pl.CostEs...  17.9 us
    all_to_all x1, waiting for transfers between devices, shards(): lax.all_to_all(sums, 'context', split_axis=0, concat_axis=0, tiled=True)  14.6 us
    pallas_call x1, Pallas kernels, attend_back(): pl.pallas_call(lambda *refs: attend_back_kernel(rel_table.shape[1], *refs...  13.9 us
    all_to_all x1, blocking collectives, shards(): lax.all_to_all(terms, 'expert', split_axis=0, concat_axis=0, tiled=True)  13.9 us
    ppermute x9, starting transfers between devices, direct_gather(): lax.ppermute(block, AXES, shifted(dim, -by))  13.5 us
  transfers between devices with their start and end apart: 29, of which 19 were waited for; matrix products, arithmetic and copies ran while one was open for 2% of the time, Pallas kernels for 14%

profile of v4, /device:TPU:1, one launch (start us, length us, event | category | flops | bytes accessed | tf_op | source)
XLA Modules:
  0.0 326.5 jit_solution(14487704718253171782)
XLA Ops:
  9.2 3.7 %project.1 = (bf16[128,768]{1,0:T(8,128)(2,1)}, bf16[16,192,128]{2,1,0:T(8,128)(2,1)}) custom-call(bf16[128,768]{1,0:T(8,128)(2,1)} %bitcast.44, f32[768]{0:T(1024)} %gain_ref.5, bf16[768,768]{1,0:T(8,128)(2,1)} %refs_1_.5, bf16[768,768]{1,0:T(8,128)(2,1)} %refs_2_.1, bf16[768,768]{1,0:T(8,128)(2,1)} %refs_3_.3), custom_call_target="tpu_custom_call" | custom-call | flops 500000000 | bytes 6000000 | tf_op jit(solution)/shard_map/project/pallas_call | solution.py:82
  12.9 9.3 %all-to-all-start = ((bf16[16,192,128]{2,1,0:T(8,128)(2,1)}), bf16[16,192,128]{2,1,0:T(8,128)(2,1)S(1)}, u32[]{:S(2)}, u32[]{:S(2)}) async-start(bf16[16,192,128]{2,1,0:T(8,128)(2,1)} %get-tuple-element.54), calls=%async_computation | async-start | bytes 1572864 | tf_op jit(solution)/shard_map/all_to_all | solution.py:880
  22.2 19.6 %all-to-all-done.refs_2_ = bf16[16,192,128]{2,1,0:T(8,128)(2,1)S(1)} async-done(((bf16[16,192,128]{2,1,0:T(8,128)(2,1)}), bf16[16,192,128]{2,1,0:T(8,128)(2,1)S(1)}, u32[]{:S(2)}, u32[]{:S(2)}) %all-to-all-start) | async-done | bytes 786464 | tf_op jit(solution)/shard_map/all_to_all | solution.py:880
  42.6 7.0 %attend.1 = (bf16[16,64,128]{2,1,0:T(8,128)(2,1)}, f32[16,64,128]{2,1,0:T(8,128)}, f32[8,8,256]{2,1,0:T(8,128)}) custom-call(s32[1]{0:T(128)} %bitcast.4.refs_0_, f32[12,32]{1,0:T(8,128)} %refs_1_.4, bf16[16,192,128]{2,1,0:T(8,128)(2,1)} %copy-done.11), custom_call_target="tpu_custom_call" | custom-call | flops 7000000000 | bytes 3000000 | tf_op jit(solution)/shard_map/attend/pallas_call | solution.py:171
  49.7 5.2 %all-to-all-start.1 = ((bf16[16,64,128]{2,1,0:T(8,128)(2,1)}), bf16[16,64,128]{2,1,0:T(8,128)(2,1)S(1)}, u32[]{:S(2)}, u32[]{:S(2)}) async-start(bf16[16,64,128]{2,1,0:T(8,128)(2,1)} %get-tuple-element.57), calls=%async_computation.1 | async-start | bytes 524288 | tf_op jit(solution)/shard_map/all_to_all | solution.py:887
  56.4 8.9 %all-to-all-done.1.refs_2_ = bf16[16,64,128]{2,1,0:T(8,128)(2,1)S(1)} async-done(((bf16[16,64,128]{2,1,0:T(8,128)(2,1)}), bf16[16,64,128]{2,1,0:T(8,128)(2,1)S(1)}, u32[]{:S(2)}, u32[]{:S(2)}) %all-to-all-start.1) | async-done | bytes 262176 | tf_op jit(solution)/shard_map/all_to_all | solution.py:887
  66.0 4.0 %dispatch.1 = (bf16[8,96,768]{2,1,0:T(8,128)(2,1)}, bf16[128,768]{1,0:T(8,128)(2,1)}, f32[128,768]{1,0:T(8,128)}, bf16[128,768]{1,0:T(8,128)(2,1)}, bf16[2,128,384]{2,1,0:T(8,128)(2,1)}, /*index=5*/f32[128,128]{1,0:T(8,128)}) custom-call(bf16[128,768]{1,0:T(8,128)(2,1)} %bitcast.45, bf16[128,768]{1,0:T(8,128)(2,1)} %bitcast.62, ...), custom_call_target="tpu_custom_call" | custom-call | flops 500000000 | bytes 4000000 | tf_op jit(solution)/shard_map/dispatch/pallas_call | solution.py:447
  69.9 5.8 %all-to-all-start.2 = ((bf16[8,96,768]{2,1,0:T(8,128)(2,1)}), bf16[8,96,768]{2,1,0:T(8,128)(2,1)S(1)}, u32[]{:S(2)}, u32[]{:S(2)}) async-start(bf16[8,96,768]{2,1,0:T(8,128)(2,1)} %get-tuple-element.58), calls=%async_computation.2 | async-start | bytes 2359296 | tf_op jit(solution)/shard_map/all_to_all | solution.py:891
  75.8 27.6 %collective-permute-done = bf16[128,768]{1,0:T(8,128)(2,1)S(1)} collective-permute-done((bf16[128,768]{1,0:T(8,128)(2,1)S(1)}, bf16[128,768]{1,0:T(8,128)(2,1)S(1)}, u32[]{:S(2)}, u32[]{:S(2)}) %collective-permute-start) | collective-permute-done | bytes 196640 | tf_op jit(solution)/shard_map/ppermute | solution.py:884
  103.5 7.2 %all-gather.3.cloned.1.call-done = bf16[6144,768]{1,0:T(8,128)(2,1)} async-done(((bf16[384,768]{1,0:T(8,128)(2,1)}), bf16[6144,768]{1,0:T(8,128)(2,1)}) %all-gather.3.cloned.1.call-update) | async-done | bytes 9437200 | tf_op jit(solution)/shard_map/all_gather | solution.py:878
  110.7 17.9 %expert_both.1 = (bf16[8,96,768]{2,1,0:T(8,128)(2,1)}, bf16[16,384,768]{2,1,0:T(8,128)(2,1)}) custom-call(bf16[8,96,768]{2,1,0:T(8,128)(2,1)} %copy-done.7, bf16[16,384,768]{2,1,0:T(8,128)(2,1)} %bitcast.69), custom_call_target="tpu_custom_call" | custom-call | flops 17999998976 | bytes 22000000 | tf_op jit(solution)/shard_map/expert_both/pallas_call | solution.py:509
  128.6 4.5 %all-to-all-start.3 = ((bf16[8,96,768]{2,1,0:T(8,128)(2,1)}), bf16[8,96,768]{2,1,0:T(8,128)(2,1)S(1)}, u32[]{:S(2)}, u32[]{:S(2)}) async-start(bf16[8,96,768]{2,1,0:T(8,128)(2,1)} %get-tuple-element.62), calls=%async_computation.3 | async-start | bytes 2359296 | tf_op jit(solution)/shard_map/all_to_all | solution.py:895
  136.3 8.5 %collective-permute-done.3 = bf16[2,128,768]{2,1,0:T(8,128)(2,1)S(1)} collective-permute-done((bf16[2,128,768]{2,1,0:T(8,128)(2,1)S(1)}, bf16[2,128,768]{2,1,0:T(8,128)(2,1)S(1)}, u32[]{:S(2)}, u32[]{:S(2)}) %collective-permute-start.3) | collective-permute-done | bytes 393248 | tf_op jit(solution)/shard_map/ppermute | solution.py:700
  144.8 7.8 %collective-permute-done.2 = bf16[2,128,768]{2,1,0:T(8,128)(2,1)S(1)} collective-permute-done((bf16[2,128,768]{2,1,0:T(8,128)(2,1)S(1)}, bf16[2,128,768]{2,1,0:T(8,128)(2,1)S(1)}, u32[]{:S(2)}, u32[]{:S(2)}) %collective-permute-start.2) | collective-permute-done | bytes 393248 | tf_op jit(solution)/shard_map/ppermute | solution.py:700
  154.6 4.6 %combine.1 = (bf16[128,768]{1,0:T(8,128)(2,1)}, f32[128,768]{1,0:T(8,128)}, bf16[16,64,128]{2,1,0:T(8,128)(2,1)}, f32[16,768]{1,0:T(8,128)}) custom-call(bf16[128,768]{1,0:T(8,128)(2,1)} %bitcast.63, bf16[8,96,768]{2,1,0:T(8,128)(2,1)} %copy-done.6, bf16[2,128,384]{2,1,0:T(8,128)(2,1)} %get-tuple-element.64.pick_ref, ...), custom_call_target="tpu_custom_call" | custom-call | flops 1000000000 | bytes 5000000 | tf_op jit(solution)/shard_map/combine/pallas_call | solution.py:621
  159.3 5.5 %all-to-all-start.4 = ((bf16[16,64,128]{2,1,0:T(8,128)(2,1)}), bf16[16,64,128]{2,1,0:T(8,128)(2,1)S(1)}, u32[]{:S(2)}, u32[]{:S(2)}) async-start(bf16[16,64,128]{2,1,0:T(8,128)(2,1)} %get-tuple-element.69), calls=%async_computation.4 | async-start | bytes 524288 | tf_op jit(solution)/shard_map/all_to_all | solution.py:903
  167.4 8.9 %all-to-all-done.4.refs_3_ = bf16[16,64,128]{2,1,0:T(8,128)(2,1)S(1)} async-done(((bf16[16,64,128]{2,1,0:T(8,128)(2,1)}), bf16[16,64,128]{2,1,0:T(8,128)(2,1)S(1)}, u32[]{:S(2)}, u32[]{:S(2)}) %all-to-all-start.4) | async-done | bytes 262176 | tf_op jit(solution)/shard_map/all_to_all | solution.py:903
  177.0 4.7 %all-to-all-start.5 = ((bf16[16,64,768]{2,1,0:T(8,128)(2,1)}), bf16[16,64,768]{2,1,0:T(8,128)(2,1)S(1)}, u32[]{:S(2)}, u32[]{:S(2)}) async-start(bf16[16,64,768]{2,1,0:T(8,128)(2,1)} %out_grad.1), calls=%async_computation.5 | async-start | bytes 3145728 | tf_op jit(solution)/shard_map/all_to_all | solution.py:904
  182.3 13.9 %attend_back.1 = (bf16[16,192,128]{2,1,0:T(8,128)(2,1)}, f32[16,128]{1,0:T(8,128)}) custom-call(s32[1]{0:T(128)} %bitcast.4.refs_0_, f32[12,32]{1,0:T(8,128)} %refs_1_.4, bf16[16,192,128]{2,1,0:T(8,128)(2,1)} %copy-done.11, bf16[16,64,128]{2,1,0:T(8,128)(2,1)} %copy-done.16, f32[16,64,128]{2,1,0:T(8,128)} %get-tuple-element.70.refs_4_, ...), custom_call_target="tpu_custom_call" | custom-call | flops 14000000000 | bytes 4000000 | tf_op jit(solution)/shard_map/attend_back/pallas_call | solution.py:296
  196.2 14.6 %all-to-all-done.5.sums_ref = bf16[16,64,768]{2,1,0:T(8,128)(2,1)S(1)} async-done(((bf16[16,64,768]{2,1,0:T(8,128)(2,1)}), bf16[16,64,768]{2,1,0:T(8,128)(2,1)S(1)}, u32[]{:S(2)}, u32[]{:S(2)}) %all-to-all-start.5) | async-done | bytes 1572896 | tf_op jit(solution)/shard_map/all_to_all | solution.py:904
  211.9 4.5 %all-to-all-start.6 = ((bf16[16,192,128]{2,1,0:T(8,128)(2,1)}), bf16[16,192,128]{2,1,0:T(8,128)(2,1)S(1)}, u32[]{:S(2)}, u32[]{:S(2)}) async-start(bf16[16,192,128]{2,1,0:T(8,128)(2,1)} %get-tuple-element.72.dqkv_ref), calls=%async_computation.6 | async-start | bytes 1572864 | tf_op jit(solution)/shard_map/all_to_all | solution.py:907
  217.1 5.1 %head_grads.1 = bf16[8,208,128]{2,1,0:T(8,128)(2,1)} custom-call(s32[4]{0:T(128)} %pad_add_fusion.place_ref.refs_0_, bf16[16,192,128]{2,1,0:T(8,128)(2,1)} %get-tuple-element.72.dqkv_ref, bf16[4,2,128,768]{3,2,1,0:T(8,128)(2,1)} %copy-done.4, bf16[4,2,128,768]{3,2,1,0:T(8,128)(2,1)} %collective-permute-done.4.other_ref, ...), custom_call_target="tpu_custom_call" | custom-call | flops 3000000000 | bytes 8000000 | tf_op jit(solution)/shard_map/head_grads/pallas_call | solution.py:368
  222.1 8.8 %all-to-all-done.6.grads_ref = bf16[16,192,128]{2,1,0:T(8,128)(2,1)S(1)} async-done(((bf16[16,192,128]{2,1,0:T(8,128)(2,1)}), bf16[16,192,128]{2,1,0:T(8,128)(2,1)S(1)}, u32[]{:S(2)}, u32[]{:S(2)}) %all-to-all-start.6) | async-done | bytes 786464 | tf_op jit(solution)/shard_map/all_to_all | solution.py:907
  231.0 13.9 %all_to_all.40.in_ref = bf16[8,208,128]{2,1,0:T(8,128)(2,1)} all-to-all(bf16[8,208,128]{2,1,0:T(8,128)(2,1)} %head_grads.1), channel_id=1, replica_groups=mesh['context'=16,'expert'=8] {'expert'}, dimensions={0} | all-to-all | bytes 851968 | tf_op jit(solution)/shard_map/all_to_all | solution.py:910
  262.3 4.5 %collective-permute-done.8 = bf16[4,208,128]{2,1,0:T(8,128)(2,1)S(1)} collective-permute-done((bf16[4,208,128]{2,1,0:T(8,128)(2,1)S(1)}, bf16[4,208,128]{2,1,0:T(8,128)(2,1)S(1)}, u32[]{:S(2)}, u32[]{:S(2)}) %collective-permute-start.8) | collective-permute-done | bytes 213024 | tf_op jit(solution)/shard_map/ppermute | solution.py:700
  270.7 4.6 %input_grad.1 = f32[128,768]{1,0:T(8,128)} custom-call(bf16[128,768]{1,0:T(8,128)(2,1)} %bitcast.46, f32[768]{0:T(1024)} %gain_ref.5, bf16[16,192,128]{2,1,0:T(8,128)(2,1)} %copy-done.1, bf16[768,768]{1,0:T(8,128)(2,1)} %refs_1_.5, bf16[768,768]{1,0:T(8,128)(2,1)} %refs_2_.1, bf16[768,768]{1,0:T(8,128)(2,1)} %refs_3_.3, ...), custom_call_target="tpu_custom_call" | custom-call | flops 500000000 | bytes 5000000 | tf_op jit(solution)/shard_map/input_grad/pallas_call | solution.py:666
  280.2 7.4 %collective-permute-done.12.refs_6_ = bf16[4,4,208,128]{3,2,1,0:T(8,128)(2,1)S(1)} collective-permute-done((bf16[4,4,208,128]{3,2,1,0:T(8,128)(2,1)S(1)}, bf16[4,4,208,128]{3,2,1,0:T(8,128)(2,1)S(1)}, u32[]{:S(2)}, u32[]{:S(2)}) %collective-permute-start.12) | collective-permute-done | bytes 852000 | tf_op jit(solution)/shard_map/ppermute | solution.py:707
  287.8 2.7 collective-permute-start.13
  290.5 3.6 %collective-permute-start.16 = (bf16[4,4,208,128]{3,2,1,0:T(8,128)(2,1)S(1)}, bf16[4,4,208,128]{3,2,1,0:T(8,128)(2,1)S(1)}, u32[]{:S(2)}, u32[]{:S(2)}) collective-permute-start(bf16[4,4,208,128]{3,2,1,0:T(8,128)(2,1)S(1)} %collective-permute-done.11.refs_5_), channel_id=1, source_target_pairs={{0,8},{1,9},{2,10},{3,11},{4,12},{5,13},{6,14},{7,15},{8,0},{9,1},... | collective-permute-start | bytes 2555912 | tf_op jit(solution)/shard_map/ppermute | solution.py:714
  294.1 3.1 collective-permute-done.14.refs_8_
  297.2 4.0 %collective-permute-start.19 = (bf16[2,4,208,128]{3,2,1,0:T(8,128)(2,1)S(1)}, bf16[2,4,208,128]{3,2,1,0:T(8,128)(2,1)S(1)}, u32[]{:S(2)}, u32[]{:S(2)}) collective-permute-start(bf16[2,4,208,128]{3,2,1,0:T(8,128)(2,1)S(1)} %collective-permute-done.14.refs_8_), channel_id=1, source_target_pairs={{0,8},{1,9},{2,10},{3,11},{4,12},{5,13},{6,14},{7,15},{8,0},{9,1},... | collective-permute-start | bytes 1277960 | tf_op jit(solution)/shard_map/ppermute | solution.py:714
  305.2 11.6 %unpack.1 = (f32[768,768]{1,0:T(8,128)}, f32[768,768]{1,0:T(8,128)}, f32[768,768]{1,0:T(8,128)}, f32[12,8,8,768]{3,2,1,0:T(8,128)}, f32[12,32]{1,0:T(8,128)}, /*...) custom-call(s32[4]{0:T(128)} %pad_add_fusion.place_ref.refs_0_, bf16[768,768]{1,0:T(8,128)(2,1)} %refs_1_.5, ...), custom_call_target="tpu_custom_call" | custom-call | flops 1000000000 | bytes 24000000 | tf_op jit(solution)/shard_map/unpack/pallas_call | solution.py:803
  (98 shorter events, 49.3 us)
Async XLA Ops:
  7.2 103.5 %all-gather.3.cloned.1.call-start = ((), (), s32[]{:S(2)}) async-start(), calls=%async_computation.10 | async-start | bytes 10027008 | tf_op jit(solution)/shard_map/all_gather | solution.py:878
  12.9 28.9 %all-to-all-start = ((bf16[16,192,128]{2,1,0:T(8,128)(2,1)}), bf16[16,192,128]{2,1,0:T(8,128)(2,1)S(1)}, u32[]{:S(2)}, u32[]{:S(2)}) async-start(bf16[16,192,128]{2,1,0:T(8,128)(2,1)} %get-tuple-element.54), calls=%async_computation | async-start | bytes 1572864 | tf_op jit(solution)/shard_map/all_to_all | solution.py:880
  49.7 15.6 %all-to-all-start.1 = ((bf16[16,64,128]{2,1,0:T(8,128)(2,1)}), bf16[16,64,128]{2,1,0:T(8,128)(2,1)S(1)}, u32[]{:S(2)}, u32[]{:S(2)}) async-start(bf16[16,64,128]{2,1,0:T(8,128)(2,1)} %get-tuple-element.57), calls=%async_computation.1 | async-start | bytes 524288 | tf_op jit(solution)/shard_map/all_to_all | solution.py:887
  69.9 33.6 %all-to-all-start.2 = ((bf16[8,96,768]{2,1,0:T(8,128)(2,1)}), bf16[8,96,768]{2,1,0:T(8,128)(2,1)S(1)}, u32[]{:S(2)}, u32[]{:S(2)}) async-start(bf16[8,96,768]{2,1,0:T(8,128)(2,1)} %get-tuple-element.58), calls=%async_computation.2 | async-start | bytes 2359296 | tf_op jit(solution)/shard_map/all_to_all | solution.py:891
  75.7 202.3 %reduce-scatter.2.cloned.1.call-start = ((), (), s32[]{:S(2)}) async-start(), calls=%async_computation.9 | async-start | bytes 10027008 | tf_op jit(solution)/shard_map/reduce_scatter | solution.py:898
  75.7 27.7 %collective-permute-start = (bf16[128,768]{1,0:T(8,128)(2,1)S(1)}, bf16[128,768]{1,0:T(8,128)(2,1)S(1)}, u32[]{:S(2)}, u32[]{:S(2)}) collective-permute-start(bf16[128,768]{1,0:T(8,128)(2,1)S(1)} %copy-done.17), channel_id=1, source_target_pairs={{0,64},{1,65},{2,66},{3,67},{4,68},{5,69},{6,70},{7,71},{8,72},{9,... | collective-permute-start | bytes 589832 | tf_op jit(solution)/shard_map/ppermute | solution.py:884
  128.6 25.0 %all-to-all-start.3 = ((bf16[8,96,768]{2,1,0:T(8,128)(2,1)}), bf16[8,96,768]{2,1,0:T(8,128)(2,1)S(1)}, u32[]{:S(2)}, u32[]{:S(2)}) async-start(bf16[8,96,768]{2,1,0:T(8,128)(2,1)} %get-tuple-element.62), calls=%async_computation.3 | async-start | bytes 2359296 | tf_op jit(solution)/shard_map/all_to_all | solution.py:895
  133.1 11.7 %collective-permute-start.3 = (bf16[2,128,768]{2,1,0:T(8,128)(2,1)S(1)}, bf16[2,128,768]{2,1,0:T(8,128)(2,1)S(1)}, u32[]{:S(2)}, u32[]{:S(2)}) collective-permute-start(bf16[2,128,768]{2,1,0:T(8,128)(2,1)S(1)} %pad_maximum_fusion.3), channel_id=1, source_target_pairs={{0,16},{1,17},{2,18},{3,19},{4,20},{5,21},{6,22},{7,23},{8,24},{9,... | collective-permute-start | bytes 1179656 | tf_op jit(solution)/shard_map/ppermute | solution.py:700
  133.6 19.0 %collective-permute-start.2 = (bf16[2,128,768]{2,1,0:T(8,128)(2,1)S(1)}, bf16[2,128,768]{2,1,0:T(8,128)(2,1)S(1)}, u32[]{:S(2)}, u32[]{:S(2)}) collective-permute-start(bf16[2,128,768]{2,1,0:T(8,128)(2,1)S(1)} %pad_maximum_fusion.3), channel_id=1, source_target_pairs={{0,32},{1,33},{2,34},{3,35},{4,36},{5,37},{6,38},{7,39},{8,40},{9,... | collective-permute-start | bytes 1179656 | tf_op jit(solution)/shard_map/ppermute | solution.py:700
  135.4 17.9 %collective-permute-start.1 = (bf16[2,128,768]{2,1,0:T(8,128)(2,1)S(1)}, bf16[2,128,768]{2,1,0:T(8,128)(2,1)S(1)}, u32[]{:S(2)}, u32[]{:S(2)}) collective-permute-start(bf16[2,128,768]{2,1,0:T(8,128)(2,1)S(1)} %pad_maximum_fusion.3), channel_id=1, source_target_pairs={{0,48},{1,49},{2,50},{3,51},{4,52},{5,53},{6,54},{7,55},{8,56},{9,... | collective-permute-start | bytes 1179656 | tf_op jit(solution)/shard_map/ppermute | solution.py:700
  153.5 28.2 %copy-start.4 = (bf16[4,2,128,768]{3,2,1,0:T(8,128)(2,1)}, bf16[4,2,128,768]{3,2,1,0:T(8,128)(2,1)S(1)}, u32[]{:S(2)}) copy-start(bf16[4,2,128,768]{3,2,1,0:T(8,128)(2,1)S(1)} %pad_maximum_fusion.mine_ref) | copy-start | bytes 4718596
  159.3 17.0 %all-to-all-start.4 = ((bf16[16,64,128]{2,1,0:T(8,128)(2,1)}), bf16[16,64,128]{2,1,0:T(8,128)(2,1)S(1)}, u32[]{:S(2)}, u32[]{:S(2)}) async-start(bf16[16,64,128]{2,1,0:T(8,128)(2,1)} %get-tuple-element.69), calls=%async_computation.4 | async-start | bytes 524288 | tf_op jit(solution)/shard_map/all_to_all | solution.py:903
  177.0 33.8 %all-to-all-start.5 = ((bf16[16,64,768]{2,1,0:T(8,128)(2,1)}), bf16[16,64,768]{2,1,0:T(8,128)(2,1)S(1)}, u32[]{:S(2)}, u32[]{:S(2)}) async-start(bf16[16,64,768]{2,1,0:T(8,128)(2,1)} %out_grad.1), calls=%async_computation.5 | async-start | bytes 3145728 | tf_op jit(solution)/shard_map/all_to_all | solution.py:904
  181.7 35.3 %collective-permute-start.4 = (bf16[4,2,128,768]{3,2,1,0:T(8,128)(2,1)S(1)}, bf16[4,2,128,768]{3,2,1,0:T(8,128)(2,1)}, u32[]{:S(2)}, u32[]{:S(2)}) collective-permute-start(bf16[4,2,128,768]{3,2,1,0:T(8,128)(2,1)S(1)} %pad_maximum_fusion.mine_ref), channel_id=1, source_target_pairs={{0,8},{1,9},{2,10},{3,11},{4,12},{5,13},{6,14},{7,15},{8,0},{9,1},... | collective-permute-start | bytes 4718600 | tf_op jit(solution)/shard_map/ppermute | solution.py:897
  211.9 19.0 %all-to-all-start.6 = ((bf16[16,192,128]{2,1,0:T(8,128)(2,1)}), bf16[16,192,128]{2,1,0:T(8,128)(2,1)S(1)}, u32[]{:S(2)}, u32[]{:S(2)}) async-start(bf16[16,192,128]{2,1,0:T(8,128)(2,1)} %get-tuple-element.72.dqkv_ref), calls=%async_computation.6 | async-start | bytes 1572864 | tf_op jit(solution)/shard_map/all_to_all | solution.py:907
  231.0 37.0 %copy-start.1 = (bf16[16,192,128]{2,1,0:T(8,128)(2,1)}, bf16[16,192,128]{2,1,0:T(8,128)(2,1)S(1)}, u32[]{:S(2)}) copy-start(bf16[16,192,128]{2,1,0:T(8,128)(2,1)S(1)} %all-to-all-done.6.grads_ref) | copy-start | bytes 2359300
  246.5 6.4 %collective-permute-start.7 = (bf16[208,128]{1,0:T(8,128)(2,1)}, bf16[208,128]{1,0:T(8,128)(2,1)S(1)}, u32[]{:S(2)}, u32[]{:S(2)}) collective-permute-start(bf16[208,128]{1,0:T(8,128)(2,1)} %add_up.1), channel_id=1, source_target_pairs={{0,16},{1,17},{2,18},{3,19},{4,20},{5,21},{6,22},{7,23},{8,24},{9,... | collective-permute-start | bytes 159752 | tf_op jit(solution)/shard_map/ppermute | solution.py:700
  249.2 5.5 %collective-permute-start.6 = (bf16[208,128]{1,0:T(8,128)(2,1)}, bf16[208,128]{1,0:T(8,128)(2,1)S(1)}, u32[]{:S(2)}, u32[]{:S(2)}) collective-permute-start(bf16[208,128]{1,0:T(8,128)(2,1)} %add_up.1), channel_id=1, source_target_pairs={{0,32},{1,33},{2,34},{3,35},{4,36},{5,37},{6,38},{7,39},{8,40},{9,... | collective-permute-start | bytes 159752 | tf_op jit(solution)/shard_map/ppermute | solution.py:700
  251.7 3.5 %collective-permute-start.5 = (bf16[208,128]{1,0:T(8,128)(2,1)}, bf16[208,128]{1,0:T(8,128)(2,1)S(1)}, u32[]{:S(2)}, u32[]{:S(2)}) collective-permute-start(bf16[208,128]{1,0:T(8,128)(2,1)} %add_up.1), channel_id=1, source_target_pairs={{0,48},{1,49},{2,50},{3,51},{4,52},{5,53},{6,54},{7,55},{8,56},{9,... | collective-permute-start | bytes 159752 | tf_op jit(solution)/shard_map/ppermute | solution.py:700
  256.0 6.3 %collective-permute-start.9 = (bf16[4,208,128]{2,1,0:T(8,128)(2,1)S(1)}, bf16[4,208,128]{2,1,0:T(8,128)(2,1)S(1)}, u32[]{:S(2)}, u32[]{:S(2)}) collective-permute-start(bf16[4,208,128]{2,1,0:T(8,128)(2,1)S(1)} %get-tuple-element.97), channel_id=1, source_target_pairs={{0,64},{1,65},{2,66},{3,67},{4,68},{5,69},{6,70},{7,71},{8,72},{9,... | collective-permute-start | bytes 638984 | tf_op jit(solution)/shard_map/ppermute | solution.py:700
  258.5 8.3 %collective-permute-start.8 = (bf16[4,208,128]{2,1,0:T(8,128)(2,1)S(1)}, bf16[4,208,128]{2,1,0:T(8,128)(2,1)S(1)}, u32[]{:S(2)}, u32[]{:S(2)}) collective-permute-start(bf16[4,208,128]{2,1,0:T(8,128)(2,1)S(1)} %get-tuple-element.97), channel_id=1, source_target_pairs={{0,65},{1,0},{2,67},{3,2},{4,69},{5,4},{6,71},{7,6},{8,73},{9,8},{... | collective-permute-start | bytes 638984 | tf_op jit(solution)/shard_map/ppermute | solution.py:700
  258.8 9.0 %collective-permute-start.10 = (bf16[4,208,128]{2,1,0:T(8,128)(2,1)S(1)}, bf16[4,208,128]{2,1,0:T(8,128)(2,1)S(1)}, u32[]{:S(2)}, u32[]{:S(2)}) collective-permute-start(bf16[4,208,128]{2,1,0:T(8,128)(2,1)S(1)} %get-tuple-element.97), channel_id=1, source_target_pairs={{0,1},{1,64},{2,3},{3,66},{4,5},{5,68},{6,7},{7,70},{8,9},{9,72},{... | collective-permute-start | bytes 638984 | tf_op jit(solution)/shard_map/ppermute | solution.py:700
  268.0 19.6 %collective-permute-start.12 = (bf16[4,4,208,128]{3,2,1,0:T(8,128)(2,1)S(1)}, bf16[4,4,208,128]{3,2,1,0:T(8,128)(2,1)S(1)}, u32[]{:S(2)}, u32[]{:S(2)}) collective-permute-start(bf16[4,4,208,128]{3,2,1,0:T(8,128)(2,1)S(1)} %pad_maximum_fusion.1.refs_4_), channel_id=1, source_target_pairs={{0,2},{1,3},{2,4},{3,5},{4,6},{5,7},{6,0},{7,1},{8,10},{9,11},{10,... | collective-permute-start | bytes 2555912 | tf_op jit(solution)/shard_map/ppermute | solution.py:707
  268.4 19.2 %collective-permute-start.11 = (bf16[4,4,208,128]{3,2,1,0:T(8,128)(2,1)S(1)}, bf16[4,4,208,128]{3,2,1,0:T(8,128)(2,1)S(1)}, u32[]{:S(2)}, u32[]{:S(2)}) collective-permute-start(bf16[4,4,208,128]{3,2,1,0:T(8,128)(2,1)S(1)} %pad_maximum_fusion.1.refs_4_), channel_id=1, source_target_pairs={{0,6},{1,7},{2,0},{3,1},{4,2},{5,3},{6,4},{7,5},{8,14},{9,15},{10,... | collective-permute-start | bytes 2555912 | tf_op jit(solution)/shard_map/ppermute | solution.py:706
  275.3 25.9 %collective-permute-start.15 = (bf16[4,4,208,128]{3,2,1,0:T(8,128)(2,1)S(1)}, bf16[4,4,208,128]{3,2,1,0:T(8,128)(2,1)}, u32[]{:S(2)}, u32[]{:S(2)}) collective-permute-start(bf16[4,4,208,128]{3,2,1,0:T(8,128)(2,1)S(1)} %pad_maximum_fusion.1.refs_4_), channel_id=1, source_target_pairs={{0,8},{1,9},{2,10},{3,11},{4,12},{5,13},{6,14},{7,15},{8,0},{9,1},... | collective-permute-start | bytes 2555912 | tf_op jit(solution)/shard_map/ppermute | solution.py:714
  287.6 9.6 %collective-permute-start.14 = (bf16[2,4,208,128]{3,2,1,0:T(8,128)(2,1)S(1)}, bf16[2,4,208,128]{3,2,1,0:T(8,128)(2,1)S(1)}, u32[]{:S(2)}, u32[]{:S(2)}) collective-permute-start(bf16[2,4,208,128]{3,2,1,0:T(8,128)(2,1)S(1)} %slice.29), channel_id=1, source_target_pairs={{0,2},{1,3},{2,4},{3,5},{4,6},{5,7},{6,0},{7,1},{8,10},{9,11},{10,... | collective-permute-start | bytes 1277960 | tf_op jit(solution)/shard_map/ppermute | solution.py:711
  287.8 29.9 %copy-start.18 = (f32[768]{0:T(1024)S(1)}, f32[768]{0:T(1024)}, u32[]{:S(2)}) copy-start(f32[768]{0:T(1024)} %gain_ref.5) | copy-start | bytes 9220
  287.8 13.4 %collective-permute-start.13 = (bf16[2,4,208,128]{3,2,1,0:T(8,128)(2,1)S(1)}, bf16[2,4,208,128]{3,2,1,0:T(8,128)(2,1)S(1)}, u32[]{:S(2)}, u32[]{:S(2)}) collective-permute-start(bf16[2,4,208,128]{3,2,1,0:T(8,128)(2,1)S(1)} %slice.28), channel_id=1, source_target_pairs={{0,6},{1,7},{2,0},{3,1},{4,2},{5,3},{6,4},{7,5},{8,14},{9,15},{10,... | collective-permute-start | bytes 1277960 | tf_op jit(solution)/shard_map/ppermute | solution.py:710
  290.5 12.7 %collective-permute-start.16 = (bf16[4,4,208,128]{3,2,1,0:T(8,128)(2,1)S(1)}, bf16[4,4,208,128]{3,2,1,0:T(8,128)(2,1)S(1)}, u32[]{:S(2)}, u32[]{:S(2)}) collective-permute-start(bf16[4,4,208,128]{3,2,1,0:T(8,128)(2,1)S(1)} %collective-permute-done.11.refs_5_), channel_id=1, source_target_pairs={{0,8},{1,9},{2,10},{3,11},{4,12},{5,13},{6,14},{7,15},{8,0},{9,1},... | collective-permute-start | bytes 2555912 | tf_op jit(solution)/shard_map/ppermute | solution.py:714
  294.1 9.1 %collective-permute-start.17 = (bf16[4,4,208,128]{3,2,1,0:T(8,128)(2,1)S(1)}, bf16[4,4,208,128]{3,2,1,0:T(8,128)(2,1)S(1)}, u32[]{:S(2)}, u32[]{:S(2)}) collective-permute-start(bf16[4,4,208,128]{3,2,1,0:T(8,128)(2,1)S(1)} %collective-permute-done.12.refs_6_), channel_id=1, source_target_pairs={{0,8},{1,9},{2,10},{3,11},{4,12},{5,13},{6,14},{7,15},{8,0},{9,1},... | collective-permute-start | bytes 2555912 | tf_op jit(solution)/shard_map/ppermute | solution.py:714
  297.2 5.4 %collective-permute-start.19 = (bf16[2,4,208,128]{3,2,1,0:T(8,128)(2,1)S(1)}, bf16[2,4,208,128]{3,2,1,0:T(8,128)(2,1)S(1)}, u32[]{:S(2)}, u32[]{:S(2)}) collective-permute-start(bf16[2,4,208,128]{3,2,1,0:T(8,128)(2,1)S(1)} %collective-permute-done.14.refs_8_), channel_id=1, source_target_pairs={{0,8},{1,9},{2,10},{3,11},{4,12},{5,13},{6,14},{7,15},{8,0},{9,1},... | collective-permute-start | bytes 1277960 | tf_op jit(solution)/shard_map/ppermute | solution.py:714
  301.2 2.0 collective-permute-start.18
  (18 other events, 92.7 us)
Sparse Core Ops, SparseCore 0:
  11.1 99.5 all-gather.2
  128.7 123.8 reduce-scatter.1

commit v5 on v4

--- a/solution.py
+++ b/solution.py
@@ -341,7 +341,7 @@
             third = third + dot(two, part, TN)[rows]
     pairs, third = pairs.T, third.T
     total = sums_ref[0].astype(F32)
-    for c in range(1, count):
+    for c in range(1, sums_ref.shape[0]):
         total = total + sums_ref[c].astype(F32)
     shares = out_ref.shape[0]
     each = width // shares
@@ -590,28 +590,33 @@
     small_ref[...] = jnp.concatenate([grad_router, jnp.broadcast_to(grad_gain, (8, width))], axis=0)
 
 
-def out_grad_kernel(att_ref, grad_mixed_ref, small_ref, sums_ref):
+def out_grad_kernel(place_ref, att_ref, grad_mixed_ref, small_ref, keep_ref, pass_ref, all_s):
     grad_wo = dot(att_ref[...], grad_mixed_ref[...].astype(BF16), TN).astype(BF16)
-    slots, each, width = sums_ref.shape
+    slots, each, width = all_s.shape
     used = width // each
     for c in range(used):
-        sums_ref[c] = grad_wo[each * c : each * c + each]
+        all_s[c] = grad_wo[each * c : each * c + each]
     for c in range(used, slots):
-        sums_ref[c] = jnp.zeros_like(sums_ref[c])
-    sums_ref[used, :16, :] = small_ref[...].astype(BF16)
-
-
-def out_grad(attended, grad_mixed, small):
+        all_s[c] = jnp.zeros_like(all_s[c])
+    all_s[used, :16, :] = small_ref[...].astype(BF16)
+    core = place_ref[3]
+    for c in range(slots // 2):
+        keep_ref[c] = all_s[2 * c + core]
+        pass_ref[c] = all_s[2 * c + 1 - core]
+
+
+def out_grad(place, attended, grad_mixed, small):
     width = attended.shape[1]
     return pl.pallas_call(
         out_grad_kernel,
         name="out_grad",
         cost_estimate=pl.CostEstimate(flops=500000000, bytes_accessed=4000000, transcendentals=0),
-        out_shape=jax.ShapeDtypeStruct((HEAD_SLOTS, 64, width), BF16),
-        in_specs=[vspec()] * 3,
-        out_specs=vspec(),
-        compiler_params=whole(),
-    )(attended, grad_mixed, small)
+        out_shape=(jax.ShapeDtypeStruct((HEAD_SLOTS // 2, 64, width), BF16),) * 2,
+        in_specs=[sspec()] + [vspec()] * 3,
+        out_specs=(vspec(),) * 2,
+        scratch_shapes=[pltpu.VMEM((HEAD_SLOTS, 64, width), BF16)],
+        compiler_params=whole(),
+    )(place, attended, grad_mixed, small)
 
 
 def combine(cotangent, back, picks, gates, mixed, second, routes, gain_two, w_router, w_out):
@@ -700,8 +705,7 @@
     return jnp.stack([block] + [lax.ppermute(block, AXES, shifted(dim, -by)) for by in (1, 2, 3)])
 
 
-def gather_all(piece, beside):
-    filled = direct_gather(direct_gather(piece, 2), 0)
+def gather_last(filled, beside):
     half = filled.shape[0] // 2
     ahead = lax.ppermute(filled, AXES, shifted(1, -1))
     behind = lax.ppermute(filled, AXES, shifted(1, 1))
@@ -764,15 +768,18 @@
     bias = []
     for j in range(width // 128):
         cols = slice(128 * j, 128 * j + 128)
-        one, two = all_s[rel(2 * j)].astype(F32), all_s[rel(2 * j + 1)].astype(F32)
-        dwq_ref[:, cols] = jnp.concatenate([one[:each, :64], two[:each, :64]], axis=1)
-        dwk_ref[:, cols] = jnp.concatenate([one[:each, 64:], two[:each, 64:]], axis=1)
-        dwv_ref[:half, cols] = jnp.concatenate([one[each:at, :64], two[each:at, :64]], axis=1)
-        dwv_ref[half:, cols] = jnp.concatenate([one[each:at, 64:], two[each:at, 64:]], axis=1)
-        bias += [one[at : at + 1], two[at : at + 1]]
+        one, two = all_s[rel(2 * j)], all_s[rel(2 * j + 1)]
+        left = jnp.concatenate([one[:at, :64], two[:at, :64]], axis=1).astype(F32)
+        right = jnp.concatenate([one[:at, 64:], two[:at, 64:]], axis=1).astype(F32)
+        dwq_ref[:, cols] = left[:each]
+        dwk_ref[:, cols] = right[:each]
+        dwv_ref[:half, cols] = left[each:]
+        dwv_ref[half:, cols] = right[each:]
+        one, two = one[at:].astype(F32), two[at:].astype(F32)
+        bias += [one[:1], two[:1]]
         for i, block in enumerate((one, two)):
             for k in range(width // 128):
-                dwo_ref[2 * j + i, :, 128 * k : 128 * k + 128] = block[at + 16 + 8 * k : at + 24 + 8 * k]
+                dwo_ref[2 * j + i, :, 128 * k : 128 * k + 128] = block[16 + 8 * k : 24 + 8 * k]
     bias_ref[...] = jnp.concatenate(bias, axis=0)[:, :buckets]
     block = all_s[rel(width // 64)].astype(F32)
     small = jnp.concatenate(
@@ -899,21 +906,27 @@
     block_out, grad_mixed, grad_heads, small = combine(
         grad_out, returned, picks, gates, mixed, second, routes_here, gain_two, w_router, w_out
     )
-    sums = out_grad(attended, grad_mixed, small)
+    keep_sums, pass_sums = out_grad(place, attended, grad_mixed, small)
+    other_sums = lax.ppermute(pass_sums, AXES, shifted(3, 1))
+    sums = (keep_sums.astype(F32) + other_sums.astype(F32)).astype(BF16)
     grad_here = lax.all_to_all(grad_heads, "context", split_axis=0, concat_axis=0, tiled=True)
-    sums = lax.all_to_all(sums, "context", split_axis=0, concat_axis=0, tiled=True)
+    same_core = [[2 * i + core for i in range(8)] for core in range(2)]
+    sums, grad_here = lax.optimization_barrier((sums, grad_here))
+    sums = lax.all_to_all(
+        sums, "context", split_axis=0, concat_axis=0, axis_index_groups=same_core, tiled=True
+    )
 
     dqkv, bias = attend_back(head, rel_table, qkv, grad_here, keep, lse)
+    terms = head_grads(place, dqkv, normed_mine, normed_other, bias, sums, experts)
+    terms = lax.all_to_all(terms, "expert", split_axis=0, concat_axis=0, tiled=True)
+    filled, dqkv = lax.optimization_barrier((direct_gather(direct_gather(add_up(terms), 2), 0), dqkv))
     grads = lax.all_to_all(dqkv, "context", split_axis=0, concat_axis=0, tiled=True)
-    terms = head_grads(place, dqkv, normed_mine, normed_other, bias, sums, experts)
-    terms, grads = lax.optimization_barrier((terms, grads))
-    terms = lax.all_to_all(terms, "expert", split_axis=0, concat_axis=0, tiled=True)
-    grad_tokens = input_grad(inputs, gain_one, grads, w_query, w_key, w_value, grad_mixed)
     own_grads = own_grads.astype(F32)
     hidden = own_grads.shape[0] // 2
-    parts, (grad_tokens, grad_in, grad_back) = gather_all(
-        add_up(terms), (grad_tokens, own_grads[:hidden], own_grads[hidden:])
-    )
+    parts, (grads, grad_in, grad_back) = gather_last(
+        filled, (grads, own_grads[:hidden], own_grads[hidden:])
+    )
+    grad_tokens = input_grad(inputs, gain_one, grads, w_query, w_key, w_value, grad_mixed)
 
     dwq, dwk, dwv, dwo, bias, small, router, gain_grad = unpack(
         place, parts, w_query, w_key, w_value, heads, buckets, experts

time: 328 us -> 313 us (0.954)
  waiting for transfers between devices: 135 us -> 120 us
  other arithmetic: 5.43 us -> 8.79 us
    all_to_all x1, waiting for transfers between devices: 14.6 us -> 2.06 us  [shards(): lax.all_to_all(sums, 'context', split_axis=0, concat_axis=0, axis_index_g...]
    all_to_all x1, starting transfers between devices: 4.53 us -> 11.5 us  [shards(): lax.all_to_all(dqkv, 'context', split_axis=0, concat_axis=0, tiled=True)]
    ppermute x9 -> x10, starting transfers between devices: 15.9 us -> 10.6 us  [the longest x5 3.48 us: gather_last(): other = tuple((lax.ppermute(part, AXES, shifted(3, 1)) for part in mine))]
    ppermute x9 -> x10, waiting for transfers between devices: 12.4 us -> 7.48 us  [the longest x1 7.46 us: gather_last(): lax.ppermute(behind[half:], AXES, shifted(1, 1))]
    unnamed x44 -> x48, local copies, waits for them, and re-layouts: 8.04 us -> 7.97 us
  transfers between devices with their start and end apart: 29 -> 30, of which waited for: 19 -> 16; matrix products, arithmetic and copies ran while one was open for 2% -> 3% of each run, Pallas kernels for 14% -> 15%
where the time goes in v5:
time: 313 us; the launch traced here: 312 us
  waiting for transfers between devices  120 us (38%)
  Pallas kernels  76.8 us (25%)
  starting transfers between devices  67.5 us (22%)
  between operations  14.3 us (5%)
  blocking collectives  12.9 us (4%)
  local copies, waits for them, and re-layouts  11.3 us (4%)
  other arithmetic  8.79 us (3%)
    ppermute x1, waiting for transfers between devices, shards(): normed_two = jnp.stack([normed, lax.ppermute(normed, AXES, shifted(0, 2))])  27.6 us
    ppermute x9, waiting for transfers between devices, direct_gather(): lax.ppermute(block, AXES, shifted(dim, -by))  26.3 us
    all_to_all x1, waiting for transfers between devices, shards(): lax.all_to_all(packed, 'context', split_axis=0, concat_axis=0, tiled=True)  19.6 us
    pallas_call x1, Pallas kernels, expert_both(): pl.pallas_call(expert_kernel, name='expert_both', cost_estimate=pl.CostEs...  17.9 us
    pallas_call x1, Pallas kernels, attend_back(): pl.pallas_call(lambda *refs: attend_back_kernel(rel_table.shape[1], *refs...  14 us
    all_to_all x1, blocking collectives, shards(): lax.all_to_all(terms, 'expert', split_axis=0, concat_axis=0, tiled=True)  12.9 us
    ppermute x9, starting transfers between devices, direct_gather(): lax.ppermute(block, AXES, shifted(dim, -by))  12.6 us
    all_to_all x1, waiting for transfers between devices, shards(): lax.all_to_all(dqkv, 'context', split_axis=0, concat_axis=0, tiled=True)  12 us
  transfers between devices with their start and end apart: 30, of which 16 were waited for; matrix products, arithmetic and copies ran while one was open for 3% of the time, Pallas kernels for 15%

profile of v5, /device:TPU:1, one launch (start us, length us, event | category | flops | bytes accessed | tf_op | source)
XLA Modules:
  0.0 311.9 jit_solution(209253169418711011)
XLA Ops:
  9.2 3.7 %project.1 = (bf16[128,768]{1,0:T(8,128)(2,1)}, bf16[16,192,128]{2,1,0:T(8,128)(2,1)}) custom-call(bf16[128,768]{1,0:T(8,128)(2,1)} %bitcast.44, f32[768]{0:T(1024)} %gain_ref.5, bf16[768,768]{1,0:T(8,128)(2,1)} %refs_1_.5, bf16[768,768]{1,0:T(8,128)(2,1)} %refs_2_.1, bf16[768,768]{1,0:T(8,128)(2,1)} %refs_3_.3), custom_call_target="tpu_custom_call" | custom-call | flops 500000000 | bytes 6000000 | tf_op jit(solution)/shard_map/project/pallas_call | solution.py:82
  12.9 9.3 %all-to-all-start = ((bf16[16,192,128]{2,1,0:T(8,128)(2,1)}), bf16[16,192,128]{2,1,0:T(8,128)(2,1)S(1)}, u32[]{:S(2)}, u32[]{:S(2)}) async-start(bf16[16,192,128]{2,1,0:T(8,128)(2,1)} %get-tuple-element.58), calls=%async_computation | async-start | bytes 1572864 | tf_op jit(solution)/shard_map/all_to_all | solution.py:887
  22.2 19.6 %all-to-all-done.refs_2_ = bf16[16,192,128]{2,1,0:T(8,128)(2,1)S(1)} async-done(((bf16[16,192,128]{2,1,0:T(8,128)(2,1)}), bf16[16,192,128]{2,1,0:T(8,128)(2,1)S(1)}, u32[]{:S(2)}, u32[]{:S(2)}) %all-to-all-start) | async-done | bytes 786464 | tf_op jit(solution)/shard_map/all_to_all | solution.py:887
  42.6 7.0 %attend.1 = (bf16[16,64,128]{2,1,0:T(8,128)(2,1)}, f32[16,64,128]{2,1,0:T(8,128)}, f32[8,8,256]{2,1,0:T(8,128)}) custom-call(s32[1]{0:T(128)} %bitcast.4.refs_0_, f32[12,32]{1,0:T(8,128)} %refs_1_.4, bf16[16,192,128]{2,1,0:T(8,128)(2,1)} %copy-done.10), custom_call_target="tpu_custom_call" | custom-call | flops 7000000000 | bytes 3000000 | tf_op jit(solution)/shard_map/attend/pallas_call | solution.py:171
  49.7 5.2 %all-to-all-start.1 = ((bf16[16,64,128]{2,1,0:T(8,128)(2,1)}), bf16[16,64,128]{2,1,0:T(8,128)(2,1)S(1)}, u32[]{:S(2)}, u32[]{:S(2)}) async-start(bf16[16,64,128]{2,1,0:T(8,128)(2,1)} %get-tuple-element.61), calls=%async_computation.1 | async-start | bytes 524288 | tf_op jit(solution)/shard_map/all_to_all | solution.py:894
  56.4 8.8 %all-to-all-done.1.refs_2_ = bf16[16,64,128]{2,1,0:T(8,128)(2,1)S(1)} async-done(((bf16[16,64,128]{2,1,0:T(8,128)(2,1)}), bf16[16,64,128]{2,1,0:T(8,128)(2,1)S(1)}, u32[]{:S(2)}, u32[]{:S(2)}) %all-to-all-start.1) | async-done | bytes 262176 | tf_op jit(solution)/shard_map/all_to_all | solution.py:894
  65.9 3.9 %dispatch.1 = (bf16[8,96,768]{2,1,0:T(8,128)(2,1)}, bf16[128,768]{1,0:T(8,128)(2,1)}, f32[128,768]{1,0:T(8,128)}, bf16[128,768]{1,0:T(8,128)(2,1)}, bf16[2,128,384]{2,1,0:T(8,128)(2,1)}, /*index=5*/f32[128,128]{1,0:T(8,128)}) custom-call(bf16[128,768]{1,0:T(8,128)(2,1)} %bitcast.45, bf16[128,768]{1,0:T(8,128)(2,1)} %bitcast.62, ...), custom_call_target="tpu_custom_call" | custom-call | flops 500000000 | bytes 4000000 | tf_op jit(solution)/shard_map/dispatch/pallas_call | solution.py:447
  69.9 5.8 %all-to-all-start.2 = ((bf16[8,96,768]{2,1,0:T(8,128)(2,1)}), bf16[8,96,768]{2,1,0:T(8,128)(2,1)S(1)}, u32[]{:S(2)}, u32[]{:S(2)}) async-start(bf16[8,96,768]{2,1,0:T(8,128)(2,1)} %get-tuple-element.62), calls=%async_computation.2 | async-start | bytes 2359296 | tf_op jit(solution)/shard_map/all_to_all | solution.py:898
  75.8 27.6 %collective-permute-done = bf16[128,768]{1,0:T(8,128)(2,1)S(1)} collective-permute-done((bf16[128,768]{1,0:T(8,128)(2,1)S(1)}, bf16[128,768]{1,0:T(8,128)(2,1)S(1)}, u32[]{:S(2)}, u32[]{:S(2)}) %collective-permute-start) | collective-permute-done | bytes 196640 | tf_op jit(solution)/shard_map/ppermute | solution.py:891
  103.5 7.2 %all-gather.3.cloned.1.call-done = bf16[6144,768]{1,0:T(8,128)(2,1)} async-done(((bf16[384,768]{1,0:T(8,128)(2,1)}), bf16[6144,768]{1,0:T(8,128)(2,1)}) %all-gather.3.cloned.1.call-update) | async-done | bytes 9437200 | tf_op jit(solution)/shard_map/all_gather | solution.py:885
  110.7 17.9 %expert_both.1 = (bf16[8,96,768]{2,1,0:T(8,128)(2,1)}, bf16[16,384,768]{2,1,0:T(8,128)(2,1)}) custom-call(bf16[8,96,768]{2,1,0:T(8,128)(2,1)} %copy-done.6, bf16[16,384,768]{2,1,0:T(8,128)(2,1)} %bitcast.69), custom_call_target="tpu_custom_call" | custom-call | flops 17999998976 | bytes 22000000 | tf_op jit(solution)/shard_map/expert_both/pallas_call | solution.py:509
  128.6 4.5 %all-to-all-start.3 = ((bf16[8,96,768]{2,1,0:T(8,128)(2,1)}), bf16[8,96,768]{2,1,0:T(8,128)(2,1)S(1)}, u32[]{:S(2)}, u32[]{:S(2)}) async-start(bf16[8,96,768]{2,1,0:T(8,128)(2,1)} %get-tuple-element.66), calls=%async_computation.3 | async-start | bytes 2359296 | tf_op jit(solution)/shard_map/all_to_all | solution.py:902
  136.9 7.8 %collective-permute-done.3 = bf16[2,128,768]{2,1,0:T(8,128)(2,1)S(1)} collective-permute-done((bf16[2,128,768]{2,1,0:T(8,128)(2,1)S(1)}, bf16[2,128,768]{2,1,0:T(8,128)(2,1)S(1)}, u32[]{:S(2)}, u32[]{:S(2)}) %collective-permute-start.3) | collective-permute-done | bytes 393248 | tf_op jit(solution)/shard_map/ppermute | solution.py:705
  144.8 7.8 %collective-permute-done.2 = bf16[2,128,768]{2,1,0:T(8,128)(2,1)S(1)} collective-permute-done((bf16[2,128,768]{2,1,0:T(8,128)(2,1)S(1)}, bf16[2,128,768]{2,1,0:T(8,128)(2,1)S(1)}, u32[]{:S(2)}, u32[]{:S(2)}) %collective-permute-start.2) | collective-permute-done | bytes 393248 | tf_op jit(solution)/shard_map/ppermute | solution.py:705
  156.5 4.7 %combine.1 = (bf16[128,768]{1,0:T(8,128)(2,1)}, f32[128,768]{1,0:T(8,128)}, bf16[16,64,128]{2,1,0:T(8,128)(2,1)}, f32[16,768]{1,0:T(8,128)}) custom-call(bf16[128,768]{1,0:T(8,128)(2,1)} %bitcast.63, bf16[8,96,768]{2,1,0:T(8,128)(2,1)} %copy-done.5, bf16[2,128,384]{2,1,0:T(8,128)(2,1)} %get-tuple-element.68.pick_ref, ...), custom_call_target="tpu_custom_call" | custom-call | flops 1000000000 | bytes 5000000 | tf_op jit(solution)/shard_map/combine/pallas_call | solution.py:626
  161.1 2.7 out_grad.1
  165.4 4.0 %all-to-all-start.4 = ((bf16[16,64,128]{2,1,0:T(8,128)(2,1)}), bf16[16,64,128]{2,1,0:T(8,128)(2,1)S(1)}, u32[]{:S(2)}, u32[]{:S(2)}) async-start(bf16[16,64,128]{2,1,0:T(8,128)(2,1)} %get-tuple-element.78), calls=%async_computation.4 | async-start | bytes 524288 | tf_op jit(solution)/shard_map/all_to_all | solution.py:912
  171.8 9.2 %all-to-all-done.4.refs_3_ = bf16[16,64,128]{2,1,0:T(8,128)(2,1)S(1)} async-done(((bf16[16,64,128]{2,1,0:T(8,128)(2,1)}), bf16[16,64,128]{2,1,0:T(8,128)(2,1)S(1)}, u32[]{:S(2)}, u32[]{:S(2)}) %all-to-all-start.4) | async-done | bytes 262176 | tf_op jit(solution)/shard_map/all_to_all | solution.py:912
  181.0 3.8 %all-to-all-start.5 = ((bf16[8,64,768]{2,1,0:T(8,128)(2,1)}), bf16[8,64,768]{2,1,0:T(8,128)(2,1)S(1)}, u32[]{:S(2)}, u32[]{:S(2)}) async-start(bf16[8,64,768]{2,1,0:T(8,128)(2,1)} %add_convert_fusion), calls=%async_computation.5 | async-start | bytes 1572864 | tf_op jit(solution)/shard_map/all_to_all | solution.py:915
  184.8 14.0 %attend_back.1 = (bf16[16,192,128]{2,1,0:T(8,128)(2,1)}, f32[16,128]{1,0:T(8,128)}) custom-call(s32[1]{0:T(128)} %bitcast.4.refs_0_, f32[12,32]{1,0:T(8,128)} %refs_1_.4, bf16[16,192,128]{2,1,0:T(8,128)(2,1)} %copy-done.10, bf16[16,64,128]{2,1,0:T(8,128)(2,1)} %copy-done.18, f32[16,64,128]{2,1,0:T(8,128)} %get-tuple-element.80.refs_4_, ...), custom_call_target="tpu_custom_call" | custom-call | flops 14000000000 | bytes 4000000 | tf_op jit(solution)/shard_map/attend_back/pallas_call | solution.py:296
  201.8 4.8 %head_grads.1 = bf16[8,208,128]{2,1,0:T(8,128)(2,1)} custom-call(s32[4]{0:T(128)} %pad_add_fusion.place_ref.refs_0_, bf16[16,192,128]{2,1,0:T(8,128)(2,1)} %get-tuple-element.87.dqkv_ref, bf16[4,2,128,768]{3,2,1,0:T(8,128)(2,1)} %copy-done.4, bf16[4,2,128,768]{3,2,1,0:T(8,128)(2,1)} %collective-permute-done.5.other_ref, ...), custom_call_target="tpu_custom_call" | custom-call | flops 3000000000 | bytes 8000000 | tf_op jit(solution)/shard_map/head_grads/pallas_call | solution.py:368
  206.6 12.9 %all_to_all.40.in_ref = bf16[8,208,128]{2,1,0:T(8,128)(2,1)} all-to-all(bf16[8,208,128]{2,1,0:T(8,128)(2,1)} %head_grads.1), channel_id=1, replica_groups=mesh['context'=16,'expert'=8] {'expert'}, dimensions={0} | all-to-all | bytes 851968 | tf_op jit(solution)/shard_map/all_to_all | solution.py:921
  223.3 3.6 %collective-permute-start.7 = (bf16[208,128]{1,0:T(8,128)(2,1)}, bf16[208,128]{1,0:T(8,128)(2,1)S(1)}, u32[]{:S(2)}, u32[]{:S(2)}) collective-permute-start(bf16[208,128]{1,0:T(8,128)(2,1)} %add_up.1), channel_id=1, source_target_pairs={{0,32},{1,33},{2,34},{3,35},{4,36},{5,37},{6,38},{7,39},{8,40},{9,... | collective-permute-start | bytes 159752 | tf_op jit(solution)/shard_map/ppermute | solution.py:705
  232.4 2.6 collective-permute-start.9
  235.1 3.2 %collective-permute-done.10 = bf16[4,208,128]{2,1,0:T(8,128)(2,1)S(1)} collective-permute-done((bf16[4,208,128]{2,1,0:T(8,128)(2,1)S(1)}, bf16[4,208,128]{2,1,0:T(8,128)(2,1)S(1)}, u32[]{:S(2)}, u32[]{:S(2)}) %collective-permute-start.10) | collective-permute-done | bytes 213024 | tf_op jit(solution)/shard_map/ppermute | solution.py:705
  238.6 2.8 collective-permute-done.11
  244.3 11.5 %all-to-all-start.7 = ((bf16[16,192,128]{2,1,0:T(8,128)(2,1)}), bf16[16,192,128]{2,1,0:T(8,128)(2,1)S(1)}, u32[]{:S(2)}, u32[]{:S(2)}) async-start(bf16[16,192,128]{2,1,0:T(8,128)(2,1)} %get-tuple-element.87.dqkv_ref), calls=%async_computation.7 | async-start | bytes 1572864 | tf_op jit(solution)/shard_map/all_to_all | solution.py:923
  258.1 12.0 %all-to-all-done.7.grads_ref = bf16[16,192,128]{2,1,0:T(8,128)(2,1)S(1)} async-done(((bf16[16,192,128]{2,1,0:T(8,128)(2,1)}), bf16[16,192,128]{2,1,0:T(8,128)(2,1)S(1)}, u32[]{:S(2)}, u32[]{:S(2)}) %all-to-all-start.7) | async-done | bytes 786464 | tf_op jit(solution)/shard_map/all_to_all | solution.py:923
  270.3 2.7 collective-permute-start.14
  274.5 7.5 %collective-permute-done.15.refs_8_ = bf16[2,4,208,128]{3,2,1,0:T(8,128)(2,1)S(1)} collective-permute-done((bf16[2,4,208,128]{3,2,1,0:T(8,128)(2,1)S(1)}, bf16[2,4,208,128]{3,2,1,0:T(8,128)(2,1)S(1)}, u32[]{:S(2)}, u32[]{:S(2)}) %collective-permute-start.15) | collective-permute-done | bytes 426016 | tf_op jit(solution)/shard_map/ppermute | solution.py:715
  283.8 4.7 %input_grad.1 = f32[128,768]{1,0:T(8,128)} custom-call(bf16[128,768]{1,0:T(8,128)(2,1)} %bitcast.46, f32[768]{0:T(1024)} %gain_ref.5, bf16[16,192,128]{2,1,0:T(8,128)(2,1)} %copy-done.1, bf16[768,768]{1,0:T(8,128)(2,1)} %refs_1_.5, bf16[768,768]{1,0:T(8,128)(2,1)} %refs_2_.1, bf16[768,768]{1,0:T(8,128)(2,1)} %refs_3_.3, ...), custom_call_target="tpu_custom_call" | custom-call | flops 500000000 | bytes 5000000 | tf_op jit(solution)/shard_map/input_grad/pallas_call | solution.py:671
  290.7 11.6 %unpack.1 = (f32[768,768]{1,0:T(8,128)}, f32[768,768]{1,0:T(8,128)}, f32[768,768]{1,0:T(8,128)}, f32[12,8,8,768]{3,2,1,0:T(8,128)}, f32[12,32]{1,0:T(8,128)}, /*...) custom-call(s32[4]{0:T(128)} %pad_add_fusion.place_ref.refs_0_, bf16[768,768]{1,0:T(8,128)(2,1)} %refs_1_.5, ...), custom_call_target="tpu_custom_call" | custom-call | flops 1000000000 | bytes 24000000 | tf_op jit(solution)/shard_map/unpack/pallas_call | solution.py:810
  (105 shorter events, 43.2 us)
Async XLA Ops:
  7.2 103.5 %all-gather.3.cloned.1.call-start = ((), (), s32[]{:S(2)}) async-start(), calls=%async_computation.10 | async-start | bytes 10027008 | tf_op jit(solution)/shard_map/all_gather | solution.py:885
  12.9 28.9 %all-to-all-start = ((bf16[16,192,128]{2,1,0:T(8,128)(2,1)}), bf16[16,192,128]{2,1,0:T(8,128)(2,1)S(1)}, u32[]{:S(2)}, u32[]{:S(2)}) async-start(bf16[16,192,128]{2,1,0:T(8,128)(2,1)} %get-tuple-element.58), calls=%async_computation | async-start | bytes 1572864 | tf_op jit(solution)/shard_map/all_to_all | solution.py:887
  49.7 15.6 %all-to-all-start.1 = ((bf16[16,64,128]{2,1,0:T(8,128)(2,1)}), bf16[16,64,128]{2,1,0:T(8,128)(2,1)S(1)}, u32[]{:S(2)}, u32[]{:S(2)}) async-start(bf16[16,64,128]{2,1,0:T(8,128)(2,1)} %get-tuple-element.61), calls=%async_computation.1 | async-start | bytes 524288 | tf_op jit(solution)/shard_map/all_to_all | solution.py:894
  69.9 33.6 %all-to-all-start.2 = ((bf16[8,96,768]{2,1,0:T(8,128)(2,1)}), bf16[8,96,768]{2,1,0:T(8,128)(2,1)S(1)}, u32[]{:S(2)}, u32[]{:S(2)}) async-start(bf16[8,96,768]{2,1,0:T(8,128)(2,1)} %get-tuple-element.62), calls=%async_computation.2 | async-start | bytes 2359296 | tf_op jit(solution)/shard_map/all_to_all | solution.py:898
  75.7 180.2 %reduce-scatter.2.cloned.1.call-start = ((), (), s32[]{:S(2)}) async-start(), calls=%async_computation.9 | async-start | bytes 10027008 | tf_op jit(solution)/shard_map/reduce_scatter | solution.py:905
  75.7 27.7 %collective-permute-start = (bf16[128,768]{1,0:T(8,128)(2,1)S(1)}, bf16[128,768]{1,0:T(8,128)(2,1)S(1)}, u32[]{:S(2)}, u32[]{:S(2)}) collective-permute-start(bf16[128,768]{1,0:T(8,128)(2,1)S(1)} %copy-done.19), channel_id=1, source_target_pairs={{0,64},{1,65},{2,66},{3,67},{4,68},{5,69},{6,70},{7,71},{8,72},{9,... | collective-permute-start | bytes 589832 | tf_op jit(solution)/shard_map/ppermute | solution.py:891
  128.6 26.8 %all-to-all-start.3 = ((bf16[8,96,768]{2,1,0:T(8,128)(2,1)}), bf16[8,96,768]{2,1,0:T(8,128)(2,1)S(1)}, u32[]{:S(2)}, u32[]{:S(2)}) async-start(bf16[8,96,768]{2,1,0:T(8,128)(2,1)} %get-tuple-element.66), calls=%async_computation.3 | async-start | bytes 2359296 | tf_op jit(solution)/shard_map/all_to_all | solution.py:902
  133.1 11.7 %collective-permute-start.3 = (bf16[2,128,768]{2,1,0:T(8,128)(2,1)S(1)}, bf16[2,128,768]{2,1,0:T(8,128)(2,1)S(1)}, u32[]{:S(2)}, u32[]{:S(2)}) collective-permute-start(bf16[2,128,768]{2,1,0:T(8,128)(2,1)S(1)} %pad_maximum_fusion.3), channel_id=1, source_target_pairs={{0,16},{1,17},{2,18},{3,19},{4,20},{5,21},{6,22},{7,23},{8,24},{9,... | collective-permute-start | bytes 1179656 | tf_op jit(solution)/shard_map/ppermute | solution.py:705
  133.6 19.0 %collective-permute-start.2 = (bf16[2,128,768]{2,1,0:T(8,128)(2,1)S(1)}, bf16[2,128,768]{2,1,0:T(8,128)(2,1)S(1)}, u32[]{:S(2)}, u32[]{:S(2)}) collective-permute-start(bf16[2,128,768]{2,1,0:T(8,128)(2,1)S(1)} %pad_maximum_fusion.3), channel_id=1, source_target_pairs={{0,32},{1,33},{2,34},{3,35},{4,36},{5,37},{6,38},{7,39},{8,40},{9,... | collective-permute-start | bytes 1179656 | tf_op jit(solution)/shard_map/ppermute | solution.py:705
  135.4 17.9 %collective-permute-start.1 = (bf16[2,128,768]{2,1,0:T(8,128)(2,1)S(1)}, bf16[2,128,768]{2,1,0:T(8,128)(2,1)S(1)}, u32[]{:S(2)}, u32[]{:S(2)}) collective-permute-start(bf16[2,128,768]{2,1,0:T(8,128)(2,1)S(1)} %pad_maximum_fusion.3), channel_id=1, source_target_pairs={{0,48},{1,49},{2,50},{3,51},{4,52},{5,53},{6,54},{7,55},{8,56},{9,... | collective-permute-start | bytes 1179656 | tf_op jit(solution)/shard_map/ppermute | solution.py:705
  163.9 5.8 %collective-permute-start.4 = (bf16[8,64,768]{2,1,0:T(8,128)(2,1)}, bf16[8,64,768]{2,1,0:T(8,128)(2,1)S(1)}, u32[]{:S(2)}, u32[]{:S(2)}) collective-permute-start(bf16[8,64,768]{2,1,0:T(8,128)(2,1)} %get-tuple-element.77), channel_id=1, source_target_pairs={{0,8},{1,9},{2,10},{3,11},{4,12},{5,13},{6,14},{7,15},{8,0},{9,1},... | collective-permute-start | bytes 2359304 | tf_op jit(solution)/shard_map/ppermute | solution.py:910
  165.4 15.6 %all-to-all-start.4 = ((bf16[16,64,128]{2,1,0:T(8,128)(2,1)}), bf16[16,64,128]{2,1,0:T(8,128)(2,1)S(1)}, u32[]{:S(2)}, u32[]{:S(2)}) async-start(bf16[16,64,128]{2,1,0:T(8,128)(2,1)} %get-tuple-element.78), calls=%async_computation.4 | async-start | bytes 524288 | tf_op jit(solution)/shard_map/all_to_all | solution.py:912
  169.5 31.4 %collective-permute-start.5 = (bf16[4,2,128,768]{3,2,1,0:T(8,128)(2,1)S(1)}, bf16[4,2,128,768]{3,2,1,0:T(8,128)(2,1)}, u32[]{:S(2)}, u32[]{:S(2)}) collective-permute-start(bf16[4,2,128,768]{3,2,1,0:T(8,128)(2,1)S(1)} %pad_maximum_fusion.mine_ref), channel_id=1, source_target_pairs={{0,8},{1,9},{2,10},{3,11},{4,12},{5,13},{6,14},{7,15},{8,0},{9,1},... | collective-permute-start | bytes 4718600 | tf_op jit(solution)/shard_map/ppermute | solution.py:904
  181.0 19.9 %all-to-all-start.5 = ((bf16[8,64,768]{2,1,0:T(8,128)(2,1)}), bf16[8,64,768]{2,1,0:T(8,128)(2,1)S(1)}, u32[]{:S(2)}, u32[]{:S(2)}) async-start(bf16[8,64,768]{2,1,0:T(8,128)(2,1)} %add_convert_fusion), calls=%async_computation.5 | async-start | bytes 1572864 | tf_op jit(solution)/shard_map/all_to_all | solution.py:915
  221.2 7.5 %collective-permute-start.8 = (bf16[208,128]{1,0:T(8,128)(2,1)}, bf16[208,128]{1,0:T(8,128)(2,1)S(1)}, u32[]{:S(2)}, u32[]{:S(2)}) collective-permute-start(bf16[208,128]{1,0:T(8,128)(2,1)} %add_up.1), channel_id=1, source_target_pairs={{0,16},{1,17},{2,18},{3,19},{4,20},{5,21},{6,22},{7,23},{8,24},{9,... | collective-permute-start | bytes 159752 | tf_op jit(solution)/shard_map/ppermute | solution.py:705
  223.3 7.8 %collective-permute-start.7 = (bf16[208,128]{1,0:T(8,128)(2,1)}, bf16[208,128]{1,0:T(8,128)(2,1)S(1)}, u32[]{:S(2)}, u32[]{:S(2)}) collective-permute-start(bf16[208,128]{1,0:T(8,128)(2,1)} %add_up.1), channel_id=1, source_target_pairs={{0,32},{1,33},{2,34},{3,35},{4,36},{5,37},{6,38},{7,39},{8,40},{9,... | collective-permute-start | bytes 159752 | tf_op jit(solution)/shard_map/ppermute | solution.py:705
  227.0 4.2 %collective-permute-start.6 = (bf16[208,128]{1,0:T(8,128)(2,1)}, bf16[208,128]{1,0:T(8,128)(2,1)S(1)}, u32[]{:S(2)}, u32[]{:S(2)}) collective-permute-start(bf16[208,128]{1,0:T(8,128)(2,1)} %add_up.1), channel_id=1, source_target_pairs={{0,48},{1,49},{2,50},{3,51},{4,52},{5,53},{6,54},{7,55},{8,56},{9,... | collective-permute-start | bytes 159752 | tf_op jit(solution)/shard_map/ppermute | solution.py:705
  232.0 6.3 %collective-permute-start.10 = (bf16[4,208,128]{2,1,0:T(8,128)(2,1)S(1)}, bf16[4,208,128]{2,1,0:T(8,128)(2,1)S(1)}, u32[]{:S(2)}, u32[]{:S(2)}) collective-permute-start(bf16[4,208,128]{2,1,0:T(8,128)(2,1)S(1)} %get-tuple-element.105), channel_id=1, source_target_pairs={{0,64},{1,65},{2,66},{3,67},{4,68},{5,69},{6,70},{7,71},{8,72},{9,... | collective-permute-start | bytes 638984 | tf_op jit(solution)/shard_map/ppermute | solution.py:705
  232.4 6.2 %collective-permute-start.9 = (bf16[4,208,128]{2,1,0:T(8,128)(2,1)S(1)}, bf16[4,208,128]{2,1,0:T(8,128)(2,1)S(1)}, u32[]{:S(2)}, u32[]{:S(2)}) collective-permute-start(bf16[4,208,128]{2,1,0:T(8,128)(2,1)S(1)} %get-tuple-element.105), channel_id=1, source_target_pairs={{0,65},{1,0},{2,67},{3,2},{4,69},{5,4},{6,71},{7,6},{8,73},{9,8},{... | collective-permute-start | bytes 638984 | tf_op jit(solution)/shard_map/ppermute | solution.py:705
  235.1 6.3 %collective-permute-start.11 = (bf16[4,208,128]{2,1,0:T(8,128)(2,1)S(1)}, bf16[4,208,128]{2,1,0:T(8,128)(2,1)S(1)}, u32[]{:S(2)}, u32[]{:S(2)}) collective-permute-start(bf16[4,208,128]{2,1,0:T(8,128)(2,1)S(1)} %get-tuple-element.105), channel_id=1, source_target_pairs={{0,1},{1,64},{2,3},{3,66},{4,5},{5,68},{6,7},{7,70},{8,9},{9,72},{... | collective-permute-start | bytes 638984 | tf_op jit(solution)/shard_map/ppermute | solution.py:705
  241.5 28.6 %collective-permute-start.13 = (bf16[4,4,208,128]{3,2,1,0:T(8,128)(2,1)S(1)}, bf16[4,4,208,128]{3,2,1,0:T(8,128)(2,1)S(1)}, u32[]{:S(2)}, u32[]{:S(2)}) collective-permute-start(bf16[4,4,208,128]{3,2,1,0:T(8,128)(2,1)S(1)} %pad_maximum_fusion.1.refs_4_), channel_id=1, source_target_pairs={{0,2},{1,3},{2,4},{3,5},{4,6},{5,7},{6,0},{7,1},{8,10},{9,11},{10,... | collective-permute-start | bytes 2555912 | tf_op jit(solution)/shard_map/ppermute | solution.py:711
  242.1 28.0 %collective-permute-start.12 = (bf16[4,4,208,128]{3,2,1,0:T(8,128)(2,1)S(1)}, bf16[4,4,208,128]{3,2,1,0:T(8,128)(2,1)S(1)}, u32[]{:S(2)}, u32[]{:S(2)}) collective-permute-start(bf16[4,4,208,128]{3,2,1,0:T(8,128)(2,1)S(1)} %pad_maximum_fusion.1.refs_4_), channel_id=1, source_target_pairs={{0,6},{1,7},{2,0},{3,1},{4,2},{5,3},{6,4},{7,5},{8,14},{9,15},{10,... | collective-permute-start | bytes 2555912 | tf_op jit(solution)/shard_map/ppermute | solution.py:710
  244.3 25.9 %all-to-all-start.7 = ((bf16[16,192,128]{2,1,0:T(8,128)(2,1)}), bf16[16,192,128]{2,1,0:T(8,128)(2,1)S(1)}, u32[]{:S(2)}, u32[]{:S(2)}) async-start(bf16[16,192,128]{2,1,0:T(8,128)(2,1)} %get-tuple-element.87.dqkv_ref), calls=%async_computation.7 | async-start | bytes 1572864 | tf_op jit(solution)/shard_map/all_to_all | solution.py:923
  255.7 32.8 %collective-permute-start.16 = (bf16[4,4,208,128]{3,2,1,0:T(8,128)(2,1)S(1)}, bf16[4,4,208,128]{3,2,1,0:T(8,128)(2,1)}, u32[]{:S(2)}, u32[]{:S(2)}) collective-permute-start(bf16[4,4,208,128]{3,2,1,0:T(8,128)(2,1)S(1)} %pad_maximum_fusion.1.refs_4_), channel_id=1, source_target_pairs={{0,8},{1,9},{2,10},{3,11},{4,12},{5,13},{6,14},{7,15},{8,0},{9,1},... | collective-permute-start | bytes 2555912 | tf_op jit(solution)/shard_map/ppermute | solution.py:718
  270.1 18.3 %copy-start.2 = (bf16[4,4,208,128]{3,2,1,0:T(8,128)(2,1)}, bf16[4,4,208,128]{3,2,1,0:T(8,128)(2,1)S(1)}, u32[]{:S(2)}) copy-start(bf16[4,4,208,128]{3,2,1,0:T(8,128)(2,1)S(1)} %collective-permute-done.13.refs_6_) | copy-start | bytes 2555908
  270.1 18.3 %copy-start.3 = (bf16[4,4,208,128]{3,2,1,0:T(8,128)(2,1)}, bf16[4,4,208,128]{3,2,1,0:T(8,128)(2,1)S(1)}, u32[]{:S(2)}) copy-start(bf16[4,4,208,128]{3,2,1,0:T(8,128)(2,1)S(1)} %collective-permute-done.12.refs_5_) | copy-start | bytes 2555908
  270.2 11.7 %collective-permute-start.15 = (bf16[2,4,208,128]{3,2,1,0:T(8,128)(2,1)S(1)}, bf16[2,4,208,128]{3,2,1,0:T(8,128)(2,1)S(1)}, u32[]{:S(2)}, u32[]{:S(2)}) collective-permute-start(bf16[2,4,208,128]{3,2,1,0:T(8,128)(2,1)S(1)} %slice.29), channel_id=1, source_target_pairs={{0,2},{1,3},{2,4},{3,5},{4,6},{5,7},{6,0},{7,1},{8,10},{9,11},{10,... | collective-permute-start | bytes 1277960 | tf_op jit(solution)/shard_map/ppermute | solution.py:715
  270.3 13.4 %collective-permute-start.14 = (bf16[2,4,208,128]{3,2,1,0:T(8,128)(2,1)S(1)}, bf16[2,4,208,128]{3,2,1,0:T(8,128)(2,1)S(1)}, u32[]{:S(2)}, u32[]{:S(2)}) collective-permute-start(bf16[2,4,208,128]{3,2,1,0:T(8,128)(2,1)S(1)} %slice.28), channel_id=1, source_target_pairs={{0,6},{1,7},{2,0},{3,1},{4,2},{5,3},{6,4},{7,5},{8,14},{9,15},{10,... | collective-permute-start | bytes 1277960 | tf_op jit(solution)/shard_map/ppermute | solution.py:714
  273.0 15.5 %collective-permute-start.17 = (bf16[4,4,208,128]{3,2,1,0:T(8,128)(2,1)S(1)}, bf16[4,4,208,128]{3,2,1,0:T(8,128)(2,1)S(1)}, u32[]{:S(2)}, u32[]{:S(2)}) collective-permute-start(bf16[4,4,208,128]{3,2,1,0:T(8,128)(2,1)S(1)} %collective-permute-done.12.refs_5_), channel_id=1, source_target_pairs={{0,8},{1,9},{2,10},{3,11},{4,12},{5,13},{6,14},{7,15},{8,0},{9,1},... | collective-permute-start | bytes 2555912 | tf_op jit(solution)/shard_map/ppermute | solution.py:718
  274.4 14.1 %collective-permute-start.18 = (bf16[4,4,208,128]{3,2,1,0:T(8,128)(2,1)S(1)}, bf16[4,4,208,128]{3,2,1,0:T(8,128)(2,1)S(1)}, u32[]{:S(2)}, u32[]{:S(2)}) collective-permute-start(bf16[4,4,208,128]{3,2,1,0:T(8,128)(2,1)S(1)} %collective-permute-done.13.refs_6_), channel_id=1, source_target_pairs={{0,8},{1,9},{2,10},{3,11},{4,12},{5,13},{6,14},{7,15},{8,0},{9,1},... | collective-permute-start | bytes 2555912 | tf_op jit(solution)/shard_map/ppermute | solution.py:718
  281.9 6.6 %collective-permute-start.20 = (bf16[2,4,208,128]{3,2,1,0:T(8,128)(2,1)S(1)}, bf16[2,4,208,128]{3,2,1,0:T(8,128)(2,1)S(1)}, u32[]{:S(2)}, u32[]{:S(2)}) collective-permute-start(bf16[2,4,208,128]{3,2,1,0:T(8,128)(2,1)S(1)} %collective-permute-done.15.refs_8_), channel_id=1, source_target_pairs={{0,8},{1,9},{2,10},{3,11},{4,12},{5,13},{6,14},{7,15},{8,0},{9,1},... | collective-permute-start | bytes 1277960 | tf_op jit(solution)/shard_map/ppermute | solution.py:718
  283.7 4.8 %collective-permute-start.19 = (bf16[2,4,208,128]{3,2,1,0:T(8,128)(2,1)S(1)}, bf16[2,4,208,128]{3,2,1,0:T(8,128)(2,1)S(1)}, u32[]{:S(2)}, u32[]{:S(2)}) collective-permute-start(bf16[2,4,208,128]{3,2,1,0:T(8,128)(2,1)S(1)} %collective-permute-done.14.refs_7_), channel_id=1, source_target_pairs={{0,8},{1,9},{2,10},{3,11},{4,12},{5,13},{6,14},{7,15},{8,0},{9,1},... | collective-permute-start | bytes 1277960 | tf_op jit(solution)/shard_map/ppermute | solution.py:718
  (21 other events, 120.1 us)
Sparse Core Ops, SparseCore 0:
  11.1 99.5 all-gather.2
  128.7 112.7 reduce-scatter.1

commit v6 on v5

--- a/solution.py
+++ b/solution.py
@@ -216,15 +216,21 @@
     count = qkv_ref.shape[0]
     blocks = length // BLK
     unpack_qkv(qkv_ref, q_s, k_s, v_s, False)
-    ones = jnp.ones((8, 64), F32)
     for c in range(count):
         kt_s[:, 128 * c : 128 * c + 128] = k_s[128 * c : 128 * c + 128, :].T
         two, kept = go_ref[c], keep_ref[c]
         go_s[128 * c : 128 * c + 64, :] = two[:, :64]
         go_s[128 * c + 64 : 128 * c + 128, :] = two[:, 64:]
         both = two.astype(F32) * kept
-        prod = jnp.concatenate([both[:, :64], both[:, 64:]], axis=0)
-        delta_s[:, 128 * c : 128 * c + 128] = dot(ones, prod, NT, HIGHEST)
+        turned = both.T
+        delta = jnp.concatenate(
+            [
+                jnp.sum(turned[:64], axis=0, keepdims=True),
+                jnp.sum(turned[64:], axis=0, keepdims=True),
+            ],
+            axis=1,
+        )
+        delta_s[:, 128 * c : 128 * c + 128] = jnp.broadcast_to(delta, (8, 128))
     bias_s[0] = bias_tile(table_ref, head, buckets, BLK, (BLK, BLK), 0)
     bias_s[1] = bias_tile(table_ref, head, buckets, 0, (BLK, BLK), 0)
     acc_s[...] = jnp.zeros_like(acc_s)
@@ -799,7 +805,10 @@
         + dwk_ref[...] * wk_ref[...].astype(F32)
         + dwv_ref[...] * wv_ref[...].astype(F32)
     )
-    gain_grad_ref[...] = dot(jnp.ones((8, width), F32), prod, NT, HIGHEST)
+    lanes = prod[:, :128]
+    for j in range(1, width // 128):
+        lanes = lanes + prod[:, 128 * j : 128 * j + 128]
+    gain_grad_ref[...] = jnp.broadcast_to(jnp.sum(lanes.T, axis=0, keepdims=True), (8, each))
 
 
 def unpack(place, parts, w_query, w_key, w_value, heads, buckets, experts):

time: 313 us -> 313 us (level)
  transfers between devices with their start and end apart: 30 -> 30, of which waited for: 16 -> 15; matrix products, arithmetic and copies ran while one was open for 3% -> 3% of each run, Pallas kernels for 15% -> 15%
where the time goes in v6:
time: 313 us; the launch traced here: 312 us
  waiting for transfers between devices  122 us (39%)
  Pallas kernels  75.4 us (24%)
  starting transfers between devices  67.3 us (22%)
  between operations  14.3 us (5%)
  blocking collectives  12.9 us (4%)
  local copies, waits for them, and re-layouts  11.3 us (4%)
  other arithmetic  8.79 us (3%)
    ppermute x1, waiting for transfers between devices, shards(): normed_two = jnp.stack([normed, lax.ppermute(normed, AXES, shifted(0, 2))])  27.6 us
    ppermute x9, waiting for transfers between devices, direct_gather(): lax.ppermute(block, AXES, shifted(dim, -by))  26.2 us
    all_to_all x1, waiting for transfers between devices, shards(): lax.all_to_all(packed, 'context', split_axis=0, concat_axis=0, tiled=True)  19.6 us
    pallas_call x1, Pallas kernels, expert_both(): pl.pallas_call(expert_kernel, name='expert_both', cost_estimate=pl.CostEs...  17.9 us
    all_to_all x1, blocking collectives, shards(): lax.all_to_all(terms, 'expert', split_axis=0, concat_axis=0, tiled=True)  12.9 us
    pallas_call x1, Pallas kernels, attend_back(): pl.pallas_call(lambda *refs: attend_back_kernel(rel_table.shape[1], *refs...  12.6 us
    ppermute x9, starting transfers between devices, direct_gather(): lax.ppermute(block, AXES, shifted(dim, -by))  12.3 us
    all_to_all x1, waiting for transfers between devices, shards(): lax.all_to_all(dqkv, 'context', split_axis=0, concat_axis=0, tiled=True)  12 us
  transfers between devices with their start and end apart: 30, of which 15 were waited for; matrix products, arithmetic and copies ran while one was open for 3% of the time, Pallas kernels for 15%

profile of v6, /device:TPU:1, one launch (start us, length us, event | category | flops | bytes accessed | tf_op | source)
XLA Modules:
  0.0 311.6 jit_solution(4539304356436171994)
XLA Ops:
  9.2 3.7 %project.1 = (bf16[128,768]{1,0:T(8,128)(2,1)}, bf16[16,192,128]{2,1,0:T(8,128)(2,1)}) custom-call(bf16[128,768]{1,0:T(8,128)(2,1)} %bitcast.44, f32[768]{0:T(1024)} %gain_ref.5, bf16[768,768]{1,0:T(8,128)(2,1)} %refs_1_.5, bf16[768,768]{1,0:T(8,128)(2,1)} %refs_2_.1, bf16[768,768]{1,0:T(8,128)(2,1)} %refs_3_.3), custom_call_target="tpu_custom_call" | custom-call | flops 500000000 | bytes 6000000 | tf_op jit(solution)/shard_map/project/pallas_call | solution.py:82
  12.9 9.3 %all-to-all-start = ((bf16[16,192,128]{2,1,0:T(8,128)(2,1)}), bf16[16,192,128]{2,1,0:T(8,128)(2,1)S(1)}, u32[]{:S(2)}, u32[]{:S(2)}) async-start(bf16[16,192,128]{2,1,0:T(8,128)(2,1)} %get-tuple-element.58), calls=%async_computation | async-start | bytes 1572864 | tf_op jit(solution)/shard_map/all_to_all | solution.py:896
  22.2 19.6 %all-to-all-done.refs_2_ = bf16[16,192,128]{2,1,0:T(8,128)(2,1)S(1)} async-done(((bf16[16,192,128]{2,1,0:T(8,128)(2,1)}), bf16[16,192,128]{2,1,0:T(8,128)(2,1)S(1)}, u32[]{:S(2)}, u32[]{:S(2)}) %all-to-all-start) | async-done | bytes 786464 | tf_op jit(solution)/shard_map/all_to_all | solution.py:896
  42.6 7.0 %attend.1 = (bf16[16,64,128]{2,1,0:T(8,128)(2,1)}, f32[16,64,128]{2,1,0:T(8,128)}, f32[8,8,256]{2,1,0:T(8,128)}) custom-call(s32[1]{0:T(128)} %bitcast.4.refs_0_, f32[12,32]{1,0:T(8,128)} %refs_1_.4, bf16[16,192,128]{2,1,0:T(8,128)(2,1)} %copy-done.10), custom_call_target="tpu_custom_call" | custom-call | flops 7000000000 | bytes 3000000 | tf_op jit(solution)/shard_map/attend/pallas_call | solution.py:171
  49.7 5.2 %all-to-all-start.1 = ((bf16[16,64,128]{2,1,0:T(8,128)(2,1)}), bf16[16,64,128]{2,1,0:T(8,128)(2,1)S(1)}, u32[]{:S(2)}, u32[]{:S(2)}) async-start(bf16[16,64,128]{2,1,0:T(8,128)(2,1)} %get-tuple-element.61), calls=%async_computation.1 | async-start | bytes 524288 | tf_op jit(solution)/shard_map/all_to_all | solution.py:903
  56.4 8.8 %all-to-all-done.1.refs_2_ = bf16[16,64,128]{2,1,0:T(8,128)(2,1)S(1)} async-done(((bf16[16,64,128]{2,1,0:T(8,128)(2,1)}), bf16[16,64,128]{2,1,0:T(8,128)(2,1)S(1)}, u32[]{:S(2)}, u32[]{:S(2)}) %all-to-all-start.1) | async-done | bytes 262176 | tf_op jit(solution)/shard_map/all_to_all | solution.py:903
  65.9 3.9 %dispatch.1 = (bf16[8,96,768]{2,1,0:T(8,128)(2,1)}, bf16[128,768]{1,0:T(8,128)(2,1)}, f32[128,768]{1,0:T(8,128)}, bf16[128,768]{1,0:T(8,128)(2,1)}, bf16[2,128,384]{2,1,0:T(8,128)(2,1)}, /*index=5*/f32[128,128]{1,0:T(8,128)}) custom-call(bf16[128,768]{1,0:T(8,128)(2,1)} %bitcast.45, bf16[128,768]{1,0:T(8,128)(2,1)} %bitcast.62, ...), custom_call_target="tpu_custom_call" | custom-call | flops 500000000 | bytes 4000000 | tf_op jit(solution)/shard_map/dispatch/pallas_call | solution.py:453
  69.9 5.8 %all-to-all-start.2 = ((bf16[8,96,768]{2,1,0:T(8,128)(2,1)}), bf16[8,96,768]{2,1,0:T(8,128)(2,1)S(1)}, u32[]{:S(2)}, u32[]{:S(2)}) async-start(bf16[8,96,768]{2,1,0:T(8,128)(2,1)} %get-tuple-element.62), calls=%async_computation.2 | async-start | bytes 2359296 | tf_op jit(solution)/shard_map/all_to_all | solution.py:907
  75.8 27.6 %collective-permute-done = bf16[128,768]{1,0:T(8,128)(2,1)S(1)} collective-permute-done((bf16[128,768]{1,0:T(8,128)(2,1)S(1)}, bf16[128,768]{1,0:T(8,128)(2,1)S(1)}, u32[]{:S(2)}, u32[]{:S(2)}) %collective-permute-start) | collective-permute-done | bytes 196640 | tf_op jit(solution)/shard_map/ppermute | solution.py:900
  103.5 7.2 %all-gather.3.cloned.1.call-done = bf16[6144,768]{1,0:T(8,128)(2,1)} async-done(((bf16[384,768]{1,0:T(8,128)(2,1)}), bf16[6144,768]{1,0:T(8,128)(2,1)}) %all-gather.3.cloned.1.call-update) | async-done | bytes 9437200 | tf_op jit(solution)/shard_map/all_gather | solution.py:894
  110.7 17.9 %expert_both.1 = (bf16[8,96,768]{2,1,0:T(8,128)(2,1)}, bf16[16,384,768]{2,1,0:T(8,128)(2,1)}) custom-call(bf16[8,96,768]{2,1,0:T(8,128)(2,1)} %copy-done.6, bf16[16,384,768]{2,1,0:T(8,128)(2,1)} %bitcast.69), custom_call_target="tpu_custom_call" | custom-call | flops 17999998976 | bytes 22000000 | tf_op jit(solution)/shard_map/expert_both/pallas_call | solution.py:515
  128.6 4.5 %all-to-all-start.3 = ((bf16[8,96,768]{2,1,0:T(8,128)(2,1)}), bf16[8,96,768]{2,1,0:T(8,128)(2,1)S(1)}, u32[]{:S(2)}, u32[]{:S(2)}) async-start(bf16[8,96,768]{2,1,0:T(8,128)(2,1)} %get-tuple-element.66), calls=%async_computation.3 | async-start | bytes 2359296 | tf_op jit(solution)/shard_map/all_to_all | solution.py:911
  136.9 7.8 %collective-permute-done.3 = bf16[2,128,768]{2,1,0:T(8,128)(2,1)S(1)} collective-permute-done((bf16[2,128,768]{2,1,0:T(8,128)(2,1)S(1)}, bf16[2,128,768]{2,1,0:T(8,128)(2,1)S(1)}, u32[]{:S(2)}, u32[]{:S(2)}) %collective-permute-start.3) | collective-permute-done | bytes 393248 | tf_op jit(solution)/shard_map/ppermute | solution.py:711
  144.8 7.8 %collective-permute-done.2 = bf16[2,128,768]{2,1,0:T(8,128)(2,1)S(1)} collective-permute-done((bf16[2,128,768]{2,1,0:T(8,128)(2,1)S(1)}, bf16[2,128,768]{2,1,0:T(8,128)(2,1)S(1)}, u32[]{:S(2)}, u32[]{:S(2)}) %collective-permute-start.2) | collective-permute-done | bytes 393248 | tf_op jit(solution)/shard_map/ppermute | solution.py:711
  156.5 4.7 %combine.1 = (bf16[128,768]{1,0:T(8,128)(2,1)}, f32[128,768]{1,0:T(8,128)}, bf16[16,64,128]{2,1,0:T(8,128)(2,1)}, f32[16,768]{1,0:T(8,128)}) custom-call(bf16[128,768]{1,0:T(8,128)(2,1)} %bitcast.63, bf16[8,96,768]{2,1,0:T(8,128)(2,1)} %copy-done.5, bf16[2,128,384]{2,1,0:T(8,128)(2,1)} %get-tuple-element.68.pick_ref, ...), custom_call_target="tpu_custom_call" | custom-call | flops 1000000000 | bytes 5000000 | tf_op jit(solution)/shard_map/combine/pallas_call | solution.py:632
  161.1 2.7 out_grad.1
  165.4 4.0 %all-to-all-start.4 = ((bf16[16,64,128]{2,1,0:T(8,128)(2,1)}), bf16[16,64,128]{2,1,0:T(8,128)(2,1)S(1)}, u32[]{:S(2)}, u32[]{:S(2)}) async-start(bf16[16,64,128]{2,1,0:T(8,128)(2,1)} %get-tuple-element.78), calls=%async_computation.4 | async-start | bytes 524288 | tf_op jit(solution)/shard_map/all_to_all | solution.py:921
  171.8 9.2 %all-to-all-done.4.refs_3_ = bf16[16,64,128]{2,1,0:T(8,128)(2,1)S(1)} async-done(((bf16[16,64,128]{2,1,0:T(8,128)(2,1)}), bf16[16,64,128]{2,1,0:T(8,128)(2,1)S(1)}, u32[]{:S(2)}, u32[]{:S(2)}) %all-to-all-start.4) | async-done | bytes 262176 | tf_op jit(solution)/shard_map/all_to_all | solution.py:921
  181.0 3.8 %all-to-all-start.5 = ((bf16[8,64,768]{2,1,0:T(8,128)(2,1)}), bf16[8,64,768]{2,1,0:T(8,128)(2,1)S(1)}, u32[]{:S(2)}, u32[]{:S(2)}) async-start(bf16[8,64,768]{2,1,0:T(8,128)(2,1)} %add_convert_fusion), calls=%async_computation.5 | async-start | bytes 1572864 | tf_op jit(solution)/shard_map/all_to_all | solution.py:924
  184.8 12.6 %attend_back.1 = (bf16[16,192,128]{2,1,0:T(8,128)(2,1)}, f32[16,128]{1,0:T(8,128)}) custom-call(s32[1]{0:T(128)} %bitcast.4.refs_0_, f32[12,32]{1,0:T(8,128)} %refs_1_.4, bf16[16,192,128]{2,1,0:T(8,128)(2,1)} %copy-done.10, bf16[16,64,128]{2,1,0:T(8,128)(2,1)} %copy-done.18, f32[16,64,128]{2,1,0:T(8,128)} %get-tuple-element.80.refs_4_, ...), custom_call_target="tpu_custom_call" | custom-call | flops 14000000000 | bytes 4000000 | tf_op jit(solution)/shard_map/attend_back/pallas_call | solution.py:302
  197.4 3.5 %all-to-all-done.5.sums_ref = bf16[8,64,768]{2,1,0:T(8,128)(2,1)S(1)} async-done(((bf16[8,64,768]{2,1,0:T(8,128)(2,1)}), bf16[8,64,768]{2,1,0:T(8,128)(2,1)S(1)}, u32[]{:S(2)}, u32[]{:S(2)}) %all-to-all-start.5) | async-done | bytes 786464 | tf_op jit(solution)/shard_map/all_to_all | solution.py:924
  201.8 4.6 %head_grads.1 = bf16[8,208,128]{2,1,0:T(8,128)(2,1)} custom-call(s32[4]{0:T(128)} %pad_add_fusion.place_ref.refs_0_, bf16[16,192,128]{2,1,0:T(8,128)(2,1)} %get-tuple-element.87.dqkv_ref, bf16[4,2,128,768]{3,2,1,0:T(8,128)(2,1)} %copy-done.4, bf16[4,2,128,768]{3,2,1,0:T(8,128)(2,1)} %collective-permute-done.5.other_ref, ...), custom_call_target="tpu_custom_call" | custom-call | flops 3000000000 | bytes 8000000 | tf_op jit(solution)/shard_map/head_grads/pallas_call | solution.py:374
  206.3 12.9 %all_to_all.40.in_ref = bf16[8,208,128]{2,1,0:T(8,128)(2,1)} all-to-all(bf16[8,208,128]{2,1,0:T(8,128)(2,1)} %head_grads.1), channel_id=1, replica_groups=mesh['context'=16,'expert'=8] {'expert'}, dimensions={0} | all-to-all | bytes 851968 | tf_op jit(solution)/shard_map/all_to_all | solution.py:930
  223.1 3.6 %collective-permute-start.7 = (bf16[208,128]{1,0:T(8,128)(2,1)}, bf16[208,128]{1,0:T(8,128)(2,1)S(1)}, u32[]{:S(2)}, u32[]{:S(2)}) collective-permute-start(bf16[208,128]{1,0:T(8,128)(2,1)} %add_up.1), channel_id=1, source_target_pairs={{0,32},{1,33},{2,34},{3,35},{4,36},{5,37},{6,38},{7,39},{8,40},{9,... | collective-permute-start | bytes 159752 | tf_op jit(solution)/shard_map/ppermute | solution.py:711
  232.1 2.7 collective-permute-start.9
  234.8 3.5 %collective-permute-done.10 = bf16[4,208,128]{2,1,0:T(8,128)(2,1)S(1)} collective-permute-done((bf16[4,208,128]{2,1,0:T(8,128)(2,1)S(1)}, bf16[4,208,128]{2,1,0:T(8,128)(2,1)S(1)}, u32[]{:S(2)}, u32[]{:S(2)}) %collective-permute-start.10) | collective-permute-done | bytes 213024 | tf_op jit(solution)/shard_map/ppermute | solution.py:711
  243.6 11.6 %all-to-all-start.7 = ((bf16[16,192,128]{2,1,0:T(8,128)(2,1)}), bf16[16,192,128]{2,1,0:T(8,128)(2,1)S(1)}, u32[]{:S(2)}, u32[]{:S(2)}) async-start(bf16[16,192,128]{2,1,0:T(8,128)(2,1)} %get-tuple-element.87.dqkv_ref), calls=%async_computation.7 | async-start | bytes 1572864 | tf_op jit(solution)/shard_map/all_to_all | solution.py:932
  257.6 12.0 %all-to-all-done.7.grads_ref = bf16[16,192,128]{2,1,0:T(8,128)(2,1)S(1)} async-done(((bf16[16,192,128]{2,1,0:T(8,128)(2,1)}), bf16[16,192,128]{2,1,0:T(8,128)(2,1)S(1)}, u32[]{:S(2)}, u32[]{:S(2)}) %all-to-all-start.7) | async-done | bytes 786464 | tf_op jit(solution)/shard_map/all_to_all | solution.py:932
  269.8 2.7 collective-permute-start.14
  273.9 7.5 %collective-permute-done.15.refs_8_ = bf16[2,4,208,128]{3,2,1,0:T(8,128)(2,1)S(1)} collective-permute-done((bf16[2,4,208,128]{3,2,1,0:T(8,128)(2,1)S(1)}, bf16[2,4,208,128]{3,2,1,0:T(8,128)(2,1)S(1)}, u32[]{:S(2)}, u32[]{:S(2)}) %collective-permute-start.15) | collective-permute-done | bytes 426016 | tf_op jit(solution)/shard_map/ppermute | solution.py:721
  283.3 4.6 %input_grad.1 = f32[128,768]{1,0:T(8,128)} custom-call(bf16[128,768]{1,0:T(8,128)(2,1)} %bitcast.46, f32[768]{0:T(1024)} %gain_ref.5, bf16[16,192,128]{2,1,0:T(8,128)(2,1)} %copy-done.1, bf16[768,768]{1,0:T(8,128)(2,1)} %refs_1_.5, bf16[768,768]{1,0:T(8,128)(2,1)} %refs_2_.1, bf16[768,768]{1,0:T(8,128)(2,1)} %refs_3_.3, ...), custom_call_target="tpu_custom_call" | custom-call | flops 500000000 | bytes 5000000 | tf_op jit(solution)/shard_map/input_grad/pallas_call | solution.py:677
  290.1 11.9 %unpack.1 = (f32[768,768]{1,0:T(8,128)}, f32[768,768]{1,0:T(8,128)}, f32[768,768]{1,0:T(8,128)}, f32[12,8,8,768]{3,2,1,0:T(8,128)}, f32[12,32]{1,0:T(8,128)}, /*...) custom-call(s32[4]{0:T(128)} %pad_add_fusion.place_ref.refs_0_, bf16[768,768]{1,0:T(8,128)(2,1)} %refs_1_.5, ...), custom_call_target="tpu_custom_call" | custom-call | flops 1000000000 | bytes 24000000 | tf_op jit(solution)/shard_map/unpack/pallas_call | solution.py:819
  (105 shorter events, 43.2 us)
Async XLA Ops:
  7.2 103.5 %all-gather.3.cloned.1.call-start = ((), (), s32[]{:S(2)}) async-start(), calls=%async_computation.10 | async-start | bytes 10027008 | tf_op jit(solution)/shard_map/all_gather | solution.py:894
  12.9 28.9 %all-to-all-start = ((bf16[16,192,128]{2,1,0:T(8,128)(2,1)}), bf16[16,192,128]{2,1,0:T(8,128)(2,1)S(1)}, u32[]{:S(2)}, u32[]{:S(2)}) async-start(bf16[16,192,128]{2,1,0:T(8,128)(2,1)} %get-tuple-element.58), calls=%async_computation | async-start | bytes 1572864 | tf_op jit(solution)/shard_map/all_to_all | solution.py:896
  49.7 15.6 %all-to-all-start.1 = ((bf16[16,64,128]{2,1,0:T(8,128)(2,1)}), bf16[16,64,128]{2,1,0:T(8,128)(2,1)S(1)}, u32[]{:S(2)}, u32[]{:S(2)}) async-start(bf16[16,64,128]{2,1,0:T(8,128)(2,1)} %get-tuple-element.61), calls=%async_computation.1 | async-start | bytes 524288 | tf_op jit(solution)/shard_map/all_to_all | solution.py:903
  69.9 33.6 %all-to-all-start.2 = ((bf16[8,96,768]{2,1,0:T(8,128)(2,1)}), bf16[8,96,768]{2,1,0:T(8,128)(2,1)S(1)}, u32[]{:S(2)}, u32[]{:S(2)}) async-start(bf16[8,96,768]{2,1,0:T(8,128)(2,1)} %get-tuple-element.62), calls=%async_computation.2 | async-start | bytes 2359296 | tf_op jit(solution)/shard_map/all_to_all | solution.py:907
  75.7 179.7 %reduce-scatter.2.cloned.1.call-start = ((), (), s32[]{:S(2)}) async-start(), calls=%async_computation.9 | async-start | bytes 10027008 | tf_op jit(solution)/shard_map/reduce_scatter | solution.py:914
  75.7 27.7 %collective-permute-start = (bf16[128,768]{1,0:T(8,128)(2,1)S(1)}, bf16[128,768]{1,0:T(8,128)(2,1)S(1)}, u32[]{:S(2)}, u32[]{:S(2)}) collective-permute-start(bf16[128,768]{1,0:T(8,128)(2,1)S(1)} %copy-done.19), channel_id=1, source_target_pairs={{0,64},{1,65},{2,66},{3,67},{4,68},{5,69},{6,70},{7,71},{8,72},{9,... | collective-permute-start | bytes 589832 | tf_op jit(solution)/shard_map/ppermute | solution.py:900
  128.6 26.8 %all-to-all-start.3 = ((bf16[8,96,768]{2,1,0:T(8,128)(2,1)}), bf16[8,96,768]{2,1,0:T(8,128)(2,1)S(1)}, u32[]{:S(2)}, u32[]{:S(2)}) async-start(bf16[8,96,768]{2,1,0:T(8,128)(2,1)} %get-tuple-element.66), calls=%async_computation.3 | async-start | bytes 2359296 | tf_op jit(solution)/shard_map/all_to_all | solution.py:911
  133.1 11.7 %collective-permute-start.3 = (bf16[2,128,768]{2,1,0:T(8,128)(2,1)S(1)}, bf16[2,128,768]{2,1,0:T(8,128)(2,1)S(1)}, u32[]{:S(2)}, u32[]{:S(2)}) collective-permute-start(bf16[2,128,768]{2,1,0:T(8,128)(2,1)S(1)} %pad_maximum_fusion.3), channel_id=1, source_target_pairs={{0,16},{1,17},{2,18},{3,19},{4,20},{5,21},{6,22},{7,23},{8,24},{9,... | collective-permute-start | bytes 1179656 | tf_op jit(solution)/shard_map/ppermute | solution.py:711
  133.6 19.0 %collective-permute-start.2 = (bf16[2,128,768]{2,1,0:T(8,128)(2,1)S(1)}, bf16[2,128,768]{2,1,0:T(8,128)(2,1)S(1)}, u32[]{:S(2)}, u32[]{:S(2)}) collective-permute-start(bf16[2,128,768]{2,1,0:T(8,128)(2,1)S(1)} %pad_maximum_fusion.3), channel_id=1, source_target_pairs={{0,32},{1,33},{2,34},{3,35},{4,36},{5,37},{6,38},{7,39},{8,40},{9,... | collective-permute-start | bytes 1179656 | tf_op jit(solution)/shard_map/ppermute | solution.py:711
  135.4 17.9 %collective-permute-start.1 = (bf16[2,128,768]{2,1,0:T(8,128)(2,1)S(1)}, bf16[2,128,768]{2,1,0:T(8,128)(2,1)S(1)}, u32[]{:S(2)}, u32[]{:S(2)}) collective-permute-start(bf16[2,128,768]{2,1,0:T(8,128)(2,1)S(1)} %pad_maximum_fusion.3), channel_id=1, source_target_pairs={{0,48},{1,49},{2,50},{3,51},{4,52},{5,53},{6,54},{7,55},{8,56},{9,... | collective-permute-start | bytes 1179656 | tf_op jit(solution)/shard_map/ppermute | solution.py:711
  163.9 5.8 %collective-permute-start.4 = (bf16[8,64,768]{2,1,0:T(8,128)(2,1)}, bf16[8,64,768]{2,1,0:T(8,128)(2,1)S(1)}, u32[]{:S(2)}, u32[]{:S(2)}) collective-permute-start(bf16[8,64,768]{2,1,0:T(8,128)(2,1)} %get-tuple-element.77), channel_id=1, source_target_pairs={{0,8},{1,9},{2,10},{3,11},{4,12},{5,13},{6,14},{7,15},{8,0},{9,1},... | collective-permute-start | bytes 2359304 | tf_op jit(solution)/shard_map/ppermute | solution.py:919
  165.4 15.6 %all-to-all-start.4 = ((bf16[16,64,128]{2,1,0:T(8,128)(2,1)}), bf16[16,64,128]{2,1,0:T(8,128)(2,1)S(1)}, u32[]{:S(2)}, u32[]{:S(2)}) async-start(bf16[16,64,128]{2,1,0:T(8,128)(2,1)} %get-tuple-element.78), calls=%async_computation.4 | async-start | bytes 524288 | tf_op jit(solution)/shard_map/all_to_all | solution.py:921
  169.5 31.4 %collective-permute-start.5 = (bf16[4,2,128,768]{3,2,1,0:T(8,128)(2,1)S(1)}, bf16[4,2,128,768]{3,2,1,0:T(8,128)(2,1)}, u32[]{:S(2)}, u32[]{:S(2)}) collective-permute-start(bf16[4,2,128,768]{3,2,1,0:T(8,128)(2,1)S(1)} %pad_maximum_fusion.mine_ref), channel_id=1, source_target_pairs={{0,8},{1,9},{2,10},{3,11},{4,12},{5,13},{6,14},{7,15},{8,0},{9,1},... | collective-permute-start | bytes 4718600 | tf_op jit(solution)/shard_map/ppermute | solution.py:913
  181.0 19.9 %all-to-all-start.5 = ((bf16[8,64,768]{2,1,0:T(8,128)(2,1)}), bf16[8,64,768]{2,1,0:T(8,128)(2,1)S(1)}, u32[]{:S(2)}, u32[]{:S(2)}) async-start(bf16[8,64,768]{2,1,0:T(8,128)(2,1)} %add_convert_fusion), calls=%async_computation.5 | async-start | bytes 1572864 | tf_op jit(solution)/shard_map/all_to_all | solution.py:924
  220.9 7.6 %collective-permute-start.8 = (bf16[208,128]{1,0:T(8,128)(2,1)}, bf16[208,128]{1,0:T(8,128)(2,1)S(1)}, u32[]{:S(2)}, u32[]{:S(2)}) collective-permute-start(bf16[208,128]{1,0:T(8,128)(2,1)} %add_up.1), channel_id=1, source_target_pairs={{0,16},{1,17},{2,18},{3,19},{4,20},{5,21},{6,22},{7,23},{8,24},{9,... | collective-permute-start | bytes 159752 | tf_op jit(solution)/shard_map/ppermute | solution.py:711
  223.1 8.1 %collective-permute-start.7 = (bf16[208,128]{1,0:T(8,128)(2,1)}, bf16[208,128]{1,0:T(8,128)(2,1)S(1)}, u32[]{:S(2)}, u32[]{:S(2)}) collective-permute-start(bf16[208,128]{1,0:T(8,128)(2,1)} %add_up.1), channel_id=1, source_target_pairs={{0,32},{1,33},{2,34},{3,35},{4,36},{5,37},{6,38},{7,39},{8,40},{9,... | collective-permute-start | bytes 159752 | tf_op jit(solution)/shard_map/ppermute | solution.py:711
  226.7 4.4 %collective-permute-start.6 = (bf16[208,128]{1,0:T(8,128)(2,1)}, bf16[208,128]{1,0:T(8,128)(2,1)S(1)}, u32[]{:S(2)}, u32[]{:S(2)}) collective-permute-start(bf16[208,128]{1,0:T(8,128)(2,1)} %add_up.1), channel_id=1, source_target_pairs={{0,48},{1,49},{2,50},{3,51},{4,52},{5,53},{6,54},{7,55},{8,56},{9,... | collective-permute-start | bytes 159752 | tf_op jit(solution)/shard_map/ppermute | solution.py:711
  232.0 6.3 %collective-permute-start.10 = (bf16[4,208,128]{2,1,0:T(8,128)(2,1)S(1)}, bf16[4,208,128]{2,1,0:T(8,128)(2,1)S(1)}, u32[]{:S(2)}, u32[]{:S(2)}) collective-permute-start(bf16[4,208,128]{2,1,0:T(8,128)(2,1)S(1)} %get-tuple-element.105), channel_id=1, source_target_pairs={{0,64},{1,65},{2,66},{3,67},{4,68},{5,69},{6,70},{7,71},{8,72},{9,... | collective-permute-start | bytes 638984 | tf_op jit(solution)/shard_map/ppermute | solution.py:711
  232.1 6.2 %collective-permute-start.9 = (bf16[4,208,128]{2,1,0:T(8,128)(2,1)S(1)}, bf16[4,208,128]{2,1,0:T(8,128)(2,1)S(1)}, u32[]{:S(2)}, u32[]{:S(2)}) collective-permute-start(bf16[4,208,128]{2,1,0:T(8,128)(2,1)S(1)} %get-tuple-element.105), channel_id=1, source_target_pairs={{0,65},{1,0},{2,67},{3,2},{4,69},{5,4},{6,71},{7,6},{8,73},{9,8},{... | collective-permute-start | bytes 638984 | tf_op jit(solution)/shard_map/ppermute | solution.py:711
  234.8 6.0 %collective-permute-start.11 = (bf16[4,208,128]{2,1,0:T(8,128)(2,1)S(1)}, bf16[4,208,128]{2,1,0:T(8,128)(2,1)S(1)}, u32[]{:S(2)}, u32[]{:S(2)}) collective-permute-start(bf16[4,208,128]{2,1,0:T(8,128)(2,1)S(1)} %get-tuple-element.105), channel_id=1, source_target_pairs={{0,1},{1,64},{2,3},{3,66},{4,5},{5,68},{6,7},{7,70},{8,9},{9,72},{... | collective-permute-start | bytes 638984 | tf_op jit(solution)/shard_map/ppermute | solution.py:711
  240.8 28.7 %collective-permute-start.13 = (bf16[4,4,208,128]{3,2,1,0:T(8,128)(2,1)S(1)}, bf16[4,4,208,128]{3,2,1,0:T(8,128)(2,1)S(1)}, u32[]{:S(2)}, u32[]{:S(2)}) collective-permute-start(bf16[4,4,208,128]{3,2,1,0:T(8,128)(2,1)S(1)} %pad_maximum_fusion.1.refs_4_), channel_id=1, source_target_pairs={{0,2},{1,3},{2,4},{3,5},{4,6},{5,7},{6,0},{7,1},{8,10},{9,11},{10,... | collective-permute-start | bytes 2555912 | tf_op jit(solution)/shard_map/ppermute | solution.py:717
  242.1 27.5 %collective-permute-start.12 = (bf16[4,4,208,128]{3,2,1,0:T(8,128)(2,1)S(1)}, bf16[4,4,208,128]{3,2,1,0:T(8,128)(2,1)S(1)}, u32[]{:S(2)}, u32[]{:S(2)}) collective-permute-start(bf16[4,4,208,128]{3,2,1,0:T(8,128)(2,1)S(1)} %pad_maximum_fusion.1.refs_4_), channel_id=1, source_target_pairs={{0,6},{1,7},{2,0},{3,1},{4,2},{5,3},{6,4},{7,5},{8,14},{9,15},{10,... | collective-permute-start | bytes 2555912 | tf_op jit(solution)/shard_map/ppermute | solution.py:716
  243.6 26.0 %all-to-all-start.7 = ((bf16[16,192,128]{2,1,0:T(8,128)(2,1)}), bf16[16,192,128]{2,1,0:T(8,128)(2,1)S(1)}, u32[]{:S(2)}, u32[]{:S(2)}) async-start(bf16[16,192,128]{2,1,0:T(8,128)(2,1)} %get-tuple-element.87.dqkv_ref), calls=%async_computation.7 | async-start | bytes 1572864 | tf_op jit(solution)/shard_map/all_to_all | solution.py:932
  255.2 32.8 %collective-permute-start.16 = (bf16[4,4,208,128]{3,2,1,0:T(8,128)(2,1)S(1)}, bf16[4,4,208,128]{3,2,1,0:T(8,128)(2,1)}, u32[]{:S(2)}, u32[]{:S(2)}) collective-permute-start(bf16[4,4,208,128]{3,2,1,0:T(8,128)(2,1)S(1)} %pad_maximum_fusion.1.refs_4_), channel_id=1, source_target_pairs={{0,8},{1,9},{2,10},{3,11},{4,12},{5,13},{6,14},{7,15},{8,0},{9,1},... | collective-permute-start | bytes 2555912 | tf_op jit(solution)/shard_map/ppermute | solution.py:724
  269.6 18.3 %copy-start.2 = (bf16[4,4,208,128]{3,2,1,0:T(8,128)(2,1)}, bf16[4,4,208,128]{3,2,1,0:T(8,128)(2,1)S(1)}, u32[]{:S(2)}) copy-start(bf16[4,4,208,128]{3,2,1,0:T(8,128)(2,1)S(1)} %collective-permute-done.13.refs_6_) | copy-start | bytes 2555908
  269.6 18.3 %copy-start.3 = (bf16[4,4,208,128]{3,2,1,0:T(8,128)(2,1)}, bf16[4,4,208,128]{3,2,1,0:T(8,128)(2,1)S(1)}, u32[]{:S(2)}) copy-start(bf16[4,4,208,128]{3,2,1,0:T(8,128)(2,1)S(1)} %collective-permute-done.12.refs_5_) | copy-start | bytes 2555908
  269.6 11.7 %collective-permute-start.15 = (bf16[2,4,208,128]{3,2,1,0:T(8,128)(2,1)S(1)}, bf16[2,4,208,128]{3,2,1,0:T(8,128)(2,1)S(1)}, u32[]{:S(2)}, u32[]{:S(2)}) collective-permute-start(bf16[2,4,208,128]{3,2,1,0:T(8,128)(2,1)S(1)} %slice.29), channel_id=1, source_target_pairs={{0,2},{1,3},{2,4},{3,5},{4,6},{5,7},{6,0},{7,1},{8,10},{9,11},{10,... | collective-permute-start | bytes 1277960 | tf_op jit(solution)/shard_map/ppermute | solution.py:721
  269.8 13.4 %collective-permute-start.14 = (bf16[2,4,208,128]{3,2,1,0:T(8,128)(2,1)S(1)}, bf16[2,4,208,128]{3,2,1,0:T(8,128)(2,1)S(1)}, u32[]{:S(2)}, u32[]{:S(2)}) collective-permute-start(bf16[2,4,208,128]{3,2,1,0:T(8,128)(2,1)S(1)} %slice.28), channel_id=1, source_target_pairs={{0,6},{1,7},{2,0},{3,1},{4,2},{5,3},{6,4},{7,5},{8,14},{9,15},{10,... | collective-permute-start | bytes 1277960 | tf_op jit(solution)/shard_map/ppermute | solution.py:720
  272.5 15.5 %collective-permute-start.17 = (bf16[4,4,208,128]{3,2,1,0:T(8,128)(2,1)S(1)}, bf16[4,4,208,128]{3,2,1,0:T(8,128)(2,1)S(1)}, u32[]{:S(2)}, u32[]{:S(2)}) collective-permute-start(bf16[4,4,208,128]{3,2,1,0:T(8,128)(2,1)S(1)} %collective-permute-done.12.refs_5_), channel_id=1, source_target_pairs={{0,8},{1,9},{2,10},{3,11},{4,12},{5,13},{6,14},{7,15},{8,0},{9,1},... | collective-permute-start | bytes 2555912 | tf_op jit(solution)/shard_map/ppermute | solution.py:724
  273.9 14.1 %collective-permute-start.18 = (bf16[4,4,208,128]{3,2,1,0:T(8,128)(2,1)S(1)}, bf16[4,4,208,128]{3,2,1,0:T(8,128)(2,1)S(1)}, u32[]{:S(2)}, u32[]{:S(2)}) collective-permute-start(bf16[4,4,208,128]{3,2,1,0:T(8,128)(2,1)S(1)} %collective-permute-done.13.refs_6_), channel_id=1, source_target_pairs={{0,8},{1,9},{2,10},{3,11},{4,12},{5,13},{6,14},{7,15},{8,0},{9,1},... | collective-permute-start | bytes 2555912 | tf_op jit(solution)/shard_map/ppermute | solution.py:724
  281.4 6.6 %collective-permute-start.20 = (bf16[2,4,208,128]{3,2,1,0:T(8,128)(2,1)S(1)}, bf16[2,4,208,128]{3,2,1,0:T(8,128)(2,1)S(1)}, u32[]{:S(2)}, u32[]{:S(2)}) collective-permute-start(bf16[2,4,208,128]{3,2,1,0:T(8,128)(2,1)S(1)} %collective-permute-done.15.refs_8_), channel_id=1, source_target_pairs={{0,8},{1,9},{2,10},{3,11},{4,12},{5,13},{6,14},{7,15},{8,0},{9,1},... | collective-permute-start | bytes 1277960 | tf_op jit(solution)/shard_map/ppermute | solution.py:724
  283.2 4.8 %collective-permute-start.19 = (bf16[2,4,208,128]{3,2,1,0:T(8,128)(2,1)S(1)}, bf16[2,4,208,128]{3,2,1,0:T(8,128)(2,1)S(1)}, u32[]{:S(2)}, u32[]{:S(2)}) collective-permute-start(bf16[2,4,208,128]{3,2,1,0:T(8,128)(2,1)S(1)} %collective-permute-done.14.refs_7_), channel_id=1, source_target_pairs={{0,8},{1,9},{2,10},{3,11},{4,12},{5,13},{6,14},{7,15},{8,0},{9,1},... | collective-permute-start | bytes 1277960 | tf_op jit(solution)/shard_map/ppermute | solution.py:724
  (21 other events, 120.4 us)
Sparse Core Ops, SparseCore 0:
  11.1 99.5 all-gather.2
  128.7 112.7 reduce-scatter.1

commit v7 on v6

--- a/solution.py
+++ b/solution.py
@@ -540,12 +540,14 @@
 
 
 def combine_kernel(
+    place_ref,
     cot_ref,
     back_ref,
     pick_ref,
     gates_ref,
     mixed_ref,
     second_ref,
+    att_ref,
     routes_ref,
     gain_ref,
     wr_ref,
@@ -553,9 +555,11 @@
     out_ref,
     grad_mixed_ref,
     heads_ref,
-    small_ref,
+    keep_ref,
+    pass_ref,
     y_s,
     dx_s,
+    all_s,
 ):
     experts, both, width = back_ref.shape
     capacity = both // 2
@@ -593,39 +597,22 @@
         heads_ref[h] = jnp.concatenate([grad_att[:64, cols], grad_att[64:, cols]], axis=1)
     for h in range(heads, HEAD_SLOTS):
         heads_ref[h] = jnp.zeros_like(heads_ref[h])
-    small_ref[...] = jnp.concatenate([grad_router, jnp.broadcast_to(grad_gain, (8, width))], axis=0)
-
-
-def out_grad_kernel(place_ref, att_ref, grad_mixed_ref, small_ref, keep_ref, pass_ref, all_s):
-    grad_wo = dot(att_ref[...], grad_mixed_ref[...].astype(BF16), TN).astype(BF16)
-    slots, each, width = all_s.shape
+    small = jnp.concatenate([grad_router, jnp.broadcast_to(grad_gain, (8, width))], axis=0)
+    grad_wo = dot(att_ref[...], grad_branch, TN).astype(BF16)
+    slots, each, unused = all_s.shape
     used = width // each
     for c in range(used):
         all_s[c] = grad_wo[each * c : each * c + each]
     for c in range(used, slots):
         all_s[c] = jnp.zeros_like(all_s[c])
-    all_s[used, :16, :] = small_ref[...].astype(BF16)
+    all_s[used, :16, :] = small.astype(BF16)
     core = place_ref[3]
     for c in range(slots // 2):
         keep_ref[c] = all_s[2 * c + core]
         pass_ref[c] = all_s[2 * c + 1 - core]
 
 
-def out_grad(place, attended, grad_mixed, small):
-    width = attended.shape[1]
-    return pl.pallas_call(
-        out_grad_kernel,
-        name="out_grad",
-        cost_estimate=pl.CostEstimate(flops=500000000, bytes_accessed=4000000, transcendentals=0),
-        out_shape=(jax.ShapeDtypeStruct((HEAD_SLOTS // 2, 64, width), BF16),) * 2,
-        in_specs=[sspec()] + [vspec()] * 3,
-        out_specs=(vspec(),) * 2,
-        scratch_shapes=[pltpu.VMEM((HEAD_SLOTS, 64, width), BF16)],
-        compiler_params=whole(),
-    )(place, attended, grad_mixed, small)
-
-
-def combine(cotangent, back, picks, gates, mixed, second, routes, gain_two, w_router, w_out):
+def combine(place, cotangent, back, picks, gates, mixed, second, attended, routes, gain_two, w_router, w_out):
     rows, width = cotangent.shape
     experts, both, unused = back.shape
     held = experts * both // 2
@@ -637,19 +624,26 @@
             jax.ShapeDtypeStruct((rows, width), BF16),
             jax.ShapeDtypeStruct((rows, width), F32),
             jax.ShapeDtypeStruct((HEAD_SLOTS, rows // 2, 128), BF16),
-            jax.ShapeDtypeStruct((16, width), F32),
-        ),
-        in_specs=[vspec()] * 10,
-        out_specs=(vspec(),) * 4,
-        scratch_shapes=[pltpu.VMEM((held, width), BF16), pltpu.VMEM((held, width), BF16)],
+            jax.ShapeDtypeStruct((HEAD_SLOTS // 2, 64, width), BF16),
+            jax.ShapeDtypeStruct((HEAD_SLOTS // 2, 64, width), BF16),
+        ),
+        in_specs=[sspec()] + [vspec()] * 11,
+        out_specs=(vspec(),) * 5,
+        scratch_shapes=[
+            pltpu.VMEM((held, width), BF16),
+            pltpu.VMEM((held, width), BF16),
+            pltpu.VMEM((HEAD_SLOTS, 64, width), BF16),
+        ],
         compiler_params=whole(),
     )(
+        place,
         cotangent,
         back,
         picks,
         gates,
         mixed,
         second,
+        attended,
         routes,
         gain_two,
         w_router,
@@ -711,7 +705,7 @@
     return jnp.stack([block] + [lax.ppermute(block, AXES, shifted(dim, -by)) for by in (1, 2, 3)])
 
 
-def gather_last(filled, beside):
+def gather_last(filled, beside, work):
     half = filled.shape[0] // 2
     ahead = lax.ppermute(filled, AXES, shifted(1, -1))
     behind = lax.ppermute(filled, AXES, shifted(1, 1))
@@ -720,6 +714,8 @@
         lax.ppermute(ahead[:half], AXES, shifted(1, -1)),
         lax.ppermute(behind[half:], AXES, shifted(1, 1)),
     )
+    across, done = lax.optimization_barrier((across, work(beside[0])))
+    beside = (done,) + tuple(beside[1:])
     mine = (filled, ahead, behind) + across
     other = tuple(lax.ppermute(part, AXES, shifted(3, 1)) for part in mine)
     return mine + other, beside
@@ -912,10 +908,9 @@
     normed_mine, returned = lax.optimization_barrier((normed_mine, returned))
     normed_other = lax.ppermute(normed_mine, AXES, shifted(3, 1))
     own_grads = lax.psum_scatter(weight_grads, "context", scatter_dimension=0, tiled=False)
-    block_out, grad_mixed, grad_heads, small = combine(
-        grad_out, returned, picks, gates, mixed, second, routes_here, gain_two, w_router, w_out
-    )
-    keep_sums, pass_sums = out_grad(place, attended, grad_mixed, small)
+    block_out, grad_mixed, grad_heads, keep_sums, pass_sums = combine(
+        place, grad_out, returned, picks, gates, mixed, second, attended, routes_here, gain_two, w_router, w_out
+    )
     other_sums = lax.ppermute(pass_sums, AXES, shifted(3, 1))
     sums = (keep_sums.astype(F32) + other_sums.astype(F32)).astype(BF16)
     grad_here = lax.all_to_all(grad_heads, "context", split_axis=0, concat_axis=0, tiled=True)
@@ -932,10 +927,11 @@
     grads = lax.all_to_all(dqkv, "context", split_axis=0, concat_axis=0, tiled=True)
     own_grads = own_grads.astype(F32)
     hidden = own_grads.shape[0] // 2
-    parts, (grads, grad_in, grad_back) = gather_last(
-        filled, (grads, own_grads[:hidden], own_grads[hidden:])
-    )
-    grad_tokens = input_grad(inputs, gain_one, grads, w_query, w_key, w_value, grad_mixed)
+    parts, (grad_tokens, grad_in, grad_back) = gather_last(
+        filled,
+        (grads, own_grads[:hidden], own_grads[hidden:]),
+        lambda here: input_grad(inputs, gain_one, here, w_query, w_key, w_value, grad_mixed),
+    )
 
     dwq, dwk, dwv, dwo, bias, small, router, gain_grad = unpack(
         place, parts, w_query, w_key, w_value, heads, buckets, experts

time: 313 us -> 309 us (0.987)
    ppermute x1, waiting for transfers between devices: 7.46 us -> 2.47 us  [gather_last(): lax.ppermute(behind[half:], AXES, shifted(1, 1))]
    all_to_all x1, starting transfers between devices: 11.6 us -> 6.83 us  [shards(): lax.all_to_all(dqkv, 'context', split_axis=0, concat_axis=0, tiled=True)]
    ppermute x9, waiting for transfers between devices: 26.2 us -> 30.7 us  [direct_gather(): lax.ppermute(block, AXES, shifted(dim, -by))]
    all_to_all x1, waiting for transfers between devices: 3.45 us -> 0.01 us  [shards(): lax.all_to_all(sums, 'context', split_axis=0, concat_axis=0, axis_index_g...]
    unnamed x48 -> x50, local copies, waits for them, and re-layouts: 7.97 us -> 7.83 us
  transfers between devices with their start and end apart: 30 -> 30, of which waited for: 15 -> 18; matrix products, arithmetic and copies ran while one was open for 3% -> 3% of each run, Pallas kernels for 15% -> 14%
where the time goes in v7:
time: 309 us; the launch traced here: 307 us
  waiting for transfers between devices  120 us (39%)
  Pallas kernels  73.1 us (24%)
  starting transfers between devices  65.4 us (21%)
  blocking collectives  14.9 us (5%)
  between operations  14.3 us (5%)
  local copies, waits for them, and re-layouts  11.2 us (4%)
  other arithmetic  8.74 us (3%)
    ppermute x9, waiting for transfers between devices, direct_gather(): lax.ppermute(block, AXES, shifted(dim, -by))  30.7 us
    ppermute x1, waiting for transfers between devices, shards(): normed_two = jnp.stack([normed, lax.ppermute(normed, AXES, shifted(0, 2))])  27.6 us
    all_to_all x1, waiting for transfers between devices, shards(): lax.all_to_all(packed, 'context', split_axis=0, concat_axis=0, tiled=True)  19.6 us
    pallas_call x1, Pallas kernels, expert_both(): pl.pallas_call(expert_kernel, name='expert_both', cost_estimate=pl.CostEs...  17.9 us
    all_to_all x1, blocking collectives, shards(): lax.all_to_all(terms, 'expert', split_axis=0, concat_axis=0, tiled=True)  14.9 us
    ppermute x9, starting transfers between devices, direct_gather(): lax.ppermute(block, AXES, shifted(dim, -by))  14.5 us
    pallas_call x1, Pallas kernels, attend_back(): pl.pallas_call(lambda *refs: attend_back_kernel(rel_table.shape[1], *refs...  12.6 us
    all_to_all x1, waiting for transfers between devices, shards(): lax.all_to_all(dqkv, 'context', split_axis=0, concat_axis=0, tiled=True)  12.1 us
  transfers between devices with their start and end apart: 30, of which 18 were waited for; matrix products, arithmetic and copies ran while one was open for 3% of the time, Pallas kernels for 14%

profile of v7, /device:TPU:1, one launch (start us, length us, event | category | flops | bytes accessed | tf_op | source)
XLA Modules:
  0.0 307.4 jit_solution(17513883674550692839)
XLA Ops:
  7.2 1.9 pad_maximum_fusion.2
  9.2 3.7 %project.1 = (bf16[128,768]{1,0:T(8,128)(2,1)}, bf16[16,192,128]{2,1,0:T(8,128)(2,1)}) custom-call(bf16[128,768]{1,0:T(8,128)(2,1)} %bitcast.44, f32[768]{0:T(1024)} %gain_ref.5, bf16[768,768]{1,0:T(8,128)(2,1)} %refs_1_.5, bf16[768,768]{1,0:T(8,128)(2,1)} %refs_2_.1, bf16[768,768]{1,0:T(8,128)(2,1)} %refs_3_.3), custom_call_target="tpu_custom_call" | custom-call | flops 500000000 | bytes 6000000 | tf_op jit(solution)/shard_map/project/pallas_call | solution.py:82
  12.9 9.3 %all-to-all-start = ((bf16[16,192,128]{2,1,0:T(8,128)(2,1)}), bf16[16,192,128]{2,1,0:T(8,128)(2,1)S(1)}, u32[]{:S(2)}, u32[]{:S(2)}) async-start(bf16[16,192,128]{2,1,0:T(8,128)(2,1)} %get-tuple-element.60), calls=%async_computation | async-start | bytes 1572864 | tf_op jit(solution)/shard_map/all_to_all | solution.py:892
  22.2 19.6 %all-to-all-done.refs_2_ = bf16[16,192,128]{2,1,0:T(8,128)(2,1)S(1)} async-done(((bf16[16,192,128]{2,1,0:T(8,128)(2,1)}), bf16[16,192,128]{2,1,0:T(8,128)(2,1)S(1)}, u32[]{:S(2)}, u32[]{:S(2)}) %all-to-all-start) | async-done | bytes 786464 | tf_op jit(solution)/shard_map/all_to_all | solution.py:892
  42.6 7.0 %attend.1 = (bf16[16,64,128]{2,1,0:T(8,128)(2,1)}, f32[16,64,128]{2,1,0:T(8,128)}, f32[8,8,256]{2,1,0:T(8,128)}) custom-call(s32[1]{0:T(128)} %bitcast.8.refs_0_, f32[12,32]{1,0:T(8,128)} %refs_1_.4, bf16[16,192,128]{2,1,0:T(8,128)(2,1)} %copy-done.11), custom_call_target="tpu_custom_call" | custom-call | flops 7000000000 | bytes 3000000 | tf_op jit(solution)/shard_map/attend/pallas_call | solution.py:171
  49.7 5.2 %all-to-all-start.1 = ((bf16[16,64,128]{2,1,0:T(8,128)(2,1)}), bf16[16,64,128]{2,1,0:T(8,128)(2,1)S(1)}, u32[]{:S(2)}, u32[]{:S(2)}) async-start(bf16[16,64,128]{2,1,0:T(8,128)(2,1)} %get-tuple-element.63), calls=%async_computation.1 | async-start | bytes 524288 | tf_op jit(solution)/shard_map/all_to_all | solution.py:899
  56.4 8.8 %all-to-all-done.1.refs_2_ = bf16[16,64,128]{2,1,0:T(8,128)(2,1)S(1)} async-done(((bf16[16,64,128]{2,1,0:T(8,128)(2,1)}), bf16[16,64,128]{2,1,0:T(8,128)(2,1)S(1)}, u32[]{:S(2)}, u32[]{:S(2)}) %all-to-all-start.1) | async-done | bytes 262176 | tf_op jit(solution)/shard_map/all_to_all | solution.py:899
  65.9 3.9 %dispatch.1 = (bf16[8,96,768]{2,1,0:T(8,128)(2,1)}, bf16[128,768]{1,0:T(8,128)(2,1)}, f32[128,768]{1,0:T(8,128)}, bf16[128,768]{1,0:T(8,128)(2,1)}, bf16[2,128,384]{2,1,0:T(8,128)(2,1)}, /*index=5*/f32[128,128]{1,0:T(8,128)}) custom-call(bf16[128,768]{1,0:T(8,128)(2,1)} %bitcast.45, bf16[128,768]{1,0:T(8,128)(2,1)} %bitcast.48, ...), custom_call_target="tpu_custom_call" | custom-call | flops 500000000 | bytes 4000000 | tf_op jit(solution)/shard_map/dispatch/pallas_call | solution.py:453
  69.9 5.8 %all-to-all-start.2 = ((bf16[8,96,768]{2,1,0:T(8,128)(2,1)}), bf16[8,96,768]{2,1,0:T(8,128)(2,1)S(1)}, u32[]{:S(2)}, u32[]{:S(2)}) async-start(bf16[8,96,768]{2,1,0:T(8,128)(2,1)} %get-tuple-element.64), calls=%async_computation.2 | async-start | bytes 2359296 | tf_op jit(solution)/shard_map/all_to_all | solution.py:903
  75.8 27.6 %collective-permute-done = bf16[128,768]{1,0:T(8,128)(2,1)S(1)} collective-permute-done((bf16[128,768]{1,0:T(8,128)(2,1)S(1)}, bf16[128,768]{1,0:T(8,128)(2,1)S(1)}, u32[]{:S(2)}, u32[]{:S(2)}) %collective-permute-start) | collective-permute-done | bytes 196640 | tf_op jit(solution)/shard_map/ppermute | solution.py:896
  103.5 7.2 %all-gather.3.cloned.1.call-done = bf16[6144,768]{1,0:T(8,128)(2,1)} async-done(((bf16[384,768]{1,0:T(8,128)(2,1)}), bf16[6144,768]{1,0:T(8,128)(2,1)}) %all-gather.3.cloned.1.call-update) | async-done | bytes 9437200 | tf_op jit(solution)/shard_map/all_gather | solution.py:890
  110.7 17.9 %expert_both.1 = (bf16[8,96,768]{2,1,0:T(8,128)(2,1)}, bf16[16,384,768]{2,1,0:T(8,128)(2,1)}) custom-call(bf16[8,96,768]{2,1,0:T(8,128)(2,1)} %copy-done.6, bf16[16,384,768]{2,1,0:T(8,128)(2,1)} %bitcast.69), custom_call_target="tpu_custom_call" | custom-call | flops 17999998976 | bytes 22000000 | tf_op jit(solution)/shard_map/expert_both/pallas_call | solution.py:515
  128.6 4.5 %all-to-all-start.3 = ((bf16[8,96,768]{2,1,0:T(8,128)(2,1)}), bf16[8,96,768]{2,1,0:T(8,128)(2,1)S(1)}, u32[]{:S(2)}, u32[]{:S(2)}) async-start(bf16[8,96,768]{2,1,0:T(8,128)(2,1)} %get-tuple-element.68), calls=%async_computation.3 | async-start | bytes 2359296 | tf_op jit(solution)/shard_map/all_to_all | solution.py:907
  136.9 7.9 %collective-permute-done.3 = bf16[2,128,768]{2,1,0:T(8,128)(2,1)S(1)} collective-permute-done((bf16[2,128,768]{2,1,0:T(8,128)(2,1)S(1)}, bf16[2,128,768]{2,1,0:T(8,128)(2,1)S(1)}, u32[]{:S(2)}, u32[]{:S(2)}) %collective-permute-start.3) | collective-permute-done | bytes 393248 | tf_op jit(solution)/shard_map/ppermute | solution.py:705
  144.8 7.8 %collective-permute-done.2 = bf16[2,128,768]{2,1,0:T(8,128)(2,1)S(1)} collective-permute-done((bf16[2,128,768]{2,1,0:T(8,128)(2,1)S(1)}, bf16[2,128,768]{2,1,0:T(8,128)(2,1)S(1)}, u32[]{:S(2)}, u32[]{:S(2)}) %collective-permute-start.2) | collective-permute-done | bytes 393248 | tf_op jit(solution)/shard_map/ppermute | solution.py:705
  156.5 5.4 %combine.1 = (bf16[128,768]{1,0:T(8,128)(2,1)}, f32[128,768]{1,0:T(8,128)}, bf16[16,64,128]{2,1,0:T(8,128)(2,1)}, bf16[8,64,768]{2,1,0:T(8,128)(2,1)}, bf16[8,64,768]{2,1,0:T(8,128)(2,1)}) custom-call(s32[4]{0:T(128)} %pad_add_fusion.place_ref.refs_0_, bf16[128,768]{1,0:T(8,128)(2,1)} %bitcast.49, bf16[8,96,768]{2,1,0:T(8,128)(2,1)} %copy-done, ...), custom_call_target="tpu_custom_call" | custom-call | flops 1000000000 | bytes 5000000 | tf_op jit(solution)/shard_map/combine/pallas_call | solution.py:619
  163.4 4.0 %all-to-all-start.4 = ((bf16[16,64,128]{2,1,0:T(8,128)(2,1)}), bf16[16,64,128]{2,1,0:T(8,128)(2,1)S(1)}, u32[]{:S(2)}, u32[]{:S(2)}) async-start(bf16[16,64,128]{2,1,0:T(8,128)(2,1)} %get-tuple-element.78), calls=%async_computation.4 | async-start | bytes 524288 | tf_op jit(solution)/shard_map/all_to_all | solution.py:916
  167.6 2.2 add_convert_fusion
  169.8 9.2 %all-to-all-done.4.refs_3_ = bf16[16,64,128]{2,1,0:T(8,128)(2,1)S(1)} async-done(((bf16[16,64,128]{2,1,0:T(8,128)(2,1)}), bf16[16,64,128]{2,1,0:T(8,128)(2,1)S(1)}, u32[]{:S(2)}, u32[]{:S(2)}) %all-to-all-start.4) | async-done | bytes 262176 | tf_op jit(solution)/shard_map/all_to_all | solution.py:916
  179.0 3.5 %all-to-all-start.5 = ((bf16[8,64,768]{2,1,0:T(8,128)(2,1)}), bf16[8,64,768]{2,1,0:T(8,128)(2,1)S(1)}, u32[]{:S(2)}, u32[]{:S(2)}) async-start(bf16[8,64,768]{2,1,0:T(8,128)(2,1)} %add_convert_fusion), calls=%async_computation.5 | async-start | bytes 1572864 | tf_op jit(solution)/shard_map/all_to_all | solution.py:919
  182.6 12.6 %attend_back.1 = (bf16[16,192,128]{2,1,0:T(8,128)(2,1)}, f32[16,128]{1,0:T(8,128)}) custom-call(s32[1]{0:T(128)} %bitcast.8.refs_0_, f32[12,32]{1,0:T(8,128)} %refs_1_.4, bf16[16,192,128]{2,1,0:T(8,128)(2,1)} %copy-done.11, bf16[16,64,128]{2,1,0:T(8,128)(2,1)} %copy-done.19, f32[16,64,128]{2,1,0:T(8,128)} %get-tuple-element.80.refs_4_, ...), custom_call_target="tpu_custom_call" | custom-call | flops 14000000000 | bytes 4000000 | tf_op jit(solution)/shard_map/attend_back/pallas_call | solution.py:302
  196.1 4.5 %head_grads.1 = bf16[8,208,128]{2,1,0:T(8,128)(2,1)} custom-call(s32[4]{0:T(128)} %pad_add_fusion.place_ref.refs_0_, bf16[16,192,128]{2,1,0:T(8,128)(2,1)} %get-tuple-element.87.dqkv_ref, bf16[4,2,128,768]{3,2,1,0:T(8,128)(2,1)} %copy-done.5, bf16[4,2,128,768]{3,2,1,0:T(8,128)(2,1)} %collective-permute-done.5.other_ref, ...), custom_call_target="tpu_custom_call" | custom-call | flops 3000000000 | bytes 8000000 | tf_op jit(solution)/shard_map/head_grads/pallas_call | solution.py:374
  200.5 14.9 %all_to_all.40.in_ref = bf16[8,208,128]{2,1,0:T(8,128)(2,1)} all-to-all(bf16[8,208,128]{2,1,0:T(8,128)(2,1)} %head_grads.1), channel_id=1, replica_groups=mesh['context'=16,'expert'=8] {'expert'}, dimensions={0} | all-to-all | bytes 851968 | tf_op jit(solution)/shard_map/all_to_all | solution.py:925
  224.2 6.1 %collective-permute-start.10 = (bf16[4,208,128]{2,1,0:T(8,128)(2,1)S(1)}, bf16[4,208,128]{2,1,0:T(8,128)(2,1)S(1)}, u32[]{:S(2)}, u32[]{:S(2)}) collective-permute-start(bf16[4,208,128]{2,1,0:T(8,128)(2,1)S(1)} %get-tuple-element.109), channel_id=1, source_target_pairs={{0,64},{1,65},{2,66},{3,67},{4,68},{5,69},{6,70},{7,71},{8,72},{9,... | collective-permute-start | bytes 638984 | tf_op jit(solution)/shard_map/ppermute | solution.py:705
  231.9 6.5 %collective-permute-done.10 = bf16[4,208,128]{2,1,0:T(8,128)(2,1)S(1)} collective-permute-done((bf16[4,208,128]{2,1,0:T(8,128)(2,1)S(1)}, bf16[4,208,128]{2,1,0:T(8,128)(2,1)S(1)}, u32[]{:S(2)}, u32[]{:S(2)}) %collective-permute-start.10) | collective-permute-done | bytes 213024 | tf_op jit(solution)/shard_map/ppermute | solution.py:705
  238.3 3.5 %collective-permute-done.9 = bf16[4,208,128]{2,1,0:T(8,128)(2,1)S(1)} collective-permute-done((bf16[4,208,128]{2,1,0:T(8,128)(2,1)S(1)}, bf16[4,208,128]{2,1,0:T(8,128)(2,1)S(1)}, u32[]{:S(2)}, u32[]{:S(2)}) %collective-permute-start.9) | collective-permute-done | bytes 213024 | tf_op jit(solution)/shard_map/ppermute | solution.py:705
  246.9 6.8 %all-to-all-start.7 = ((bf16[16,192,128]{2,1,0:T(8,128)(2,1)}), bf16[16,192,128]{2,1,0:T(8,128)(2,1)S(1)}, u32[]{:S(2)}, u32[]{:S(2)}) async-start(bf16[16,192,128]{2,1,0:T(8,128)(2,1)} %get-tuple-element.87.dqkv_ref), calls=%async_computation.7 | async-start | bytes 1572864 | tf_op jit(solution)/shard_map/all_to_all | solution.py:927
  256.0 12.1 %all-to-all-done.7.grads_ref = bf16[16,192,128]{2,1,0:T(8,128)(2,1)S(1)} async-done(((bf16[16,192,128]{2,1,0:T(8,128)(2,1)}), bf16[16,192,128]{2,1,0:T(8,128)(2,1)S(1)}, u32[]{:S(2)}, u32[]{:S(2)}) %all-to-all-start.7) | async-done | bytes 786464 | tf_op jit(solution)/shard_map/all_to_all | solution.py:927
  268.3 2.7 collective-permute-start.14
  272.9 4.6 %input_grad.1 = f32[128,768]{1,0:T(8,128)} custom-call(bf16[128,768]{1,0:T(8,128)(2,1)} %bitcast.46, f32[768]{0:T(1024)} %gain_ref.5, bf16[16,192,128]{2,1,0:T(8,128)(2,1)} %copy-done.2, bf16[768,768]{1,0:T(8,128)(2,1)} %refs_1_.5, bf16[768,768]{1,0:T(8,128)(2,1)} %refs_2_.1, bf16[768,768]{1,0:T(8,128)(2,1)} %refs_3_.3, f32[128,768]{1,0:T(8,128)} %get-tuple-element.92.mixed_ref), custom_call_target="tpu_custom_call" | custom-call | flops 500000000 | bytes 5000000 | tf_op jit(solution)/shard_map/input_grad/pallas_call | solution.py:671
  277.5 2.5 collective-permute-done.15.refs_8_
  285.8 11.9 %unpack.1 = (f32[768,768]{1,0:T(8,128)}, f32[768,768]{1,0:T(8,128)}, f32[768,768]{1,0:T(8,128)}, f32[12,8,8,768]{3,2,1,0:T(8,128)}, f32[12,32]{1,0:T(8,128)}, /*...) custom-call(s32[4]{0:T(128)} %pad_add_fusion.place_ref.refs_0_, bf16[768,768]{1,0:T(8,128)(2,1)} %refs_1_.5, ...), custom_call_target="tpu_custom_call" | custom-call | flops 1000000000 | bytes 24000000 | tf_op jit(solution)/shard_map/unpack/pallas_call | solution.py:815
  (106 shorter events, 42.0 us)
Async XLA Ops:
  7.2 103.5 %all-gather.3.cloned.1.call-start = ((), (), s32[]{:S(2)}) async-start(), calls=%async_computation.10 | async-start | bytes 10027008 | tf_op jit(solution)/shard_map/all_gather | solution.py:890
  12.9 28.9 %all-to-all-start = ((bf16[16,192,128]{2,1,0:T(8,128)(2,1)}), bf16[16,192,128]{2,1,0:T(8,128)(2,1)S(1)}, u32[]{:S(2)}, u32[]{:S(2)}) async-start(bf16[16,192,128]{2,1,0:T(8,128)(2,1)} %get-tuple-element.60), calls=%async_computation | async-start | bytes 1572864 | tf_op jit(solution)/shard_map/all_to_all | solution.py:892
  49.7 15.6 %all-to-all-start.1 = ((bf16[16,64,128]{2,1,0:T(8,128)(2,1)}), bf16[16,64,128]{2,1,0:T(8,128)(2,1)S(1)}, u32[]{:S(2)}, u32[]{:S(2)}) async-start(bf16[16,64,128]{2,1,0:T(8,128)(2,1)} %get-tuple-element.63), calls=%async_computation.1 | async-start | bytes 524288 | tf_op jit(solution)/shard_map/all_to_all | solution.py:899
  69.9 33.6 %all-to-all-start.2 = ((bf16[8,96,768]{2,1,0:T(8,128)(2,1)}), bf16[8,96,768]{2,1,0:T(8,128)(2,1)S(1)}, u32[]{:S(2)}, u32[]{:S(2)}) async-start(bf16[8,96,768]{2,1,0:T(8,128)(2,1)} %get-tuple-element.64), calls=%async_computation.2 | async-start | bytes 2359296 | tf_op jit(solution)/shard_map/all_to_all | solution.py:903
  75.7 178.1 %reduce-scatter.2.cloned.1.call-start = ((), (), s32[]{:S(2)}) async-start(), calls=%async_computation.9 | async-start | bytes 10027008 | tf_op jit(solution)/shard_map/reduce_scatter | solution.py:910
  75.7 27.7 %collective-permute-start = (bf16[128,768]{1,0:T(8,128)(2,1)S(1)}, bf16[128,768]{1,0:T(8,128)(2,1)S(1)}, u32[]{:S(2)}, u32[]{:S(2)}) collective-permute-start(bf16[128,768]{1,0:T(8,128)(2,1)S(1)} %copy-done.20), channel_id=1, source_target_pairs={{0,64},{1,65},{2,66},{3,67},{4,68},{5,69},{6,70},{7,71},{8,72},{9,... | collective-permute-start | bytes 589832 | tf_op jit(solution)/shard_map/ppermute | solution.py:896
  128.6 26.8 %all-to-all-start.3 = ((bf16[8,96,768]{2,1,0:T(8,128)(2,1)}), bf16[8,96,768]{2,1,0:T(8,128)(2,1)S(1)}, u32[]{:S(2)}, u32[]{:S(2)}) async-start(bf16[8,96,768]{2,1,0:T(8,128)(2,1)} %get-tuple-element.68), calls=%async_computation.3 | async-start | bytes 2359296 | tf_op jit(solution)/shard_map/all_to_all | solution.py:907
  133.1 11.7 %collective-permute-start.3 = (bf16[2,128,768]{2,1,0:T(8,128)(2,1)S(1)}, bf16[2,128,768]{2,1,0:T(8,128)(2,1)S(1)}, u32[]{:S(2)}, u32[]{:S(2)}) collective-permute-start(bf16[2,128,768]{2,1,0:T(8,128)(2,1)S(1)} %pad_maximum_fusion.3), channel_id=1, source_target_pairs={{0,16},{1,17},{2,18},{3,19},{4,20},{5,21},{6,22},{7,23},{8,24},{9,... | collective-permute-start | bytes 1179656 | tf_op jit(solution)/shard_map/ppermute | solution.py:705
  133.6 19.0 %collective-permute-start.2 = (bf16[2,128,768]{2,1,0:T(8,128)(2,1)S(1)}, bf16[2,128,768]{2,1,0:T(8,128)(2,1)S(1)}, u32[]{:S(2)}, u32[]{:S(2)}) collective-permute-start(bf16[2,128,768]{2,1,0:T(8,128)(2,1)S(1)} %pad_maximum_fusion.3), channel_id=1, source_target_pairs={{0,32},{1,33},{2,34},{3,35},{4,36},{5,37},{6,38},{7,39},{8,40},{9,... | collective-permute-start | bytes 1179656 | tf_op jit(solution)/shard_map/ppermute | solution.py:705
  135.4 17.9 %collective-permute-start.1 = (bf16[2,128,768]{2,1,0:T(8,128)(2,1)S(1)}, bf16[2,128,768]{2,1,0:T(8,128)(2,1)S(1)}, u32[]{:S(2)}, u32[]{:S(2)}) collective-permute-start(bf16[2,128,768]{2,1,0:T(8,128)(2,1)S(1)} %pad_maximum_fusion.3), channel_id=1, source_target_pairs={{0,48},{1,49},{2,50},{3,51},{4,52},{5,53},{6,54},{7,55},{8,56},{9,... | collective-permute-start | bytes 1179656 | tf_op jit(solution)/shard_map/ppermute | solution.py:705
  155.4 39.8 %copy-start.5 = (bf16[4,2,128,768]{3,2,1,0:T(8,128)(2,1)}, bf16[4,2,128,768]{3,2,1,0:T(8,128)(2,1)S(1)}, u32[]{:S(2)}) copy-start(bf16[4,2,128,768]{3,2,1,0:T(8,128)(2,1)S(1)} %pad_maximum_fusion.mine_ref) | copy-start | bytes 4718596
  161.9 5.8 %collective-permute-start.4 = (bf16[8,64,768]{2,1,0:T(8,128)(2,1)}, bf16[8,64,768]{2,1,0:T(8,128)(2,1)S(1)}, u32[]{:S(2)}, u32[]{:S(2)}) collective-permute-start(bf16[8,64,768]{2,1,0:T(8,128)(2,1)} %get-tuple-element.77), channel_id=1, source_target_pairs={{0,8},{1,9},{2,10},{3,11},{4,12},{5,13},{6,14},{7,15},{8,0},{9,1},... | collective-permute-start | bytes 2359304 | tf_op jit(solution)/shard_map/ppermute | solution.py:914
  163.4 15.6 %all-to-all-start.4 = ((bf16[16,64,128]{2,1,0:T(8,128)(2,1)}), bf16[16,64,128]{2,1,0:T(8,128)(2,1)S(1)}, u32[]{:S(2)}, u32[]{:S(2)}) async-start(bf16[16,64,128]{2,1,0:T(8,128)(2,1)} %get-tuple-element.78), calls=%async_computation.4 | async-start | bytes 524288 | tf_op jit(solution)/shard_map/all_to_all | solution.py:916
  167.5 27.7 %collective-permute-start.5 = (bf16[4,2,128,768]{3,2,1,0:T(8,128)(2,1)S(1)}, bf16[4,2,128,768]{3,2,1,0:T(8,128)(2,1)}, u32[]{:S(2)}, u32[]{:S(2)}) collective-permute-start(bf16[4,2,128,768]{3,2,1,0:T(8,128)(2,1)S(1)} %pad_maximum_fusion.mine_ref), channel_id=1, source_target_pairs={{0,8},{1,9},{2,10},{3,11},{4,12},{5,13},{6,14},{7,15},{8,0},{9,1},... | collective-permute-start | bytes 4718600 | tf_op jit(solution)/shard_map/ppermute | solution.py:909
  179.0 16.1 %all-to-all-start.5 = ((bf16[8,64,768]{2,1,0:T(8,128)(2,1)}), bf16[8,64,768]{2,1,0:T(8,128)(2,1)S(1)}, u32[]{:S(2)}, u32[]{:S(2)}) async-start(bf16[8,64,768]{2,1,0:T(8,128)(2,1)} %add_convert_fusion), calls=%async_computation.5 | async-start | bytes 1572864 | tf_op jit(solution)/shard_map/all_to_all | solution.py:919
  217.2 4.4 %collective-permute-start.8 = (bf16[208,128]{1,0:T(8,128)(2,1)}, bf16[208,128]{1,0:T(8,128)(2,1)S(1)}, u32[]{:S(2)}, u32[]{:S(2)}) collective-permute-start(bf16[208,128]{1,0:T(8,128)(2,1)} %add_up.1), channel_id=1, source_target_pairs={{0,16},{1,17},{2,18},{3,19},{4,20},{5,21},{6,22},{7,23},{8,24},{9,... | collective-permute-start | bytes 159752 | tf_op jit(solution)/shard_map/ppermute | solution.py:705
  218.5 4.7 %collective-permute-start.7 = (bf16[208,128]{1,0:T(8,128)(2,1)}, bf16[208,128]{1,0:T(8,128)(2,1)S(1)}, u32[]{:S(2)}, u32[]{:S(2)}) collective-permute-start(bf16[208,128]{1,0:T(8,128)(2,1)} %add_up.1), channel_id=1, source_target_pairs={{0,32},{1,33},{2,34},{3,35},{4,36},{5,37},{6,38},{7,39},{8,40},{9,... | collective-permute-start | bytes 159752 | tf_op jit(solution)/shard_map/ppermute | solution.py:705
  220.2 3.2 %collective-permute-start.6 = (bf16[208,128]{1,0:T(8,128)(2,1)}, bf16[208,128]{1,0:T(8,128)(2,1)S(1)}, u32[]{:S(2)}, u32[]{:S(2)}) collective-permute-start(bf16[208,128]{1,0:T(8,128)(2,1)} %add_up.1), channel_id=1, source_target_pairs={{0,48},{1,49},{2,50},{3,51},{4,52},{5,53},{6,54},{7,55},{8,56},{9,... | collective-permute-start | bytes 159752 | tf_op jit(solution)/shard_map/ppermute | solution.py:705
  224.2 14.1 %collective-permute-start.10 = (bf16[4,208,128]{2,1,0:T(8,128)(2,1)S(1)}, bf16[4,208,128]{2,1,0:T(8,128)(2,1)S(1)}, u32[]{:S(2)}, u32[]{:S(2)}) collective-permute-start(bf16[4,208,128]{2,1,0:T(8,128)(2,1)S(1)} %get-tuple-element.109), channel_id=1, source_target_pairs={{0,64},{1,65},{2,66},{3,67},{4,68},{5,69},{6,70},{7,71},{8,72},{9,... | collective-permute-start | bytes 638984 | tf_op jit(solution)/shard_map/ppermute | solution.py:705
  230.4 11.4 %collective-permute-start.9 = (bf16[4,208,128]{2,1,0:T(8,128)(2,1)S(1)}, bf16[4,208,128]{2,1,0:T(8,128)(2,1)S(1)}, u32[]{:S(2)}, u32[]{:S(2)}) collective-permute-start(bf16[4,208,128]{2,1,0:T(8,128)(2,1)S(1)} %get-tuple-element.109), channel_id=1, source_target_pairs={{0,65},{1,0},{2,67},{3,2},{4,69},{5,4},{6,71},{7,6},{8,73},{9,8},{... | collective-permute-start | bytes 638984 | tf_op jit(solution)/shard_map/ppermute | solution.py:705
  230.4 13.2 %collective-permute-start.11 = (bf16[4,208,128]{2,1,0:T(8,128)(2,1)S(1)}, bf16[4,208,128]{2,1,0:T(8,128)(2,1)S(1)}, u32[]{:S(2)}, u32[]{:S(2)}) collective-permute-start(bf16[4,208,128]{2,1,0:T(8,128)(2,1)S(1)} %get-tuple-element.109), channel_id=1, source_target_pairs={{0,1},{1,64},{2,3},{3,66},{4,5},{5,68},{6,7},{7,70},{8,9},{9,72},{... | collective-permute-start | bytes 638984 | tf_op jit(solution)/shard_map/ppermute | solution.py:705
  243.7 27.3 %copy-start.1 = (bf16[4,4,208,128]{3,2,1,0:T(8,128)(2,1)}, bf16[4,4,208,128]{3,2,1,0:T(8,128)(2,1)S(1)}, u32[]{:S(2)}) copy-start(bf16[4,4,208,128]{3,2,1,0:T(8,128)(2,1)S(1)} %pad_maximum_fusion.1.refs_4_) | copy-start | bytes 2555908
  243.7 24.5 %collective-permute-start.13 = (bf16[4,4,208,128]{3,2,1,0:T(8,128)(2,1)S(1)}, bf16[4,4,208,128]{3,2,1,0:T(8,128)(2,1)S(1)}, u32[]{:S(2)}, u32[]{:S(2)}) collective-permute-start(bf16[4,4,208,128]{3,2,1,0:T(8,128)(2,1)S(1)} %pad_maximum_fusion.1.refs_4_), channel_id=1, source_target_pairs={{0,2},{1,3},{2,4},{3,5},{4,6},{5,7},{6,0},{7,1},{8,10},{9,11},{10,... | collective-permute-start | bytes 2555912 | tf_op jit(solution)/shard_map/ppermute | solution.py:711
  245.4 22.8 %collective-permute-start.12 = (bf16[4,4,208,128]{3,2,1,0:T(8,128)(2,1)S(1)}, bf16[4,4,208,128]{3,2,1,0:T(8,128)(2,1)S(1)}, u32[]{:S(2)}, u32[]{:S(2)}) collective-permute-start(bf16[4,4,208,128]{3,2,1,0:T(8,128)(2,1)S(1)} %pad_maximum_fusion.1.refs_4_), channel_id=1, source_target_pairs={{0,6},{1,7},{2,0},{3,1},{4,2},{5,3},{6,4},{7,5},{8,14},{9,15},{10,... | collective-permute-start | bytes 2555912 | tf_op jit(solution)/shard_map/ppermute | solution.py:710
  246.9 21.2 %all-to-all-start.7 = ((bf16[16,192,128]{2,1,0:T(8,128)(2,1)}), bf16[16,192,128]{2,1,0:T(8,128)(2,1)S(1)}, u32[]{:S(2)}, u32[]{:S(2)}) async-start(bf16[16,192,128]{2,1,0:T(8,128)(2,1)} %get-tuple-element.87.dqkv_ref), calls=%async_computation.7 | async-start | bytes 1572864 | tf_op jit(solution)/shard_map/all_to_all | solution.py:927
  268.2 11.7 %collective-permute-start.15 = (bf16[2,4,208,128]{3,2,1,0:T(8,128)(2,1)S(1)}, bf16[2,4,208,128]{3,2,1,0:T(8,128)(2,1)S(1)}, u32[]{:S(2)}, u32[]{:S(2)}) collective-permute-start(bf16[2,4,208,128]{3,2,1,0:T(8,128)(2,1)S(1)} %slice.29), channel_id=1, source_target_pairs={{0,2},{1,3},{2,4},{3,5},{4,6},{5,7},{6,0},{7,1},{8,10},{9,11},{10,... | collective-permute-start | bytes 1277960 | tf_op jit(solution)/shard_map/ppermute | solution.py:715
  268.3 11.7 %collective-permute-start.14 = (bf16[2,4,208,128]{3,2,1,0:T(8,128)(2,1)S(1)}, bf16[2,4,208,128]{3,2,1,0:T(8,128)(2,1)S(1)}, u32[]{:S(2)}, u32[]{:S(2)}) collective-permute-start(bf16[2,4,208,128]{3,2,1,0:T(8,128)(2,1)S(1)} %slice.28), channel_id=1, source_target_pairs={{0,6},{1,7},{2,0},{3,1},{4,2},{5,3},{6,4},{7,5},{8,14},{9,15},{10,... | collective-permute-start | bytes 1277960 | tf_op jit(solution)/shard_map/ppermute | solution.py:714
  271.0 10.9 %collective-permute-start.16 = (bf16[4,4,208,128]{3,2,1,0:T(8,128)(2,1)S(1)}, bf16[4,4,208,128]{3,2,1,0:T(8,128)(2,1)S(1)}, u32[]{:S(2)}, u32[]{:S(2)}) collective-permute-start(bf16[4,4,208,128]{3,2,1,0:T(8,128)(2,1)S(1)} %pad_maximum_fusion.1.refs_4_), channel_id=1, source_target_pairs={{0,8},{1,9},{2,10},{3,11},{4,12},{5,13},{6,14},{7,15},{8,0},{9,1},... | collective-permute-start | bytes 2555912 | tf_op jit(solution)/shard_map/ppermute | solution.py:720
  272.4 11.4 %collective-permute-start.17 = (bf16[4,4,208,128]{3,2,1,0:T(8,128)(2,1)S(1)}, bf16[4,4,208,128]{3,2,1,0:T(8,128)(2,1)S(1)}, u32[]{:S(2)}, u32[]{:S(2)}) collective-permute-start(bf16[4,4,208,128]{3,2,1,0:T(8,128)(2,1)S(1)} %collective-permute-done.12.refs_5_), channel_id=1, source_target_pairs={{0,8},{1,9},{2,10},{3,11},{4,12},{5,13},{6,14},{7,15},{8,0},{9,1},... | collective-permute-start | bytes 2555912 | tf_op jit(solution)/shard_map/ppermute | solution.py:720
  272.4 11.4 %collective-permute-start.18 = (bf16[4,4,208,128]{3,2,1,0:T(8,128)(2,1)S(1)}, bf16[4,4,208,128]{3,2,1,0:T(8,128)(2,1)S(1)}, u32[]{:S(2)}, u32[]{:S(2)}) collective-permute-start(bf16[4,4,208,128]{3,2,1,0:T(8,128)(2,1)S(1)} %collective-permute-done.13.refs_6_), channel_id=1, source_target_pairs={{0,8},{1,9},{2,10},{3,11},{4,12},{5,13},{6,14},{7,15},{8,0},{9,1},... | collective-permute-start | bytes 2555912 | tf_op jit(solution)/shard_map/ppermute | solution.py:720
  280.0 3.2 %collective-permute-start.19 = (bf16[2,4,208,128]{3,2,1,0:T(8,128)(2,1)S(1)}, bf16[2,4,208,128]{3,2,1,0:T(8,128)(2,1)S(1)}, u32[]{:S(2)}, u32[]{:S(2)}) collective-permute-start(bf16[2,4,208,128]{3,2,1,0:T(8,128)(2,1)S(1)} %collective-permute-done.14.refs_7_), channel_id=1, source_target_pairs={{0,8},{1,9},{2,10},{3,11},{4,12},{5,13},{6,14},{7,15},{8,0},{9,1},... | collective-permute-start | bytes 1277960 | tf_op jit(solution)/shard_map/ppermute | solution.py:720
  281.8 2.0 collective-permute-start.20
  (22 other events, 104.6 us)
Sparse Core Ops, SparseCore 0:
  11.1 99.5 all-gather.2
  128.7 119.1 reduce-scatter.1
